TPU v7x, 32 devices: a whole 2x2x4 slice. The times are simulated.
32 devices in a mesh: dom: 16 (over z, y, core), feat: 2 (over x).
Axes of the slice: x: 2, y: 2, z: 4, core: 2. Of those that a mesh axis runs over, the one named last changes fastest.
Arguments:
- node_features: bfloat16 [16384, 128], P('dom'), may hold values from -6 to 6
- weight: bfloat16 [128, 256], P(None, 'feat'), may hold values from -0.5 to 0.5
- bias: float32 [256], P('feat'), may hold values from -3 to 3
- tile_values: bfloat16 [1536, 128, 128], P('dom')
- tile_src: int32 [1536], P('dom'), may hold values from 0 to 7
- tile_dst: int32 [1536], P('dom'), may hold values from 0 to 31, as said below
- tile_counts: int32 [16], P('dom'), may hold values from 4 to 96
- out_grad: bfloat16 [16384, 256], P('dom', 'feat'), may hold values from -6 to 6
Outputs:
- output: bfloat16 [16384, 256], P('dom', 'feat')
- weight_grad: float32 [128, 256], P(None, 'feat')
- bias_grad: float32 [256], P('feat')
- input_grad: bfloat16 [16384, 128], P('dom', 'feat')
Inputs may be any that keep to these rules, and one draw needn't show every extreme that they name: The partition offset tile_dst[k] // 8 of slot k of a partition equals k mod 4.
All inputs are finite; a program needn't handle non-finite values.
Results may differ from a plain program's by a relative error of at most 0.0075.
Values may be sent and summed in bfloat16 or wider, within the bound.
No kernel may reach another device: no remote copies, remote signals or barrier semaphores. Data moves between devices by JAX's collectives and lax.ppermute only.
A program may use at most 64 MiB of HBM per device.

v0:
```python
import functools

import jax
import jax.numpy as jnp
from jax import lax
from jax.experimental import pallas as pl
from jax.experimental.pallas import tpu as pltpu
from jax.sharding import PartitionSpec as P

BLOCK = 128
REACH = 4
SUM_FLOPS = 10**9
SRC_UNIT = 2**16
F32 = jnp.float32
BF16 = jnp.bfloat16
VMEM = pl.BlockSpec(memory_space=pltpu.VMEM)
SMEM = pl.BlockSpec(memory_space=pltpu.SMEM)
HBM = pl.BlockSpec(memory_space=pltpu.HBM)


def call(kernel, out_shape, in_specs, out_specs, scratch=(), flops=0):
    return pl.pallas_call(
        kernel,
        out_shape=out_shape,
        in_specs=in_specs,
        out_specs=out_specs,
        scratch_shapes=list(scratch),
        compiler_params=pltpu.CompilerParams(vmem_limit_bytes=24 * 1024 * 1024),
        cost_estimate=pl.CostEstimate(flops=flops, bytes_accessed=2**20, transcendentals=0),
    )


def groups_at_once(groups):
    return next(m for m in (12, 8, 6, 4, 3, 2, 1) if groups % m == 0)


def in_hbm(a):
    return pltpu.with_memory_space_constraint(a, pltpu.HBM)


def own_core():
    return lax.rem(lax.axis_index("dom"), 2)


def slot_loop(count, groups, body):
    m = groups_at_once(groups)
    pair = 2 if m % 2 == 0 else 1

    def chunk(i, carry):
        @pl.when(i * (m * REACH) < count)
        def _():
            for u in range(0, m, pair):
                body([i * m + u + v for v in range(pair)])

        return carry

    lax.fori_loop(0, groups // m, chunk, 0)


def side_by_side(lefts, tiles, contract):
    if len(tiles) == 1:
        left, right = lefts[0], tiles[0]
    else:
        left = jnp.concatenate(lefts, axis=1)
        none = jnp.zeros_like(tiles[0])
        right = jnp.concatenate(
            [jnp.concatenate([tiles[0], none], axis=1), jnp.concatenate([none, tiles[1]], axis=1)], axis=0
        )
    out = lax.dot_general(left, right, (((1,), (contract,)), ((), ())), preferred_element_type=F32)
    return [out[:, i * BLOCK : (i + 1) * BLOCK] for i in range(len(tiles))]


def source(entry):
    return lax.shift_right_logical(entry, 16)


def target(entry, o, blocks):
    return lax.bitwise_and(entry, SRC_UNIT - 1) - o * blocks


def push(xt, tiles, index, count, acc, js, o):
    blocks = xt.shape[0]
    ks = [j * REACH + o for j in js]
    outs = side_by_side([xt[source(index[k])] for k in ks], [tiles[j] for j in js], 1)
    for k, out in zip(ks, outs):
        acc[jnp.where(k < count, target(index[k], o, blocks), blocks)] += out


def pull(block, tiles, index, count, acc, js, o):
    blocks = acc.shape[0] - 1
    ks = [j * REACH + o for j in js]
    outs = side_by_side([block(target(index[k], o, blocks)) for k in ks], [tiles[j] for j in js], 0)
    for k, out in zip(ks, outs):
        acc[jnp.where(k < count, source(index[k]), blocks)] += out


def push_all(xt, index, count, *planes):
    def body(js):
        for tiles, acc, o in planes:
            push(xt, tiles, index, count, acc, js, o)

    slot_loop(count, planes[0][0].shape[0], body)


def pull_all(index, count, *planes):
    def body(js):
        for block, tiles, acc, o in planes:
            pull(block, tiles, index, count, acc, js, o)

    slot_loop(count, planes[0][1].shape[0], body)


def forward_swap_kernel(
    count, src_hbm, dst_hbm, x_hbm, tiles_hbm, tiles1, tiles2, tiles3, xt, swap, index, src, dst, x, acc, sems
):
    blocks, width, _ = xt.shape
    o = 3 - 2 * own_core()
    loads = [
        pltpu.make_async_copy(a, b, sems.at[i])
        for i, (a, b) in enumerate(
            (
                (src_hbm, src),
                (dst_hbm, dst),
                (x_hbm, x),
                (tiles_hbm.at[:, o], tiles1),
                (tiles_hbm.at[:, 2], tiles2),
                (tiles_hbm.at[:, 4 - o], tiles3),
            )
        )
    ]
    for c in loads:
        c.start()
    acc[...] = jnp.zeros_like(acc)
    row = lax.broadcasted_iota(jnp.int32, (width, x.shape[1]), 0)
    column = lax.broadcasted_iota(jnp.int32, (width, x.shape[1]), 1)
    pick = (column == row + lax.axis_index("feat") * width).astype(BF16)
    for c in loads[:2]:
        c.wait()
    for k in range(src.shape[0]):
        index[k] = src[k] * SRC_UNIT + dst[k]
    loads[2].wait()
    for b in range(blocks):
        xt[b] = lax.dot_general(
            pick, x[b * BLOCK : (b + 1) * BLOCK, :], (((1,), (1,)), ((), ())), preferred_element_type=F32
        ).astype(BF16)
    loads[3].wait()
    push_all(xt, index, count[0], (tiles1, acc, o))
    swap[...] = acc[:blocks].astype(BF16)
    for c in loads[4:]:
        c.wait()


def forward_send_kernel(count, index, xt, tiles2, tiles3, acc2, direct, acc):
    acc2[...] = jnp.zeros_like(acc2)
    acc[...] = jnp.zeros_like(acc)
    push_all(xt, index, count[0], (tiles2, acc2, 2), (tiles3, acc, 1 + 2 * own_core()))
    direct[...] = acc[: direct.shape[0]].astype(BF16)


def forward_own_kernel(count, index, xt, tiles_hbm, acc, tiles0, sem):
    load = pltpu.make_async_copy(tiles_hbm.at[:, 0], tiles0, sem)
    load.start()
    acc[...] = jnp.zeros_like(acc)
    load.wait()
    push_all(xt, index, count[0], (tiles0, acc, 0))


def sum_kernel(n, first, *refs):
    for out in refs[n:]:
        blocks = out.shape[0]
        total = None
        for r in refs[:n]:
            part = r[...] if r.shape[0] == blocks else r[first : first + blocks]
            total = part.astype(F32) if total is None else total + part.astype(F32)
        out[...] = total.astype(out.dtype)
        first += blocks


def join_kernel(parts, *refs):
    out = refs[-1]
    halves = [refs[i : i + parts] for i in range(0, len(refs) - 1, parts)]
    first = 0
    for half in halves:
        blocks = half[0].shape[0]
        total = half[0][...].astype(F32)
        for r in half[1:]:
            total = total + r[...].astype(F32)
        out[first : first + blocks] = total.astype(out.dtype)
        first += blocks


def middle_kernel(parts, first, bias_ref, w_ref, og_ref, *refs):
    h_refs, (act, ht, grads), g_refs = refs[:parts], refs[parts : parts + 3], refs[parts + 3 :]
    blocks, width, _ = h_refs[0].shape
    f_in = w_ref.shape[0]
    me = lax.axis_index("feat")
    for q in range(parts):
        row = pl.multiple_of(lax.rem(me + q, parts) * width, width)
        for b in range(blocks):
            ht[pl.ds(row, width), b * BLOCK : (b + 1) * BLOCK] = h_refs[q][b]
    ht[f_in:, :] = jnp.ones((ht.shape[0] - f_in, ht.shape[1]), BF16)
    for b in range(blocks):
        rows = slice(b * BLOCK, (b + 1) * BLOCK)
        pre = lax.dot_general(
            ht[:f_in, rows], w_ref[...], (((0,), (0,)), ((), ())), preferred_element_type=F32
        ) + bias_ref[...]
        s = jax.nn.sigmoid(pre)
        act[rows, :] = (pre * s).astype(BF16)
        og = og_ref[(first + b) * BLOCK : (first + b + 1) * BLOCK, :].astype(F32)
        grad = (og * s * (1.0 + pre * (1.0 - s))).astype(BF16)
        grads[rows, :] = grad
        for q in range(parts):
            row = pl.multiple_of(lax.rem(me + q, parts) * width, width)
            g_refs[q][b] = lax.dot_general(
                w_ref[pl.ds(row, width), :], grad, (((1,), (1,)), ((), ())), preferred_element_type=F32
            ).astype(g_refs[q].dtype)


def weight_grad_kernel(n, *refs):
    hts, grads, (mine, other) = refs[:n], refs[n : 2 * n], refs[2 * n :]
    full = sum(jnp.dot(h[...], g[...], preferred_element_type=F32) for h, g in zip(hts, grads))
    full = full.astype(BF16)
    rows = mine.shape[0]
    low, high = full[:rows], full[rows:]
    first = own_core() == 0
    mine[...] = jnp.where(first, low, high)
    other[...] = jnp.where(first, high, low)


def swap_payload_kernel(g, *refs):
    parts, out = refs[:-1], refs[-1]
    blocks, width, _ = g.shape
    for b in range(blocks):
        out[b * width : (b + 1) * width, :] = g[b]
    total = paired_sum([r[...] for r in parts]).astype(BF16)
    rows, hid = total.shape
    if hid < out.shape[1]:
        out[blocks * width :, :] = jnp.zeros((rows, out.shape[1]), BF16)
    out[blocks * width :, :hid] = total


def backward_own_kernel(count, index, tiles, g, *refs):
    acts, (acc, out, sems) = refs[:-3], refs[-3:]
    copies, first = [], 0
    for i, act in enumerate(acts):
        rows = act.shape[0]
        copies.append(pltpu.make_async_copy(act, out.at[pl.ds(first, rows)], sems.at[i]))
        copies[-1].start()
        first += rows
    acc[...] = jnp.zeros_like(acc)
    pull_all(index, count[0], (lambda d: g[d], tiles, acc, 0))
    for c in copies:
        c.wait()


def backward_near_kernel(count, index, tiles2, tiles3, g2, g3, acc2, acc3):
    acc2[...] = jnp.zeros_like(acc2)
    acc3[...] = jnp.zeros_like(acc3)
    pull_all(
        index,
        count[0],
        (lambda d: g2[d], tiles2, acc2, 2),
        (lambda d: g3[d], tiles3, acc3, 1 + 2 * own_core()),
    )


def backward_last_kernel(count, index, tiles, sent, got, acc0, acc2, accd, out, wg, bias, acc):
    blocks, width = acc.shape[0] - 1, acc.shape[1]
    f_in, hid = wg.shape
    acc[...] = jnp.zeros_like(acc)
    core = own_core()

    def block(d):
        return got[pl.ds(pl.multiple_of(d * width, width), width), :]

    pull_all(index, count[0], (block, tiles, acc, 3 - 2 * core))
    for b in range(blocks):
        total = acc[b] + acc0[b] + acc2[b] + accd[b]
        out[:, b * BLOCK : (b + 1) * BLOCK] = total.astype(BF16)
    a, b = (r[blocks * width :, :hid].astype(F32) for r in (sent, got))
    low, high = jnp.where(core == 0, a, b), jnp.where(core == 0, b, a)
    rows = low.shape[0]
    wg[:rows, :] = low
    wg[rows:, :] = high[: f_in - rows]
    bias[...] = high[f_in - rows : f_in - rows + 1]


def paired_sum(parts):
    parts = [p.astype(F32) for p in parts]
    while len(parts) > 1:
        parts = [parts[i] + parts[i + 1] for i in range(0, len(parts), 2)]
    return parts[0]


def paired_sum_kernel(*refs):
    refs[-1][...] = paired_sum([r[...] for r in refs[:-1]]).astype(refs[-1].dtype)


def moved(block, axis, target):
    n = lax.axis_size(axis)
    return lax.ppermute(block, axis, [(i, target(i) % n) for i in range(n)])


def radices(n):
    out = []
    while n > 1:
        r = 4 if n % 4 == 0 else 2
        out.append(r)
        n //= r
    return out


def exchanged(part, axis, stride, r):
    return [part] + [moved(part, axis, lambda i, s=s: i ^ (s * stride)) for s in range(1, r)]


def shards(node_features, weight, bias, tile_values, tile_src, tile_dst, tile_counts, out_grad):
    nodes, f_in = node_features.shape
    hid = weight.shape[1]
    blocks = nodes // BLOCK
    parts = lax.axis_size("feat")
    width = f_in // parts
    capacity = tile_values.shape[0]
    groups = capacity // REACH
    piece = jax.ShapeDtypeStruct((blocks, width, BLOCK), BF16)
    totals = jax.ShapeDtypeStruct((blocks + 1, width, BLOCK), F32)
    acc = pltpu.VMEM(totals.shape, F32)
    tiles = tile_values.reshape(groups, REACH, BLOCK, BLOCK)
    plane = jax.ShapeDtypeStruct((groups, BLOCK, BLOCK), BF16)
    slots = jax.ShapeDtypeStruct((capacity,), jnp.int32)
    rows = jax.ShapeDtypeStruct((nodes, hid), BF16)
    gradient = jax.ShapeDtypeStruct(((f_in + 32) // 2, hid), BF16)
    flops = 2 * capacity * BLOCK * BLOCK * width // REACH

    def swapped(i):
        return i ^ 1

    tiles1, tiles2, tiles3, xt, swap, index = call(
        forward_swap_kernel,
        [plane, plane, plane, piece, piece, slots],
        [SMEM] + [HBM] * 4,
        [VMEM] * 5 + [SMEM],
        [
            pltpu.SMEM((capacity,), jnp.int32),
            pltpu.SMEM((capacity,), jnp.int32),
            pltpu.VMEM(node_features.shape, BF16),
            acc,
            pltpu.SemaphoreType.DMA((6,)),
        ],
        flops,
    )(tile_counts, *(in_hbm(a) for a in (tile_src, tile_dst, node_features, tiles)))
    index = (tile_counts, index)
    swap = moved(swap, "dom", swapped)
    acc2, direct = call(
        forward_send_kernel, [totals, piece], [SMEM] * 2 + [VMEM] * 3, [VMEM] * 2, [acc], 2 * flops
    )(*index, xt, tiles2, tiles3)
    cut = 2 if blocks % 2 == 0 else 1
    starts = range(0, blocks, blocks // cut)
    half = jax.ShapeDtypeStruct((blocks // cut, width, BLOCK), BF16)
    half_wide = jax.ShapeDtypeStruct(half.shape, F32)
    half_rows = jax.ShapeDtypeStruct((nodes // cut, hid), BF16)
    half_columns = jax.ShapeDtypeStruct((f_in + 32, nodes // cut), BF16)
    chip = call(functools.partial(sum_kernel, 2, 0), [half] * cut, [VMEM] * 2, [VMEM] * cut)(acc2, swap)
    chip = [moved(c, "dom", lambda i: i + 2) for c in chip]
    direct = moved(direct, "dom", lambda i: i + 1 + 2 * (i % 2))
    acc0, tiles0 = call(
        forward_own_kernel,
        [totals, plane],
        [SMEM] * 2 + [VMEM, HBM],
        [VMEM] * 2,
        [pltpu.SemaphoreType.DMA],
        flops,
    )(*index, xt, in_hbm(tiles))
    h_lists = []
    for first, c in zip(starts, chip):
        (h,) = call(functools.partial(sum_kernel, 3, first), [half], [VMEM] * 3, [VMEM])(acc0, direct, c)
        h_lists.append([h] + [moved(h, "feat", lambda i, q=q: i - q) for q in range(1, parts)])
    acts, hts, grads, g_list = [], [], [], []
    for first, hs in zip(starts, h_lists):
        act, ht, grad, g_own, *g_others = call(
            functools.partial(middle_kernel, parts, first),
            [half_rows, half_columns, half_rows, half_wide] + [half] * (parts - 1),
            [VMEM] * (3 + parts),
            [VMEM] * (3 + parts),
            (),
            4 * nodes * f_in * hid // cut,
        )(bias.reshape(1, hid), weight, out_grad, *hs)
        acts.append(act)
        hts.append(ht)
        grads.append(grad)
        g_list += [g_own] + [moved(g, "feat", lambda i, q=q + 1: i + q) for q, g in enumerate(g_others)]
    wg, wg_other = call(
        functools.partial(weight_grad_kernel, cut),
        [gradient, gradient],
        [VMEM] * (2 * cut),
        [VMEM, VMEM],
        (),
        2 * nodes * f_in * hid,
    )(*hts, *grads)
    r, *more = radices(lax.axis_size("dom"))
    wgs = [wg] + [moved(wg_other if s % 2 else wg, "dom", lambda i, s=s: i ^ s) for s in range(1, r)]
    (g,) = call(functools.partial(join_kernel, parts), [piece], [VMEM] * len(g_list), [VMEM])(*g_list)
    g_chip = moved(g, "dom", lambda i: i - 2)
    g_direct = moved(g, "dom", lambda i: i - 3 + 2 * (i % 2))
    stride = r
    for r in more:
        (wg,) = call(paired_sum_kernel, [gradient], [VMEM] * len(wgs), [VMEM], (), SUM_FLOPS)(*wgs)
        wgs = exchanged(wg, "dom", stride, r)
        stride *= r
    back0, output = call(
        backward_own_kernel,
        [totals, rows],
        [SMEM] * 2 + [VMEM] * (2 + cut),
        [VMEM, HBM],
        [pltpu.SemaphoreType.DMA((cut,))],
        flops,
    )(*index, tiles0, g, *acts)
    g_direct, g_chip, back0, *wgs = lax.optimization_barrier((g_direct, g_chip, back0, *wgs))
    payload = jax.ShapeDtypeStruct((blocks * width + gradient.shape[0], BLOCK), BF16)
    (sent,) = call(swap_payload_kernel, [payload], [VMEM] * (1 + len(wgs)), [VMEM])(g_chip, *wgs)
    got = moved(sent, "dom", swapped)
    back2, backd = call(
        backward_near_kernel, [totals, totals], [SMEM] * 2 + [VMEM] * 4, [VMEM] * 2, (), 2 * flops
    )(*index, tiles2, tiles3, g_chip, g_direct)
    input_grad, weight_grad, bias_grad = call(
        backward_last_kernel,
        [
            jax.ShapeDtypeStruct((width, nodes), BF16),
            jax.ShapeDtypeStruct((f_in, hid), F32),
            jax.ShapeDtypeStruct((1, hid), F32),
        ],
        [SMEM] * 2 + [VMEM] * 6,
        [VMEM] * 3,
        [acc],
        flops,
    )(*index, tiles1, sent, got, back0, back2, backd)
    return output, weight_grad, bias_grad.reshape(hid), input_grad.T


def solution(mesh):
    return jax.shard_map(
        shards,
        mesh=mesh,
        in_specs=(
            P("dom", None),
            P(None, "feat"),
            P("feat"),
            P("dom", None, None),
            P("dom"),
            P("dom"),
            P("dom"),
            P("dom", "feat"),
        ),
        out_specs=(P("dom", "feat"), P(None, "feat"), P("feat"), P("dom", "feat")),
        check_vma=False,
    )
```

profile of v0, /device:TPU:0, one launch (start us, length us, event | category | flops | bytes accessed | tf_op | source)
XLA Modules:
  0.0 39.1 jit_solution(3752274531060792566)
XLA Ops:
  1.3 2.3 %shard_map.111 = (bf16[24,128,128]{2,1,0:T(8,128)(2,1)S(1)}, bf16[24,128,128]{2,1,0:T(8,128)(2,1)S(1)}, bf16[24,128,128]{2,1,0:T(8,128)(2,1)S(1)}, bf16[8,64,128...) custom-call(s32[1]{0:T(128)S(6)} %copy.12.count, s32[96]{0:T(128)} %src_hbm.1, s32[96]{0:T(128)} %dst_hbm.1, ...), custom_call_target="tpu_custom_call" | custom-call | flops 50331648 | bytes 1048576 | tf_op jit(solution)/shard_map/pallas_call | solution.py:338
  3.6 0.5 %collective-permute-start.1 = (bf16[8,64,128]{2,1,0:T(8,128)(2,1)S(1)}, bf16[8,64,128]{2,1,0:T(8,128)(2,1)S(1)}, u32[]{:S(2)}, u32[]{:S(2)}) collective-permute-start(bf16[8,64,128]{2,1,0:T(8,128)(2,1)S(1)} %get-tuple-element.50), channel_id=1, source_target_pairs={{0,2},{2,0},{4,6},{6,4},{8,10},{10,8},{12,14},{14,12},{16,18},{18,... | collective-permute-start | bytes 393224 | tf_op jit(solution)/shard_map/ppermute | solution.py:301
  4.2 1.2 %shard_map.113 = (f32[9,64,128]{2,1,0:T(8,128)S(1)}, bf16[8,64,128]{2,1,0:T(8,128)(2,1)S(1)}) custom-call(s32[1]{0:T(128)S(6)} %copy.12.count, s32[96]{0:T(128)S(1)} %get-tuple-element.42.index, bf16[8,64,128]{2,1,0:T(8,128)(2,1)S(1)} %get-tuple-element.43.xt, bf16[24,128,128]{2,1,0:T(8,128)(2,1)S(1)} %get-tuple-element.46.tiles2, ...), custom_call_target="tpu_custom_call" | custom-call | flops 100663296 | bytes 1048576 | tf_op jit(solution)/shard_map/pallas_call | solution.py:354
  5.5 3.6 %collective-permute-start.5 = (bf16[4,64,128]{2,1,0:T(8,128)(2,1)S(1)}, bf16[4,64,128]{2,1,0:T(8,128)(2,1)S(1)}, u32[]{:S(2)}, u32[]{:S(2)}) collective-permute-start(bf16[4,64,128]{2,1,0:T(8,128)(2,1)S(1)} %get-tuple-element.54), channel_id=1, source_target_pairs={{0,4},{2,6},{4,8},{6,10},{8,12},{10,14},{12,16},{14,18},{16,20},{1... | collective-permute-start | bytes 196616 | tf_op jit(solution)/shard_map/ppermute | solution.py:301
  9.1 1.4 %collective-permute-start.2 = (bf16[4,64,128]{2,1,0:T(8,128)(2,1)S(1)}, bf16[4,64,128]{2,1,0:T(8,128)(2,1)S(1)}, u32[]{:S(2)}, u32[]{:S(2)}) collective-permute-start(bf16[4,64,128]{2,1,0:T(8,128)(2,1)S(1)} %get-tuple-element.51), channel_id=1, source_target_pairs={{0,4},{2,6},{4,8},{6,10},{8,12},{10,14},{12,16},{14,18},{16,20},{1... | collective-permute-start | bytes 196616 | tf_op jit(solution)/shard_map/ppermute | solution.py:301
  10.5 2.1 %shard_map.112 = (f32[9,64,128]{2,1,0:T(8,128)S(1)}, bf16[24,128,128]{2,1,0:T(8,128)(2,1)S(1)}) custom-call(s32[1]{0:T(128)S(6)} %copy.12.count, s32[96]{0:T(128)S(1)} %get-tuple-element.42.index, bf16[8,64,128]{2,1,0:T(8,128)(2,1)S(1)} %get-tuple-element.43.xt, bf16[24,4,128,128]{3,2,1,0:T(8,128)(2,1)} %bitcast.7), custom_call_target="tpu_custom_call" | custom-call | flops 50331648 | bytes 1048576 | tf_op jit(solution)/shard_map/pallas_call | solution.py:366
  12.8 2.6 %collective-permute-done.5.refs_2_ = bf16[4,64,128]{2,1,0:T(8,128)(2,1)S(1)} collective-permute-done((bf16[4,64,128]{2,1,0:T(8,128)(2,1)S(1)}, bf16[4,64,128]{2,1,0:T(8,128)(2,1)S(1)}, u32[]{:S(2)}, u32[]{:S(2)}) %collective-permute-start.5) | collective-permute-done | bytes 65568 | tf_op jit(solution)/shard_map/ppermute | solution.py:301
  15.4 1.6 %collective-permute-start.6 = (bf16[4,64,128]{2,1,0:T(8,128)(2,1)S(1)}, bf16[4,64,128]{2,1,0:T(8,128)(2,1)S(1)}, u32[]{:S(2)}, u32[]{:S(2)}) collective-permute-start(bf16[4,64,128]{2,1,0:T(8,128)(2,1)S(1)} %shard_map.117.refs_0_), channel_id=1, source_target_pairs={{0,1},{1,0},{2,3},{3,2},{4,5},{5,4},{6,7},{7,6},{8,9},{9,8},{10,11... | collective-permute-start | bytes 196616 | tf_op jit(solution)/shard_map/ppermute | solution.py:301
  17.0 1.4 %collective-permute-start.3 = (bf16[4,64,128]{2,1,0:T(8,128)(2,1)S(1)}, bf16[4,64,128]{2,1,0:T(8,128)(2,1)S(1)}, u32[]{:S(2)}, u32[]{:S(2)}) collective-permute-start(bf16[4,64,128]{2,1,0:T(8,128)(2,1)S(1)} %shard_map.115.refs_0_), channel_id=1, source_target_pairs={{0,1},{1,0},{2,3},{3,2},{4,5},{5,4},{6,7},{7,6},{8,9},{9,8},{10,11... | collective-permute-start | bytes 196616 | tf_op jit(solution)/shard_map/ppermute | solution.py:301
  18.4 1.7 %collective-permute-done.6.refs_1_ = bf16[4,64,128]{2,1,0:T(8,128)(2,1)S(1)} collective-permute-done((bf16[4,64,128]{2,1,0:T(8,128)(2,1)S(1)}, bf16[4,64,128]{2,1,0:T(8,128)(2,1)S(1)}, u32[]{:S(2)}, u32[]{:S(2)}) %collective-permute-start.6) | collective-permute-done | bytes 65568 | tf_op jit(solution)/shard_map/ppermute | solution.py:301
  20.1 0.9 %shard_map.118 = (bf16[512,128]{1,0:T(8,128)(2,1)S(1)}, bf16[160,512]{1,0:T(8,128)(2,1)S(1)}, bf16[512,128]{1,0:T(8,128)(2,1)S(1)}, f32[4,64,128]{2,1,0:T(8,128)S(1)}, bf16[4,64,128]{2,1,0:T(8,128)(2,1)S(1)}) custom-call(f32[1,128]{1,0:T(1,128)S(1)} %bitcast.4, bf16[128,128]{1,0:T(8,128)(2,1)S(1)} %copy-done.1, bf16[1024,128]{1,0:T(8,128)(2,1)S(1)} %copy-done, ...), custom_call_target="tpu_custom_call" | custom-call | flops 33554432 | bytes 1048576 | tf_op jit(solution)/shard_map/pallas_call | solution.py:380
  21.0 1.5 %collective-permute-start.7 = (bf16[4,64,128]{2,1,0:T(8,128)(2,1)S(1)}, bf16[4,64,128]{2,1,0:T(8,128)(2,1)S(1)}, u32[]{:S(2)}, u32[]{:S(2)}) collective-permute-start(bf16[4,64,128]{2,1,0:T(8,128)(2,1)S(1)} %get-tuple-element.56), channel_id=1, source_target_pairs={{0,1},{1,0},{2,3},{3,2},{4,5},{5,4},{6,7},{7,6},{8,9},{9,8},{10,11... | collective-permute-start | bytes 196616 | tf_op jit(solution)/shard_map/ppermute | solution.py:301
  22.5 0.9 %shard_map.116 = (bf16[512,128]{1,0:T(8,128)(2,1)S(1)}, bf16[160,512]{1,0:T(8,128)(2,1)S(1)}, bf16[512,128]{1,0:T(8,128)(2,1)S(1)}, f32[4,64,128]{2,1,0:T(8,128)S(1)}, bf16[4,64,128]{2,1,0:T(8,128)(2,1)S(1)}) custom-call(f32[1,128]{1,0:T(1,128)S(1)} %bitcast.5, bf16[128,128]{1,0:T(8,128)(2,1)S(1)} %copy-done.1, bf16[1024,128]{1,0:T(8,128)(2,1)S(1)} %copy-done, ...), custom_call_target="tpu_custom_call" | custom-call | flops 33554432 | bytes 1048576 | tf_op jit(solution)/shard_map/pallas_call | solution.py:380
  23.4 0.9 %collective-permute-start.4 = (bf16[4,64,128]{2,1,0:T(8,128)(2,1)S(1)}, bf16[4,64,128]{2,1,0:T(8,128)(2,1)S(1)}, u32[]{:S(2)}, u32[]{:S(2)}) collective-permute-start(bf16[4,64,128]{2,1,0:T(8,128)(2,1)S(1)} %get-tuple-element.53), channel_id=1, source_target_pairs={{0,1},{1,0},{2,3},{3,2},{4,5},{5,4},{6,7},{7,6},{8,9},{9,8},{10,11... | collective-permute-start | bytes 196616 | tf_op jit(solution)/shard_map/ppermute | solution.py:301
  25.0 0.8 %collective-permute-start.12 = (bf16[80,128]{1,0:T(8,128)(2,1)S(1)}, bf16[80,128]{1,0:T(8,128)(2,1)S(1)}, u32[]{:S(2)}, u32[]{:S(2)}) collective-permute-start(bf16[80,128]{1,0:T(8,128)(2,1)S(1)} %get-tuple-element.67), channel_id=1, source_target_pairs={{0,6},{2,4},{4,2},{6,0},{8,14},{10,12},{12,10},{14,8},{16,22},{18,... | collective-permute-start | bytes 61448 | tf_op jit(solution)/shard_map/ppermute | solution.py:301
  25.8 1.0 %collective-permute-start.10 = (bf16[80,128]{1,0:T(8,128)(2,1)S(1)}, bf16[80,128]{1,0:T(8,128)(2,1)S(1)}, u32[]{:S(2)}, u32[]{:S(2)}) collective-permute-start(bf16[80,128]{1,0:T(8,128)(2,1)S(1)} %get-tuple-element.67), channel_id=1, source_target_pairs={{0,2},{2,0},{4,6},{6,4},{8,10},{10,8},{12,14},{14,12},{16,18},{18,... | collective-permute-start | bytes 61448 | tf_op jit(solution)/shard_map/ppermute | solution.py:301
  26.7 1.0 %collective-permute-done.4.refs_1_ = bf16[4,64,128]{2,1,0:T(8,128)(2,1)S(1)} collective-permute-done((bf16[4,64,128]{2,1,0:T(8,128)(2,1)S(1)}, bf16[4,64,128]{2,1,0:T(8,128)(2,1)S(1)}, u32[]{:S(2)}, u32[]{:S(2)}) %collective-permute-start.4) | collective-permute-done | bytes 65568 | tf_op jit(solution)/shard_map/ppermute | solution.py:301
  27.7 1.8 %collective-permute-start.9 = (bf16[8,64,128]{2,1,0:T(8,128)(2,1)S(1)}, bf16[8,64,128]{2,1,0:T(8,128)(2,1)S(1)}, u32[]{:S(2)}, u32[]{:S(2)}) collective-permute-start(bf16[8,64,128]{2,1,0:T(8,128)(2,1)S(1)} %shard_map.119.g), channel_id=1, source_target_pairs={{0,28},{2,30},{4,0},{6,2},{8,4},{10,6},{12,8},{14,10},{16,12},{18,... | collective-permute-start | bytes 393224 | tf_op jit(solution)/shard_map/ppermute | solution.py:301
  29.6 1.3 %collective-permute-start.15 = (bf16[80,128]{1,0:T(8,128)(2,1)S(1)}, bf16[80,128]{1,0:T(8,128)(2,1)S(1)}, u32[]{:S(2)}, u32[]{:S(2)}) collective-permute-start(bf16[80,128]{1,0:T(8,128)(2,1)S(1)} %shard_map.122.refs_0_), channel_id=1, source_target_pairs={{0,24},{2,26},{4,28},{6,30},{8,16},{10,18},{12,20},{14,22},{16,8},... | collective-permute-start | bytes 61448 | tf_op jit(solution)/shard_map/ppermute | solution.py:301
  31.2 2.8 %collective-permute-start.13 = (bf16[80,128]{1,0:T(8,128)(2,1)S(1)}, bf16[80,128]{1,0:T(8,128)(2,1)S(1)}, u32[]{:S(2)}, u32[]{:S(2)}) collective-permute-start(bf16[80,128]{1,0:T(8,128)(2,1)S(1)} %shard_map.122.refs_0_), channel_id=1, source_target_pairs={{0,8},{2,10},{4,12},{6,14},{8,0},{10,2},{12,4},{14,6},{16,24},{18,... | collective-permute-start | bytes 61448 | tf_op jit(solution)/shard_map/ppermute | solution.py:301
  34.0 1.3 %shard_map.120 = (f32[9,64,128]{2,1,0:T(8,128)S(1)}, bf16[1024,128]{1,0:T(8,128)(2,1)}) custom-call(s32[1]{0:T(128)S(6)} %copy.12.count, s32[96]{0:T(128)S(1)} %get-tuple-element.42.index, bf16[24,128,128]{2,1,0:T(8,128)(2,1)S(1)} %get-tuple-element.44.tiles, bf16[8,64,128]{2,1,0:T(8,128)(2,1)S(1)} %shard_map.119.g, ...), custom_call_target="tpu_custom_call" | custom-call | flops 50331648 | bytes 1048576 | tf_op jit(solution)/shard_map/pallas_call | solution.py:410
  35.3 0.6 %collective-permute-done.15.refs_3_ = bf16[80,128]{1,0:T(8,128)(2,1)S(1)} collective-permute-done((bf16[80,128]{1,0:T(8,128)(2,1)S(1)}, bf16[80,128]{1,0:T(8,128)(2,1)S(1)}, u32[]{:S(2)}, u32[]{:S(2)}) %collective-permute-start.15) | collective-permute-done | bytes 20512 | tf_op jit(solution)/shard_map/ppermute | solution.py:301
  36.1 1.0 %shard_map.124 = (f32[9,64,128]{2,1,0:T(8,128)S(1)}, f32[9,64,128]{2,1,0:T(8,128)S(1)}) custom-call(s32[1]{0:T(128)S(6)} %copy.12.count, s32[96]{0:T(128)S(1)} %get-tuple-element.42.index, bf16[24,128,128]{2,1,0:T(8,128)(2,1)S(1)} %get-tuple-element.46.tiles2, bf16[24,128,128]{2,1,0:T(8,128)(2,1)S(1)} %get-tuple-element.47.tiles3, ...), custom_call_target="tpu_custom_call" | custom-call | flops 100663296 | bytes 1048576 | tf_op jit(solution)/shard_map/pallas_call | solution.py:422
  37.5 1.6 %shard_map.125 = (bf16[64,1024]{1,0:T(8,128)(2,1)}, f32[128,128]{1,0:T(8,128)}, f32[1,128]{1,0:T(1,128)}) custom-call(s32[1]{0:T(128)S(6)} %copy.12.count, s32[96]{0:T(128)S(1)} %get-tuple-element.42.index, bf16[24,128,128]{2,1,0:T(8,128)(2,1)S(1)} %get-tuple-element.60.tiles, bf16[592,128]{1,0:T(8,128)(2,1)S(1)} %shard_map.123.sent, ...), custom_call_target="tpu_custom_call" | custom-call | flops 50331648 | bytes 1048576 | tf_op jit(solution)/shard_map/pallas_call | solution.py:425
  (31 shorter events, 2.2 us)
Async XLA Ops:
  3.6 1.9 %collective-permute-start.1 = (bf16[8,64,128]{2,1,0:T(8,128)(2,1)S(1)}, bf16[8,64,128]{2,1,0:T(8,128)(2,1)S(1)}, u32[]{:S(2)}, u32[]{:S(2)}) collective-permute-start(bf16[8,64,128]{2,1,0:T(8,128)(2,1)S(1)} %get-tuple-element.50), channel_id=1, source_target_pairs={{0,2},{2,0},{4,6},{6,4},{8,10},{10,8},{12,14},{14,12},{16,18},{18,... | collective-permute-start | bytes 393224 | tf_op jit(solution)/shard_map/ppermute | solution.py:301
  4.2 15.9 %copy-start = (bf16[1024,128]{1,0:T(8,128)(2,1)S(1)}, bf16[1024,128]{1,0:T(8,128)(2,1)}, u32[]{:S(2)}) copy-start(bf16[1024,128]{1,0:T(8,128)(2,1)} %og_ref.3) | copy-start | bytes 786436
  4.2 15.9 %copy-start.1 = (bf16[128,128]{1,0:T(8,128)(2,1)S(1)}, bf16[128,128]{1,0:T(8,128)(2,1)}, u32[]{:S(2)}) copy-start(bf16[128,128]{1,0:T(8,128)(2,1)} %w_ref.3) | copy-start | bytes 98308
  4.2 15.9 %copy-start.2 = (f32[128]{0:T(128)S(1)}, f32[128]{0:T(128)}, u32[]{:S(2)}) copy-start(f32[128]{0:T(128)} %param.10) | copy-start | bytes 1540
  5.4 7.4 %collective-permute-start = (bf16[8,64,128]{2,1,0:T(8,128)(2,1)S(1)}, bf16[8,64,128]{2,1,0:T(8,128)(2,1)S(1)}, u32[]{:S(2)}, u32[]{:S(2)}) collective-permute-start(bf16[8,64,128]{2,1,0:T(8,128)(2,1)S(1)} %get-tuple-element.48), channel_id=1, source_target_pairs={{0,2},{2,8},{4,6},{6,12},{8,10},{10,16},{12,14},{14,20},{16,18},{1... | collective-permute-start | bytes 393224 | tf_op jit(solution)/shard_map/ppermute | solution.py:301
  5.5 9.9 %collective-permute-start.5 = (bf16[4,64,128]{2,1,0:T(8,128)(2,1)S(1)}, bf16[4,64,128]{2,1,0:T(8,128)(2,1)S(1)}, u32[]{:S(2)}, u32[]{:S(2)}) collective-permute-start(bf16[4,64,128]{2,1,0:T(8,128)(2,1)S(1)} %get-tuple-element.54), channel_id=1, source_target_pairs={{0,4},{2,6},{4,8},{6,10},{8,12},{10,14},{12,16},{14,18},{16,20},{1... | collective-permute-start | bytes 196616 | tf_op jit(solution)/shard_map/ppermute | solution.py:301
  9.1 7.9 %collective-permute-start.2 = (bf16[4,64,128]{2,1,0:T(8,128)(2,1)S(1)}, bf16[4,64,128]{2,1,0:T(8,128)(2,1)S(1)}, u32[]{:S(2)}, u32[]{:S(2)}) collective-permute-start(bf16[4,64,128]{2,1,0:T(8,128)(2,1)S(1)} %get-tuple-element.51), channel_id=1, source_target_pairs={{0,4},{2,6},{4,8},{6,10},{8,12},{10,14},{12,16},{14,18},{16,20},{1... | collective-permute-start | bytes 196616 | tf_op jit(solution)/shard_map/ppermute | solution.py:301
  15.4 4.6 %collective-permute-start.6 = (bf16[4,64,128]{2,1,0:T(8,128)(2,1)S(1)}, bf16[4,64,128]{2,1,0:T(8,128)(2,1)S(1)}, u32[]{:S(2)}, u32[]{:S(2)}) collective-permute-start(bf16[4,64,128]{2,1,0:T(8,128)(2,1)S(1)} %shard_map.117.refs_0_), channel_id=1, source_target_pairs={{0,1},{1,0},{2,3},{3,2},{4,5},{5,4},{6,7},{7,6},{8,9},{9,8},{10,11... | collective-permute-start | bytes 196616 | tf_op jit(solution)/shard_map/ppermute | solution.py:301
  17.0 5.5 %collective-permute-start.3 = (bf16[4,64,128]{2,1,0:T(8,128)(2,1)S(1)}, bf16[4,64,128]{2,1,0:T(8,128)(2,1)S(1)}, u32[]{:S(2)}, u32[]{:S(2)}) collective-permute-start(bf16[4,64,128]{2,1,0:T(8,128)(2,1)S(1)} %shard_map.115.refs_0_), channel_id=1, source_target_pairs={{0,1},{1,0},{2,3},{3,2},{4,5},{5,4},{6,7},{7,6},{8,9},{9,8},{10,11... | collective-permute-start | bytes 196616 | tf_op jit(solution)/shard_map/ppermute | solution.py:301
  21.0 5.7 %collective-permute-start.7 = (bf16[4,64,128]{2,1,0:T(8,128)(2,1)S(1)}, bf16[4,64,128]{2,1,0:T(8,128)(2,1)S(1)}, u32[]{:S(2)}, u32[]{:S(2)}) collective-permute-start(bf16[4,64,128]{2,1,0:T(8,128)(2,1)S(1)} %get-tuple-element.56), channel_id=1, source_target_pairs={{0,1},{1,0},{2,3},{3,2},{4,5},{5,4},{6,7},{7,6},{8,9},{9,8},{10,11... | collective-permute-start | bytes 196616 | tf_op jit(solution)/shard_map/ppermute | solution.py:301
  23.4 4.3 %collective-permute-start.4 = (bf16[4,64,128]{2,1,0:T(8,128)(2,1)S(1)}, bf16[4,64,128]{2,1,0:T(8,128)(2,1)S(1)}, u32[]{:S(2)}, u32[]{:S(2)}) collective-permute-start(bf16[4,64,128]{2,1,0:T(8,128)(2,1)S(1)} %get-tuple-element.53), channel_id=1, source_target_pairs={{0,1},{1,0},{2,3},{3,2},{4,5},{5,4},{6,7},{7,6},{8,9},{9,8},{10,11... | collective-permute-start | bytes 196616 | tf_op jit(solution)/shard_map/ppermute | solution.py:301
  24.5 5.0 %collective-permute-start.11 = (bf16[80,128]{1,0:T(8,128)(2,1)S(1)}, bf16[80,128]{1,0:T(8,128)(2,1)S(1)}, u32[]{:S(2)}, u32[]{:S(2)}) collective-permute-start(bf16[80,128]{1,0:T(8,128)(2,1)S(1)} %get-tuple-element.66.refs_0_), channel_id=1, source_target_pairs={{0,4},{2,6},{4,0},{6,2},{8,12},{10,14},{12,8},{14,10},{16,20},{18,... | collective-permute-start | bytes 61448 | tf_op jit(solution)/shard_map/ppermute | solution.py:301
  25.0 4.5 %collective-permute-start.12 = (bf16[80,128]{1,0:T(8,128)(2,1)S(1)}, bf16[80,128]{1,0:T(8,128)(2,1)S(1)}, u32[]{:S(2)}, u32[]{:S(2)}) collective-permute-start(bf16[80,128]{1,0:T(8,128)(2,1)S(1)} %get-tuple-element.67), channel_id=1, source_target_pairs={{0,6},{2,4},{4,2},{6,0},{8,14},{10,12},{12,10},{14,8},{16,22},{18,... | collective-permute-start | bytes 61448 | tf_op jit(solution)/shard_map/ppermute | solution.py:301
  25.8 3.7 %collective-permute-start.10 = (bf16[80,128]{1,0:T(8,128)(2,1)S(1)}, bf16[80,128]{1,0:T(8,128)(2,1)S(1)}, u32[]{:S(2)}, u32[]{:S(2)}) collective-permute-start(bf16[80,128]{1,0:T(8,128)(2,1)S(1)} %get-tuple-element.67), channel_id=1, source_target_pairs={{0,2},{2,0},{4,6},{6,4},{8,10},{10,8},{12,14},{14,12},{16,18},{18,... | collective-permute-start | bytes 61448 | tf_op jit(solution)/shard_map/ppermute | solution.py:301
  27.7 8.3 %collective-permute-start.9 = (bf16[8,64,128]{2,1,0:T(8,128)(2,1)S(1)}, bf16[8,64,128]{2,1,0:T(8,128)(2,1)S(1)}, u32[]{:S(2)}, u32[]{:S(2)}) collective-permute-start(bf16[8,64,128]{2,1,0:T(8,128)(2,1)S(1)} %shard_map.119.g), channel_id=1, source_target_pairs={{0,28},{2,30},{4,0},{6,2},{8,4},{10,6},{12,8},{14,10},{16,12},{18,... | collective-permute-start | bytes 393224 | tf_op jit(solution)/shard_map/ppermute | solution.py:301
  29.5 6.5 %collective-permute-start.8 = (bf16[8,64,128]{2,1,0:T(8,128)(2,1)S(1)}, bf16[8,64,128]{2,1,0:T(8,128)(2,1)S(1)}, u32[]{:S(2)}, u32[]{:S(2)}) collective-permute-start(bf16[8,64,128]{2,1,0:T(8,128)(2,1)S(1)} %shard_map.119.g), channel_id=1, source_target_pairs={{0,26},{2,0},{4,30},{6,4},{8,2},{10,8},{12,6},{14,12},{16,10},{18,... | collective-permute-start | bytes 393224 | tf_op jit(solution)/shard_map/ppermute | solution.py:301
  29.6 6.3 %collective-permute-start.15 = (bf16[80,128]{1,0:T(8,128)(2,1)S(1)}, bf16[80,128]{1,0:T(8,128)(2,1)S(1)}, u32[]{:S(2)}, u32[]{:S(2)}) collective-permute-start(bf16[80,128]{1,0:T(8,128)(2,1)S(1)} %shard_map.122.refs_0_), channel_id=1, source_target_pairs={{0,24},{2,26},{4,28},{6,30},{8,16},{10,18},{12,20},{14,22},{16,8},... | collective-permute-start | bytes 61448 | tf_op jit(solution)/shard_map/ppermute | solution.py:301
  30.8 5.0 %collective-permute-start.14 = (bf16[80,128]{1,0:T(8,128)(2,1)S(1)}, bf16[80,128]{1,0:T(8,128)(2,1)S(1)}, u32[]{:S(2)}, u32[]{:S(2)}) collective-permute-start(bf16[80,128]{1,0:T(8,128)(2,1)S(1)} %shard_map.122.refs_0_), channel_id=1, source_target_pairs={{0,16},{2,18},{4,20},{6,22},{8,24},{10,26},{12,28},{14,30},{16,0},... | collective-permute-start | bytes 61448 | tf_op jit(solution)/shard_map/ppermute | solution.py:301
  31.2 4.8 %collective-permute-start.13 = (bf16[80,128]{1,0:T(8,128)(2,1)S(1)}, bf16[80,128]{1,0:T(8,128)(2,1)S(1)}, u32[]{:S(2)}, u32[]{:S(2)}) collective-permute-start(bf16[80,128]{1,0:T(8,128)(2,1)S(1)} %shard_map.122.refs_0_), channel_id=1, source_target_pairs={{0,8},{2,10},{4,12},{6,14},{8,0},{10,2},{12,4},{14,6},{16,24},{18,... | collective-permute-start | bytes 61448 | tf_op jit(solution)/shard_map/ppermute | solution.py:301
  36.1 1.4 %collective-permute-start.16 = (bf16[592,128]{1,0:T(8,128)(2,1)S(1)}, bf16[592,128]{1,0:T(8,128)(2,1)S(1)}, u32[]{:S(2)}, u32[]{:S(2)}) collective-permute-start(bf16[592,128]{1,0:T(8,128)(2,1)S(1)} %shard_map.123.sent), channel_id=1, source_target_pairs={{0,2},{2,0},{4,6},{6,4},{8,10},{10,8},{12,14},{14,12},{16,18},{18,... | collective-permute-start | bytes 454664 | tf_op jit(solution)/shard_map/ppermute | solution.py:301
where the time goes:
time: 39.4 us; the launch traced here: 39.1 us
  starting transfers between devices  19.5 us (49%)
  Pallas kernels  11.7 us (30%)
  waiting for transfers between devices  6.55 us (17%)
  between operations  1.39 us (4%)
    ppermute x17, starting transfers between devices, moved(): return lax.ppermute(block, axis, [(i, target(i) % n) for i in range(n)])  19.5 us
    ppermute x17, waiting for transfers between devices, moved(): return lax.ppermute(block, axis, [(i, target(i) % n) for i in range(n)])  6.55 us
    pallas_call x1, Pallas kernels, shards(): call(forward_swap_kernel, [plane, plane, plane, piece, piece, slots], [SM...  2.35 us
    pallas_call x1, Pallas kernels, shards(): call(forward_own_kernel, [totals, plane], [SMEM] * 2 + [VMEM, HBM], [VMEM...  2.09 us
    pallas_call x2, Pallas kernels, shards(): call(functools.partial(middle_kernel, parts, first), [half_rows, half_col...  1.81 us
    pallas_call x1, Pallas kernels, shards(): call(backward_last_kernel, [jax.ShapeDtypeStruct((width, nodes), BF16), j...  1.61 us
    pallas_call x1, Pallas kernels, shards(): call(backward_own_kernel, [totals, rows], [SMEM] * 2 + [VMEM] * (2 + cut)...  1.25 us
    pallas_call x1, Pallas kernels, shards(): call(forward_send_kernel, [totals, piece], [SMEM] * 2 + [VMEM] * 3, [VMEM...  1.21 us
  transfers between devices with their start and end apart: 17, of which 7 were waited for; matrix products, arithmetic and copies ran while one was open for 0% of the time, Pallas kernels for 20%

commit v1 on v0

--- a/solution.py
+++ b/solution.py
@@ -44,30 +44,16 @@
 
 def slot_loop(count, groups, body):
     m = groups_at_once(groups)
-    pair = 2 if m % 2 == 0 else 1
 
     def chunk(i, carry):
         @pl.when(i * (m * REACH) < count)
         def _():
-            for u in range(0, m, pair):
-                body([i * m + u + v for v in range(pair)])
+            for u in range(m):
+                body(i * m + u)
 
         return carry
 
     lax.fori_loop(0, groups // m, chunk, 0)
-
-
-def side_by_side(lefts, tiles, contract):
-    if len(tiles) == 1:
-        left, right = lefts[0], tiles[0]
-    else:
-        left = jnp.concatenate(lefts, axis=1)
-        none = jnp.zeros_like(tiles[0])
-        right = jnp.concatenate(
-            [jnp.concatenate([tiles[0], none], axis=1), jnp.concatenate([none, tiles[1]], axis=1)], axis=0
-        )
-    out = lax.dot_general(left, right, (((1,), (contract,)), ((), ())), preferred_element_type=F32)
-    return [out[:, i * BLOCK : (i + 1) * BLOCK] for i in range(len(tiles))]
 
 
 def source(entry):
@@ -78,34 +64,34 @@
     return lax.bitwise_and(entry, SRC_UNIT - 1) - o * blocks
 
 
-def push(xt, tiles, index, count, acc, js, o):
+def push(xt, tiles, index, count, acc, j, o):
     blocks = xt.shape[0]
-    ks = [j * REACH + o for j in js]
-    outs = side_by_side([xt[source(index[k])] for k in ks], [tiles[j] for j in js], 1)
-    for k, out in zip(ks, outs):
-        acc[jnp.where(k < count, target(index[k], o, blocks), blocks)] += out
-
-
-def pull(block, tiles, index, count, acc, js, o):
+    k = j * REACH + o
+    entry = index[k]
+    out = lax.dot_general(xt[source(entry)], tiles[j], (((1,), (1,)), ((), ())), preferred_element_type=F32)
+    acc[jnp.where(k < count, target(entry, o, blocks), blocks)] += out
+
+
+def pull(block, tiles, index, count, acc, j, o):
     blocks = acc.shape[0] - 1
-    ks = [j * REACH + o for j in js]
-    outs = side_by_side([block(target(index[k], o, blocks)) for k in ks], [tiles[j] for j in js], 0)
-    for k, out in zip(ks, outs):
-        acc[jnp.where(k < count, source(index[k]), blocks)] += out
+    k = j * REACH + o
+    entry = index[k]
+    out = jnp.dot(block(target(entry, o, blocks)), tiles[j], preferred_element_type=F32)
+    acc[jnp.where(k < count, source(entry), blocks)] += out
 
 
 def push_all(xt, index, count, *planes):
-    def body(js):
+    def body(j):
         for tiles, acc, o in planes:
-            push(xt, tiles, index, count, acc, js, o)
+            push(xt, tiles, index, count, acc, j, o)
 
     slot_loop(count, planes[0][0].shape[0], body)
 
 
 def pull_all(index, count, *planes):
-    def body(js):
+    def body(j):
         for block, tiles, acc, o in planes:
-            pull(block, tiles, index, count, acc, js, o)
+            pull(block, tiles, index, count, acc, j, o)
 
     slot_loop(count, planes[0][1].shape[0], body)
 
@@ -150,18 +136,18 @@
         c.wait()
 
 
-def forward_send_kernel(count, index, xt, tiles2, tiles3, acc2, direct, acc):
+def forward_send_kernel(count, index, xt, tiles2, tiles3, tiles_hbm, acc2, direct, tiles0, acc, sem):
+    load = pltpu.make_async_copy(tiles_hbm.at[:, 0], tiles0, sem)
+    load.start()
     acc2[...] = jnp.zeros_like(acc2)
     acc[...] = jnp.zeros_like(acc)
     push_all(xt, index, count[0], (tiles2, acc2, 2), (tiles3, acc, 1 + 2 * own_core()))
     direct[...] = acc[: direct.shape[0]].astype(BF16)
-
-
-def forward_own_kernel(count, index, xt, tiles_hbm, acc, tiles0, sem):
-    load = pltpu.make_async_copy(tiles_hbm.at[:, 0], tiles0, sem)
-    load.start()
+    load.wait()
+
+
+def forward_own_kernel(count, index, xt, tiles0, acc):
     acc[...] = jnp.zeros_like(acc)
-    load.wait()
     push_all(xt, index, count[0], (tiles0, acc, 0))
 
 
@@ -264,18 +250,18 @@
     )
 
 
-def backward_last_kernel(count, index, tiles, sent, got, acc0, acc2, accd, out, wg, bias, acc):
-    blocks, width = acc.shape[0] - 1, acc.shape[1]
+def backward_last_kernel(count, index, tiles1, sent, got, acc0, acc2, acc3, out, wg, bias, acc1):
+    blocks, width = acc1.shape[0] - 1, acc1.shape[1]
     f_in, hid = wg.shape
-    acc[...] = jnp.zeros_like(acc)
+    acc1[...] = jnp.zeros_like(acc1)
     core = own_core()
 
     def block(d):
         return got[pl.ds(pl.multiple_of(d * width, width), width), :]
 
-    pull_all(index, count[0], (block, tiles, acc, 3 - 2 * core))
+    pull_all(index, count[0], (block, tiles1, acc1, 3 - 2 * core))
     for b in range(blocks):
-        total = acc[b] + acc0[b] + acc2[b] + accd[b]
+        total = (acc0[b] + acc2[b]) + (acc1[b] + acc3[b])
         out[:, b * BLOCK : (b + 1) * BLOCK] = total.astype(BF16)
     a, b = (r[blocks * width :, :hid].astype(F32) for r in (sent, got))
     low, high = jnp.where(core == 0, a, b), jnp.where(core == 0, b, a)
@@ -351,9 +337,14 @@
     )(tile_counts, *(in_hbm(a) for a in (tile_src, tile_dst, node_features, tiles)))
     index = (tile_counts, index)
     swap = moved(swap, "dom", swapped)
-    acc2, direct = call(
-        forward_send_kernel, [totals, piece], [SMEM] * 2 + [VMEM] * 3, [VMEM] * 2, [acc], 2 * flops
-    )(*index, xt, tiles2, tiles3)
+    acc2, direct, tiles0 = call(
+        forward_send_kernel,
+        [totals, piece, plane],
+        [SMEM] * 2 + [VMEM] * 3 + [HBM],
+        [VMEM] * 3,
+        [acc, pltpu.SemaphoreType.DMA],
+        2 * flops,
+    )(*index, xt, tiles2, tiles3, in_hbm(tiles))
     cut = 2 if blocks % 2 == 0 else 1
     starts = range(0, blocks, blocks // cut)
     half = jax.ShapeDtypeStruct((blocks // cut, width, BLOCK), BF16)
@@ -363,14 +354,7 @@
     chip = call(functools.partial(sum_kernel, 2, 0), [half] * cut, [VMEM] * 2, [VMEM] * cut)(acc2, swap)
     chip = [moved(c, "dom", lambda i: i + 2) for c in chip]
     direct = moved(direct, "dom", lambda i: i + 1 + 2 * (i % 2))
-    acc0, tiles0 = call(
-        forward_own_kernel,
-        [totals, plane],
-        [SMEM] * 2 + [VMEM, HBM],
-        [VMEM] * 2,
-        [pltpu.SemaphoreType.DMA],
-        flops,
-    )(*index, xt, in_hbm(tiles))
+    (acc0,) = call(forward_own_kernel, [totals], [SMEM] * 2 + [VMEM] * 2, [VMEM], (), flops)(*index, xt, tiles0)
     h_lists = []
     for first, c in zip(starts, chip):
         (h,) = call(functools.partial(sum_kernel, 3, first), [half], [VMEM] * 3, [VMEM])(acc0, direct, c)
@@ -419,7 +403,7 @@
     payload = jax.ShapeDtypeStruct((blocks * width + gradient.shape[0], BLOCK), BF16)
     (sent,) = call(swap_payload_kernel, [payload], [VMEM] * (1 + len(wgs)), [VMEM])(g_chip, *wgs)
     got = moved(sent, "dom", swapped)
-    back2, backd = call(
+    back2, back3 = call(
         backward_near_kernel, [totals, totals], [SMEM] * 2 + [VMEM] * 4, [VMEM] * 2, (), 2 * flops
     )(*index, tiles2, tiles3, g_chip, g_direct)
     input_grad, weight_grad, bias_grad = call(
@@ -433,7 +417,7 @@
         [VMEM] * 3,
         [acc],
         flops,
-    )(*index, tiles1, sent, got, back0, back2, backd)
+    )(*index, tiles1, sent, got, back0, back2, back3)
     return output, weight_grad, bias_grad.reshape(hid), input_grad.T
 
 

time: 39.4 us -> 38.9 us (0.987)
  waiting for transfers between devices: 6.55 us -> 7.27 us
  Pallas kernels: 11.7 us -> 11 us
  starting transfers between devices: 19.5 us -> 18.9 us
    ppermute x17, waiting for transfers between devices: 6.55 us -> 7.27 us  [moved(): return lax.ppermute(block, axis, [(i, target(i) % n) for i in range(n)])]
    pallas_call x2, Pallas kernels: 3.3 us -> 2.65 us  [the longest x1 1.7 us: shards(): call(forward_send_kernel, [totals, piece, plane], [SMEM] * 2 + [VMEM] * 3...]
    ppermute x17, starting transfers between devices: 19.5 us -> 18.9 us  [moved(): return lax.ppermute(block, axis, [(i, target(i) % n) for i in range(n)])]
  transfers between devices with their start and end apart: 17 -> 17, of which waited for: 7 -> 8; matrix products, arithmetic and copies ran while one was open for 0% -> 0% of each run, Pallas kernels for 20% -> 18%
where the time goes in v1:
time: 38.9 us; the launch traced here: 38.5 us
  starting transfers between devices  18.9 us (49%)
  Pallas kernels  11 us (28%)
  waiting for transfers between devices  7.27 us (19%)
  between operations  1.4 us (4%)
    ppermute x17, starting transfers between devices, moved(): return lax.ppermute(block, axis, [(i, target(i) % n) for i in range(n)])  18.9 us
    ppermute x17, waiting for transfers between devices, moved(): return lax.ppermute(block, axis, [(i, target(i) % n) for i in range(n)])  7.27 us
    pallas_call x1, Pallas kernels, shards(): call(forward_swap_kernel, [plane, plane, plane, piece, piece, slots], [SM...  2.35 us
    pallas_call x2, Pallas kernels, shards(): call(functools.partial(middle_kernel, parts, first), [half_rows, half_col...  1.81 us
    pallas_call x1, Pallas kernels, shards(): call(forward_send_kernel, [totals, piece, plane], [SMEM] * 2 + [VMEM] * 3...  1.7 us
    pallas_call x1, Pallas kernels, shards(): call(backward_last_kernel, [jax.ShapeDtypeStruct((width, nodes), BF16), j...  1.59 us
    pallas_call x1, Pallas kernels, shards(): call(backward_own_kernel, [totals, rows], [SMEM] * 2 + [VMEM] * (2 + cut)...  1.25 us
    pallas_call x1, Pallas kernels, shards(): call(backward_near_kernel, [totals, totals], [SMEM] * 2 + [VMEM] * 4, [VM...  0.95 us
  transfers between devices with their start and end apart: 17, of which 8 were waited for; matrix products, arithmetic and copies ran while one was open for 0% of the time, Pallas kernels for 18%

profile of v1, /device:TPU:0, one launch (start us, length us, event | category | flops | bytes accessed | tf_op | source)
XLA Modules:
  0.0 38.5 jit_solution(735640374995880902)
XLA Ops:
  1.3 2.3 %shard_map.111 = (bf16[24,128,128]{2,1,0:T(8,128)(2,1)S(1)}, bf16[24,128,128]{2,1,0:T(8,128)(2,1)S(1)}, bf16[24,128,128]{2,1,0:T(8,128)(2,1)S(1)}, bf16[8,64,128...) custom-call(s32[1]{0:T(128)S(6)} %copy.12.count, s32[96]{0:T(128)} %src_hbm.1, s32[96]{0:T(128)} %dst_hbm.1, ...), custom_call_target="tpu_custom_call" | custom-call | flops 50331648 | bytes 1048576 | tf_op jit(solution)/shard_map/pallas_call | solution.py:324
  3.6 0.5 %collective-permute-start.1 = (bf16[8,64,128]{2,1,0:T(8,128)(2,1)S(1)}, bf16[8,64,128]{2,1,0:T(8,128)(2,1)S(1)}, u32[]{:S(2)}, u32[]{:S(2)}) collective-permute-start(bf16[8,64,128]{2,1,0:T(8,128)(2,1)S(1)} %get-tuple-element.48), channel_id=1, source_target_pairs={{0,2},{2,0},{4,6},{6,4},{8,10},{10,8},{12,14},{14,12},{16,18},{18,... | collective-permute-start | bytes 393224 | tf_op jit(solution)/shard_map/ppermute | solution.py:287
  4.2 1.7 %shard_map.112 = (f32[9,64,128]{2,1,0:T(8,128)S(1)}, bf16[8,64,128]{2,1,0:T(8,128)(2,1)S(1)}, bf16[24,128,128]{2,1,0:T(8,128)(2,1)S(1)}) custom-call(s32[1]{0:T(128)S(6)} %copy.12.count, s32[96]{0:T(128)S(1)} %get-tuple-element.41.index, bf16[8,64,128]{2,1,0:T(8,128)(2,1)S(1)} %get-tuple-element.42.xt, bf16[24,128,128]{2,1,0:T(8,128)(2,1)S(1)} %get-tuple-element.43.tiles2, ...), custom_call_target="tpu_custom_call" | custom-call | flops 100663296 | bytes 1048576 | tf_op jit(solution)/shard_map/pallas_call | solution.py:340
  6.0 3.0 %collective-permute-start.5 = (bf16[4,64,128]{2,1,0:T(8,128)(2,1)S(1)}, bf16[4,64,128]{2,1,0:T(8,128)(2,1)S(1)}, u32[]{:S(2)}, u32[]{:S(2)}) collective-permute-start(bf16[4,64,128]{2,1,0:T(8,128)(2,1)S(1)} %get-tuple-element.52), channel_id=1, source_target_pairs={{0,4},{2,6},{4,8},{6,10},{8,12},{10,14},{12,16},{14,18},{16,20},{1... | collective-permute-start | bytes 196616 | tf_op jit(solution)/shard_map/ppermute | solution.py:287
  9.0 1.7 %collective-permute-start.2 = (bf16[4,64,128]{2,1,0:T(8,128)(2,1)S(1)}, bf16[4,64,128]{2,1,0:T(8,128)(2,1)S(1)}, u32[]{:S(2)}, u32[]{:S(2)}) collective-permute-start(bf16[4,64,128]{2,1,0:T(8,128)(2,1)S(1)} %get-tuple-element.49), channel_id=1, source_target_pairs={{0,4},{2,6},{4,8},{6,10},{8,12},{10,14},{12,16},{14,18},{16,20},{1... | collective-permute-start | bytes 196616 | tf_op jit(solution)/shard_map/ppermute | solution.py:287
  10.7 0.9 %shard_map.113.refs_0_ = f32[9,64,128]{2,1,0:T(8,128)S(1)} custom-call(s32[1]{0:T(128)S(6)} %copy.12.count, s32[96]{0:T(128)S(1)} %get-tuple-element.41.index, bf16[8,64,128]{2,1,0:T(8,128)(2,1)S(1)} %get-tuple-element.42.xt, bf16[24,128,128]{2,1,0:T(8,128)(2,1)S(1)} %get-tuple-element.45.tiles0.tiles), custom_call_target="tpu_custom_call" | custom-call | flops 50331648 | bytes 1048576 | tf_op jit(solution)/shard_map/pallas_call | solution.py:357
  11.7 1.6 %collective-permute-done.refs_1_ = bf16[8,64,128]{2,1,0:T(8,128)(2,1)S(1)} collective-permute-done((bf16[8,64,128]{2,1,0:T(8,128)(2,1)S(1)}, bf16[8,64,128]{2,1,0:T(8,128)(2,1)S(1)}, u32[]{:S(2)}, u32[]{:S(2)}) %collective-permute-start) | collective-permute-done | bytes 131104 | tf_op jit(solution)/shard_map/ppermute | solution.py:287
  13.3 1.7 %collective-permute-done.5.refs_2_ = bf16[4,64,128]{2,1,0:T(8,128)(2,1)S(1)} collective-permute-done((bf16[4,64,128]{2,1,0:T(8,128)(2,1)S(1)}, bf16[4,64,128]{2,1,0:T(8,128)(2,1)S(1)}, u32[]{:S(2)}, u32[]{:S(2)}) %collective-permute-start.5) | collective-permute-done | bytes 65568 | tf_op jit(solution)/shard_map/ppermute | solution.py:287
  15.0 1.7 %collective-permute-start.6 = (bf16[4,64,128]{2,1,0:T(8,128)(2,1)S(1)}, bf16[4,64,128]{2,1,0:T(8,128)(2,1)S(1)}, u32[]{:S(2)}, u32[]{:S(2)}) collective-permute-start(bf16[4,64,128]{2,1,0:T(8,128)(2,1)S(1)} %shard_map.117.refs_0_), channel_id=1, source_target_pairs={{0,1},{1,0},{2,3},{3,2},{4,5},{5,4},{6,7},{7,6},{8,9},{9,8},{10,11... | collective-permute-start | bytes 196616 | tf_op jit(solution)/shard_map/ppermute | solution.py:287
  16.8 1.6 %collective-permute-start.3 = (bf16[4,64,128]{2,1,0:T(8,128)(2,1)S(1)}, bf16[4,64,128]{2,1,0:T(8,128)(2,1)S(1)}, u32[]{:S(2)}, u32[]{:S(2)}) collective-permute-start(bf16[4,64,128]{2,1,0:T(8,128)(2,1)S(1)} %shard_map.115.refs_0_), channel_id=1, source_target_pairs={{0,1},{1,0},{2,3},{3,2},{4,5},{5,4},{6,7},{7,6},{8,9},{9,8},{10,11... | collective-permute-start | bytes 196616 | tf_op jit(solution)/shard_map/ppermute | solution.py:287
  18.3 1.6 %collective-permute-done.6.refs_1_ = bf16[4,64,128]{2,1,0:T(8,128)(2,1)S(1)} collective-permute-done((bf16[4,64,128]{2,1,0:T(8,128)(2,1)S(1)}, bf16[4,64,128]{2,1,0:T(8,128)(2,1)S(1)}, u32[]{:S(2)}, u32[]{:S(2)}) %collective-permute-start.6) | collective-permute-done | bytes 65568 | tf_op jit(solution)/shard_map/ppermute | solution.py:287
  20.0 0.9 %shard_map.118 = (bf16[512,128]{1,0:T(8,128)(2,1)S(1)}, bf16[160,512]{1,0:T(8,128)(2,1)S(1)}, bf16[512,128]{1,0:T(8,128)(2,1)S(1)}, f32[4,64,128]{2,1,0:T(8,128)S(1)}, bf16[4,64,128]{2,1,0:T(8,128)(2,1)S(1)}) custom-call(f32[1,128]{1,0:T(1,128)S(1)} %bitcast.4, bf16[128,128]{1,0:T(8,128)(2,1)S(1)} %copy-done.1, bf16[1024,128]{1,0:T(8,128)(2,1)S(1)} %copy-done, ...), custom_call_target="tpu_custom_call" | custom-call | flops 33554432 | bytes 1048576 | tf_op jit(solution)/shard_map/pallas_call | solution.py:364
  20.9 1.8 %collective-permute-start.7 = (bf16[4,64,128]{2,1,0:T(8,128)(2,1)S(1)}, bf16[4,64,128]{2,1,0:T(8,128)(2,1)S(1)}, u32[]{:S(2)}, u32[]{:S(2)}) collective-permute-start(bf16[4,64,128]{2,1,0:T(8,128)(2,1)S(1)} %get-tuple-element.54), channel_id=1, source_target_pairs={{0,1},{1,0},{2,3},{3,2},{4,5},{5,4},{6,7},{7,6},{8,9},{9,8},{10,11... | collective-permute-start | bytes 196616 | tf_op jit(solution)/shard_map/ppermute | solution.py:287
  22.6 0.9 %shard_map.116 = (bf16[512,128]{1,0:T(8,128)(2,1)S(1)}, bf16[160,512]{1,0:T(8,128)(2,1)S(1)}, bf16[512,128]{1,0:T(8,128)(2,1)S(1)}, f32[4,64,128]{2,1,0:T(8,128)S(1)}, bf16[4,64,128]{2,1,0:T(8,128)(2,1)S(1)}) custom-call(f32[1,128]{1,0:T(1,128)S(1)} %bitcast.5, bf16[128,128]{1,0:T(8,128)(2,1)S(1)} %copy-done.1, bf16[1024,128]{1,0:T(8,128)(2,1)S(1)} %copy-done, ...), custom_call_target="tpu_custom_call" | custom-call | flops 33554432 | bytes 1048576 | tf_op jit(solution)/shard_map/pallas_call | solution.py:364
  24.3 0.8 %collective-permute-start.12 = (bf16[80,128]{1,0:T(8,128)(2,1)S(1)}, bf16[80,128]{1,0:T(8,128)(2,1)S(1)}, u32[]{:S(2)}, u32[]{:S(2)}) collective-permute-start(bf16[80,128]{1,0:T(8,128)(2,1)S(1)} %get-tuple-element.65), channel_id=1, source_target_pairs={{0,6},{2,4},{4,2},{6,0},{8,14},{10,12},{12,10},{14,8},{16,22},{18,... | collective-permute-start | bytes 61448 | tf_op jit(solution)/shard_map/ppermute | solution.py:287
  25.1 1.3 %collective-permute-start.10 = (bf16[80,128]{1,0:T(8,128)(2,1)S(1)}, bf16[80,128]{1,0:T(8,128)(2,1)S(1)}, u32[]{:S(2)}, u32[]{:S(2)}) collective-permute-start(bf16[80,128]{1,0:T(8,128)(2,1)S(1)} %get-tuple-element.65), channel_id=1, source_target_pairs={{0,2},{2,0},{4,6},{6,4},{8,10},{10,8},{12,14},{14,12},{16,18},{18,... | collective-permute-start | bytes 61448 | tf_op jit(solution)/shard_map/ppermute | solution.py:287
  26.4 1.4 %collective-permute-done.4.refs_1_ = bf16[4,64,128]{2,1,0:T(8,128)(2,1)S(1)} collective-permute-done((bf16[4,64,128]{2,1,0:T(8,128)(2,1)S(1)}, bf16[4,64,128]{2,1,0:T(8,128)(2,1)S(1)}, u32[]{:S(2)}, u32[]{:S(2)}) %collective-permute-start.4) | collective-permute-done | bytes 65568 | tf_op jit(solution)/shard_map/ppermute | solution.py:287
  27.9 1.3 %collective-permute-start.9 = (bf16[8,64,128]{2,1,0:T(8,128)(2,1)S(1)}, bf16[8,64,128]{2,1,0:T(8,128)(2,1)S(1)}, u32[]{:S(2)}, u32[]{:S(2)}) collective-permute-start(bf16[8,64,128]{2,1,0:T(8,128)(2,1)S(1)} %shard_map.119.g), channel_id=1, source_target_pairs={{0,28},{2,30},{4,0},{6,2},{8,4},{10,6},{12,8},{14,10},{16,12},{18,... | collective-permute-start | bytes 393224 | tf_op jit(solution)/shard_map/ppermute | solution.py:287
  29.2 0.6 %collective-permute-start.15 = (bf16[80,128]{1,0:T(8,128)(2,1)S(1)}, bf16[80,128]{1,0:T(8,128)(2,1)S(1)}, u32[]{:S(2)}, u32[]{:S(2)}) collective-permute-start(bf16[80,128]{1,0:T(8,128)(2,1)S(1)} %shard_map.122.refs_0_), channel_id=1, source_target_pairs={{0,24},{2,26},{4,28},{6,30},{8,16},{10,18},{12,20},{14,22},{16,8},... | collective-permute-start | bytes 61448 | tf_op jit(solution)/shard_map/ppermute | solution.py:287
  29.8 1.1 %collective-permute-start.14 = (bf16[80,128]{1,0:T(8,128)(2,1)S(1)}, bf16[80,128]{1,0:T(8,128)(2,1)S(1)}, u32[]{:S(2)}, u32[]{:S(2)}) collective-permute-start(bf16[80,128]{1,0:T(8,128)(2,1)S(1)} %shard_map.122.refs_0_), channel_id=1, source_target_pairs={{0,16},{2,18},{4,20},{6,22},{8,24},{10,26},{12,28},{14,30},{16,0},... | collective-permute-start | bytes 61448 | tf_op jit(solution)/shard_map/ppermute | solution.py:287
  31.0 2.7 %collective-permute-start.13 = (bf16[80,128]{1,0:T(8,128)(2,1)S(1)}, bf16[80,128]{1,0:T(8,128)(2,1)S(1)}, u32[]{:S(2)}, u32[]{:S(2)}) collective-permute-start(bf16[80,128]{1,0:T(8,128)(2,1)S(1)} %shard_map.122.refs_0_), channel_id=1, source_target_pairs={{0,8},{2,10},{4,12},{6,14},{8,0},{10,2},{12,4},{14,6},{16,24},{18,... | collective-permute-start | bytes 61448 | tf_op jit(solution)/shard_map/ppermute | solution.py:287
  33.7 1.3 %shard_map.120 = (f32[9,64,128]{2,1,0:T(8,128)S(1)}, bf16[1024,128]{1,0:T(8,128)(2,1)}) custom-call(s32[1]{0:T(128)S(6)} %copy.12.count, s32[96]{0:T(128)S(1)} %get-tuple-element.41.index, bf16[24,128,128]{2,1,0:T(8,128)(2,1)S(1)} %get-tuple-element.45.tiles0.tiles, bf16[8,64,128]{2,1,0:T(8,128)(2,1)S(1)} %shard_map.119.g, ...), custom_call_target="tpu_custom_call" | custom-call | flops 50331648 | bytes 1048576 | tf_op jit(solution)/shard_map/pallas_call | solution.py:394
  35.6 1.0 %shard_map.124 = (f32[9,64,128]{2,1,0:T(8,128)S(1)}, f32[9,64,128]{2,1,0:T(8,128)S(1)}) custom-call(s32[1]{0:T(128)S(6)} %copy.12.count, s32[96]{0:T(128)S(1)} %get-tuple-element.41.index, bf16[24,128,128]{2,1,0:T(8,128)(2,1)S(1)} %get-tuple-element.43.tiles2, bf16[24,128,128]{2,1,0:T(8,128)(2,1)S(1)} %get-tuple-element.44.tiles3, ...), custom_call_target="tpu_custom_call" | custom-call | flops 100663296 | bytes 1048576 | tf_op jit(solution)/shard_map/pallas_call | solution.py:406
  36.9 1.6 %shard_map.125 = (bf16[64,1024]{1,0:T(8,128)(2,1)}, f32[128,128]{1,0:T(8,128)}, f32[1,128]{1,0:T(1,128)}) custom-call(s32[1]{0:T(128)S(6)} %copy.12.count, s32[96]{0:T(128)S(1)} %get-tuple-element.41.index, bf16[24,128,128]{2,1,0:T(8,128)(2,1)S(1)} %get-tuple-element.58.tiles1, bf16[592,128]{1,0:T(8,128)(2,1)S(1)} %shard_map.123.sent, ...), custom_call_target="tpu_custom_call" | custom-call | flops 50331648 | bytes 1048576 | tf_op jit(solution)/shard_map/pallas_call | solution.py:409
  (31 shorter events, 2.0 us)
Async XLA Ops:
  3.6 2.3 %collective-permute-start.1 = (bf16[8,64,128]{2,1,0:T(8,128)(2,1)S(1)}, bf16[8,64,128]{2,1,0:T(8,128)(2,1)S(1)}, u32[]{:S(2)}, u32[]{:S(2)}) collective-permute-start(bf16[8,64,128]{2,1,0:T(8,128)(2,1)S(1)} %get-tuple-element.48), channel_id=1, source_target_pairs={{0,2},{2,0},{4,6},{6,4},{8,10},{10,8},{12,14},{14,12},{16,18},{18,... | collective-permute-start | bytes 393224 | tf_op jit(solution)/shard_map/ppermute | solution.py:287
  4.2 15.8 %copy-start = (bf16[1024,128]{1,0:T(8,128)(2,1)S(1)}, bf16[1024,128]{1,0:T(8,128)(2,1)}, u32[]{:S(2)}) copy-start(bf16[1024,128]{1,0:T(8,128)(2,1)} %og_ref.3) | copy-start | bytes 786436
  4.2 15.8 %copy-start.1 = (bf16[128,128]{1,0:T(8,128)(2,1)S(1)}, bf16[128,128]{1,0:T(8,128)(2,1)}, u32[]{:S(2)}) copy-start(bf16[128,128]{1,0:T(8,128)(2,1)} %w_ref.3) | copy-start | bytes 98308
  4.2 15.8 %copy-start.2 = (f32[128]{0:T(128)S(1)}, f32[128]{0:T(128)}, u32[]{:S(2)}) copy-start(f32[128]{0:T(128)} %param.10) | copy-start | bytes 1540
  5.9 7.4 %collective-permute-start = (bf16[8,64,128]{2,1,0:T(8,128)(2,1)S(1)}, bf16[8,64,128]{2,1,0:T(8,128)(2,1)S(1)}, u32[]{:S(2)}, u32[]{:S(2)}) collective-permute-start(bf16[8,64,128]{2,1,0:T(8,128)(2,1)S(1)} %get-tuple-element.46), channel_id=1, source_target_pairs={{0,2},{2,8},{4,6},{6,12},{8,10},{10,16},{12,14},{14,20},{16,18},{1... | collective-permute-start | bytes 393224 | tf_op jit(solution)/shard_map/ppermute | solution.py:287
  6.0 9.0 %collective-permute-start.5 = (bf16[4,64,128]{2,1,0:T(8,128)(2,1)S(1)}, bf16[4,64,128]{2,1,0:T(8,128)(2,1)S(1)}, u32[]{:S(2)}, u32[]{:S(2)}) collective-permute-start(bf16[4,64,128]{2,1,0:T(8,128)(2,1)S(1)} %get-tuple-element.52), channel_id=1, source_target_pairs={{0,4},{2,6},{4,8},{6,10},{8,12},{10,14},{12,16},{14,18},{16,20},{1... | collective-permute-start | bytes 196616 | tf_op jit(solution)/shard_map/ppermute | solution.py:287
  9.0 7.7 %collective-permute-start.2 = (bf16[4,64,128]{2,1,0:T(8,128)(2,1)S(1)}, bf16[4,64,128]{2,1,0:T(8,128)(2,1)S(1)}, u32[]{:S(2)}, u32[]{:S(2)}) collective-permute-start(bf16[4,64,128]{2,1,0:T(8,128)(2,1)S(1)} %get-tuple-element.49), channel_id=1, source_target_pairs={{0,4},{2,6},{4,8},{6,10},{8,12},{10,14},{12,16},{14,18},{16,20},{1... | collective-permute-start | bytes 196616 | tf_op jit(solution)/shard_map/ppermute | solution.py:287
  15.0 4.9 %collective-permute-start.6 = (bf16[4,64,128]{2,1,0:T(8,128)(2,1)S(1)}, bf16[4,64,128]{2,1,0:T(8,128)(2,1)S(1)}, u32[]{:S(2)}, u32[]{:S(2)}) collective-permute-start(bf16[4,64,128]{2,1,0:T(8,128)(2,1)S(1)} %shard_map.117.refs_0_), channel_id=1, source_target_pairs={{0,1},{1,0},{2,3},{3,2},{4,5},{5,4},{6,7},{7,6},{8,9},{9,8},{10,11... | collective-permute-start | bytes 196616 | tf_op jit(solution)/shard_map/ppermute | solution.py:287
  16.8 5.9 %collective-permute-start.3 = (bf16[4,64,128]{2,1,0:T(8,128)(2,1)S(1)}, bf16[4,64,128]{2,1,0:T(8,128)(2,1)S(1)}, u32[]{:S(2)}, u32[]{:S(2)}) collective-permute-start(bf16[4,64,128]{2,1,0:T(8,128)(2,1)S(1)} %shard_map.115.refs_0_), channel_id=1, source_target_pairs={{0,1},{1,0},{2,3},{3,2},{4,5},{5,4},{6,7},{7,6},{8,9},{9,8},{10,11... | collective-permute-start | bytes 196616 | tf_op jit(solution)/shard_map/ppermute | solution.py:287
  20.9 5.5 %collective-permute-start.7 = (bf16[4,64,128]{2,1,0:T(8,128)(2,1)S(1)}, bf16[4,64,128]{2,1,0:T(8,128)(2,1)S(1)}, u32[]{:S(2)}, u32[]{:S(2)}) collective-permute-start(bf16[4,64,128]{2,1,0:T(8,128)(2,1)S(1)} %get-tuple-element.54), channel_id=1, source_target_pairs={{0,1},{1,0},{2,3},{3,2},{4,5},{5,4},{6,7},{7,6},{8,9},{9,8},{10,11... | collective-permute-start | bytes 196616 | tf_op jit(solution)/shard_map/ppermute | solution.py:287
  23.6 4.3 %collective-permute-start.4 = (bf16[4,64,128]{2,1,0:T(8,128)(2,1)S(1)}, bf16[4,64,128]{2,1,0:T(8,128)(2,1)S(1)}, u32[]{:S(2)}, u32[]{:S(2)}) collective-permute-start(bf16[4,64,128]{2,1,0:T(8,128)(2,1)S(1)} %get-tuple-element.51), channel_id=1, source_target_pairs={{0,1},{1,0},{2,3},{3,2},{4,5},{5,4},{6,7},{7,6},{8,9},{9,8},{10,11... | collective-permute-start | bytes 196616 | tf_op jit(solution)/shard_map/ppermute | solution.py:287
  24.2 5.0 %collective-permute-start.11 = (bf16[80,128]{1,0:T(8,128)(2,1)S(1)}, bf16[80,128]{1,0:T(8,128)(2,1)S(1)}, u32[]{:S(2)}, u32[]{:S(2)}) collective-permute-start(bf16[80,128]{1,0:T(8,128)(2,1)S(1)} %get-tuple-element.64.refs_0_), channel_id=1, source_target_pairs={{0,4},{2,6},{4,0},{6,2},{8,12},{10,14},{12,8},{14,10},{16,20},{18,... | collective-permute-start | bytes 61448 | tf_op jit(solution)/shard_map/ppermute | solution.py:287
  24.3 4.9 %collective-permute-start.12 = (bf16[80,128]{1,0:T(8,128)(2,1)S(1)}, bf16[80,128]{1,0:T(8,128)(2,1)S(1)}, u32[]{:S(2)}, u32[]{:S(2)}) collective-permute-start(bf16[80,128]{1,0:T(8,128)(2,1)S(1)} %get-tuple-element.65), channel_id=1, source_target_pairs={{0,6},{2,4},{4,2},{6,0},{8,14},{10,12},{12,10},{14,8},{16,22},{18,... | collective-permute-start | bytes 61448 | tf_op jit(solution)/shard_map/ppermute | solution.py:287
  25.1 4.1 %collective-permute-start.10 = (bf16[80,128]{1,0:T(8,128)(2,1)S(1)}, bf16[80,128]{1,0:T(8,128)(2,1)S(1)}, u32[]{:S(2)}, u32[]{:S(2)}) collective-permute-start(bf16[80,128]{1,0:T(8,128)(2,1)S(1)} %get-tuple-element.65), channel_id=1, source_target_pairs={{0,2},{2,0},{4,6},{6,4},{8,10},{10,8},{12,14},{14,12},{16,18},{18,... | collective-permute-start | bytes 61448 | tf_op jit(solution)/shard_map/ppermute | solution.py:287
  27.9 7.6 %collective-permute-start.9 = (bf16[8,64,128]{2,1,0:T(8,128)(2,1)S(1)}, bf16[8,64,128]{2,1,0:T(8,128)(2,1)S(1)}, u32[]{:S(2)}, u32[]{:S(2)}) collective-permute-start(bf16[8,64,128]{2,1,0:T(8,128)(2,1)S(1)} %shard_map.119.g), channel_id=1, source_target_pairs={{0,28},{2,30},{4,0},{6,2},{8,4},{10,6},{12,8},{14,10},{16,12},{18,... | collective-permute-start | bytes 393224 | tf_op jit(solution)/shard_map/ppermute | solution.py:287
  29.2 6.3 %collective-permute-start.8 = (bf16[8,64,128]{2,1,0:T(8,128)(2,1)S(1)}, bf16[8,64,128]{2,1,0:T(8,128)(2,1)S(1)}, u32[]{:S(2)}, u32[]{:S(2)}) collective-permute-start(bf16[8,64,128]{2,1,0:T(8,128)(2,1)S(1)} %shard_map.119.g), channel_id=1, source_target_pairs={{0,26},{2,0},{4,30},{6,4},{8,2},{10,8},{12,6},{14,12},{16,10},{18,... | collective-permute-start | bytes 393224 | tf_op jit(solution)/shard_map/ppermute | solution.py:287
  29.2 5.8 %collective-permute-start.15 = (bf16[80,128]{1,0:T(8,128)(2,1)S(1)}, bf16[80,128]{1,0:T(8,128)(2,1)S(1)}, u32[]{:S(2)}, u32[]{:S(2)}) collective-permute-start(bf16[80,128]{1,0:T(8,128)(2,1)S(1)} %shard_map.122.refs_0_), channel_id=1, source_target_pairs={{0,24},{2,26},{4,28},{6,30},{8,16},{10,18},{12,20},{14,22},{16,8},... | collective-permute-start | bytes 61448 | tf_op jit(solution)/shard_map/ppermute | solution.py:287
  29.8 5.5 %collective-permute-start.14 = (bf16[80,128]{1,0:T(8,128)(2,1)S(1)}, bf16[80,128]{1,0:T(8,128)(2,1)S(1)}, u32[]{:S(2)}, u32[]{:S(2)}) collective-permute-start(bf16[80,128]{1,0:T(8,128)(2,1)S(1)} %shard_map.122.refs_0_), channel_id=1, source_target_pairs={{0,16},{2,18},{4,20},{6,22},{8,24},{10,26},{12,28},{14,30},{16,0},... | collective-permute-start | bytes 61448 | tf_op jit(solution)/shard_map/ppermute | solution.py:287
  31.0 4.5 %collective-permute-start.13 = (bf16[80,128]{1,0:T(8,128)(2,1)S(1)}, bf16[80,128]{1,0:T(8,128)(2,1)S(1)}, u32[]{:S(2)}, u32[]{:S(2)}) collective-permute-start(bf16[80,128]{1,0:T(8,128)(2,1)S(1)} %shard_map.122.refs_0_), channel_id=1, source_target_pairs={{0,8},{2,10},{4,12},{6,14},{8,0},{10,2},{12,4},{14,6},{16,24},{18,... | collective-permute-start | bytes 61448 | tf_op jit(solution)/shard_map/ppermute | solution.py:287
  35.5 1.4 %collective-permute-start.16 = (bf16[592,128]{1,0:T(8,128)(2,1)S(1)}, bf16[592,128]{1,0:T(8,128)(2,1)S(1)}, u32[]{:S(2)}, u32[]{:S(2)}) collective-permute-start(bf16[592,128]{1,0:T(8,128)(2,1)S(1)} %shard_map.123.sent), channel_id=1, source_target_pairs={{0,2},{2,0},{4,6},{6,4},{8,10},{10,8},{12,14},{14,12},{16,18},{18,... | collective-permute-start | bytes 454664 | tf_op jit(solution)/shard_map/ppermute | solution.py:287

commit v2 on v1

--- a/solution.py
+++ b/solution.py
@@ -9,8 +9,10 @@
 
 BLOCK = 128
 REACH = 4
+PLANE = 4
 SUM_FLOPS = 10**9
 SRC_UNIT = 2**16
+PIECES = 4
 F32 = jnp.float32
 BF16 = jnp.bfloat16
 VMEM = pl.BlockSpec(memory_space=pltpu.VMEM)
@@ -80,6 +82,24 @@
     acc[jnp.where(k < count, source(entry), blocks)] += out
 
 
+class Copy:
+    def __init__(self, source, destination, sems, first, pieces):
+        rows = destination.shape[0] // pieces
+        cuts = [pl.ds(i * rows, rows) for i in range(pieces)]
+        self.pieces = [
+            pltpu.make_async_copy(source.at[cut], destination.at[cut], sems.at[first + i])
+            for i, cut in enumerate(cuts)
+        ]
+
+    def start(self):
+        for p in self.pieces:
+            p.start()
+
+    def wait(self):
+        for p in self.pieces:
+            p.wait()
+
+
 def push_all(xt, index, count, *planes):
     def body(j):
         for tiles, acc, o in planes:
@@ -102,7 +122,7 @@
     blocks, width, _ = xt.shape
     o = 3 - 2 * own_core()
     loads = [
-        pltpu.make_async_copy(a, b, sems.at[i])
+        Copy(a, b, sems, i * PIECES, PIECES if i > 1 else 1)
         for i, (a, b) in enumerate(
             (
                 (src_hbm, src),
@@ -136,8 +156,8 @@
         c.wait()
 
 
-def forward_send_kernel(count, index, xt, tiles2, tiles3, tiles_hbm, acc2, direct, tiles0, acc, sem):
-    load = pltpu.make_async_copy(tiles_hbm.at[:, 0], tiles0, sem)
+def forward_send_kernel(count, index, xt, tiles2, tiles3, tiles_hbm, acc2, direct, tiles0, acc, sems):
+    load = Copy(tiles_hbm.at[:, 0], tiles0, sems, 0, PIECES)
     load.start()
     acc2[...] = jnp.zeros_like(acc2)
     acc[...] = jnp.zeros_like(acc)
@@ -203,9 +223,14 @@
 
 
 def weight_grad_kernel(n, *refs):
-    hts, grads, (mine, other) = refs[:n], refs[n : 2 * n], refs[2 * n :]
+    hts, grads, out = refs[:n], refs[n : 2 * n], refs[2 * n]
     full = sum(jnp.dot(h[...], g[...], preferred_element_type=F32) for h, g in zip(hts, grads))
-    full = full.astype(BF16)
+    out[...] = full.astype(BF16)
+
+
+def halves_kernel(*refs):
+    parts, (mine, other) = refs[:-2], refs[-2:]
+    full = paired_sum([r[...] for r in parts]).astype(BF16)
     rows = mine.shape[0]
     low, high = full[:rows], full[rows:]
     first = own_core() == 0
@@ -315,7 +340,8 @@
     plane = jax.ShapeDtypeStruct((groups, BLOCK, BLOCK), BF16)
     slots = jax.ShapeDtypeStruct((capacity,), jnp.int32)
     rows = jax.ShapeDtypeStruct((nodes, hid), BF16)
-    gradient = jax.ShapeDtypeStruct(((f_in + 32) // 2, hid), BF16)
+    gradient = jax.ShapeDtypeStruct((f_in + 32, hid), BF16)
+    half_gradient = jax.ShapeDtypeStruct(((f_in + 32) // 2, hid), BF16)
     flops = 2 * capacity * BLOCK * BLOCK * width // REACH
 
     def swapped(i):
@@ -331,7 +357,7 @@
             pltpu.SMEM((capacity,), jnp.int32),
             pltpu.VMEM(node_features.shape, BF16),
             acc,
-            pltpu.SemaphoreType.DMA((6,)),
+            pltpu.SemaphoreType.DMA((6 * PIECES,)),
         ],
         flops,
     )(tile_counts, *(in_hbm(a) for a in (tile_src, tile_dst, node_features, tiles)))
@@ -342,7 +368,7 @@
         [totals, piece, plane],
         [SMEM] * 2 + [VMEM] * 3 + [HBM],
         [VMEM] * 3,
-        [acc, pltpu.SemaphoreType.DMA],
+        [acc, pltpu.SemaphoreType.DMA((PIECES,))],
         2 * flops,
     )(*index, xt, tiles2, tiles3, in_hbm(tiles))
     cut = 2 if blocks % 2 == 0 else 1
@@ -373,24 +399,27 @@
         hts.append(ht)
         grads.append(grad)
         g_list += [g_own] + [moved(g, "feat", lambda i, q=q + 1: i + q) for q, g in enumerate(g_others)]
-    wg, wg_other = call(
+    (wg,) = call(
         functools.partial(weight_grad_kernel, cut),
-        [gradient, gradient],
+        [gradient],
         [VMEM] * (2 * cut),
-        [VMEM, VMEM],
+        [VMEM],
         (),
         2 * nodes * f_in * hid,
     )(*hts, *grads)
-    r, *more = radices(lax.axis_size("dom"))
-    wgs = [wg] + [moved(wg_other if s % 2 else wg, "dom", lambda i, s=s: i ^ s) for s in range(1, r)]
+    far, stride = lax.axis_size("dom") // PLANE, PLANE
+    for r in radices(far):
+        if stride > PLANE:
+            (wg,) = call(paired_sum_kernel, [gradient], [VMEM] * len(wgs), [VMEM], (), SUM_FLOPS)(*wgs)
+        wgs = exchanged(wg, "dom", stride, r)
+        stride *= r
     (g,) = call(functools.partial(join_kernel, parts), [piece], [VMEM] * len(g_list), [VMEM])(*g_list)
     g_chip = moved(g, "dom", lambda i: i - 2)
     g_direct = moved(g, "dom", lambda i: i - 3 + 2 * (i % 2))
-    stride = r
-    for r in more:
-        (wg,) = call(paired_sum_kernel, [gradient], [VMEM] * len(wgs), [VMEM], (), SUM_FLOPS)(*wgs)
-        wgs = exchanged(wg, "dom", stride, r)
-        stride *= r
+    mine, other = call(
+        halves_kernel, [half_gradient] * 2, [VMEM] * len(wgs), [VMEM] * 2, (), SUM_FLOPS
+    )(*wgs)
+    wgs = [mine] + [moved(other if s % 2 else mine, "dom", lambda i, s=s: i ^ s) for s in range(1, PLANE)]
     back0, output = call(
         backward_own_kernel,
         [totals, rows],
@@ -400,7 +429,7 @@
         flops,
     )(*index, tiles0, g, *acts)
     g_direct, g_chip, back0, *wgs = lax.optimization_barrier((g_direct, g_chip, back0, *wgs))
-    payload = jax.ShapeDtypeStruct((blocks * width + gradient.shape[0], BLOCK), BF16)
+    payload = jax.ShapeDtypeStruct((blocks * width + half_gradient.shape[0], BLOCK), BF16)
     (sent,) = call(swap_payload_kernel, [payload], [VMEM] * (1 + len(wgs)), [VMEM])(g_chip, *wgs)
     got = moved(sent, "dom", swapped)
     back2, back3 = call(

time: 38.9 us -> 39.4 us (1.013)
  Pallas kernels: 11 us -> 11.4 us
  transfers between devices with their start and end apart: 17 -> 17, of which waited for: 8 -> 7; matrix products, arithmetic and copies ran while one was open for 0% -> 0% of each run, Pallas kernels for 18% -> 18%
where the time goes in v2:
time: 39.4 us; the launch traced here: 39.2 us
  starting transfers between devices  18.8 us (48%)
  Pallas kernels  11.4 us (29%)
  waiting for transfers between devices  7.57 us (19%)
  between operations  1.39 us (4%)
    ppermute x17, starting transfers between devices, moved(): return lax.ppermute(block, axis, [(i, target(i) % n) for i in range(n)])  18.8 us
    ppermute x17, waiting for transfers between devices, moved(): return lax.ppermute(block, axis, [(i, target(i) % n) for i in range(n)])  7.57 us
    pallas_call x1, Pallas kernels, shards(): call(forward_swap_kernel, [plane, plane, plane, piece, piece, slots], [SM...  2.61 us
    pallas_call x1, Pallas kernels, shards(): call(forward_send_kernel, [totals, piece, plane], [SMEM] * 2 + [VMEM] * 3...  1.81 us
    pallas_call x2, Pallas kernels, shards(): call(functools.partial(middle_kernel, parts, first), [half_rows, half_col...  1.81 us
    pallas_call x1, Pallas kernels, shards(): call(backward_last_kernel, [jax.ShapeDtypeStruct((width, nodes), BF16), j...  1.59 us
    pallas_call x1, Pallas kernels, shards(): call(backward_own_kernel, [totals, rows], [SMEM] * 2 + [VMEM] * (2 + cut)...  1.25 us
    pallas_call x1, Pallas kernels, shards(): call(forward_own_kernel, [totals], [SMEM] * 2 + [VMEM] * 2, [VMEM], (), f...  0.95 us
  transfers between devices with their start and end apart: 17, of which 7 were waited for; matrix products, arithmetic and copies ran while one was open for 0% of the time, Pallas kernels for 18%

profile of v2, /device:TPU:0, one launch (start us, length us, event | category | flops | bytes accessed | tf_op | source)
XLA Modules:
  0.0 39.2 jit_solution(10322347643046204387)
XLA Ops:
  1.3 2.6 %shard_map.111 = (bf16[24,128,128]{2,1,0:T(8,128)(2,1)S(1)}, bf16[24,128,128]{2,1,0:T(8,128)(2,1)S(1)}, bf16[24,128,128]{2,1,0:T(8,128)(2,1)S(1)}, bf16[8,64,128...) custom-call(s32[1]{0:T(128)S(6)} %copy.12.count, s32[96]{0:T(128)} %src_hbm.1, s32[96]{0:T(128)} %dst_hbm.1, ...), custom_call_target="tpu_custom_call" | custom-call | flops 50331648 | bytes 1048576 | tf_op jit(solution)/shard_map/pallas_call | solution.py:350
  3.9 0.5 %collective-permute-start.1 = (bf16[8,64,128]{2,1,0:T(8,128)(2,1)S(1)}, bf16[8,64,128]{2,1,0:T(8,128)(2,1)S(1)}, u32[]{:S(2)}, u32[]{:S(2)}) collective-permute-start(bf16[8,64,128]{2,1,0:T(8,128)(2,1)S(1)} %get-tuple-element.48), channel_id=1, source_target_pairs={{0,2},{2,0},{4,6},{6,4},{8,10},{10,8},{12,14},{14,12},{16,18},{18,... | collective-permute-start | bytes 393224 | tf_op jit(solution)/shard_map/ppermute | solution.py:312
  4.4 1.8 %shard_map.112 = (f32[9,64,128]{2,1,0:T(8,128)S(1)}, bf16[8,64,128]{2,1,0:T(8,128)(2,1)S(1)}, bf16[24,128,128]{2,1,0:T(8,128)(2,1)S(1)}) custom-call(s32[1]{0:T(128)S(6)} %copy.12.count, s32[96]{0:T(128)S(1)} %get-tuple-element.41.index, bf16[8,64,128]{2,1,0:T(8,128)(2,1)S(1)} %get-tuple-element.42.xt, bf16[24,128,128]{2,1,0:T(8,128)(2,1)S(1)} %get-tuple-element.43.tiles2, ...), custom_call_target="tpu_custom_call" | custom-call | flops 100663296 | bytes 1048576 | tf_op jit(solution)/shard_map/pallas_call | solution.py:366
  6.4 3.0 %collective-permute-start.5 = (bf16[4,64,128]{2,1,0:T(8,128)(2,1)S(1)}, bf16[4,64,128]{2,1,0:T(8,128)(2,1)S(1)}, u32[]{:S(2)}, u32[]{:S(2)}) collective-permute-start(bf16[4,64,128]{2,1,0:T(8,128)(2,1)S(1)} %get-tuple-element.52), channel_id=1, source_target_pairs={{0,4},{2,6},{4,8},{6,10},{8,12},{10,14},{12,16},{14,18},{16,20},{1... | collective-permute-start | bytes 196616 | tf_op jit(solution)/shard_map/ppermute | solution.py:312
  9.4 1.5 %collective-permute-start.2 = (bf16[4,64,128]{2,1,0:T(8,128)(2,1)S(1)}, bf16[4,64,128]{2,1,0:T(8,128)(2,1)S(1)}, u32[]{:S(2)}, u32[]{:S(2)}) collective-permute-start(bf16[4,64,128]{2,1,0:T(8,128)(2,1)S(1)} %get-tuple-element.49), channel_id=1, source_target_pairs={{0,4},{2,6},{4,8},{6,10},{8,12},{10,14},{12,16},{14,18},{16,20},{1... | collective-permute-start | bytes 196616 | tf_op jit(solution)/shard_map/ppermute | solution.py:312
  10.9 0.9 %shard_map.113.refs_0_ = f32[9,64,128]{2,1,0:T(8,128)S(1)} custom-call(s32[1]{0:T(128)S(6)} %copy.12.count, s32[96]{0:T(128)S(1)} %get-tuple-element.41.index, bf16[8,64,128]{2,1,0:T(8,128)(2,1)S(1)} %get-tuple-element.42.xt, bf16[24,128,128]{2,1,0:T(8,128)(2,1)S(1)} %get-tuple-element.45.tiles0.tiles), custom_call_target="tpu_custom_call" | custom-call | flops 50331648 | bytes 1048576 | tf_op jit(solution)/shard_map/pallas_call | solution.py:383
  11.9 1.8 %collective-permute-done.refs_1_ = bf16[8,64,128]{2,1,0:T(8,128)(2,1)S(1)} collective-permute-done((bf16[8,64,128]{2,1,0:T(8,128)(2,1)S(1)}, bf16[8,64,128]{2,1,0:T(8,128)(2,1)S(1)}, u32[]{:S(2)}, u32[]{:S(2)}) %collective-permute-start) | collective-permute-done | bytes 131104 | tf_op jit(solution)/shard_map/ppermute | solution.py:312
  13.7 1.7 %collective-permute-done.5.refs_2_ = bf16[4,64,128]{2,1,0:T(8,128)(2,1)S(1)} collective-permute-done((bf16[4,64,128]{2,1,0:T(8,128)(2,1)S(1)}, bf16[4,64,128]{2,1,0:T(8,128)(2,1)S(1)}, u32[]{:S(2)}, u32[]{:S(2)}) %collective-permute-start.5) | collective-permute-done | bytes 65568 | tf_op jit(solution)/shard_map/ppermute | solution.py:312
  15.4 1.7 %collective-permute-start.6 = (bf16[4,64,128]{2,1,0:T(8,128)(2,1)S(1)}, bf16[4,64,128]{2,1,0:T(8,128)(2,1)S(1)}, u32[]{:S(2)}, u32[]{:S(2)}) collective-permute-start(bf16[4,64,128]{2,1,0:T(8,128)(2,1)S(1)} %shard_map.117.refs_0_), channel_id=1, source_target_pairs={{0,1},{1,0},{2,3},{3,2},{4,5},{5,4},{6,7},{7,6},{8,9},{9,8},{10,11... | collective-permute-start | bytes 196616 | tf_op jit(solution)/shard_map/ppermute | solution.py:312
  17.2 1.6 %collective-permute-start.3 = (bf16[4,64,128]{2,1,0:T(8,128)(2,1)S(1)}, bf16[4,64,128]{2,1,0:T(8,128)(2,1)S(1)}, u32[]{:S(2)}, u32[]{:S(2)}) collective-permute-start(bf16[4,64,128]{2,1,0:T(8,128)(2,1)S(1)} %shard_map.115.refs_0_), channel_id=1, source_target_pairs={{0,1},{1,0},{2,3},{3,2},{4,5},{5,4},{6,7},{7,6},{8,9},{9,8},{10,11... | collective-permute-start | bytes 196616 | tf_op jit(solution)/shard_map/ppermute | solution.py:312
  18.7 1.6 %collective-permute-done.6.refs_1_ = bf16[4,64,128]{2,1,0:T(8,128)(2,1)S(1)} collective-permute-done((bf16[4,64,128]{2,1,0:T(8,128)(2,1)S(1)}, bf16[4,64,128]{2,1,0:T(8,128)(2,1)S(1)}, u32[]{:S(2)}, u32[]{:S(2)}) %collective-permute-start.6) | collective-permute-done | bytes 65568 | tf_op jit(solution)/shard_map/ppermute | solution.py:312
  20.3 0.9 %shard_map.118 = (bf16[512,128]{1,0:T(8,128)(2,1)S(1)}, bf16[160,512]{1,0:T(8,128)(2,1)S(1)}, bf16[512,128]{1,0:T(8,128)(2,1)S(1)}, f32[4,64,128]{2,1,0:T(8,128)S(1)}, bf16[4,64,128]{2,1,0:T(8,128)(2,1)S(1)}) custom-call(f32[1,128]{1,0:T(1,128)S(1)} %bitcast.4, bf16[128,128]{1,0:T(8,128)(2,1)S(1)} %copy-done.1, bf16[1024,128]{1,0:T(8,128)(2,1)S(1)} %copy-done, ...), custom_call_target="tpu_custom_call" | custom-call | flops 33554432 | bytes 1048576 | tf_op jit(solution)/shard_map/pallas_call | solution.py:390
  21.2 1.8 %collective-permute-start.7 = (bf16[4,64,128]{2,1,0:T(8,128)(2,1)S(1)}, bf16[4,64,128]{2,1,0:T(8,128)(2,1)S(1)}, u32[]{:S(2)}, u32[]{:S(2)}) collective-permute-start(bf16[4,64,128]{2,1,0:T(8,128)(2,1)S(1)} %get-tuple-element.54), channel_id=1, source_target_pairs={{0,1},{1,0},{2,3},{3,2},{4,5},{5,4},{6,7},{7,6},{8,9},{9,8},{10,11... | collective-permute-start | bytes 196616 | tf_op jit(solution)/shard_map/ppermute | solution.py:312
  23.0 0.9 %shard_map.116 = (bf16[512,128]{1,0:T(8,128)(2,1)S(1)}, bf16[160,512]{1,0:T(8,128)(2,1)S(1)}, bf16[512,128]{1,0:T(8,128)(2,1)S(1)}, f32[4,64,128]{2,1,0:T(8,128)S(1)}, bf16[4,64,128]{2,1,0:T(8,128)(2,1)S(1)}) custom-call(f32[1,128]{1,0:T(1,128)S(1)} %bitcast.5, bf16[128,128]{1,0:T(8,128)(2,1)S(1)} %copy-done.1, bf16[1024,128]{1,0:T(8,128)(2,1)S(1)} %copy-done, ...), custom_call_target="tpu_custom_call" | custom-call | flops 33554432 | bytes 1048576 | tf_op jit(solution)/shard_map/pallas_call | solution.py:390
  23.9 0.4 %collective-permute-start.4 = (bf16[4,64,128]{2,1,0:T(8,128)(2,1)S(1)}, bf16[4,64,128]{2,1,0:T(8,128)(2,1)S(1)}, u32[]{:S(2)}, u32[]{:S(2)}) collective-permute-start(bf16[4,64,128]{2,1,0:T(8,128)(2,1)S(1)} %get-tuple-element.51), channel_id=1, source_target_pairs={{0,1},{1,0},{2,3},{3,2},{4,5},{5,4},{6,7},{7,6},{8,9},{9,8},{10,11... | collective-permute-start | bytes 196616 | tf_op jit(solution)/shard_map/ppermute | solution.py:312
  24.6 1.8 %collective-permute-start.12 = (bf16[160,128]{1,0:T(8,128)(2,1)S(1)}, bf16[160,128]{1,0:T(8,128)(2,1)S(1)}, u32[]{:S(2)}, u32[]{:S(2)}) collective-permute-start(bf16[160,128]{1,0:T(8,128)(2,1)S(1)} %shard_map.121.refs_0_), channel_id=1, source_target_pairs={{0,24},{2,26},{4,28},{6,30},{8,16},{10,18},{12,20},{14,22},{16,8},... | collective-permute-start | bytes 122888 | tf_op jit(solution)/shard_map/ppermute | solution.py:312
  26.3 2.7 %collective-permute-start.10 = (bf16[160,128]{1,0:T(8,128)(2,1)S(1)}, bf16[160,128]{1,0:T(8,128)(2,1)S(1)}, u32[]{:S(2)}, u32[]{:S(2)}) collective-permute-start(bf16[160,128]{1,0:T(8,128)(2,1)S(1)} %shard_map.121.refs_0_), channel_id=1, source_target_pairs={{0,8},{2,10},{4,12},{6,14},{8,0},{10,2},{12,4},{14,6},{16,24},{18,... | collective-permute-start | bytes 122888 | tf_op jit(solution)/shard_map/ppermute | solution.py:312
  29.1 1.4 %collective-permute-start.9 = (bf16[8,64,128]{2,1,0:T(8,128)(2,1)S(1)}, bf16[8,64,128]{2,1,0:T(8,128)(2,1)S(1)}, u32[]{:S(2)}, u32[]{:S(2)}) collective-permute-start(bf16[8,64,128]{2,1,0:T(8,128)(2,1)S(1)} %shard_map.119.g), channel_id=1, source_target_pairs={{0,28},{2,30},{4,0},{6,2},{8,4},{10,6},{12,8},{14,10},{16,12},{18,... | collective-permute-start | bytes 393224 | tf_op jit(solution)/shard_map/ppermute | solution.py:312
  30.5 0.4 %collective-permute-done.12.refs_3_ = bf16[160,128]{1,0:T(8,128)(2,1)S(1)} collective-permute-done((bf16[160,128]{1,0:T(8,128)(2,1)S(1)}, bf16[160,128]{1,0:T(8,128)(2,1)S(1)}, u32[]{:S(2)}, u32[]{:S(2)}) %collective-permute-start.12) | collective-permute-done | bytes 40992 | tf_op jit(solution)/shard_map/ppermute | solution.py:312
  30.9 1.3 %collective-permute-done.11.refs_2_ = bf16[160,128]{1,0:T(8,128)(2,1)S(1)} collective-permute-done((bf16[160,128]{1,0:T(8,128)(2,1)S(1)}, bf16[160,128]{1,0:T(8,128)(2,1)S(1)}, u32[]{:S(2)}, u32[]{:S(2)}) %collective-permute-start.11) | collective-permute-done | bytes 40992 | tf_op jit(solution)/shard_map/ppermute | solution.py:312
  32.4 2.0 %collective-permute-start.13 = (bf16[80,128]{1,0:T(8,128)(2,1)S(1)}, bf16[80,128]{1,0:T(8,128)(2,1)S(1)}, u32[]{:S(2)}, u32[]{:S(2)}) collective-permute-start(bf16[80,128]{1,0:T(8,128)(2,1)S(1)} %get-tuple-element.65), channel_id=1, source_target_pairs={{0,2},{2,0},{4,6},{6,4},{8,10},{10,8},{12,14},{14,12},{16,18},{18,... | collective-permute-start | bytes 61448 | tf_op jit(solution)/shard_map/ppermute | solution.py:312
  34.5 1.3 %shard_map.120 = (f32[9,64,128]{2,1,0:T(8,128)S(1)}, bf16[1024,128]{1,0:T(8,128)(2,1)}) custom-call(s32[1]{0:T(128)S(6)} %copy.12.count, s32[96]{0:T(128)S(1)} %get-tuple-element.41.index, bf16[24,128,128]{2,1,0:T(8,128)(2,1)S(1)} %get-tuple-element.45.tiles0.tiles, bf16[8,64,128]{2,1,0:T(8,128)(2,1)S(1)} %shard_map.119.g, ...), custom_call_target="tpu_custom_call" | custom-call | flops 50331648 | bytes 1048576 | tf_op jit(solution)/shard_map/pallas_call | solution.py:423
  36.3 0.9 %shard_map.124 = (f32[9,64,128]{2,1,0:T(8,128)S(1)}, f32[9,64,128]{2,1,0:T(8,128)S(1)}) custom-call(s32[1]{0:T(128)S(6)} %copy.12.count, s32[96]{0:T(128)S(1)} %get-tuple-element.41.index, bf16[24,128,128]{2,1,0:T(8,128)(2,1)S(1)} %get-tuple-element.43.tiles2, bf16[24,128,128]{2,1,0:T(8,128)(2,1)S(1)} %get-tuple-element.44.tiles3, ...), custom_call_target="tpu_custom_call" | custom-call | flops 100663296 | bytes 1048576 | tf_op jit(solution)/shard_map/pallas_call | solution.py:435
  37.6 1.6 %shard_map.125 = (bf16[64,1024]{1,0:T(8,128)(2,1)}, f32[128,128]{1,0:T(8,128)}, f32[1,128]{1,0:T(1,128)}) custom-call(s32[1]{0:T(128)S(6)} %copy.12.count, s32[96]{0:T(128)S(1)} %get-tuple-element.41.index, bf16[24,128,128]{2,1,0:T(8,128)(2,1)S(1)} %get-tuple-element.58.tiles1, bf16[592,128]{1,0:T(8,128)(2,1)S(1)} %shard_map.123.sent, ...), custom_call_target="tpu_custom_call" | custom-call | flops 50331648 | bytes 1048576 | tf_op jit(solution)/shard_map/pallas_call | solution.py:438
  (31 shorter events, 1.6 us)
Async XLA Ops:
  3.9 2.5 %collective-permute-start.1 = (bf16[8,64,128]{2,1,0:T(8,128)(2,1)S(1)}, bf16[8,64,128]{2,1,0:T(8,128)(2,1)S(1)}, u32[]{:S(2)}, u32[]{:S(2)}) collective-permute-start(bf16[8,64,128]{2,1,0:T(8,128)(2,1)S(1)} %get-tuple-element.48), channel_id=1, source_target_pairs={{0,2},{2,0},{4,6},{6,4},{8,10},{10,8},{12,14},{14,12},{16,18},{18,... | collective-permute-start | bytes 393224 | tf_op jit(solution)/shard_map/ppermute | solution.py:312
  4.4 15.9 %copy-start = (bf16[1024,128]{1,0:T(8,128)(2,1)S(1)}, bf16[1024,128]{1,0:T(8,128)(2,1)}, u32[]{:S(2)}) copy-start(bf16[1024,128]{1,0:T(8,128)(2,1)} %og_ref.3) | copy-start | bytes 786436
  4.4 15.9 %copy-start.1 = (bf16[128,128]{1,0:T(8,128)(2,1)S(1)}, bf16[128,128]{1,0:T(8,128)(2,1)}, u32[]{:S(2)}) copy-start(bf16[128,128]{1,0:T(8,128)(2,1)} %w_ref.3) | copy-start | bytes 98308
  4.4 15.9 %copy-start.2 = (f32[128]{0:T(128)S(1)}, f32[128]{0:T(128)}, u32[]{:S(2)}) copy-start(f32[128]{0:T(128)} %param.10) | copy-start | bytes 1540
  6.2 7.4 %collective-permute-start = (bf16[8,64,128]{2,1,0:T(8,128)(2,1)S(1)}, bf16[8,64,128]{2,1,0:T(8,128)(2,1)S(1)}, u32[]{:S(2)}, u32[]{:S(2)}) collective-permute-start(bf16[8,64,128]{2,1,0:T(8,128)(2,1)S(1)} %get-tuple-element.46), channel_id=1, source_target_pairs={{0,2},{2,8},{4,6},{6,12},{8,10},{10,16},{12,14},{14,20},{16,18},{1... | collective-permute-start | bytes 393224 | tf_op jit(solution)/shard_map/ppermute | solution.py:312
  6.4 9.0 %collective-permute-start.5 = (bf16[4,64,128]{2,1,0:T(8,128)(2,1)S(1)}, bf16[4,64,128]{2,1,0:T(8,128)(2,1)S(1)}, u32[]{:S(2)}, u32[]{:S(2)}) collective-permute-start(bf16[4,64,128]{2,1,0:T(8,128)(2,1)S(1)} %get-tuple-element.52), channel_id=1, source_target_pairs={{0,4},{2,6},{4,8},{6,10},{8,12},{10,14},{12,16},{14,18},{16,20},{1... | collective-permute-start | bytes 196616 | tf_op jit(solution)/shard_map/ppermute | solution.py:312
  9.4 7.7 %collective-permute-start.2 = (bf16[4,64,128]{2,1,0:T(8,128)(2,1)S(1)}, bf16[4,64,128]{2,1,0:T(8,128)(2,1)S(1)}, u32[]{:S(2)}, u32[]{:S(2)}) collective-permute-start(bf16[4,64,128]{2,1,0:T(8,128)(2,1)S(1)} %get-tuple-element.49), channel_id=1, source_target_pairs={{0,4},{2,6},{4,8},{6,10},{8,12},{10,14},{12,16},{14,18},{16,20},{1... | collective-permute-start | bytes 196616 | tf_op jit(solution)/shard_map/ppermute | solution.py:312
  15.4 4.9 %collective-permute-start.6 = (bf16[4,64,128]{2,1,0:T(8,128)(2,1)S(1)}, bf16[4,64,128]{2,1,0:T(8,128)(2,1)S(1)}, u32[]{:S(2)}, u32[]{:S(2)}) collective-permute-start(bf16[4,64,128]{2,1,0:T(8,128)(2,1)S(1)} %shard_map.117.refs_0_), channel_id=1, source_target_pairs={{0,1},{1,0},{2,3},{3,2},{4,5},{5,4},{6,7},{7,6},{8,9},{9,8},{10,11... | collective-permute-start | bytes 196616 | tf_op jit(solution)/shard_map/ppermute | solution.py:312
  17.2 5.9 %collective-permute-start.3 = (bf16[4,64,128]{2,1,0:T(8,128)(2,1)S(1)}, bf16[4,64,128]{2,1,0:T(8,128)(2,1)S(1)}, u32[]{:S(2)}, u32[]{:S(2)}) collective-permute-start(bf16[4,64,128]{2,1,0:T(8,128)(2,1)S(1)} %shard_map.115.refs_0_), channel_id=1, source_target_pairs={{0,1},{1,0},{2,3},{3,2},{4,5},{5,4},{6,7},{7,6},{8,9},{9,8},{10,11... | collective-permute-start | bytes 196616 | tf_op jit(solution)/shard_map/ppermute | solution.py:312
  21.2 7.8 %collective-permute-start.7 = (bf16[4,64,128]{2,1,0:T(8,128)(2,1)S(1)}, bf16[4,64,128]{2,1,0:T(8,128)(2,1)S(1)}, u32[]{:S(2)}, u32[]{:S(2)}) collective-permute-start(bf16[4,64,128]{2,1,0:T(8,128)(2,1)S(1)} %get-tuple-element.54), channel_id=1, source_target_pairs={{0,1},{1,0},{2,3},{3,2},{4,5},{5,4},{6,7},{7,6},{8,9},{9,8},{10,11... | collective-permute-start | bytes 196616 | tf_op jit(solution)/shard_map/ppermute | solution.py:312
  23.9 5.1 %collective-permute-start.4 = (bf16[4,64,128]{2,1,0:T(8,128)(2,1)S(1)}, bf16[4,64,128]{2,1,0:T(8,128)(2,1)S(1)}, u32[]{:S(2)}, u32[]{:S(2)}) collective-permute-start(bf16[4,64,128]{2,1,0:T(8,128)(2,1)S(1)} %get-tuple-element.51), channel_id=1, source_target_pairs={{0,1},{1,0},{2,3},{3,2},{4,5},{5,4},{6,7},{7,6},{8,9},{9,8},{10,11... | collective-permute-start | bytes 196616 | tf_op jit(solution)/shard_map/ppermute | solution.py:312
  24.6 6.3 %collective-permute-start.12 = (bf16[160,128]{1,0:T(8,128)(2,1)S(1)}, bf16[160,128]{1,0:T(8,128)(2,1)S(1)}, u32[]{:S(2)}, u32[]{:S(2)}) collective-permute-start(bf16[160,128]{1,0:T(8,128)(2,1)S(1)} %shard_map.121.refs_0_), channel_id=1, source_target_pairs={{0,24},{2,26},{4,28},{6,30},{8,16},{10,18},{12,20},{14,22},{16,8},... | collective-permute-start | bytes 122888 | tf_op jit(solution)/shard_map/ppermute | solution.py:312
  26.3 5.9 %collective-permute-start.11 = (bf16[160,128]{1,0:T(8,128)(2,1)S(1)}, bf16[160,128]{1,0:T(8,128)(2,1)S(1)}, u32[]{:S(2)}, u32[]{:S(2)}) collective-permute-start(bf16[160,128]{1,0:T(8,128)(2,1)S(1)} %shard_map.121.refs_0_), channel_id=1, source_target_pairs={{0,16},{2,18},{4,20},{6,22},{8,24},{10,26},{12,28},{14,30},{16,0},... | collective-permute-start | bytes 122888 | tf_op jit(solution)/shard_map/ppermute | solution.py:312
  26.3 5.9 %collective-permute-start.10 = (bf16[160,128]{1,0:T(8,128)(2,1)S(1)}, bf16[160,128]{1,0:T(8,128)(2,1)S(1)}, u32[]{:S(2)}, u32[]{:S(2)}) collective-permute-start(bf16[160,128]{1,0:T(8,128)(2,1)S(1)} %shard_map.121.refs_0_), channel_id=1, source_target_pairs={{0,8},{2,10},{4,12},{6,14},{8,0},{10,2},{12,4},{14,6},{16,24},{18,... | collective-permute-start | bytes 122888 | tf_op jit(solution)/shard_map/ppermute | solution.py:312
  29.1 7.0 %collective-permute-start.9 = (bf16[8,64,128]{2,1,0:T(8,128)(2,1)S(1)}, bf16[8,64,128]{2,1,0:T(8,128)(2,1)S(1)}, u32[]{:S(2)}, u32[]{:S(2)}) collective-permute-start(bf16[8,64,128]{2,1,0:T(8,128)(2,1)S(1)} %shard_map.119.g), channel_id=1, source_target_pairs={{0,28},{2,30},{4,0},{6,2},{8,4},{10,6},{12,8},{14,10},{16,12},{18,... | collective-permute-start | bytes 393224 | tf_op jit(solution)/shard_map/ppermute | solution.py:312
  30.5 5.7 %collective-permute-start.8 = (bf16[8,64,128]{2,1,0:T(8,128)(2,1)S(1)}, bf16[8,64,128]{2,1,0:T(8,128)(2,1)S(1)}, u32[]{:S(2)}, u32[]{:S(2)}) collective-permute-start(bf16[8,64,128]{2,1,0:T(8,128)(2,1)S(1)} %shard_map.119.g), channel_id=1, source_target_pairs={{0,26},{2,0},{4,30},{6,4},{8,2},{10,8},{12,6},{14,12},{16,10},{18,... | collective-permute-start | bytes 393224 | tf_op jit(solution)/shard_map/ppermute | solution.py:312
  32.3 3.8 %collective-permute-start.14 = (bf16[80,128]{1,0:T(8,128)(2,1)S(1)}, bf16[80,128]{1,0:T(8,128)(2,1)S(1)}, u32[]{:S(2)}, u32[]{:S(2)}) collective-permute-start(bf16[80,128]{1,0:T(8,128)(2,1)S(1)} %get-tuple-element.67.refs_0_), channel_id=1, source_target_pairs={{0,4},{2,6},{4,0},{6,2},{8,12},{10,14},{12,8},{14,10},{16,20},{18,... | collective-permute-start | bytes 61448 | tf_op jit(solution)/shard_map/ppermute | solution.py:312
  32.3 3.8 %collective-permute-start.15 = (bf16[80,128]{1,0:T(8,128)(2,1)S(1)}, bf16[80,128]{1,0:T(8,128)(2,1)S(1)}, u32[]{:S(2)}, u32[]{:S(2)}) collective-permute-start(bf16[80,128]{1,0:T(8,128)(2,1)S(1)} %get-tuple-element.65), channel_id=1, source_target_pairs={{0,6},{2,4},{4,2},{6,0},{8,14},{10,12},{12,10},{14,8},{16,22},{18,... | collective-permute-start | bytes 61448 | tf_op jit(solution)/shard_map/ppermute | solution.py:312
  32.4 3.7 %collective-permute-start.13 = (bf16[80,128]{1,0:T(8,128)(2,1)S(1)}, bf16[80,128]{1,0:T(8,128)(2,1)S(1)}, u32[]{:S(2)}, u32[]{:S(2)}) collective-permute-start(bf16[80,128]{1,0:T(8,128)(2,1)S(1)} %get-tuple-element.65), channel_id=1, source_target_pairs={{0,2},{2,0},{4,6},{6,4},{8,10},{10,8},{12,14},{14,12},{16,18},{18,... | collective-permute-start | bytes 61448 | tf_op jit(solution)/shard_map/ppermute | solution.py:312
  36.2 1.4 %collective-permute-start.16 = (bf16[592,128]{1,0:T(8,128)(2,1)S(1)}, bf16[592,128]{1,0:T(8,128)(2,1)S(1)}, u32[]{:S(2)}, u32[]{:S(2)}) collective-permute-start(bf16[592,128]{1,0:T(8,128)(2,1)S(1)} %shard_map.123.sent), channel_id=1, source_target_pairs={{0,2},{2,0},{4,6},{6,4},{8,10},{10,8},{12,14},{14,12},{16,18},{18,... | collective-permute-start | bytes 454664 | tf_op jit(solution)/shard_map/ppermute | solution.py:312

commit v3 on v1

--- a/solution.py
+++ b/solution.py
@@ -136,18 +136,22 @@
         c.wait()
 
 
-def forward_send_kernel(count, index, xt, tiles2, tiles3, tiles_hbm, acc2, direct, tiles0, acc, sem):
-    load = pltpu.make_async_copy(tiles_hbm.at[:, 0], tiles0, sem)
-    load.start()
+def forward_send_kernel(count, index, xt, tiles2, tiles3, acc2, *refs):
+    direct, acc = refs[:-1], refs[-1]
     acc2[...] = jnp.zeros_like(acc2)
     acc[...] = jnp.zeros_like(acc)
     push_all(xt, index, count[0], (tiles2, acc2, 2), (tiles3, acc, 1 + 2 * own_core()))
-    direct[...] = acc[: direct.shape[0]].astype(BF16)
+    first = 0
+    for d in direct:
+        d[...] = acc[first : first + d.shape[0]].astype(BF16)
+        first += d.shape[0]
+
+
+def forward_own_kernel(count, index, xt, tiles_hbm, acc, tiles0, sem):
+    load = pltpu.make_async_copy(tiles_hbm.at[:, 0], tiles0, sem)
+    load.start()
+    acc[...] = jnp.zeros_like(acc)
     load.wait()
-
-
-def forward_own_kernel(count, index, xt, tiles0, acc):
-    acc[...] = jnp.zeros_like(acc)
     push_all(xt, index, count[0], (tiles0, acc, 0))
 
 
@@ -337,27 +341,35 @@
     )(tile_counts, *(in_hbm(a) for a in (tile_src, tile_dst, node_features, tiles)))
     index = (tile_counts, index)
     swap = moved(swap, "dom", swapped)
-    acc2, direct, tiles0 = call(
-        forward_send_kernel,
-        [totals, piece, plane],
-        [SMEM] * 2 + [VMEM] * 3 + [HBM],
-        [VMEM] * 3,
-        [acc, pltpu.SemaphoreType.DMA],
-        2 * flops,
-    )(*index, xt, tiles2, tiles3, in_hbm(tiles))
     cut = 2 if blocks % 2 == 0 else 1
     starts = range(0, blocks, blocks // cut)
     half = jax.ShapeDtypeStruct((blocks // cut, width, BLOCK), BF16)
     half_wide = jax.ShapeDtypeStruct(half.shape, F32)
     half_rows = jax.ShapeDtypeStruct((nodes // cut, hid), BF16)
     half_columns = jax.ShapeDtypeStruct((f_in + 32, nodes // cut), BF16)
+    acc2, *direct = call(
+        forward_send_kernel,
+        [totals] + [half] * cut,
+        [SMEM] * 2 + [VMEM] * 3,
+        [VMEM] * (1 + cut),
+        [acc],
+        2 * flops,
+    )(*index, xt, tiles2, tiles3)
     chip = call(functools.partial(sum_kernel, 2, 0), [half] * cut, [VMEM] * 2, [VMEM] * cut)(acc2, swap)
     chip = [moved(c, "dom", lambda i: i + 2) for c in chip]
-    direct = moved(direct, "dom", lambda i: i + 1 + 2 * (i % 2))
-    (acc0,) = call(forward_own_kernel, [totals], [SMEM] * 2 + [VMEM] * 2, [VMEM], (), flops)(*index, xt, tiles0)
+    acc0, tiles0 = call(
+        forward_own_kernel,
+        [totals, plane],
+        [SMEM] * 2 + [VMEM, HBM],
+        [VMEM] * 2,
+        [pltpu.SemaphoreType.DMA],
+        flops,
+    )(*index, xt, in_hbm(tiles))
+    acc0, direct[0] = lax.optimization_barrier((acc0, direct[0]))
+    direct = [moved(d, "dom", lambda i: i + 1 + 2 * (i % 2)) for d in direct]
     h_lists = []
-    for first, c in zip(starts, chip):
-        (h,) = call(functools.partial(sum_kernel, 3, first), [half], [VMEM] * 3, [VMEM])(acc0, direct, c)
+    for first, c, d in zip(starts, chip, direct):
+        (h,) = call(functools.partial(sum_kernel, 3, first), [half], [VMEM] * 3, [VMEM])(acc0, d, c)
         h_lists.append([h] + [moved(h, "feat", lambda i, q=q: i - q) for q in range(1, parts)])
     acts, hts, grads, g_list = [], [], [], []
     for first, hs in zip(starts, h_lists):

time: 38.9 us -> 40.6 us (1.044)
  starting transfers between devices: 18.9 us -> 20.9 us
  waiting for transfers between devices: 7.27 us -> 6.2 us
  Pallas kernels: 11 us -> 11.6 us
    ppermute x17 -> x18, starting transfers between devices: 18.9 us -> 20.9 us  [moved(): return lax.ppermute(block, axis, [(i, target(i) % n) for i in range(n)])]
    ppermute x17 -> x18, waiting for transfers between devices: 7.27 us -> 6.2 us  [moved(): return lax.ppermute(block, axis, [(i, target(i) % n) for i in range(n)])]
    pallas_call x2, Pallas kernels: 2.65 us -> 3.32 us  [the longest x1 2.08 us: shards(): call(forward_own_kernel, [totals, plane], [SMEM] * 2 + [VMEM, HBM], [VMEM...]
  transfers between devices with their start and end apart: 17 -> 18, of which waited for: 8 -> 6; matrix products, arithmetic and copies ran while one was open for 0% -> 0% of each run, Pallas kernels for 18% -> 19%
where the time goes in v3:
time: 40.6 us; the launch traced here: 40.2 us
  starting transfers between devices  20.9 us (51%)
  Pallas kernels  11.6 us (29%)
  waiting for transfers between devices  6.2 us (15%)
  between operations  1.41 us (3%)
    ppermute x18, starting transfers between devices, moved(): return lax.ppermute(block, axis, [(i, target(i) % n) for i in range(n)])  20.9 us
    ppermute x18, waiting for transfers between devices, moved(): return lax.ppermute(block, axis, [(i, target(i) % n) for i in range(n)])  6.2 us
    pallas_call x1, Pallas kernels, shards(): call(forward_swap_kernel, [plane, plane, plane, piece, piece, slots], [SM...  2.35 us
    pallas_call x1, Pallas kernels, shards(): call(forward_own_kernel, [totals, plane], [SMEM] * 2 + [VMEM, HBM], [VMEM...  2.08 us
    pallas_call x2, Pallas kernels, shards(): call(functools.partial(middle_kernel, parts, first), [half_rows, half_col...  1.8 us
    pallas_call x1, Pallas kernels, shards(): call(backward_last_kernel, [jax.ShapeDtypeStruct((width, nodes), BF16), j...  1.58 us
    pallas_call x1, Pallas kernels, shards(): call(backward_own_kernel, [totals, rows], [SMEM] * 2 + [VMEM] * (2 + cut)...  1.25 us
    pallas_call x1, Pallas kernels, shards(): call(forward_send_kernel, [totals] + [half] * cut, [SMEM] * 2 + [VMEM] *...  1.24 us
  transfers between devices with their start and end apart: 18, of which 6 were waited for; matrix products, arithmetic and copies ran while one was open for 0% of the time, Pallas kernels for 19%

profile of v3, /device:TPU:0, one launch (start us, length us, event | category | flops | bytes accessed | tf_op | source)
XLA Modules:
  0.0 40.2 jit_solution(7461873352552312341)
XLA Ops:
  1.3 2.3 %shard_map.111 = (bf16[24,128,128]{2,1,0:T(8,128)(2,1)S(1)}, bf16[24,128,128]{2,1,0:T(8,128)(2,1)S(1)}, bf16[24,128,128]{2,1,0:T(8,128)(2,1)S(1)}, bf16[8,64,128...) custom-call(s32[1]{0:T(128)S(6)} %copy.12.count, s32[96]{0:T(128)} %src_hbm.1, s32[96]{0:T(128)} %dst_hbm.1, ...), custom_call_target="tpu_custom_call" | custom-call | flops 50331648 | bytes 1048576 | tf_op jit(solution)/shard_map/pallas_call | solution.py:328
  3.6 0.8 %collective-permute-start.1 = (bf16[8,64,128]{2,1,0:T(8,128)(2,1)S(1)}, bf16[8,64,128]{2,1,0:T(8,128)(2,1)S(1)}, u32[]{:S(2)}, u32[]{:S(2)}) collective-permute-start(bf16[8,64,128]{2,1,0:T(8,128)(2,1)S(1)} %get-tuple-element.55), channel_id=1, source_target_pairs={{0,2},{2,0},{4,6},{6,4},{8,10},{10,8},{12,14},{14,12},{16,18},{18,... | collective-permute-start | bytes 393224 | tf_op jit(solution)/shard_map/ppermute | solution.py:291
  4.5 1.2 %shard_map.113 = (f32[9,64,128]{2,1,0:T(8,128)S(1)}, bf16[4,64,128]{2,1,0:T(8,128)(2,1)S(1)}, bf16[4,64,128]{2,1,0:T(8,128)(2,1)S(1)}) custom-call(s32[1]{0:T(128)S(6)} %copy.12.count, s32[96]{0:T(128)S(1)} %get-tuple-element.45.index, bf16[8,64,128]{2,1,0:T(8,128)(2,1)S(1)} %get-tuple-element.46.xt, bf16[24,128,128]{2,1,0:T(8,128)(2,1)S(1)} %get-tuple-element.49.tiles2, ...), custom_call_target="tpu_custom_call" | custom-call | flops 100663296 | bytes 1048576 | tf_op jit(solution)/shard_map/pallas_call | solution.py:350
  5.7 0.7 %collective-permute-start.5 = (bf16[4,64,128]{2,1,0:T(8,128)(2,1)S(1)}, bf16[4,64,128]{2,1,0:T(8,128)(2,1)S(1)}, u32[]{:S(2)}, u32[]{:S(2)}) collective-permute-start(bf16[4,64,128]{2,1,0:T(8,128)(2,1)S(1)} %get-tuple-element.59), channel_id=1, source_target_pairs={{0,2},{2,8},{4,6},{6,12},{8,10},{10,16},{12,14},{14,20},{16,18},{1... | collective-permute-start | bytes 196616 | tf_op jit(solution)/shard_map/ppermute | solution.py:291
  6.5 2.6 %collective-permute-start.6 = (bf16[4,64,128]{2,1,0:T(8,128)(2,1)S(1)}, bf16[4,64,128]{2,1,0:T(8,128)(2,1)S(1)}, u32[]{:S(2)}, u32[]{:S(2)}) collective-permute-start(bf16[4,64,128]{2,1,0:T(8,128)(2,1)S(1)} %get-tuple-element.60), channel_id=1, source_target_pairs={{0,4},{2,6},{4,8},{6,10},{8,12},{10,14},{12,16},{14,18},{16,20},{1... | collective-permute-start | bytes 196616 | tf_op jit(solution)/shard_map/ppermute | solution.py:291
  9.1 2.1 %shard_map.112 = (f32[9,64,128]{2,1,0:T(8,128)S(1)}, bf16[24,128,128]{2,1,0:T(8,128)(2,1)S(1)}) custom-call(s32[1]{0:T(128)S(6)} %copy.12.count, s32[96]{0:T(128)S(1)} %get-tuple-element.45.index, bf16[8,64,128]{2,1,0:T(8,128)(2,1)S(1)} %get-tuple-element.46.xt, bf16[24,4,128,128]{3,2,1,0:T(8,128)(2,1)} %bitcast.7), custom_call_target="tpu_custom_call" | custom-call | flops 50331648 | bytes 1048576 | tf_op jit(solution)/shard_map/pallas_call | solution.py:360
  11.2 0.9 %collective-permute-start = (bf16[4,64,128]{2,1,0:T(8,128)(2,1)S(1)}, bf16[4,64,128]{2,1,0:T(8,128)(2,1)S(1)}, u32[]{:S(2)}, u32[]{:S(2)}) collective-permute-start(bf16[4,64,128]{2,1,0:T(8,128)(2,1)S(1)} %get-tuple-element.53), channel_id=1, source_target_pairs={{0,2},{2,8},{4,6},{6,12},{8,10},{10,16},{12,14},{14,20},{16,18},{1... | collective-permute-start | bytes 196616 | tf_op jit(solution)/shard_map/ppermute | solution.py:291
  12.0 1.2 %collective-permute-start.2 = (bf16[4,64,128]{2,1,0:T(8,128)(2,1)S(1)}, bf16[4,64,128]{2,1,0:T(8,128)(2,1)S(1)}, u32[]{:S(2)}, u32[]{:S(2)}) collective-permute-start(bf16[4,64,128]{2,1,0:T(8,128)(2,1)S(1)} %get-tuple-element.56), channel_id=1, source_target_pairs={{0,4},{2,6},{4,8},{6,10},{8,12},{10,14},{12,16},{14,18},{16,20},{1... | collective-permute-start | bytes 196616 | tf_op jit(solution)/shard_map/ppermute | solution.py:291
  13.2 1.3 %collective-permute-done.6.refs_2_ = bf16[4,64,128]{2,1,0:T(8,128)(2,1)S(1)} collective-permute-done((bf16[4,64,128]{2,1,0:T(8,128)(2,1)S(1)}, bf16[4,64,128]{2,1,0:T(8,128)(2,1)S(1)}, u32[]{:S(2)}, u32[]{:S(2)}) %collective-permute-start.6) | collective-permute-done | bytes 65568 | tf_op jit(solution)/shard_map/ppermute | solution.py:291
  14.5 2.3 %collective-permute-start.7 = (bf16[4,64,128]{2,1,0:T(8,128)(2,1)S(1)}, bf16[4,64,128]{2,1,0:T(8,128)(2,1)S(1)}, u32[]{:S(2)}, u32[]{:S(2)}) collective-permute-start(bf16[4,64,128]{2,1,0:T(8,128)(2,1)S(1)} %shard_map.117.refs_0_), channel_id=1, source_target_pairs={{0,1},{1,0},{2,3},{3,2},{4,5},{5,4},{6,7},{7,6},{8,9},{9,8},{10,11... | collective-permute-start | bytes 196616 | tf_op jit(solution)/shard_map/ppermute | solution.py:291
  16.9 2.2 %collective-permute-done.2.refs_2_ = bf16[4,64,128]{2,1,0:T(8,128)(2,1)S(1)} collective-permute-done((bf16[4,64,128]{2,1,0:T(8,128)(2,1)S(1)}, bf16[4,64,128]{2,1,0:T(8,128)(2,1)S(1)}, u32[]{:S(2)}, u32[]{:S(2)}) %collective-permute-start.2) | collective-permute-done | bytes 65568 | tf_op jit(solution)/shard_map/ppermute | solution.py:291
  19.1 1.6 %collective-permute-start.3 = (bf16[4,64,128]{2,1,0:T(8,128)(2,1)S(1)}, bf16[4,64,128]{2,1,0:T(8,128)(2,1)S(1)}, u32[]{:S(2)}, u32[]{:S(2)}) collective-permute-start(bf16[4,64,128]{2,1,0:T(8,128)(2,1)S(1)} %shard_map.115.refs_0_), channel_id=1, source_target_pairs={{0,1},{1,0},{2,3},{3,2},{4,5},{5,4},{6,7},{7,6},{8,9},{9,8},{10,11... | collective-permute-start | bytes 196616 | tf_op jit(solution)/shard_map/ppermute | solution.py:291
  20.7 0.9 %shard_map.118 = (bf16[512,128]{1,0:T(8,128)(2,1)S(1)}, bf16[160,512]{1,0:T(8,128)(2,1)S(1)}, bf16[512,128]{1,0:T(8,128)(2,1)S(1)}, f32[4,64,128]{2,1,0:T(8,128)S(1)}, bf16[4,64,128]{2,1,0:T(8,128)(2,1)S(1)}) custom-call(f32[1,128]{1,0:T(1,128)S(1)} %bitcast.4, bf16[128,128]{1,0:T(8,128)(2,1)S(1)} %copy-done.1, bf16[1024,128]{1,0:T(8,128)(2,1)S(1)} %copy-done, ...), custom_call_target="tpu_custom_call" | custom-call | flops 33554432 | bytes 1048576 | tf_op jit(solution)/shard_map/pallas_call | solution.py:376
  22.2 1.3 %collective-permute-done.3.refs_1_ = bf16[4,64,128]{2,1,0:T(8,128)(2,1)S(1)} collective-permute-done((bf16[4,64,128]{2,1,0:T(8,128)(2,1)S(1)}, bf16[4,64,128]{2,1,0:T(8,128)(2,1)S(1)}, u32[]{:S(2)}, u32[]{:S(2)}) %collective-permute-start.3) | collective-permute-done | bytes 65568 | tf_op jit(solution)/shard_map/ppermute | solution.py:291
  23.5 0.9 %shard_map.116 = (bf16[512,128]{1,0:T(8,128)(2,1)S(1)}, bf16[160,512]{1,0:T(8,128)(2,1)S(1)}, bf16[512,128]{1,0:T(8,128)(2,1)S(1)}, f32[4,64,128]{2,1,0:T(8,128)S(1)}, bf16[4,64,128]{2,1,0:T(8,128)(2,1)S(1)}) custom-call(f32[1,128]{1,0:T(1,128)S(1)} %bitcast.5, bf16[128,128]{1,0:T(8,128)(2,1)S(1)} %copy-done.1, bf16[1024,128]{1,0:T(8,128)(2,1)S(1)} %copy-done, ...), custom_call_target="tpu_custom_call" | custom-call | flops 33554432 | bytes 1048576 | tf_op jit(solution)/shard_map/pallas_call | solution.py:376
  24.4 2.0 %collective-permute-start.4 = (bf16[4,64,128]{2,1,0:T(8,128)(2,1)S(1)}, bf16[4,64,128]{2,1,0:T(8,128)(2,1)S(1)}, u32[]{:S(2)}, u32[]{:S(2)}) collective-permute-start(bf16[4,64,128]{2,1,0:T(8,128)(2,1)S(1)} %get-tuple-element.58), channel_id=1, source_target_pairs={{0,1},{1,0},{2,3},{3,2},{4,5},{5,4},{6,7},{7,6},{8,9},{9,8},{10,11... | collective-permute-start | bytes 196616 | tf_op jit(solution)/shard_map/ppermute | solution.py:291
  26.8 2.0 %collective-permute-start.11 = (bf16[80,128]{1,0:T(8,128)(2,1)S(1)}, bf16[80,128]{1,0:T(8,128)(2,1)S(1)}, u32[]{:S(2)}, u32[]{:S(2)}) collective-permute-start(bf16[80,128]{1,0:T(8,128)(2,1)S(1)} %get-tuple-element.73), channel_id=1, source_target_pairs={{0,2},{2,0},{4,6},{6,4},{8,10},{10,8},{12,14},{14,12},{16,18},{18,... | collective-permute-start | bytes 61448 | tf_op jit(solution)/shard_map/ppermute | solution.py:291
  29.4 1.0 %collective-permute-start.9 = (bf16[8,64,128]{2,1,0:T(8,128)(2,1)S(1)}, bf16[8,64,128]{2,1,0:T(8,128)(2,1)S(1)}, u32[]{:S(2)}, u32[]{:S(2)}) collective-permute-start(bf16[8,64,128]{2,1,0:T(8,128)(2,1)S(1)} %shard_map.119.g), channel_id=1, source_target_pairs={{0,26},{2,0},{4,30},{6,4},{8,2},{10,8},{12,6},{14,12},{16,10},{18,... | collective-permute-start | bytes 393224 | tf_op jit(solution)/shard_map/ppermute | solution.py:291
  30.5 1.0 %collective-permute-start.16 = (bf16[80,128]{1,0:T(8,128)(2,1)S(1)}, bf16[80,128]{1,0:T(8,128)(2,1)S(1)}, u32[]{:S(2)}, u32[]{:S(2)}) collective-permute-start(bf16[80,128]{1,0:T(8,128)(2,1)S(1)} %shard_map.122.refs_0_), channel_id=1, source_target_pairs={{0,24},{2,26},{4,28},{6,30},{8,16},{10,18},{12,20},{14,22},{16,8},... | collective-permute-start | bytes 61448 | tf_op jit(solution)/shard_map/ppermute | solution.py:291
  31.4 1.1 %collective-permute-start.15 = (bf16[80,128]{1,0:T(8,128)(2,1)S(1)}, bf16[80,128]{1,0:T(8,128)(2,1)S(1)}, u32[]{:S(2)}, u32[]{:S(2)}) collective-permute-start(bf16[80,128]{1,0:T(8,128)(2,1)S(1)} %shard_map.122.refs_0_), channel_id=1, source_target_pairs={{0,16},{2,18},{4,20},{6,22},{8,24},{10,26},{12,28},{14,30},{16,0},... | collective-permute-start | bytes 61448 | tf_op jit(solution)/shard_map/ppermute | solution.py:291
  32.6 2.4 %collective-permute-start.14 = (bf16[80,128]{1,0:T(8,128)(2,1)S(1)}, bf16[80,128]{1,0:T(8,128)(2,1)S(1)}, u32[]{:S(2)}, u32[]{:S(2)}) collective-permute-start(bf16[80,128]{1,0:T(8,128)(2,1)S(1)} %shard_map.122.refs_0_), channel_id=1, source_target_pairs={{0,8},{2,10},{4,12},{6,14},{8,0},{10,2},{12,4},{14,6},{16,24},{18,... | collective-permute-start | bytes 61448 | tf_op jit(solution)/shard_map/ppermute | solution.py:291
  34.9 1.3 %shard_map.120 = (f32[9,64,128]{2,1,0:T(8,128)S(1)}, bf16[1024,128]{1,0:T(8,128)(2,1)}) custom-call(s32[1]{0:T(128)S(6)} %copy.12.count, s32[96]{0:T(128)S(1)} %get-tuple-element.45.index, bf16[24,128,128]{2,1,0:T(8,128)(2,1)S(1)} %get-tuple-element.47.tiles, bf16[8,64,128]{2,1,0:T(8,128)(2,1)S(1)} %shard_map.119.g, ...), custom_call_target="tpu_custom_call" | custom-call | flops 50331648 | bytes 1048576 | tf_op jit(solution)/shard_map/pallas_call | solution.py:406
  37.2 0.9 %shard_map.124 = (f32[9,64,128]{2,1,0:T(8,128)S(1)}, f32[9,64,128]{2,1,0:T(8,128)S(1)}) custom-call(s32[1]{0:T(128)S(6)} %copy.12.count, s32[96]{0:T(128)S(1)} %get-tuple-element.45.index, bf16[24,128,128]{2,1,0:T(8,128)(2,1)S(1)} %get-tuple-element.49.tiles2, bf16[24,128,128]{2,1,0:T(8,128)(2,1)S(1)} %get-tuple-element.50.tiles3, ...), custom_call_target="tpu_custom_call" | custom-call | flops 100663296 | bytes 1048576 | tf_op jit(solution)/shard_map/pallas_call | solution.py:418
  38.6 1.6 %shard_map.125 = (bf16[64,1024]{1,0:T(8,128)(2,1)}, f32[128,128]{1,0:T(8,128)}, f32[1,128]{1,0:T(1,128)}) custom-call(s32[1]{0:T(128)S(6)} %copy.12.count, s32[96]{0:T(128)S(1)} %get-tuple-element.45.index, bf16[24,128,128]{2,1,0:T(8,128)(2,1)S(1)} %get-tuple-element.66.tiles1, bf16[592,128]{1,0:T(8,128)(2,1)S(1)} %shard_map.123.sent, ...), custom_call_target="tpu_custom_call" | custom-call | flops 50331648 | bytes 1048576 | tf_op jit(solution)/shard_map/pallas_call | solution.py:421
  (33 shorter events, 3.1 us)
Async XLA Ops:
  3.6 2.8 %collective-permute-start.1 = (bf16[8,64,128]{2,1,0:T(8,128)(2,1)S(1)}, bf16[8,64,128]{2,1,0:T(8,128)(2,1)S(1)}, u32[]{:S(2)}, u32[]{:S(2)}) collective-permute-start(bf16[8,64,128]{2,1,0:T(8,128)(2,1)S(1)} %get-tuple-element.55), channel_id=1, source_target_pairs={{0,2},{2,0},{4,6},{6,4},{8,10},{10,8},{12,14},{14,12},{16,18},{18,... | collective-permute-start | bytes 393224 | tf_op jit(solution)/shard_map/ppermute | solution.py:291
  4.5 16.2 %copy-start = (bf16[1024,128]{1,0:T(8,128)(2,1)S(1)}, bf16[1024,128]{1,0:T(8,128)(2,1)}, u32[]{:S(2)}) copy-start(bf16[1024,128]{1,0:T(8,128)(2,1)} %og_ref.3) | copy-start | bytes 786436
  4.5 16.2 %copy-start.1 = (bf16[128,128]{1,0:T(8,128)(2,1)S(1)}, bf16[128,128]{1,0:T(8,128)(2,1)}, u32[]{:S(2)}) copy-start(bf16[128,128]{1,0:T(8,128)(2,1)} %w_ref.3) | copy-start | bytes 98308
  4.5 16.2 %copy-start.2 = (f32[128]{0:T(128)S(1)}, f32[128]{0:T(128)}, u32[]{:S(2)}) copy-start(f32[128]{0:T(128)} %param.10) | copy-start | bytes 1540
  5.7 7.5 %collective-permute-start.5 = (bf16[4,64,128]{2,1,0:T(8,128)(2,1)S(1)}, bf16[4,64,128]{2,1,0:T(8,128)(2,1)S(1)}, u32[]{:S(2)}, u32[]{:S(2)}) collective-permute-start(bf16[4,64,128]{2,1,0:T(8,128)(2,1)S(1)} %get-tuple-element.59), channel_id=1, source_target_pairs={{0,2},{2,8},{4,6},{6,12},{8,10},{10,16},{12,14},{14,20},{16,18},{1... | collective-permute-start | bytes 196616 | tf_op jit(solution)/shard_map/ppermute | solution.py:291
  6.5 8.0 %collective-permute-start.6 = (bf16[4,64,128]{2,1,0:T(8,128)(2,1)S(1)}, bf16[4,64,128]{2,1,0:T(8,128)(2,1)S(1)}, u32[]{:S(2)}, u32[]{:S(2)}) collective-permute-start(bf16[4,64,128]{2,1,0:T(8,128)(2,1)S(1)} %get-tuple-element.60), channel_id=1, source_target_pairs={{0,4},{2,6},{4,8},{6,10},{8,12},{10,14},{12,16},{14,18},{16,20},{1... | collective-permute-start | bytes 196616 | tf_op jit(solution)/shard_map/ppermute | solution.py:291
  11.2 5.7 %collective-permute-start = (bf16[4,64,128]{2,1,0:T(8,128)(2,1)S(1)}, bf16[4,64,128]{2,1,0:T(8,128)(2,1)S(1)}, u32[]{:S(2)}, u32[]{:S(2)}) collective-permute-start(bf16[4,64,128]{2,1,0:T(8,128)(2,1)S(1)} %get-tuple-element.53), channel_id=1, source_target_pairs={{0,2},{2,8},{4,6},{6,12},{8,10},{10,16},{12,14},{14,20},{16,18},{1... | collective-permute-start | bytes 196616 | tf_op jit(solution)/shard_map/ppermute | solution.py:291
  12.0 7.1 %collective-permute-start.2 = (bf16[4,64,128]{2,1,0:T(8,128)(2,1)S(1)}, bf16[4,64,128]{2,1,0:T(8,128)(2,1)S(1)}, u32[]{:S(2)}, u32[]{:S(2)}) collective-permute-start(bf16[4,64,128]{2,1,0:T(8,128)(2,1)S(1)} %get-tuple-element.56), channel_id=1, source_target_pairs={{0,4},{2,6},{4,8},{6,10},{8,12},{10,14},{12,16},{14,18},{16,20},{1... | collective-permute-start | bytes 196616 | tf_op jit(solution)/shard_map/ppermute | solution.py:291
  14.5 6.1 %collective-permute-start.7 = (bf16[4,64,128]{2,1,0:T(8,128)(2,1)S(1)}, bf16[4,64,128]{2,1,0:T(8,128)(2,1)S(1)}, u32[]{:S(2)}, u32[]{:S(2)}) collective-permute-start(bf16[4,64,128]{2,1,0:T(8,128)(2,1)S(1)} %shard_map.117.refs_0_), channel_id=1, source_target_pairs={{0,1},{1,0},{2,3},{3,2},{4,5},{5,4},{6,7},{7,6},{8,9},{9,8},{10,11... | collective-permute-start | bytes 196616 | tf_op jit(solution)/shard_map/ppermute | solution.py:291
  19.1 4.3 %collective-permute-start.3 = (bf16[4,64,128]{2,1,0:T(8,128)(2,1)S(1)}, bf16[4,64,128]{2,1,0:T(8,128)(2,1)S(1)}, u32[]{:S(2)}, u32[]{:S(2)}) collective-permute-start(bf16[4,64,128]{2,1,0:T(8,128)(2,1)S(1)} %shard_map.115.refs_0_), channel_id=1, source_target_pairs={{0,1},{1,0},{2,3},{3,2},{4,5},{5,4},{6,7},{7,6},{8,9},{9,8},{10,11... | collective-permute-start | bytes 196616 | tf_op jit(solution)/shard_map/ppermute | solution.py:291
  21.6 7.2 %collective-permute-start.8 = (bf16[4,64,128]{2,1,0:T(8,128)(2,1)S(1)}, bf16[4,64,128]{2,1,0:T(8,128)(2,1)S(1)}, u32[]{:S(2)}, u32[]{:S(2)}) collective-permute-start(bf16[4,64,128]{2,1,0:T(8,128)(2,1)S(1)} %get-tuple-element.62), channel_id=1, source_target_pairs={{0,1},{1,0},{2,3},{3,2},{4,5},{5,4},{6,7},{7,6},{8,9},{9,8},{10,11... | collective-permute-start | bytes 196616 | tf_op jit(solution)/shard_map/ppermute | solution.py:291
  24.4 4.5 %collective-permute-start.4 = (bf16[4,64,128]{2,1,0:T(8,128)(2,1)S(1)}, bf16[4,64,128]{2,1,0:T(8,128)(2,1)S(1)}, u32[]{:S(2)}, u32[]{:S(2)}) collective-permute-start(bf16[4,64,128]{2,1,0:T(8,128)(2,1)S(1)} %get-tuple-element.58), channel_id=1, source_target_pairs={{0,1},{1,0},{2,3},{3,2},{4,5},{5,4},{6,7},{7,6},{8,9},{9,8},{10,11... | collective-permute-start | bytes 196616 | tf_op jit(solution)/shard_map/ppermute | solution.py:291
  26.6 3.8 %collective-permute-start.12 = (bf16[80,128]{1,0:T(8,128)(2,1)S(1)}, bf16[80,128]{1,0:T(8,128)(2,1)S(1)}, u32[]{:S(2)}, u32[]{:S(2)}) collective-permute-start(bf16[80,128]{1,0:T(8,128)(2,1)S(1)} %get-tuple-element.72.refs_0_), channel_id=1, source_target_pairs={{0,4},{2,6},{4,0},{6,2},{8,12},{10,14},{12,8},{14,10},{16,20},{18,... | collective-permute-start | bytes 61448 | tf_op jit(solution)/shard_map/ppermute | solution.py:291
  26.7 3.8 %collective-permute-start.13 = (bf16[80,128]{1,0:T(8,128)(2,1)S(1)}, bf16[80,128]{1,0:T(8,128)(2,1)S(1)}, u32[]{:S(2)}, u32[]{:S(2)}) collective-permute-start(bf16[80,128]{1,0:T(8,128)(2,1)S(1)} %get-tuple-element.73), channel_id=1, source_target_pairs={{0,6},{2,4},{4,2},{6,0},{8,14},{10,12},{12,10},{14,8},{16,22},{18,... | collective-permute-start | bytes 61448 | tf_op jit(solution)/shard_map/ppermute | solution.py:291
  26.8 3.7 %collective-permute-start.11 = (bf16[80,128]{1,0:T(8,128)(2,1)S(1)}, bf16[80,128]{1,0:T(8,128)(2,1)S(1)}, u32[]{:S(2)}, u32[]{:S(2)}) collective-permute-start(bf16[80,128]{1,0:T(8,128)(2,1)S(1)} %get-tuple-element.73), channel_id=1, source_target_pairs={{0,2},{2,0},{4,6},{6,4},{8,10},{10,8},{12,14},{14,12},{16,18},{18,... | collective-permute-start | bytes 61448 | tf_op jit(solution)/shard_map/ppermute | solution.py:291
  28.9 8.2 %collective-permute-start.10 = (bf16[8,64,128]{2,1,0:T(8,128)(2,1)S(1)}, bf16[8,64,128]{2,1,0:T(8,128)(2,1)S(1)}, u32[]{:S(2)}, u32[]{:S(2)}) collective-permute-start(bf16[8,64,128]{2,1,0:T(8,128)(2,1)S(1)} %shard_map.119.g), channel_id=1, source_target_pairs={{0,28},{2,30},{4,0},{6,2},{8,4},{10,6},{12,8},{14,10},{16,12},{18,... | collective-permute-start | bytes 393224 | tf_op jit(solution)/shard_map/ppermute | solution.py:291
  29.4 7.7 %collective-permute-start.9 = (bf16[8,64,128]{2,1,0:T(8,128)(2,1)S(1)}, bf16[8,64,128]{2,1,0:T(8,128)(2,1)S(1)}, u32[]{:S(2)}, u32[]{:S(2)}) collective-permute-start(bf16[8,64,128]{2,1,0:T(8,128)(2,1)S(1)} %shard_map.119.g), channel_id=1, source_target_pairs={{0,26},{2,0},{4,30},{6,4},{8,2},{10,8},{12,6},{14,12},{16,10},{18,... | collective-permute-start | bytes 393224 | tf_op jit(solution)/shard_map/ppermute | solution.py:291
  30.5 6.4 %collective-permute-start.16 = (bf16[80,128]{1,0:T(8,128)(2,1)S(1)}, bf16[80,128]{1,0:T(8,128)(2,1)S(1)}, u32[]{:S(2)}, u32[]{:S(2)}) collective-permute-start(bf16[80,128]{1,0:T(8,128)(2,1)S(1)} %shard_map.122.refs_0_), channel_id=1, source_target_pairs={{0,24},{2,26},{4,28},{6,30},{8,16},{10,18},{12,20},{14,22},{16,8},... | collective-permute-start | bytes 61448 | tf_op jit(solution)/shard_map/ppermute | solution.py:291
  31.4 5.6 %collective-permute-start.15 = (bf16[80,128]{1,0:T(8,128)(2,1)S(1)}, bf16[80,128]{1,0:T(8,128)(2,1)S(1)}, u32[]{:S(2)}, u32[]{:S(2)}) collective-permute-start(bf16[80,128]{1,0:T(8,128)(2,1)S(1)} %shard_map.122.refs_0_), channel_id=1, source_target_pairs={{0,16},{2,18},{4,20},{6,22},{8,24},{10,26},{12,28},{14,30},{16,0},... | collective-permute-start | bytes 61448 | tf_op jit(solution)/shard_map/ppermute | solution.py:291
  32.6 4.5 %collective-permute-start.14 = (bf16[80,128]{1,0:T(8,128)(2,1)S(1)}, bf16[80,128]{1,0:T(8,128)(2,1)S(1)}, u32[]{:S(2)}, u32[]{:S(2)}) collective-permute-start(bf16[80,128]{1,0:T(8,128)(2,1)S(1)} %shard_map.122.refs_0_), channel_id=1, source_target_pairs={{0,8},{2,10},{4,12},{6,14},{8,0},{10,2},{12,4},{14,6},{16,24},{18,... | collective-permute-start | bytes 61448 | tf_op jit(solution)/shard_map/ppermute | solution.py:291
  37.1 1.4 %collective-permute-start.17 = (bf16[592,128]{1,0:T(8,128)(2,1)S(1)}, bf16[592,128]{1,0:T(8,128)(2,1)S(1)}, u32[]{:S(2)}, u32[]{:S(2)}) collective-permute-start(bf16[592,128]{1,0:T(8,128)(2,1)S(1)} %shard_map.123.sent), channel_id=1, source_target_pairs={{0,2},{2,0},{4,6},{6,4},{8,10},{10,8},{12,14},{14,12},{16,18},{18,... | collective-permute-start | bytes 454664 | tf_op jit(solution)/shard_map/ppermute | solution.py:291

commit v4 on v1

--- a/solution.py
+++ b/solution.py
@@ -136,18 +136,39 @@
         c.wait()
 
 
-def forward_send_kernel(count, index, xt, tiles2, tiles3, tiles_hbm, acc2, direct, tiles0, acc, sem):
-    load = pltpu.make_async_copy(tiles_hbm.at[:, 0], tiles0, sem)
-    load.start()
+def forward_send_kernel(count, index, xt, tiles2, tiles3, acc2, direct, acc):
     acc2[...] = jnp.zeros_like(acc2)
     acc[...] = jnp.zeros_like(acc)
     push_all(xt, index, count[0], (tiles2, acc2, 2), (tiles3, acc, 1 + 2 * own_core()))
     direct[...] = acc[: direct.shape[0]].astype(BF16)
+
+
+def unit(n):
+    shape = (n, n)
+    return (lax.broadcasted_iota(jnp.int32, shape, 0) == lax.broadcasted_iota(jnp.int32, shape, 1)).astype(BF16)
+
+
+def turned(block):
+    n = block.shape[1]
+    return lax.dot_general(
+        unit(n), block, (((1,), (1,)), ((), ())), preferred_element_type=F32
+    ).astype(BF16)
+
+
+def forward_own_kernel(
+    count, index, xt, bias_ref, w_ref, og_hbm, tiles_hbm, acc, tiles0, bias_t, w_t, og_t, og_ref, sems
+):
+    load_og = pltpu.make_async_copy(og_hbm, og_ref, sems.at[0])
+    load_og.start()
+    load = pltpu.make_async_copy(tiles_hbm.at[:, 0], tiles0, sems.at[1])
+    load.start()
+    acc[...] = jnp.zeros_like(acc)
+    bias_t[...] = jnp.broadcast_to(bias_ref[...], (BLOCK, bias_ref.shape[1])).T
+    w_t[...] = turned(w_ref[...])
+    load_og.wait()
+    for first in range(0, og_ref.shape[0], BLOCK):
+        og_t[:, first : first + BLOCK] = turned(og_ref[first : first + BLOCK, :])
     load.wait()
-
-
-def forward_own_kernel(count, index, xt, tiles0, acc):
-    acc[...] = jnp.zeros_like(acc)
     push_all(xt, index, count[0], (tiles0, acc, 0))
 
 
@@ -175,36 +196,36 @@
         first += blocks
 
 
-def middle_kernel(parts, first, bias_ref, w_ref, og_ref, *refs):
+def middle_kernel(parts, first, bias_ref, w_ref, w_t_ref, og_ref, *refs):
     h_refs, (act, ht, grads), g_refs = refs[:parts], refs[parts : parts + 3], refs[parts + 3 :]
     blocks, width, _ = h_refs[0].shape
     f_in = w_ref.shape[0]
     me = lax.axis_index("feat")
+    rows = [pl.multiple_of(lax.rem(me + q, parts) * width, width) for q in range(parts)]
     for q in range(parts):
-        row = pl.multiple_of(lax.rem(me + q, parts) * width, width)
         for b in range(blocks):
-            ht[pl.ds(row, width), b * BLOCK : (b + 1) * BLOCK] = h_refs[q][b]
+            ht[pl.ds(rows[q], width), b * BLOCK : (b + 1) * BLOCK] = h_refs[q][b]
     ht[f_in:, :] = jnp.ones((ht.shape[0] - f_in, ht.shape[1]), BF16)
     for b in range(blocks):
-        rows = slice(b * BLOCK, (b + 1) * BLOCK)
-        pre = lax.dot_general(
-            ht[:f_in, rows], w_ref[...], (((0,), (0,)), ((), ())), preferred_element_type=F32
-        ) + bias_ref[...]
+        cols = slice(b * BLOCK, (b + 1) * BLOCK)
+        pre = jnp.dot(w_t_ref[...], ht[:f_in, cols], preferred_element_type=F32) + bias_ref[...]
         s = jax.nn.sigmoid(pre)
-        act[rows, :] = (pre * s).astype(BF16)
-        og = og_ref[(first + b) * BLOCK : (first + b + 1) * BLOCK, :].astype(F32)
+        act[:, cols] = (pre * s).astype(BF16)
+        og = og_ref[:, (first + b) * BLOCK : (first + b + 1) * BLOCK].astype(F32)
         grad = (og * s * (1.0 + pre * (1.0 - s))).astype(BF16)
-        grads[rows, :] = grad
+        grads[:, cols] = grad
         for q in range(parts):
-            row = pl.multiple_of(lax.rem(me + q, parts) * width, width)
-            g_refs[q][b] = lax.dot_general(
-                w_ref[pl.ds(row, width), :], grad, (((1,), (1,)), ((), ())), preferred_element_type=F32
+            g_refs[q][b] = jnp.dot(
+                w_ref[pl.ds(rows[q], width), :], grad, preferred_element_type=F32
             ).astype(g_refs[q].dtype)
 
 
 def weight_grad_kernel(n, *refs):
     hts, grads, (mine, other) = refs[:n], refs[n : 2 * n], refs[2 * n :]
-    full = sum(jnp.dot(h[...], g[...], preferred_element_type=F32) for h, g in zip(hts, grads))
+    full = sum(
+        lax.dot_general(h[...], g[...], (((1,), (1,)), ((), ())), preferred_element_type=F32)
+        for h, g in zip(hts, grads)
+    )
     full = full.astype(BF16)
     rows = mine.shape[0]
     low, high = full[:rows], full[rows:]
@@ -226,13 +247,15 @@
 
 
 def backward_own_kernel(count, index, tiles, g, *refs):
-    acts, (acc, out, sems) = refs[:-3], refs[-3:]
+    acts, (acc, out, rows, sems) = refs[:-4], refs[-4:]
     copies, first = [], 0
     for i, act in enumerate(acts):
-        rows = act.shape[0]
-        copies.append(pltpu.make_async_copy(act, out.at[pl.ds(first, rows)], sems.at[i]))
+        for col in range(0, act.shape[1], BLOCK):
+            rows[first + col : first + col + BLOCK, :] = turned(act[:, col : col + BLOCK])
+        part = pl.ds(first, act.shape[1])
+        copies.append(pltpu.make_async_copy(rows.at[part], out.at[part], sems.at[i]))
         copies[-1].start()
-        first += rows
+        first += act.shape[1]
     acc[...] = jnp.zeros_like(acc)
     pull_all(index, count[0], (lambda d: g[d], tiles, acc, 0))
     for c in copies:
@@ -337,24 +360,32 @@
     )(tile_counts, *(in_hbm(a) for a in (tile_src, tile_dst, node_features, tiles)))
     index = (tile_counts, index)
     swap = moved(swap, "dom", swapped)
-    acc2, direct, tiles0 = call(
-        forward_send_kernel,
-        [totals, piece, plane],
-        [SMEM] * 2 + [VMEM] * 3 + [HBM],
-        [VMEM] * 3,
-        [acc, pltpu.SemaphoreType.DMA],
-        2 * flops,
-    )(*index, xt, tiles2, tiles3, in_hbm(tiles))
+    acc2, direct = call(
+        forward_send_kernel, [totals, piece], [SMEM] * 2 + [VMEM] * 3, [VMEM] * 2, [acc], 2 * flops
+    )(*index, xt, tiles2, tiles3)
     cut = 2 if blocks % 2 == 0 else 1
     starts = range(0, blocks, blocks // cut)
     half = jax.ShapeDtypeStruct((blocks // cut, width, BLOCK), BF16)
     half_wide = jax.ShapeDtypeStruct(half.shape, F32)
-    half_rows = jax.ShapeDtypeStruct((nodes // cut, hid), BF16)
+    half_rows = jax.ShapeDtypeStruct((hid, nodes // cut), BF16)
     half_columns = jax.ShapeDtypeStruct((f_in + 32, nodes // cut), BF16)
     chip = call(functools.partial(sum_kernel, 2, 0), [half] * cut, [VMEM] * 2, [VMEM] * cut)(acc2, swap)
     chip = [moved(c, "dom", lambda i: i + 2) for c in chip]
     direct = moved(direct, "dom", lambda i: i + 1 + 2 * (i % 2))
-    (acc0,) = call(forward_own_kernel, [totals], [SMEM] * 2 + [VMEM] * 2, [VMEM], (), flops)(*index, xt, tiles0)
+    acc0, tiles0, bias_t, w_t, og_t = call(
+        forward_own_kernel,
+        [
+            totals,
+            plane,
+            jax.ShapeDtypeStruct((hid, BLOCK), F32),
+            jax.ShapeDtypeStruct((hid, f_in), BF16),
+            jax.ShapeDtypeStruct((hid, nodes), BF16),
+        ],
+        [SMEM] * 2 + [VMEM] * 3 + [HBM] * 2,
+        [VMEM] * 5,
+        [pltpu.VMEM(out_grad.shape, BF16), pltpu.SemaphoreType.DMA((2,))],
+        flops,
+    )(*index, xt, bias.reshape(1, hid), weight, in_hbm(out_grad), in_hbm(tiles))
     h_lists = []
     for first, c in zip(starts, chip):
         (h,) = call(functools.partial(sum_kernel, 3, first), [half], [VMEM] * 3, [VMEM])(acc0, direct, c)
@@ -364,11 +395,11 @@
         act, ht, grad, g_own, *g_others = call(
             functools.partial(middle_kernel, parts, first),
             [half_rows, half_columns, half_rows, half_wide] + [half] * (parts - 1),
-            [VMEM] * (3 + parts),
+            [VMEM] * (4 + parts),
             [VMEM] * (3 + parts),
             (),
             4 * nodes * f_in * hid // cut,
-        )(bias.reshape(1, hid), weight, out_grad, *hs)
+        )(bias_t, weight, w_t, og_t, *hs)
         acts.append(act)
         hts.append(ht)
         grads.append(grad)
@@ -396,7 +427,7 @@
         [totals, rows],
         [SMEM] * 2 + [VMEM] * (2 + cut),
         [VMEM, HBM],
-        [pltpu.SemaphoreType.DMA((cut,))],
+        [pltpu.VMEM(rows.shape, BF16), pltpu.SemaphoreType.DMA((cut,))],
         flops,
     )(*index, tiles0, g, *acts)
     g_direct, g_chip, back0, *wgs = lax.optimization_barrier((g_direct, g_chip, back0, *wgs))

time: 38.9 us -> 39 us (level)
  Pallas kernels: 11 us -> 13.8 us
  starting transfers between devices: 18.9 us -> 17.2 us
  waiting for transfers between devices: 7.27 us -> 5.99 us
    pallas_call x2, Pallas kernels: 2.65 us -> 4.47 us  [the longest x1 2.59 us: shards(): call(forward_own_kernel, [totals, plane, jax.ShapeDtypeStruct((hid, BLOCK...]
    ppermute x17, starting transfers between devices: 18.9 us -> 17.2 us  [moved(): return lax.ppermute(block, axis, [(i, target(i) % n) for i in range(n)])]
    ppermute x17, waiting for transfers between devices: 7.27 us -> 5.99 us  [moved(): return lax.ppermute(block, axis, [(i, target(i) % n) for i in range(n)])]
  transfers between devices with their start and end apart: 17 -> 17, of which waited for: 8 -> 7; matrix products, arithmetic and copies ran while one was open for 0% -> 0% of each run, Pallas kernels for 18% -> 24%
where the time goes in v4:
time: 39 us; the launch traced here: 38.4 us
  starting transfers between devices  17.2 us (44%)
  Pallas kernels  13.8 us (35%)
  waiting for transfers between devices  5.99 us (15%)
  between operations  1.43 us (4%)
    ppermute x17, starting transfers between devices, moved(): return lax.ppermute(block, axis, [(i, target(i) % n) for i in range(n)])  17.2 us
    ppermute x17, waiting for transfers between devices, moved(): return lax.ppermute(block, axis, [(i, target(i) % n) for i in range(n)])  5.99 us
    pallas_call x1, Pallas kernels, shards(): call(forward_swap_kernel, [plane, plane, plane, piece, piece, slots], [SM...  2.66 us
    pallas_call x1, Pallas kernels, shards(): call(forward_own_kernel, [totals, plane, jax.ShapeDtypeStruct((hid, BLOCK...  2.59 us
    pallas_call x1, Pallas kernels, shards(): call(forward_send_kernel, [totals, piece], [SMEM] * 2 + [VMEM] * 3, [VMEM...  1.88 us
    pallas_call x1, Pallas kernels, shards(): call(backward_last_kernel, [jax.ShapeDtypeStruct((width, nodes), BF16), j...  1.82 us
    pallas_call x2, Pallas kernels, shards(): call(functools.partial(middle_kernel, parts, first), [half_rows, half_col...  1.64 us
    pallas_call x1, Pallas kernels, shards(): call(backward_own_kernel, [totals, rows], [SMEM] * 2 + [VMEM] * (2 + cut)...  1.51 us
  transfers between devices with their start and end apart: 17, of which 7 were waited for; matrix products, arithmetic and copies ran while one was open for 0% of the time, Pallas kernels for 24%

profile of v4, /device:TPU:0, one launch (start us, length us, event | category | flops | bytes accessed | tf_op | source)
XLA Modules:
  0.0 38.4 jit_solution(3085028534722605348)
XLA Ops:
  1.3 2.7 %shard_map.111 = (bf16[24,128,128]{2,1,0:T(8,128)(2,1)S(1)}, bf16[24,128,128]{2,1,0:T(8,128)(2,1)S(1)}, bf16[24,128,128]{2,1,0:T(8,128)(2,1)S(1)}, bf16[8,64,128...) custom-call(s32[1]{0:T(128)S(6)} %copy.12.count, s32[96]{0:T(128)} %src_hbm.1, s32[96]{0:T(128)} %dst_hbm.1, ...), custom_call_target="tpu_custom_call" | custom-call | flops 50331648 | bytes 1048576 | tf_op jit(solution)/shard_map/pallas_call | solution.py:347
  4.0 0.5 %collective-permute-start.1 = (bf16[8,64,128]{2,1,0:T(8,128)(2,1)S(1)}, bf16[8,64,128]{2,1,0:T(8,128)(2,1)S(1)}, u32[]{:S(2)}, u32[]{:S(2)}) collective-permute-start(bf16[8,64,128]{2,1,0:T(8,128)(2,1)S(1)} %get-tuple-element.56), channel_id=1, source_target_pairs={{0,2},{2,0},{4,6},{6,4},{8,10},{10,8},{12,14},{14,12},{16,18},{18,... | collective-permute-start | bytes 393224 | tf_op jit(solution)/shard_map/ppermute | solution.py:310
  4.5 1.9 %shard_map.113 = (f32[9,64,128]{2,1,0:T(8,128)S(1)}, bf16[8,64,128]{2,1,0:T(8,128)(2,1)S(1)}) custom-call(s32[1]{0:T(128)S(6)} %copy.12.count, s32[96]{0:T(128)S(1)} %get-tuple-element.45.index, bf16[8,64,128]{2,1,0:T(8,128)(2,1)S(1)} %get-tuple-element.46.xt, bf16[24,128,128]{2,1,0:T(8,128)(2,1)S(1)} %get-tuple-element.52.tiles2, ...), custom_call_target="tpu_custom_call" | custom-call | flops 100663296 | bytes 1048576 | tf_op jit(solution)/shard_map/pallas_call | solution.py:363
  6.5 2.1 %collective-permute-start.5 = (bf16[4,64,128]{2,1,0:T(8,128)(2,1)S(1)}, bf16[4,64,128]{2,1,0:T(8,128)(2,1)S(1)}, u32[]{:S(2)}, u32[]{:S(2)}) collective-permute-start(bf16[4,64,128]{2,1,0:T(8,128)(2,1)S(1)} %get-tuple-element.60), channel_id=1, source_target_pairs={{0,4},{2,6},{4,8},{6,10},{8,12},{10,14},{12,16},{14,18},{16,20},{1... | collective-permute-start | bytes 196616 | tf_op jit(solution)/shard_map/ppermute | solution.py:310
  8.6 1.5 %collective-permute-start.2 = (bf16[4,64,128]{2,1,0:T(8,128)(2,1)S(1)}, bf16[4,64,128]{2,1,0:T(8,128)(2,1)S(1)}, u32[]{:S(2)}, u32[]{:S(2)}) collective-permute-start(bf16[4,64,128]{2,1,0:T(8,128)(2,1)S(1)} %get-tuple-element.57), channel_id=1, source_target_pairs={{0,4},{2,6},{4,8},{6,10},{8,12},{10,14},{12,16},{14,18},{16,20},{1... | collective-permute-start | bytes 196616 | tf_op jit(solution)/shard_map/ppermute | solution.py:310
  10.1 2.6 %shard_map.112 = (f32[9,64,128]{2,1,0:T(8,128)S(1)}, bf16[24,128,128]{2,1,0:T(8,128)(2,1)S(1)}, f32[128,128]{1,0:T(8,128)S(1)}, bf16[128,128]{1,0:T(8,128)(2,1)S(1)}, bf16[128,1024]{1,0:T(8,128)(2,1)S(1)}) custom-call(s32[1]{0:T(128)S(6)} %copy.12.count, s32[96]{0:T(128)S(1)} %get-tuple-element.45.index, bf16[8,64,128]{2,1,0:T(8,128)(2,1)S(1)} %get-tuple-element.46.xt, ...), custom_call_target="tpu_custom_call" | custom-call | flops 50331648 | bytes 1048576 | tf_op jit(solution)/shard_map/pallas_call | solution.py:375
  12.9 1.7 %collective-permute-done.5.refs_2_ = bf16[4,64,128]{2,1,0:T(8,128)(2,1)S(1)} collective-permute-done((bf16[4,64,128]{2,1,0:T(8,128)(2,1)S(1)}, bf16[4,64,128]{2,1,0:T(8,128)(2,1)S(1)}, u32[]{:S(2)}, u32[]{:S(2)}) %collective-permute-start.5) | collective-permute-done | bytes 65568 | tf_op jit(solution)/shard_map/ppermute | solution.py:310
  14.6 2.6 %collective-permute-start.6 = (bf16[4,64,128]{2,1,0:T(8,128)(2,1)S(1)}, bf16[4,64,128]{2,1,0:T(8,128)(2,1)S(1)}, u32[]{:S(2)}, u32[]{:S(2)}) collective-permute-start(bf16[4,64,128]{2,1,0:T(8,128)(2,1)S(1)} %shard_map.117.refs_0_), channel_id=1, source_target_pairs={{0,1},{1,0},{2,3},{3,2},{4,5},{5,4},{6,7},{7,6},{8,9},{9,8},{10,11... | collective-permute-start | bytes 196616 | tf_op jit(solution)/shard_map/ppermute | solution.py:310
  17.2 1.0 %collective-permute-start.3 = (bf16[4,64,128]{2,1,0:T(8,128)(2,1)S(1)}, bf16[4,64,128]{2,1,0:T(8,128)(2,1)S(1)}, u32[]{:S(2)}, u32[]{:S(2)}) collective-permute-start(bf16[4,64,128]{2,1,0:T(8,128)(2,1)S(1)} %shard_map.115.refs_0_), channel_id=1, source_target_pairs={{0,1},{1,0},{2,3},{3,2},{4,5},{5,4},{6,7},{7,6},{8,9},{9,8},{10,11... | collective-permute-start | bytes 196616 | tf_op jit(solution)/shard_map/ppermute | solution.py:310
  18.2 1.9 %collective-permute-done.6.refs_1_ = bf16[4,64,128]{2,1,0:T(8,128)(2,1)S(1)} collective-permute-done((bf16[4,64,128]{2,1,0:T(8,128)(2,1)S(1)}, bf16[4,64,128]{2,1,0:T(8,128)(2,1)S(1)}, u32[]{:S(2)}, u32[]{:S(2)}) %collective-permute-start.6) | collective-permute-done | bytes 65568 | tf_op jit(solution)/shard_map/ppermute | solution.py:310
  20.1 0.8 %shard_map.118 = (bf16[128,512]{1,0:T(8,128)(2,1)S(1)}, bf16[160,512]{1,0:T(8,128)(2,1)S(1)}, bf16[128,512]{1,0:T(8,128)(2,1)S(1)}, f32[4,64,128]{2,1,0:T(8,128)S(1)}, bf16[4,64,128]{2,1,0:T(8,128)(2,1)S(1)}) custom-call(f32[128,128]{1,0:T(8,128)S(1)} %get-tuple-element.48.bias_ref, bf16[128,128]{1,0:T(8,128)(2,1)S(1)} %copy-done, ...), custom_call_target="tpu_custom_call" | custom-call | flops 33554432 | bytes 1048576 | tf_op jit(solution)/shard_map/pallas_call | solution.py:395
  20.9 1.9 %collective-permute-start.7 = (bf16[4,64,128]{2,1,0:T(8,128)(2,1)S(1)}, bf16[4,64,128]{2,1,0:T(8,128)(2,1)S(1)}, u32[]{:S(2)}, u32[]{:S(2)}) collective-permute-start(bf16[4,64,128]{2,1,0:T(8,128)(2,1)S(1)} %get-tuple-element.62), channel_id=1, source_target_pairs={{0,1},{1,0},{2,3},{3,2},{4,5},{5,4},{6,7},{7,6},{8,9},{9,8},{10,11... | collective-permute-start | bytes 196616 | tf_op jit(solution)/shard_map/ppermute | solution.py:310
  22.8 0.8 %shard_map.116 = (bf16[128,512]{1,0:T(8,128)(2,1)S(1)}, bf16[160,512]{1,0:T(8,128)(2,1)S(1)}, bf16[128,512]{1,0:T(8,128)(2,1)S(1)}, f32[4,64,128]{2,1,0:T(8,128)S(1)}, bf16[4,64,128]{2,1,0:T(8,128)(2,1)S(1)}) custom-call(f32[128,128]{1,0:T(8,128)S(1)} %get-tuple-element.48.bias_ref, bf16[128,128]{1,0:T(8,128)(2,1)S(1)} %copy-done, ...), custom_call_target="tpu_custom_call" | custom-call | flops 33554432 | bytes 1048576 | tf_op jit(solution)/shard_map/pallas_call | solution.py:395
  23.7 0.2 shard_map.121
  24.3 1.9 %collective-permute-start.10 = (bf16[80,128]{1,0:T(8,128)(2,1)S(1)}, bf16[80,128]{1,0:T(8,128)(2,1)S(1)}, u32[]{:S(2)}, u32[]{:S(2)}) collective-permute-start(bf16[80,128]{1,0:T(8,128)(2,1)S(1)} %get-tuple-element.73), channel_id=1, source_target_pairs={{0,2},{2,0},{4,6},{6,4},{8,10},{10,8},{12,14},{14,12},{16,18},{18,... | collective-permute-start | bytes 61448 | tf_op jit(solution)/shard_map/ppermute | solution.py:310
  26.2 1.6 %collective-permute-done.4.refs_1_ = bf16[4,64,128]{2,1,0:T(8,128)(2,1)S(1)} collective-permute-done((bf16[4,64,128]{2,1,0:T(8,128)(2,1)S(1)}, bf16[4,64,128]{2,1,0:T(8,128)(2,1)S(1)}, u32[]{:S(2)}, u32[]{:S(2)}) %collective-permute-start.4) | collective-permute-done | bytes 65568 | tf_op jit(solution)/shard_map/ppermute | solution.py:310
  27.9 0.6 %collective-permute-start.9 = (bf16[8,64,128]{2,1,0:T(8,128)(2,1)S(1)}, bf16[8,64,128]{2,1,0:T(8,128)(2,1)S(1)}, u32[]{:S(2)}, u32[]{:S(2)}) collective-permute-start(bf16[8,64,128]{2,1,0:T(8,128)(2,1)S(1)} %shard_map.119.g), channel_id=1, source_target_pairs={{0,28},{2,30},{4,0},{6,2},{8,4},{10,6},{12,8},{14,10},{16,12},{18,... | collective-permute-start | bytes 393224 | tf_op jit(solution)/shard_map/ppermute | solution.py:310
  28.6 1.4 %collective-permute-start.15 = (bf16[80,128]{1,0:T(8,128)(2,1)S(1)}, bf16[80,128]{1,0:T(8,128)(2,1)S(1)}, u32[]{:S(2)}, u32[]{:S(2)}) collective-permute-start(bf16[80,128]{1,0:T(8,128)(2,1)S(1)} %shard_map.122.refs_0_), channel_id=1, source_target_pairs={{0,24},{2,26},{4,28},{6,30},{8,16},{10,18},{12,20},{14,22},{16,8},... | collective-permute-start | bytes 61448 | tf_op jit(solution)/shard_map/ppermute | solution.py:310
  30.0 0.6 %collective-permute-start.14 = (bf16[80,128]{1,0:T(8,128)(2,1)S(1)}, bf16[80,128]{1,0:T(8,128)(2,1)S(1)}, u32[]{:S(2)}, u32[]{:S(2)}) collective-permute-start(bf16[80,128]{1,0:T(8,128)(2,1)S(1)} %shard_map.122.refs_0_), channel_id=1, source_target_pairs={{0,16},{2,18},{4,20},{6,22},{8,24},{10,26},{12,28},{14,30},{16,0},... | collective-permute-start | bytes 61448 | tf_op jit(solution)/shard_map/ppermute | solution.py:310
  30.6 2.4 %collective-permute-start.13 = (bf16[80,128]{1,0:T(8,128)(2,1)S(1)}, bf16[80,128]{1,0:T(8,128)(2,1)S(1)}, u32[]{:S(2)}, u32[]{:S(2)}) collective-permute-start(bf16[80,128]{1,0:T(8,128)(2,1)S(1)} %shard_map.122.refs_0_), channel_id=1, source_target_pairs={{0,8},{2,10},{4,12},{6,14},{8,0},{10,2},{12,4},{14,6},{16,24},{18,... | collective-permute-start | bytes 61448 | tf_op jit(solution)/shard_map/ppermute | solution.py:310
  33.0 1.5 %shard_map.120 = (f32[9,64,128]{2,1,0:T(8,128)S(1)}, bf16[1024,128]{1,0:T(8,128)(2,1)}) custom-call(s32[1]{0:T(128)S(6)} %copy.12.count, s32[96]{0:T(128)S(1)} %get-tuple-element.45.index, bf16[24,128,128]{2,1,0:T(8,128)(2,1)S(1)} %get-tuple-element.47.tiles, bf16[8,64,128]{2,1,0:T(8,128)(2,1)S(1)} %shard_map.119.g, ...), custom_call_target="tpu_custom_call" | custom-call | flops 50331648 | bytes 1048576 | tf_op jit(solution)/shard_map/pallas_call | solution.py:425
  34.6 0.4 %collective-permute-done.15.refs_3_ = bf16[80,128]{1,0:T(8,128)(2,1)S(1)} collective-permute-done((bf16[80,128]{1,0:T(8,128)(2,1)S(1)}, bf16[80,128]{1,0:T(8,128)(2,1)S(1)}, u32[]{:S(2)}, u32[]{:S(2)}) %collective-permute-start.15) | collective-permute-done | bytes 20512 | tf_op jit(solution)/shard_map/ppermute | solution.py:310
  35.3 1.3 %shard_map.124 = (f32[9,64,128]{2,1,0:T(8,128)S(1)}, f32[9,64,128]{2,1,0:T(8,128)S(1)}) custom-call(s32[1]{0:T(128)S(6)} %copy.12.count, s32[96]{0:T(128)S(1)} %get-tuple-element.45.index, bf16[24,128,128]{2,1,0:T(8,128)(2,1)S(1)} %get-tuple-element.52.tiles2, bf16[24,128,128]{2,1,0:T(8,128)(2,1)S(1)} %get-tuple-element.53.tiles3, ...), custom_call_target="tpu_custom_call" | custom-call | flops 100663296 | bytes 1048576 | tf_op jit(solution)/shard_map/pallas_call | solution.py:437
  36.6 1.8 %shard_map.125 = (bf16[64,1024]{1,0:T(8,128)(2,1)}, f32[128,128]{1,0:T(8,128)}, f32[1,128]{1,0:T(1,128)}) custom-call(s32[1]{0:T(128)S(6)} %copy.12.count, s32[96]{0:T(128)S(1)} %get-tuple-element.45.index, bf16[24,128,128]{2,1,0:T(8,128)(2,1)S(1)} %get-tuple-element.66.tiles1, bf16[592,128]{1,0:T(8,128)(2,1)S(1)} %shard_map.123.sent, ...), custom_call_target="tpu_custom_call" | custom-call | flops 50331648 | bytes 1048576 | tf_op jit(solution)/shard_map/pallas_call | solution.py:440
  (29 shorter events, 1.2 us)
Async XLA Ops:
  0.6 9.5 %copy-start = (bf16[128,128]{1,0:T(8,128)(2,1)S(1)}, bf16[128,128]{1,0:T(8,128)(2,1)}, u32[]{:S(2)}) copy-start(bf16[128,128]{1,0:T(8,128)(2,1)} %w_ref.5) | copy-start | bytes 98308
  0.6 9.5 %copy-start.1 = (f32[128]{0:T(128)S(1)}, f32[128]{0:T(128)}, u32[]{:S(2)}) copy-start(f32[128]{0:T(128)} %param.10) | copy-start | bytes 1540
  4.0 2.5 %collective-permute-start.1 = (bf16[8,64,128]{2,1,0:T(8,128)(2,1)S(1)}, bf16[8,64,128]{2,1,0:T(8,128)(2,1)S(1)}, u32[]{:S(2)}, u32[]{:S(2)}) collective-permute-start(bf16[8,64,128]{2,1,0:T(8,128)(2,1)S(1)} %get-tuple-element.56), channel_id=1, source_target_pairs={{0,2},{2,0},{4,6},{6,4},{8,10},{10,8},{12,14},{14,12},{16,18},{18,... | collective-permute-start | bytes 393224 | tf_op jit(solution)/shard_map/ppermute | solution.py:310
  6.4 6.5 %collective-permute-start = (bf16[8,64,128]{2,1,0:T(8,128)(2,1)S(1)}, bf16[8,64,128]{2,1,0:T(8,128)(2,1)S(1)}, u32[]{:S(2)}, u32[]{:S(2)}) collective-permute-start(bf16[8,64,128]{2,1,0:T(8,128)(2,1)S(1)} %get-tuple-element.54), channel_id=1, source_target_pairs={{0,2},{2,8},{4,6},{6,12},{8,10},{10,16},{12,14},{14,20},{16,18},{1... | collective-permute-start | bytes 393224 | tf_op jit(solution)/shard_map/ppermute | solution.py:310
  6.5 8.0 %collective-permute-start.5 = (bf16[4,64,128]{2,1,0:T(8,128)(2,1)S(1)}, bf16[4,64,128]{2,1,0:T(8,128)(2,1)S(1)}, u32[]{:S(2)}, u32[]{:S(2)}) collective-permute-start(bf16[4,64,128]{2,1,0:T(8,128)(2,1)S(1)} %get-tuple-element.60), channel_id=1, source_target_pairs={{0,4},{2,6},{4,8},{6,10},{8,12},{10,14},{12,16},{14,18},{16,20},{1... | collective-permute-start | bytes 196616 | tf_op jit(solution)/shard_map/ppermute | solution.py:310
  8.6 8.6 %collective-permute-start.2 = (bf16[4,64,128]{2,1,0:T(8,128)(2,1)S(1)}, bf16[4,64,128]{2,1,0:T(8,128)(2,1)S(1)}, u32[]{:S(2)}, u32[]{:S(2)}) collective-permute-start(bf16[4,64,128]{2,1,0:T(8,128)(2,1)S(1)} %get-tuple-element.57), channel_id=1, source_target_pairs={{0,4},{2,6},{4,8},{6,10},{8,12},{10,14},{12,16},{14,18},{16,20},{1... | collective-permute-start | bytes 196616 | tf_op jit(solution)/shard_map/ppermute | solution.py:310
  14.6 5.5 %collective-permute-start.6 = (bf16[4,64,128]{2,1,0:T(8,128)(2,1)S(1)}, bf16[4,64,128]{2,1,0:T(8,128)(2,1)S(1)}, u32[]{:S(2)}, u32[]{:S(2)}) collective-permute-start(bf16[4,64,128]{2,1,0:T(8,128)(2,1)S(1)} %shard_map.117.refs_0_), channel_id=1, source_target_pairs={{0,1},{1,0},{2,3},{3,2},{4,5},{5,4},{6,7},{7,6},{8,9},{9,8},{10,11... | collective-permute-start | bytes 196616 | tf_op jit(solution)/shard_map/ppermute | solution.py:310
  17.2 5.5 %collective-permute-start.3 = (bf16[4,64,128]{2,1,0:T(8,128)(2,1)S(1)}, bf16[4,64,128]{2,1,0:T(8,128)(2,1)S(1)}, u32[]{:S(2)}, u32[]{:S(2)}) collective-permute-start(bf16[4,64,128]{2,1,0:T(8,128)(2,1)S(1)} %shard_map.115.refs_0_), channel_id=1, source_target_pairs={{0,1},{1,0},{2,3},{3,2},{4,5},{5,4},{6,7},{7,6},{8,9},{9,8},{10,11... | collective-permute-start | bytes 196616 | tf_op jit(solution)/shard_map/ppermute | solution.py:310
  20.9 5.3 %collective-permute-start.7 = (bf16[4,64,128]{2,1,0:T(8,128)(2,1)S(1)}, bf16[4,64,128]{2,1,0:T(8,128)(2,1)S(1)}, u32[]{:S(2)}, u32[]{:S(2)}) collective-permute-start(bf16[4,64,128]{2,1,0:T(8,128)(2,1)S(1)} %get-tuple-element.62), channel_id=1, source_target_pairs={{0,1},{1,0},{2,3},{3,2},{4,5},{5,4},{6,7},{7,6},{8,9},{9,8},{10,11... | collective-permute-start | bytes 196616 | tf_op jit(solution)/shard_map/ppermute | solution.py:310
  23.6 4.3 %collective-permute-start.4 = (bf16[4,64,128]{2,1,0:T(8,128)(2,1)S(1)}, bf16[4,64,128]{2,1,0:T(8,128)(2,1)S(1)}, u32[]{:S(2)}, u32[]{:S(2)}) collective-permute-start(bf16[4,64,128]{2,1,0:T(8,128)(2,1)S(1)} %get-tuple-element.59), channel_id=1, source_target_pairs={{0,1},{1,0},{2,3},{3,2},{4,5},{5,4},{6,7},{7,6},{8,9},{9,8},{10,11... | collective-permute-start | bytes 196616 | tf_op jit(solution)/shard_map/ppermute | solution.py:310
  24.0 4.5 %collective-permute-start.11 = (bf16[80,128]{1,0:T(8,128)(2,1)S(1)}, bf16[80,128]{1,0:T(8,128)(2,1)S(1)}, u32[]{:S(2)}, u32[]{:S(2)}) collective-permute-start(bf16[80,128]{1,0:T(8,128)(2,1)S(1)} %get-tuple-element.72.refs_0_), channel_id=1, source_target_pairs={{0,4},{2,6},{4,0},{6,2},{8,12},{10,14},{12,8},{14,10},{16,20},{18,... | collective-permute-start | bytes 61448 | tf_op jit(solution)/shard_map/ppermute | solution.py:310
  24.1 4.5 %collective-permute-start.12 = (bf16[80,128]{1,0:T(8,128)(2,1)S(1)}, bf16[80,128]{1,0:T(8,128)(2,1)S(1)}, u32[]{:S(2)}, u32[]{:S(2)}) collective-permute-start(bf16[80,128]{1,0:T(8,128)(2,1)S(1)} %get-tuple-element.73), channel_id=1, source_target_pairs={{0,6},{2,4},{4,2},{6,0},{8,14},{10,12},{12,10},{14,8},{16,22},{18,... | collective-permute-start | bytes 61448 | tf_op jit(solution)/shard_map/ppermute | solution.py:310
  24.3 4.3 %collective-permute-start.10 = (bf16[80,128]{1,0:T(8,128)(2,1)S(1)}, bf16[80,128]{1,0:T(8,128)(2,1)S(1)}, u32[]{:S(2)}, u32[]{:S(2)}) collective-permute-start(bf16[80,128]{1,0:T(8,128)(2,1)S(1)} %get-tuple-element.73), channel_id=1, source_target_pairs={{0,2},{2,0},{4,6},{6,4},{8,10},{10,8},{12,14},{14,12},{16,18},{18,... | collective-permute-start | bytes 61448 | tf_op jit(solution)/shard_map/ppermute | solution.py:310
  27.9 7.3 %collective-permute-start.9 = (bf16[8,64,128]{2,1,0:T(8,128)(2,1)S(1)}, bf16[8,64,128]{2,1,0:T(8,128)(2,1)S(1)}, u32[]{:S(2)}, u32[]{:S(2)}) collective-permute-start(bf16[8,64,128]{2,1,0:T(8,128)(2,1)S(1)} %shard_map.119.g), channel_id=1, source_target_pairs={{0,28},{2,30},{4,0},{6,2},{8,4},{10,6},{12,8},{14,10},{16,12},{18,... | collective-permute-start | bytes 393224 | tf_op jit(solution)/shard_map/ppermute | solution.py:310
  28.5 6.6 %collective-permute-start.8 = (bf16[8,64,128]{2,1,0:T(8,128)(2,1)S(1)}, bf16[8,64,128]{2,1,0:T(8,128)(2,1)S(1)}, u32[]{:S(2)}, u32[]{:S(2)}) collective-permute-start(bf16[8,64,128]{2,1,0:T(8,128)(2,1)S(1)} %shard_map.119.g), channel_id=1, source_target_pairs={{0,26},{2,0},{4,30},{6,4},{8,2},{10,8},{12,6},{14,12},{16,10},{18,... | collective-permute-start | bytes 393224 | tf_op jit(solution)/shard_map/ppermute | solution.py:310
  28.6 6.4 %collective-permute-start.15 = (bf16[80,128]{1,0:T(8,128)(2,1)S(1)}, bf16[80,128]{1,0:T(8,128)(2,1)S(1)}, u32[]{:S(2)}, u32[]{:S(2)}) collective-permute-start(bf16[80,128]{1,0:T(8,128)(2,1)S(1)} %shard_map.122.refs_0_), channel_id=1, source_target_pairs={{0,24},{2,26},{4,28},{6,30},{8,16},{10,18},{12,20},{14,22},{16,8},... | collective-permute-start | bytes 61448 | tf_op jit(solution)/shard_map/ppermute | solution.py:310
  30.0 4.9 %collective-permute-start.14 = (bf16[80,128]{1,0:T(8,128)(2,1)S(1)}, bf16[80,128]{1,0:T(8,128)(2,1)S(1)}, u32[]{:S(2)}, u32[]{:S(2)}) collective-permute-start(bf16[80,128]{1,0:T(8,128)(2,1)S(1)} %shard_map.122.refs_0_), channel_id=1, source_target_pairs={{0,16},{2,18},{4,20},{6,22},{8,24},{10,26},{12,28},{14,30},{16,0},... | collective-permute-start | bytes 61448 | tf_op jit(solution)/shard_map/ppermute | solution.py:310
  30.6 4.5 %collective-permute-start.13 = (bf16[80,128]{1,0:T(8,128)(2,1)S(1)}, bf16[80,128]{1,0:T(8,128)(2,1)S(1)}, u32[]{:S(2)}, u32[]{:S(2)}) collective-permute-start(bf16[80,128]{1,0:T(8,128)(2,1)S(1)} %shard_map.122.refs_0_), channel_id=1, source_target_pairs={{0,8},{2,10},{4,12},{6,14},{8,0},{10,2},{12,4},{14,6},{16,24},{18,... | collective-permute-start | bytes 61448 | tf_op jit(solution)/shard_map/ppermute | solution.py:310
  35.2 1.4 %collective-permute-start.16 = (bf16[592,128]{1,0:T(8,128)(2,1)S(1)}, bf16[592,128]{1,0:T(8,128)(2,1)S(1)}, u32[]{:S(2)}, u32[]{:S(2)}) collective-permute-start(bf16[592,128]{1,0:T(8,128)(2,1)S(1)} %shard_map.123.sent), channel_id=1, source_target_pairs={{0,2},{2,0},{4,6},{6,4},{8,10},{10,8},{12,14},{14,12},{16,18},{18,... | collective-permute-start | bytes 454664 | tf_op jit(solution)/shard_map/ppermute | solution.py:310

commit v5 on v4

--- a/solution.py
+++ b/solution.py
@@ -96,10 +96,22 @@
     slot_loop(count, planes[0][1].shape[0], body)
 
 
+def unit(n):
+    shape = (n, n)
+    return (lax.broadcasted_iota(jnp.int32, shape, 0) == lax.broadcasted_iota(jnp.int32, shape, 1)).astype(BF16)
+
+
+def turned(block):
+    n = block.shape[1]
+    return lax.dot_general(
+        unit(n), block, (((1,), (1,)), ((), ())), preferred_element_type=F32
+    ).astype(BF16)
+
+
 def forward_swap_kernel(
     count, src_hbm, dst_hbm, x_hbm, tiles_hbm, tiles1, tiles2, tiles3, xt, swap, index, src, dst, x, acc, sems
 ):
-    blocks, width, _ = xt.shape
+    blocks = xt.shape[0]
     o = 3 - 2 * own_core()
     loads = [
         pltpu.make_async_copy(a, b, sems.at[i])
@@ -117,18 +129,13 @@
     for c in loads:
         c.start()
     acc[...] = jnp.zeros_like(acc)
-    row = lax.broadcasted_iota(jnp.int32, (width, x.shape[1]), 0)
-    column = lax.broadcasted_iota(jnp.int32, (width, x.shape[1]), 1)
-    pick = (column == row + lax.axis_index("feat") * width).astype(BF16)
     for c in loads[:2]:
         c.wait()
     for k in range(src.shape[0]):
         index[k] = src[k] * SRC_UNIT + dst[k]
     loads[2].wait()
     for b in range(blocks):
-        xt[b] = lax.dot_general(
-            pick, x[b * BLOCK : (b + 1) * BLOCK, :], (((1,), (1,)), ((), ())), preferred_element_type=F32
-        ).astype(BF16)
+        xt[b] = turned(x[b * BLOCK : (b + 1) * BLOCK, :])
     loads[3].wait()
     push_all(xt, index, count[0], (tiles1, acc, o))
     swap[...] = acc[:blocks].astype(BF16)
@@ -141,18 +148,6 @@
     acc[...] = jnp.zeros_like(acc)
     push_all(xt, index, count[0], (tiles2, acc2, 2), (tiles3, acc, 1 + 2 * own_core()))
     direct[...] = acc[: direct.shape[0]].astype(BF16)
-
-
-def unit(n):
-    shape = (n, n)
-    return (lax.broadcasted_iota(jnp.int32, shape, 0) == lax.broadcasted_iota(jnp.int32, shape, 1)).astype(BF16)
-
-
-def turned(block):
-    n = block.shape[1]
-    return lax.dot_general(
-        unit(n), block, (((1,), (1,)), ((), ())), preferred_element_type=F32
-    ).astype(BF16)
 
 
 def forward_own_kernel(
@@ -196,19 +191,17 @@
         first += blocks
 
 
-def middle_kernel(parts, first, bias_ref, w_ref, w_t_ref, og_ref, *refs):
-    h_refs, (act, ht, grads), g_refs = refs[:parts], refs[parts : parts + 3], refs[parts + 3 :]
-    blocks, width, _ = h_refs[0].shape
-    f_in = w_ref.shape[0]
+def middle_kernel(parts, first, bias_ref, w_ref, w_t_ref, og_ref, h_ref, act, ht, grads, *g_refs):
+    blocks, f_in, _ = h_ref.shape
+    width = f_in // parts
     me = lax.axis_index("feat")
     rows = [pl.multiple_of(lax.rem(me + q, parts) * width, width) for q in range(parts)]
-    for q in range(parts):
-        for b in range(blocks):
-            ht[pl.ds(rows[q], width), b * BLOCK : (b + 1) * BLOCK] = h_refs[q][b]
+    for b in range(blocks):
+        ht[:f_in, b * BLOCK : (b + 1) * BLOCK] = h_ref[b]
     ht[f_in:, :] = jnp.ones((ht.shape[0] - f_in, ht.shape[1]), BF16)
     for b in range(blocks):
         cols = slice(b * BLOCK, (b + 1) * BLOCK)
-        pre = jnp.dot(w_t_ref[...], ht[:f_in, cols], preferred_element_type=F32) + bias_ref[...]
+        pre = jnp.dot(w_t_ref[...], h_ref[b], preferred_element_type=F32) + bias_ref[...]
         s = jax.nn.sigmoid(pre)
         act[:, cols] = (pre * s).astype(BF16)
         og = og_ref[:, (first + b) * BLOCK : (first + b + 1) * BLOCK].astype(F32)
@@ -333,6 +326,9 @@
     groups = capacity // REACH
     piece = jax.ShapeDtypeStruct((blocks, width, BLOCK), BF16)
     totals = jax.ShapeDtypeStruct((blocks + 1, width, BLOCK), F32)
+    piece_x = jax.ShapeDtypeStruct((blocks, f_in, BLOCK), BF16)
+    totals_x = jax.ShapeDtypeStruct((blocks + 1, f_in, BLOCK), F32)
+    acc_x = pltpu.VMEM(totals_x.shape, F32)
     acc = pltpu.VMEM(totals.shape, F32)
     tiles = tile_values.reshape(groups, REACH, BLOCK, BLOCK)
     plane = jax.ShapeDtypeStruct((groups, BLOCK, BLOCK), BF16)
@@ -346,14 +342,14 @@
 
     tiles1, tiles2, tiles3, xt, swap, index = call(
         forward_swap_kernel,
-        [plane, plane, plane, piece, piece, slots],
+        [plane, plane, plane, piece_x, piece_x, slots],
         [SMEM] + [HBM] * 4,
         [VMEM] * 5 + [SMEM],
         [
             pltpu.SMEM((capacity,), jnp.int32),
             pltpu.SMEM((capacity,), jnp.int32),
             pltpu.VMEM(node_features.shape, BF16),
-            acc,
+            acc_x,
             pltpu.SemaphoreType.DMA((6,)),
         ],
         flops,
@@ -361,21 +357,22 @@
     index = (tile_counts, index)
     swap = moved(swap, "dom", swapped)
     acc2, direct = call(
-        forward_send_kernel, [totals, piece], [SMEM] * 2 + [VMEM] * 3, [VMEM] * 2, [acc], 2 * flops
+        forward_send_kernel, [totals_x, piece_x], [SMEM] * 2 + [VMEM] * 3, [VMEM] * 2, [acc_x], 2 * flops
     )(*index, xt, tiles2, tiles3)
     cut = 2 if blocks % 2 == 0 else 1
     starts = range(0, blocks, blocks // cut)
     half = jax.ShapeDtypeStruct((blocks // cut, width, BLOCK), BF16)
+    half_x = jax.ShapeDtypeStruct((blocks // cut, f_in, BLOCK), BF16)
     half_wide = jax.ShapeDtypeStruct(half.shape, F32)
     half_rows = jax.ShapeDtypeStruct((hid, nodes // cut), BF16)
     half_columns = jax.ShapeDtypeStruct((f_in + 32, nodes // cut), BF16)
-    chip = call(functools.partial(sum_kernel, 2, 0), [half] * cut, [VMEM] * 2, [VMEM] * cut)(acc2, swap)
+    chip = call(functools.partial(sum_kernel, 2, 0), [half_x] * cut, [VMEM] * 2, [VMEM] * cut)(acc2, swap)
     chip = [moved(c, "dom", lambda i: i + 2) for c in chip]
     direct = moved(direct, "dom", lambda i: i + 1 + 2 * (i % 2))
     acc0, tiles0, bias_t, w_t, og_t = call(
         forward_own_kernel,
         [
-            totals,
+            totals_x,
             plane,
             jax.ShapeDtypeStruct((hid, BLOCK), F32),
             jax.ShapeDtypeStruct((hid, f_in), BF16),
@@ -386,20 +383,20 @@
         [pltpu.VMEM(out_grad.shape, BF16), pltpu.SemaphoreType.DMA((2,))],
         flops,
     )(*index, xt, bias.reshape(1, hid), weight, in_hbm(out_grad), in_hbm(tiles))
-    h_lists = []
+    h_list = []
     for first, c in zip(starts, chip):
-        (h,) = call(functools.partial(sum_kernel, 3, first), [half], [VMEM] * 3, [VMEM])(acc0, direct, c)
-        h_lists.append([h] + [moved(h, "feat", lambda i, q=q: i - q) for q in range(1, parts)])
+        (h,) = call(functools.partial(sum_kernel, 3, first), [half_x], [VMEM] * 3, [VMEM])(acc0, direct, c)
+        h_list.append(h)
     acts, hts, grads, g_list = [], [], [], []
-    for first, hs in zip(starts, h_lists):
+    for first, h in zip(starts, h_list):
         act, ht, grad, g_own, *g_others = call(
             functools.partial(middle_kernel, parts, first),
             [half_rows, half_columns, half_rows, half_wide] + [half] * (parts - 1),
-            [VMEM] * (4 + parts),
+            [VMEM] * 5,
             [VMEM] * (3 + parts),
             (),
             4 * nodes * f_in * hid // cut,
-        )(bias_t, weight, w_t, og_t, *hs)
+        )(bias_t, weight, w_t, og_t, h)
         acts.append(act)
         hts.append(ht)
         grads.append(grad)

time: 39 us -> 37.1 us (0.951)
  Pallas kernels: 13.8 us -> 12.1 us
  starting transfers between devices: 17.2 us -> 18.7 us
  waiting for transfers between devices: 5.99 us -> 4.67 us
    ppermute x17 -> x15, starting transfers between devices: 17.2 us -> 18.7 us  [moved(): return lax.ppermute(block, axis, [(i, target(i) % n) for i in range(n)])]
    ppermute x17 -> x15, waiting for transfers between devices: 5.99 us -> 4.67 us  [moved(): return lax.ppermute(block, axis, [(i, target(i) % n) for i in range(n)])]
    pallas_call x6, Pallas kernels: 7.21 us -> 6.09 us  [the longest x1 2.35 us: shards(): call(forward_swap_kernel, [plane, plane, plane, piece_x, piece_x, slots],...]
  transfers between devices with their start and end apart: 17 -> 15, of which waited for: 7 -> 5; matrix products, arithmetic and copies ran while one was open for 0% -> 0% of each run, Pallas kernels for 24% -> 22%
where the time goes in v5:
time: 37.1 us; the launch traced here: 36.9 us
  starting transfers between devices  18.7 us (50%)
  Pallas kernels  12.1 us (33%)
  waiting for transfers between devices  4.67 us (13%)
  between operations  1.43 us (4%)
    ppermute x15, starting transfers between devices, moved(): return lax.ppermute(block, axis, [(i, target(i) % n) for i in range(n)])  18.7 us
    ppermute x15, waiting for transfers between devices, moved(): return lax.ppermute(block, axis, [(i, target(i) % n) for i in range(n)])  4.67 us
    pallas_call x1, Pallas kernels, shards(): call(forward_swap_kernel, [plane, plane, plane, piece_x, piece_x, slots],...  2.35 us
    pallas_call x1, Pallas kernels, shards(): call(forward_own_kernel, [totals_x, plane, jax.ShapeDtypeStruct((hid, BLO...  2.25 us
    pallas_call x2, Pallas kernels, shards(): call(functools.partial(middle_kernel, parts, first), [half_rows, half_col...  1.62 us
    pallas_call x1, Pallas kernels, shards(): call(backward_last_kernel, [jax.ShapeDtypeStruct((width, nodes), BF16), j...  1.58 us
    pallas_call x1, Pallas kernels, shards(): call(backward_own_kernel, [totals, rows], [SMEM] * 2 + [VMEM] * (2 + cut)...  1.51 us
    pallas_call x1, Pallas kernels, shards(): call(forward_send_kernel, [totals_x, piece_x], [SMEM] * 2 + [VMEM] * 3, [...  1.33 us
  transfers between devices with their start and end apart: 15, of which 5 were waited for; matrix products, arithmetic and copies ran while one was open for 0% of the time, Pallas kernels for 22%

profile of v5, /device:TPU:0, one launch (start us, length us, event | category | flops | bytes accessed | tf_op | source)
XLA Modules:
  0.0 36.9 jit_solution(4787483732512083519)
XLA Ops:
  1.3 2.3 %shard_map.111 = (bf16[24,128,128]{2,1,0:T(8,128)(2,1)S(1)}, bf16[24,128,128]{2,1,0:T(8,128)(2,1)S(1)}, bf16[24,128,128]{2,1,0:T(8,128)(2,1)S(1)}, bf16[8,128,12...) custom-call(s32[1]{0:T(128)S(6)} %copy.12.count, s32[96]{0:T(128)} %src_hbm.1, s32[96]{0:T(128)} %dst_hbm.1, ...), custom_call_target="tpu_custom_call" | custom-call | flops 50331648 | bytes 1048576 | tf_op jit(solution)/shard_map/pallas_call | solution.py:343
  3.7 0.9 %collective-permute-start.1 = (bf16[8,128,128]{2,1,0:T(8,128)(2,1)S(1)}, bf16[8,128,128]{2,1,0:T(8,128)(2,1)S(1)}, u32[]{:S(2)}, u32[]{:S(2)}) collective-permute-start(bf16[8,128,128]{2,1,0:T(8,128)(2,1)S(1)} %get-tuple-element.56), channel_id=1, source_target_pairs={{0,2},{2,0},{4,6},{6,4},{8,10},{10,8},{12,14},{14,12},{16,18},{18,... | collective-permute-start | bytes 786440 | tf_op jit(solution)/shard_map/ppermute | solution.py:303
  4.6 1.3 %shard_map.113 = (f32[9,128,128]{2,1,0:T(8,128)S(1)}, bf16[8,128,128]{2,1,0:T(8,128)(2,1)S(1)}) custom-call(s32[1]{0:T(128)S(6)} %copy.12.count, s32[96]{0:T(128)S(1)} %get-tuple-element.45.index, bf16[8,128,128]{2,1,0:T(8,128)(2,1)S(1)} %get-tuple-element.46.xt, bf16[24,128,128]{2,1,0:T(8,128)(2,1)S(1)} %get-tuple-element.52.tiles2, ...), custom_call_target="tpu_custom_call" | custom-call | flops 100663296 | bytes 1048576 | tf_op jit(solution)/shard_map/pallas_call | solution.py:359
  5.9 0.7 %collective-permute-start = (bf16[8,128,128]{2,1,0:T(8,128)(2,1)S(1)}, bf16[8,128,128]{2,1,0:T(8,128)(2,1)S(1)}, u32[]{:S(2)}, u32[]{:S(2)}) collective-permute-start(bf16[8,128,128]{2,1,0:T(8,128)(2,1)S(1)} %get-tuple-element.54), channel_id=1, source_target_pairs={{0,2},{2,8},{4,6},{6,12},{8,10},{10,16},{12,14},{14,20},{16,18},{1... | collective-permute-start | bytes 786440 | tf_op jit(solution)/shard_map/ppermute | solution.py:303
  6.7 2.0 %collective-permute-start.2 = (bf16[4,128,128]{2,1,0:T(8,128)(2,1)S(1)}, bf16[4,128,128]{2,1,0:T(8,128)(2,1)S(1)}, u32[]{:S(2)}, u32[]{:S(2)}) collective-permute-start(bf16[4,128,128]{2,1,0:T(8,128)(2,1)S(1)} %get-tuple-element.57), channel_id=1, source_target_pairs={{0,4},{2,6},{4,8},{6,10},{8,12},{10,14},{12,16},{14,18},{16,20},{1... | collective-permute-start | bytes 393224 | tf_op jit(solution)/shard_map/ppermute | solution.py:303
  8.7 1.5 %collective-permute-start.4 = (bf16[4,128,128]{2,1,0:T(8,128)(2,1)S(1)}, bf16[4,128,128]{2,1,0:T(8,128)(2,1)S(1)}, u32[]{:S(2)}, u32[]{:S(2)}) collective-permute-start(bf16[4,128,128]{2,1,0:T(8,128)(2,1)S(1)} %get-tuple-element.60), channel_id=1, source_target_pairs={{0,4},{2,6},{4,8},{6,10},{8,12},{10,14},{12,16},{14,18},{16,20},{1... | collective-permute-start | bytes 393224 | tf_op jit(solution)/shard_map/ppermute | solution.py:303
  10.3 2.3 %shard_map.112 = (f32[9,128,128]{2,1,0:T(8,128)S(1)}, bf16[24,128,128]{2,1,0:T(8,128)(2,1)S(1)}, f32[128,128]{1,0:T(8,128)S(1)}, bf16[128,128]{1,0:T(8,128)(2,1)S(1)}, bf16[128,1024]{1,0:T(8,128)(2,1)S(1)}) custom-call(s32[1]{0:T(128)S(6)} %copy.12.count, s32[96]{0:T(128)S(1)} %get-tuple-element.45.index, bf16[8,128,128]{2,1,0:T(8,128)(2,1)S(1)} %get-tuple-element.46.xt, ...), custom_call_target="tpu_custom_call" | custom-call | flops 50331648 | bytes 1048576 | tf_op jit(solution)/shard_map/pallas_call | solution.py:372
  12.5 1.8 %collective-permute-done.refs_1_ = bf16[8,128,128]{2,1,0:T(8,128)(2,1)S(1)} collective-permute-done((bf16[8,128,128]{2,1,0:T(8,128)(2,1)S(1)}, bf16[8,128,128]{2,1,0:T(8,128)(2,1)S(1)}, u32[]{:S(2)}, u32[]{:S(2)}) %collective-permute-start) | collective-permute-done | bytes 262176 | tf_op jit(solution)/shard_map/ppermute | solution.py:303
  14.3 1.7 %collective-permute-done.2.refs_2_ = bf16[4,128,128]{2,1,0:T(8,128)(2,1)S(1)} collective-permute-done((bf16[4,128,128]{2,1,0:T(8,128)(2,1)S(1)}, bf16[4,128,128]{2,1,0:T(8,128)(2,1)S(1)}, u32[]{:S(2)}, u32[]{:S(2)}) %collective-permute-start.2) | collective-permute-done | bytes 131104 | tf_op jit(solution)/shard_map/ppermute | solution.py:303
  16.1 0.8 %shard_map.116 = (bf16[128,512]{1,0:T(8,128)(2,1)S(1)}, bf16[160,512]{1,0:T(8,128)(2,1)S(1)}, bf16[128,512]{1,0:T(8,128)(2,1)S(1)}, f32[4,64,128]{2,1,0:T(8,128)S(1)}, bf16[4,64,128]{2,1,0:T(8,128)(2,1)S(1)}) custom-call(f32[128,128]{1,0:T(8,128)S(1)} %get-tuple-element.48.bias_ref, bf16[128,128]{1,0:T(8,128)(2,1)S(1)} %copy-done, ...), custom_call_target="tpu_custom_call" | custom-call | flops 33554432 | bytes 1048576 | tf_op jit(solution)/shard_map/pallas_call | solution.py:392
  17.0 2.4 %collective-permute-start.3 = (bf16[4,64,128]{2,1,0:T(8,128)(2,1)S(1)}, bf16[4,64,128]{2,1,0:T(8,128)(2,1)S(1)}, u32[]{:S(2)}, u32[]{:S(2)}) collective-permute-start(bf16[4,64,128]{2,1,0:T(8,128)(2,1)S(1)} %get-tuple-element.59), channel_id=1, source_target_pairs={{0,1},{1,0},{2,3},{3,2},{4,5},{5,4},{6,7},{7,6},{8,9},{9,8},{10,11... | collective-permute-start | bytes 196616 | tf_op jit(solution)/shard_map/ppermute | solution.py:303
  19.4 0.8 %shard_map.118 = (bf16[128,512]{1,0:T(8,128)(2,1)S(1)}, bf16[160,512]{1,0:T(8,128)(2,1)S(1)}, bf16[128,512]{1,0:T(8,128)(2,1)S(1)}, f32[4,64,128]{2,1,0:T(8,128)S(1)}, bf16[4,64,128]{2,1,0:T(8,128)(2,1)S(1)}) custom-call(f32[128,128]{1,0:T(8,128)S(1)} %get-tuple-element.48.bias_ref, bf16[128,128]{1,0:T(8,128)(2,1)S(1)} %copy-done, ...), custom_call_target="tpu_custom_call" | custom-call | flops 33554432 | bytes 1048576 | tf_op jit(solution)/shard_map/pallas_call | solution.py:392
  20.2 1.9 %collective-permute-start.5 = (bf16[4,64,128]{2,1,0:T(8,128)(2,1)S(1)}, bf16[4,64,128]{2,1,0:T(8,128)(2,1)S(1)}, u32[]{:S(2)}, u32[]{:S(2)}) collective-permute-start(bf16[4,64,128]{2,1,0:T(8,128)(2,1)S(1)} %get-tuple-element.62), channel_id=1, source_target_pairs={{0,1},{1,0},{2,3},{3,2},{4,5},{5,4},{6,7},{7,6},{8,9},{9,8},{10,11... | collective-permute-start | bytes 196616 | tf_op jit(solution)/shard_map/ppermute | solution.py:303
  22.5 2.0 %collective-permute-start.10 = (bf16[80,128]{1,0:T(8,128)(2,1)S(1)}, bf16[80,128]{1,0:T(8,128)(2,1)S(1)}, u32[]{:S(2)}, u32[]{:S(2)}) collective-permute-start(bf16[80,128]{1,0:T(8,128)(2,1)S(1)} %get-tuple-element.73), channel_id=1, source_target_pairs={{0,6},{2,4},{4,2},{6,0},{8,14},{10,12},{12,10},{14,8},{16,22},{18,... | collective-permute-start | bytes 61448 | tf_op jit(solution)/shard_map/ppermute | solution.py:303
  24.7 1.5 %collective-permute-start.7 = (bf16[8,64,128]{2,1,0:T(8,128)(2,1)S(1)}, bf16[8,64,128]{2,1,0:T(8,128)(2,1)S(1)}, u32[]{:S(2)}, u32[]{:S(2)}) collective-permute-start(bf16[8,64,128]{2,1,0:T(8,128)(2,1)S(1)} %shard_map.119.g), channel_id=1, source_target_pairs={{0,28},{2,30},{4,0},{6,2},{8,4},{10,6},{12,8},{14,10},{16,12},{18,... | collective-permute-start | bytes 393224 | tf_op jit(solution)/shard_map/ppermute | solution.py:303
  26.2 0.9 %collective-permute-start.6 = (bf16[8,64,128]{2,1,0:T(8,128)(2,1)S(1)}, bf16[8,64,128]{2,1,0:T(8,128)(2,1)S(1)}, u32[]{:S(2)}, u32[]{:S(2)}) collective-permute-start(bf16[8,64,128]{2,1,0:T(8,128)(2,1)S(1)} %shard_map.119.g), channel_id=1, source_target_pairs={{0,26},{2,0},{4,30},{6,4},{8,2},{10,8},{12,6},{14,12},{16,10},{18,... | collective-permute-start | bytes 393224 | tf_op jit(solution)/shard_map/ppermute | solution.py:303
  27.2 0.8 %collective-permute-start.13 = (bf16[80,128]{1,0:T(8,128)(2,1)S(1)}, bf16[80,128]{1,0:T(8,128)(2,1)S(1)}, u32[]{:S(2)}, u32[]{:S(2)}) collective-permute-start(bf16[80,128]{1,0:T(8,128)(2,1)S(1)} %shard_map.122.refs_0_), channel_id=1, source_target_pairs={{0,24},{2,26},{4,28},{6,30},{8,16},{10,18},{12,20},{14,22},{16,8},... | collective-permute-start | bytes 61448 | tf_op jit(solution)/shard_map/ppermute | solution.py:303
  27.9 1.5 %collective-permute-start.12 = (bf16[80,128]{1,0:T(8,128)(2,1)S(1)}, bf16[80,128]{1,0:T(8,128)(2,1)S(1)}, u32[]{:S(2)}, u32[]{:S(2)}) collective-permute-start(bf16[80,128]{1,0:T(8,128)(2,1)S(1)} %shard_map.122.refs_0_), channel_id=1, source_target_pairs={{0,16},{2,18},{4,20},{6,22},{8,24},{10,26},{12,28},{14,30},{16,0},... | collective-permute-start | bytes 61448 | tf_op jit(solution)/shard_map/ppermute | solution.py:303
  29.5 2.2 %collective-permute-start.11 = (bf16[80,128]{1,0:T(8,128)(2,1)S(1)}, bf16[80,128]{1,0:T(8,128)(2,1)S(1)}, u32[]{:S(2)}, u32[]{:S(2)}) collective-permute-start(bf16[80,128]{1,0:T(8,128)(2,1)S(1)} %shard_map.122.refs_0_), channel_id=1, source_target_pairs={{0,8},{2,10},{4,12},{6,14},{8,0},{10,2},{12,4},{14,6},{16,24},{18,... | collective-permute-start | bytes 61448 | tf_op jit(solution)/shard_map/ppermute | solution.py:303
  31.6 1.5 %shard_map.120 = (f32[9,64,128]{2,1,0:T(8,128)S(1)}, bf16[1024,128]{1,0:T(8,128)(2,1)}) custom-call(s32[1]{0:T(128)S(6)} %copy.12.count, s32[96]{0:T(128)S(1)} %get-tuple-element.45.index, bf16[24,128,128]{2,1,0:T(8,128)(2,1)S(1)} %get-tuple-element.47.tiles, bf16[8,64,128]{2,1,0:T(8,128)(2,1)S(1)} %shard_map.119.g, ...), custom_call_target="tpu_custom_call" | custom-call | flops 50331648 | bytes 1048576 | tf_op jit(solution)/shard_map/pallas_call | solution.py:422
  33.2 0.4 %collective-permute-done.13.refs_3_ = bf16[80,128]{1,0:T(8,128)(2,1)S(1)} collective-permute-done((bf16[80,128]{1,0:T(8,128)(2,1)S(1)}, bf16[80,128]{1,0:T(8,128)(2,1)S(1)}, u32[]{:S(2)}, u32[]{:S(2)}) %collective-permute-start.13) | collective-permute-done | bytes 20512 | tf_op jit(solution)/shard_map/ppermute | solution.py:303
  33.9 0.9 %shard_map.124 = (f32[9,64,128]{2,1,0:T(8,128)S(1)}, f32[9,64,128]{2,1,0:T(8,128)S(1)}) custom-call(s32[1]{0:T(128)S(6)} %copy.12.count, s32[96]{0:T(128)S(1)} %get-tuple-element.45.index, bf16[24,128,128]{2,1,0:T(8,128)(2,1)S(1)} %get-tuple-element.52.tiles2, bf16[24,128,128]{2,1,0:T(8,128)(2,1)S(1)} %get-tuple-element.53.tiles3, ...), custom_call_target="tpu_custom_call" | custom-call | flops 100663296 | bytes 1048576 | tf_op jit(solution)/shard_map/pallas_call | solution.py:434
  34.9 0.4 %collective-permute-done.14.got = bf16[592,128]{1,0:T(8,128)(2,1)S(1)} collective-permute-done((bf16[592,128]{1,0:T(8,128)(2,1)S(1)}, bf16[592,128]{1,0:T(8,128)(2,1)S(1)}, u32[]{:S(2)}, u32[]{:S(2)}) %collective-permute-start.14) | collective-permute-done | bytes 151584 | tf_op jit(solution)/shard_map/ppermute | solution.py:303
  35.3 1.6 %shard_map.125 = (bf16[64,1024]{1,0:T(8,128)(2,1)}, f32[128,128]{1,0:T(8,128)}, f32[1,128]{1,0:T(1,128)}) custom-call(s32[1]{0:T(128)S(6)} %copy.12.count, s32[96]{0:T(128)S(1)} %get-tuple-element.45.index, bf16[24,128,128]{2,1,0:T(8,128)(2,1)S(1)} %get-tuple-element.66.tiles1, bf16[592,128]{1,0:T(8,128)(2,1)S(1)} %shard_map.123.sent, ...), custom_call_target="tpu_custom_call" | custom-call | flops 50331648 | bytes 1048576 | tf_op jit(solution)/shard_map/pallas_call | solution.py:437
  (25 shorter events, 1.1 us)
Async XLA Ops:
  0.6 9.6 %copy-start = (bf16[128,128]{1,0:T(8,128)(2,1)S(1)}, bf16[128,128]{1,0:T(8,128)(2,1)}, u32[]{:S(2)}) copy-start(bf16[128,128]{1,0:T(8,128)(2,1)} %w_ref.5) | copy-start | bytes 98308
  0.6 9.6 %copy-start.1 = (f32[128]{0:T(128)S(1)}, f32[128]{0:T(128)}, u32[]{:S(2)}) copy-start(f32[128]{0:T(128)} %param.10) | copy-start | bytes 1540
  3.7 3.0 %collective-permute-start.1 = (bf16[8,128,128]{2,1,0:T(8,128)(2,1)S(1)}, bf16[8,128,128]{2,1,0:T(8,128)(2,1)S(1)}, u32[]{:S(2)}, u32[]{:S(2)}) collective-permute-start(bf16[8,128,128]{2,1,0:T(8,128)(2,1)S(1)} %get-tuple-element.56), channel_id=1, source_target_pairs={{0,2},{2,0},{4,6},{6,4},{8,10},{10,8},{12,14},{14,12},{16,18},{18,... | collective-permute-start | bytes 786440 | tf_op jit(solution)/shard_map/ppermute | solution.py:303
  5.9 8.4 %collective-permute-start = (bf16[8,128,128]{2,1,0:T(8,128)(2,1)S(1)}, bf16[8,128,128]{2,1,0:T(8,128)(2,1)S(1)}, u32[]{:S(2)}, u32[]{:S(2)}) collective-permute-start(bf16[8,128,128]{2,1,0:T(8,128)(2,1)S(1)} %get-tuple-element.54), channel_id=1, source_target_pairs={{0,2},{2,8},{4,6},{6,12},{8,10},{10,16},{12,14},{14,20},{16,18},{1... | collective-permute-start | bytes 786440 | tf_op jit(solution)/shard_map/ppermute | solution.py:303
  6.7 9.4 %collective-permute-start.2 = (bf16[4,128,128]{2,1,0:T(8,128)(2,1)S(1)}, bf16[4,128,128]{2,1,0:T(8,128)(2,1)S(1)}, u32[]{:S(2)}, u32[]{:S(2)}) collective-permute-start(bf16[4,128,128]{2,1,0:T(8,128)(2,1)S(1)} %get-tuple-element.57), channel_id=1, source_target_pairs={{0,4},{2,6},{4,8},{6,10},{8,12},{10,14},{12,16},{14,18},{16,20},{1... | collective-permute-start | bytes 393224 | tf_op jit(solution)/shard_map/ppermute | solution.py:303
  8.7 10.6 %collective-permute-start.4 = (bf16[4,128,128]{2,1,0:T(8,128)(2,1)S(1)}, bf16[4,128,128]{2,1,0:T(8,128)(2,1)S(1)}, u32[]{:S(2)}, u32[]{:S(2)}) collective-permute-start(bf16[4,128,128]{2,1,0:T(8,128)(2,1)S(1)} %get-tuple-element.60), channel_id=1, source_target_pairs={{0,4},{2,6},{4,8},{6,10},{8,12},{10,14},{12,16},{14,18},{16,20},{1... | collective-permute-start | bytes 393224 | tf_op jit(solution)/shard_map/ppermute | solution.py:303
  17.0 7.7 %collective-permute-start.3 = (bf16[4,64,128]{2,1,0:T(8,128)(2,1)S(1)}, bf16[4,64,128]{2,1,0:T(8,128)(2,1)S(1)}, u32[]{:S(2)}, u32[]{:S(2)}) collective-permute-start(bf16[4,64,128]{2,1,0:T(8,128)(2,1)S(1)} %get-tuple-element.59), channel_id=1, source_target_pairs={{0,1},{1,0},{2,3},{3,2},{4,5},{5,4},{6,7},{7,6},{8,9},{9,8},{10,11... | collective-permute-start | bytes 196616 | tf_op jit(solution)/shard_map/ppermute | solution.py:303
  20.2 4.4 %collective-permute-start.5 = (bf16[4,64,128]{2,1,0:T(8,128)(2,1)S(1)}, bf16[4,64,128]{2,1,0:T(8,128)(2,1)S(1)}, u32[]{:S(2)}, u32[]{:S(2)}) collective-permute-start(bf16[4,64,128]{2,1,0:T(8,128)(2,1)S(1)} %get-tuple-element.62), channel_id=1, source_target_pairs={{0,1},{1,0},{2,3},{3,2},{4,5},{5,4},{6,7},{7,6},{8,9},{9,8},{10,11... | collective-permute-start | bytes 196616 | tf_op jit(solution)/shard_map/ppermute | solution.py:303
  22.4 4.7 %collective-permute-start.9 = (bf16[80,128]{1,0:T(8,128)(2,1)S(1)}, bf16[80,128]{1,0:T(8,128)(2,1)S(1)}, u32[]{:S(2)}, u32[]{:S(2)}) collective-permute-start(bf16[80,128]{1,0:T(8,128)(2,1)S(1)} %get-tuple-element.72.refs_0_), channel_id=1, source_target_pairs={{0,4},{2,6},{4,0},{6,2},{8,12},{10,14},{12,8},{14,10},{16,20},{18,... | collective-permute-start | bytes 61448 | tf_op jit(solution)/shard_map/ppermute | solution.py:303
  22.5 4.6 %collective-permute-start.10 = (bf16[80,128]{1,0:T(8,128)(2,1)S(1)}, bf16[80,128]{1,0:T(8,128)(2,1)S(1)}, u32[]{:S(2)}, u32[]{:S(2)}) collective-permute-start(bf16[80,128]{1,0:T(8,128)(2,1)S(1)} %get-tuple-element.73), channel_id=1, source_target_pairs={{0,6},{2,4},{4,2},{6,0},{8,14},{10,12},{12,10},{14,8},{16,22},{18,... | collective-permute-start | bytes 61448 | tf_op jit(solution)/shard_map/ppermute | solution.py:303
  24.5 2.7 %collective-permute-start.8 = (bf16[80,128]{1,0:T(8,128)(2,1)S(1)}, bf16[80,128]{1,0:T(8,128)(2,1)S(1)}, u32[]{:S(2)}, u32[]{:S(2)}) collective-permute-start(bf16[80,128]{1,0:T(8,128)(2,1)S(1)} %get-tuple-element.73), channel_id=1, source_target_pairs={{0,2},{2,0},{4,6},{6,4},{8,10},{10,8},{12,14},{14,12},{16,18},{18,... | collective-permute-start | bytes 61448 | tf_op jit(solution)/shard_map/ppermute | solution.py:303
  24.7 9.1 %collective-permute-start.7 = (bf16[8,64,128]{2,1,0:T(8,128)(2,1)S(1)}, bf16[8,64,128]{2,1,0:T(8,128)(2,1)S(1)}, u32[]{:S(2)}, u32[]{:S(2)}) collective-permute-start(bf16[8,64,128]{2,1,0:T(8,128)(2,1)S(1)} %shard_map.119.g), channel_id=1, source_target_pairs={{0,28},{2,30},{4,0},{6,2},{8,4},{10,6},{12,8},{14,10},{16,12},{18,... | collective-permute-start | bytes 393224 | tf_op jit(solution)/shard_map/ppermute | solution.py:303
  26.2 7.6 %collective-permute-start.6 = (bf16[8,64,128]{2,1,0:T(8,128)(2,1)S(1)}, bf16[8,64,128]{2,1,0:T(8,128)(2,1)S(1)}, u32[]{:S(2)}, u32[]{:S(2)}) collective-permute-start(bf16[8,64,128]{2,1,0:T(8,128)(2,1)S(1)} %shard_map.119.g), channel_id=1, source_target_pairs={{0,26},{2,0},{4,30},{6,4},{8,2},{10,8},{12,6},{14,12},{16,10},{18,... | collective-permute-start | bytes 393224 | tf_op jit(solution)/shard_map/ppermute | solution.py:303
  27.2 6.4 %collective-permute-start.13 = (bf16[80,128]{1,0:T(8,128)(2,1)S(1)}, bf16[80,128]{1,0:T(8,128)(2,1)S(1)}, u32[]{:S(2)}, u32[]{:S(2)}) collective-permute-start(bf16[80,128]{1,0:T(8,128)(2,1)S(1)} %shard_map.122.refs_0_), channel_id=1, source_target_pairs={{0,24},{2,26},{4,28},{6,30},{8,16},{10,18},{12,20},{14,22},{16,8},... | collective-permute-start | bytes 61448 | tf_op jit(solution)/shard_map/ppermute | solution.py:303
  27.9 5.9 %collective-permute-start.12 = (bf16[80,128]{1,0:T(8,128)(2,1)S(1)}, bf16[80,128]{1,0:T(8,128)(2,1)S(1)}, u32[]{:S(2)}, u32[]{:S(2)}) collective-permute-start(bf16[80,128]{1,0:T(8,128)(2,1)S(1)} %shard_map.122.refs_0_), channel_id=1, source_target_pairs={{0,16},{2,18},{4,20},{6,22},{8,24},{10,26},{12,28},{14,30},{16,0},... | collective-permute-start | bytes 61448 | tf_op jit(solution)/shard_map/ppermute | solution.py:303
  29.5 4.4 %collective-permute-start.11 = (bf16[80,128]{1,0:T(8,128)(2,1)S(1)}, bf16[80,128]{1,0:T(8,128)(2,1)S(1)}, u32[]{:S(2)}, u32[]{:S(2)}) collective-permute-start(bf16[80,128]{1,0:T(8,128)(2,1)S(1)} %shard_map.122.refs_0_), channel_id=1, source_target_pairs={{0,8},{2,10},{4,12},{6,14},{8,0},{10,2},{12,4},{14,6},{16,24},{18,... | collective-permute-start | bytes 61448 | tf_op jit(solution)/shard_map/ppermute | solution.py:303
  33.9 1.4 %collective-permute-start.14 = (bf16[592,128]{1,0:T(8,128)(2,1)S(1)}, bf16[592,128]{1,0:T(8,128)(2,1)S(1)}, u32[]{:S(2)}, u32[]{:S(2)}) collective-permute-start(bf16[592,128]{1,0:T(8,128)(2,1)S(1)} %shard_map.123.sent), channel_id=1, source_target_pairs={{0,2},{2,0},{4,6},{6,4},{8,10},{10,8},{12,14},{14,12},{16,18},{18,... | collective-permute-start | bytes 454664 | tf_op jit(solution)/shard_map/ppermute | solution.py:303

commit v6 on v5

--- a/solution.py
+++ b/solution.py
@@ -143,11 +143,15 @@
         c.wait()
 
 
-def forward_send_kernel(count, index, xt, tiles2, tiles3, acc2, direct, acc):
+def forward_send_kernel(count, index, xt, tiles2, tiles3, acc2, *refs):
+    direct, acc = refs[:-1], refs[-1]
     acc2[...] = jnp.zeros_like(acc2)
     acc[...] = jnp.zeros_like(acc)
     push_all(xt, index, count[0], (tiles2, acc2, 2), (tiles3, acc, 1 + 2 * own_core()))
-    direct[...] = acc[: direct.shape[0]].astype(BF16)
+    first = 0
+    for d in direct:
+        d[...] = acc[first : first + d.shape[0]].astype(BF16)
+        first += d.shape[0]
 
 
 def forward_own_kernel(
@@ -356,9 +360,6 @@
     )(tile_counts, *(in_hbm(a) for a in (tile_src, tile_dst, node_features, tiles)))
     index = (tile_counts, index)
     swap = moved(swap, "dom", swapped)
-    acc2, direct = call(
-        forward_send_kernel, [totals_x, piece_x], [SMEM] * 2 + [VMEM] * 3, [VMEM] * 2, [acc_x], 2 * flops
-    )(*index, xt, tiles2, tiles3)
     cut = 2 if blocks % 2 == 0 else 1
     starts = range(0, blocks, blocks // cut)
     half = jax.ShapeDtypeStruct((blocks // cut, width, BLOCK), BF16)
@@ -366,9 +367,18 @@
     half_wide = jax.ShapeDtypeStruct(half.shape, F32)
     half_rows = jax.ShapeDtypeStruct((hid, nodes // cut), BF16)
     half_columns = jax.ShapeDtypeStruct((f_in + 32, nodes // cut), BF16)
+    acc2, *direct = call(
+        forward_send_kernel,
+        [totals_x] + [half_x] * cut,
+        [SMEM] * 2 + [VMEM] * 3,
+        [VMEM] * (1 + cut),
+        [acc_x],
+        2 * flops,
+    )(*index, xt, tiles2, tiles3)
     chip = call(functools.partial(sum_kernel, 2, 0), [half_x] * cut, [VMEM] * 2, [VMEM] * cut)(acc2, swap)
+    chip = lax.optimization_barrier((*chip, *direct[1:]))
+    direct, chip = [direct[0], *chip[cut:]], chip[:cut]
     chip = [moved(c, "dom", lambda i: i + 2) for c in chip]
-    direct = moved(direct, "dom", lambda i: i + 1 + 2 * (i % 2))
     acc0, tiles0, bias_t, w_t, og_t = call(
         forward_own_kernel,
         [
@@ -383,9 +393,10 @@
         [pltpu.VMEM(out_grad.shape, BF16), pltpu.SemaphoreType.DMA((2,))],
         flops,
     )(*index, xt, bias.reshape(1, hid), weight, in_hbm(out_grad), in_hbm(tiles))
+    direct = [moved(d, "dom", lambda i: i + 1 + 2 * (i % 2)) for d in direct]
     h_list = []
-    for first, c in zip(starts, chip):
-        (h,) = call(functools.partial(sum_kernel, 3, first), [half_x], [VMEM] * 3, [VMEM])(acc0, direct, c)
+    for first, c, d in zip(starts, chip, direct):
+        (h,) = call(functools.partial(sum_kernel, 3, first), [half_x], [VMEM] * 3, [VMEM])(acc0, d, c)
         h_list.append(h)
     acts, hts, grads, g_list = [], [], [], []
     for first, h in zip(starts, h_list):

time: 37.1 us -> 37.1 us (level)
  starting transfers between devices: 18.7 us -> 18.3 us
    ppermute x15 -> x16, starting transfers between devices: 18.7 us -> 18.3 us  [moved(): return lax.ppermute(block, axis, [(i, target(i) % n) for i in range(n)])]
    ppermute x15 -> x16, waiting for transfers between devices: 4.67 us -> 5.04 us  [moved(): return lax.ppermute(block, axis, [(i, target(i) % n) for i in range(n)])]
  transfers between devices with their start and end apart: 15 -> 16, of which waited for: 5 -> 6; matrix products, arithmetic and copies ran while one was open for 0% -> 0% of each run, Pallas kernels for 22% -> 22%
where the time goes in v6:
time: 37.1 us; the launch traced here: 36.8 us
  starting transfers between devices  18.3 us (49%)
  Pallas kernels  12.1 us (33%)
  waiting for transfers between devices  5.04 us (14%)
  between operations  1.43 us (4%)
    ppermute x16, starting transfers between devices, moved(): return lax.ppermute(block, axis, [(i, target(i) % n) for i in range(n)])  18.3 us
    ppermute x16, waiting for transfers between devices, moved(): return lax.ppermute(block, axis, [(i, target(i) % n) for i in range(n)])  5.04 us
    pallas_call x1, Pallas kernels, shards(): call(forward_swap_kernel, [plane, plane, plane, piece_x, piece_x, slots],...  2.35 us
    pallas_call x1, Pallas kernels, shards(): call(forward_own_kernel, [totals_x, plane, jax.ShapeDtypeStruct((hid, BLO...  2.26 us
    pallas_call x2, Pallas kernels, shards(): call(functools.partial(middle_kernel, parts, first), [half_rows, half_col...  1.62 us
    pallas_call x1, Pallas kernels, shards(): call(backward_last_kernel, [jax.ShapeDtypeStruct((width, nodes), BF16), j...  1.58 us
    pallas_call x1, Pallas kernels, shards(): call(backward_own_kernel, [totals, rows], [SMEM] * 2 + [VMEM] * (2 + cut)...  1.51 us
    pallas_call x1, Pallas kernels, shards(): call(forward_send_kernel, [totals_x] + [half_x] * cut, [SMEM] * 2 + [VMEM...  1.33 us
  transfers between devices with their start and end apart: 16, of which 6 were waited for; matrix products, arithmetic and copies ran while one was open for 0% of the time, Pallas kernels for 22%

profile of v6, /device:TPU:0, one launch (start us, length us, event | category | flops | bytes accessed | tf_op | source)
XLA Modules:
  0.0 36.8 jit_solution(11537506874816936974)
XLA Ops:
  1.3 2.3 %shard_map.111 = (bf16[24,128,128]{2,1,0:T(8,128)(2,1)S(1)}, bf16[24,128,128]{2,1,0:T(8,128)(2,1)S(1)}, bf16[24,128,128]{2,1,0:T(8,128)(2,1)S(1)}, bf16[8,128,12...) custom-call(s32[1]{0:T(128)S(6)} %copy.12.count, s32[96]{0:T(128)} %src_hbm.1, s32[96]{0:T(128)} %dst_hbm.1, ...), custom_call_target="tpu_custom_call" | custom-call | flops 50331648 | bytes 1048576 | tf_op jit(solution)/shard_map/pallas_call | solution.py:347
  3.7 0.5 %collective-permute-start.1 = (bf16[8,128,128]{2,1,0:T(8,128)(2,1)S(1)}, bf16[8,128,128]{2,1,0:T(8,128)(2,1)S(1)}, u32[]{:S(2)}, u32[]{:S(2)}) collective-permute-start(bf16[8,128,128]{2,1,0:T(8,128)(2,1)S(1)} %get-tuple-element.60), channel_id=1, source_target_pairs={{0,2},{2,0},{4,6},{6,4},{8,10},{10,8},{12,14},{14,12},{16,18},{18,... | collective-permute-start | bytes 786440 | tf_op jit(solution)/shard_map/ppermute | solution.py:307
  4.2 1.3 %shard_map.113 = (f32[9,128,128]{2,1,0:T(8,128)S(1)}, bf16[4,128,128]{2,1,0:T(8,128)(2,1)S(1)}, bf16[4,128,128]{2,1,0:T(8,128)(2,1)S(1)}) custom-call(s32[1]{0:T(128)S(6)} %copy.12.count, s32[96]{0:T(128)S(1)} %get-tuple-element.49.index, bf16[8,128,128]{2,1,0:T(8,128)(2,1)S(1)} %get-tuple-element.50.xt, bf16[24,128,128]{2,1,0:T(8,128)(2,1)S(1)} %get-tuple-element.56.tiles2, ...), custom_call_target="tpu_custom_call" | custom-call | flops 100663296 | bytes 1048576 | tf_op jit(solution)/shard_map/pallas_call | solution.py:370
  5.9 3.5 %collective-permute-start.5 = (bf16[4,128,128]{2,1,0:T(8,128)(2,1)S(1)}, bf16[4,128,128]{2,1,0:T(8,128)(2,1)S(1)}, u32[]{:S(2)}, u32[]{:S(2)}) collective-permute-start(bf16[4,128,128]{2,1,0:T(8,128)(2,1)S(1)} %get-tuple-element.68), channel_id=1, source_target_pairs={{0,4},{2,6},{4,8},{6,10},{8,12},{10,14},{12,16},{14,18},{16,20},{1... | collective-permute-start | bytes 393224 | tf_op jit(solution)/shard_map/ppermute | solution.py:307
  9.4 0.4 %collective-permute-start = (bf16[4,128,128]{2,1,0:T(8,128)(2,1)S(1)}, bf16[4,128,128]{2,1,0:T(8,128)(2,1)S(1)}, u32[]{:S(2)}, u32[]{:S(2)}) collective-permute-start(bf16[4,128,128]{2,1,0:T(8,128)(2,1)S(1)} %get-tuple-element.58), channel_id=1, source_target_pairs={{0,2},{2,8},{4,6},{6,12},{8,10},{10,16},{12,14},{14,20},{16,18},{1... | collective-permute-start | bytes 393224 | tf_op jit(solution)/shard_map/ppermute | solution.py:307
  9.8 1.5 %collective-permute-start.2 = (bf16[4,128,128]{2,1,0:T(8,128)(2,1)S(1)}, bf16[4,128,128]{2,1,0:T(8,128)(2,1)S(1)}, u32[]{:S(2)}, u32[]{:S(2)}) collective-permute-start(bf16[4,128,128]{2,1,0:T(8,128)(2,1)S(1)} %get-tuple-element.64), channel_id=1, source_target_pairs={{0,4},{2,6},{4,8},{6,10},{8,12},{10,14},{12,16},{14,18},{16,20},{1... | collective-permute-start | bytes 393224 | tf_op jit(solution)/shard_map/ppermute | solution.py:307
  11.3 2.3 %shard_map.112 = (f32[9,128,128]{2,1,0:T(8,128)S(1)}, bf16[24,128,128]{2,1,0:T(8,128)(2,1)S(1)}, f32[128,128]{1,0:T(8,128)S(1)}, bf16[128,128]{1,0:T(8,128)(2,1)S(1)}, bf16[128,1024]{1,0:T(8,128)(2,1)S(1)}) custom-call(s32[1]{0:T(128)S(6)} %copy.12.count, s32[96]{0:T(128)S(1)} %get-tuple-element.49.index, bf16[8,128,128]{2,1,0:T(8,128)(2,1)S(1)} %get-tuple-element.50.xt, ...), custom_call_target="tpu_custom_call" | custom-call | flops 50331648 | bytes 1048576 | tf_op jit(solution)/shard_map/pallas_call | solution.py:382
  13.6 3.1 %collective-permute-done.5.refs_2_ = bf16[4,128,128]{2,1,0:T(8,128)(2,1)S(1)} collective-permute-done((bf16[4,128,128]{2,1,0:T(8,128)(2,1)S(1)}, bf16[4,128,128]{2,1,0:T(8,128)(2,1)S(1)}, u32[]{:S(2)}, u32[]{:S(2)}) %collective-permute-start.5) | collective-permute-done | bytes 131104 | tf_op jit(solution)/shard_map/ppermute | solution.py:307
  16.7 0.8 %shard_map.118 = (bf16[128,512]{1,0:T(8,128)(2,1)S(1)}, bf16[160,512]{1,0:T(8,128)(2,1)S(1)}, bf16[128,512]{1,0:T(8,128)(2,1)S(1)}, f32[4,64,128]{2,1,0:T(8,128)S(1)}, bf16[4,64,128]{2,1,0:T(8,128)(2,1)S(1)}) custom-call(f32[128,128]{1,0:T(8,128)S(1)} %get-tuple-element.52.bias_ref, bf16[128,128]{1,0:T(8,128)(2,1)S(1)} %copy-done, ...), custom_call_target="tpu_custom_call" | custom-call | flops 33554432 | bytes 1048576 | tf_op jit(solution)/shard_map/pallas_call | solution.py:403
  17.6 1.5 %collective-permute-start.6 = (bf16[4,64,128]{2,1,0:T(8,128)(2,1)S(1)}, bf16[4,64,128]{2,1,0:T(8,128)(2,1)S(1)}, u32[]{:S(2)}, u32[]{:S(2)}) collective-permute-start(bf16[4,64,128]{2,1,0:T(8,128)(2,1)S(1)} %get-tuple-element.70), channel_id=1, source_target_pairs={{0,1},{1,0},{2,3},{3,2},{4,5},{5,4},{6,7},{7,6},{8,9},{9,8},{10,11... | collective-permute-start | bytes 196616 | tf_op jit(solution)/shard_map/ppermute | solution.py:307
  19.1 0.4 %collective-permute-done.2.refs_2_ = bf16[4,128,128]{2,1,0:T(8,128)(2,1)S(1)} collective-permute-done((bf16[4,128,128]{2,1,0:T(8,128)(2,1)S(1)}, bf16[4,128,128]{2,1,0:T(8,128)(2,1)S(1)}, u32[]{:S(2)}, u32[]{:S(2)}) %collective-permute-start.2) | collective-permute-done | bytes 131104 | tf_op jit(solution)/shard_map/ppermute | solution.py:307
  19.6 0.8 %shard_map.116 = (bf16[128,512]{1,0:T(8,128)(2,1)S(1)}, bf16[160,512]{1,0:T(8,128)(2,1)S(1)}, bf16[128,512]{1,0:T(8,128)(2,1)S(1)}, f32[4,64,128]{2,1,0:T(8,128)S(1)}, bf16[4,64,128]{2,1,0:T(8,128)(2,1)S(1)}) custom-call(f32[128,128]{1,0:T(8,128)S(1)} %get-tuple-element.52.bias_ref, bf16[128,128]{1,0:T(8,128)(2,1)S(1)} %copy-done, ...), custom_call_target="tpu_custom_call" | custom-call | flops 33554432 | bytes 1048576 | tf_op jit(solution)/shard_map/pallas_call | solution.py:403
  20.4 1.5 %collective-permute-start.3 = (bf16[4,64,128]{2,1,0:T(8,128)(2,1)S(1)}, bf16[4,64,128]{2,1,0:T(8,128)(2,1)S(1)}, u32[]{:S(2)}, u32[]{:S(2)}) collective-permute-start(bf16[4,64,128]{2,1,0:T(8,128)(2,1)S(1)} %get-tuple-element.66), channel_id=1, source_target_pairs={{0,1},{1,0},{2,3},{3,2},{4,5},{5,4},{6,7},{7,6},{8,9},{9,8},{10,11... | collective-permute-start | bytes 196616 | tf_op jit(solution)/shard_map/ppermute | solution.py:307
  22.1 1.4 %collective-permute-start.10 = (bf16[80,128]{1,0:T(8,128)(2,1)S(1)}, bf16[80,128]{1,0:T(8,128)(2,1)S(1)}, u32[]{:S(2)}, u32[]{:S(2)}) collective-permute-start(bf16[80,128]{1,0:T(8,128)(2,1)S(1)} %get-tuple-element.80.refs_0_), channel_id=1, source_target_pairs={{0,4},{2,6},{4,0},{6,2},{8,12},{10,14},{12,8},{14,10},{16,20},{18,... | collective-permute-start | bytes 61448 | tf_op jit(solution)/shard_map/ppermute | solution.py:307
  23.5 1.7 %collective-permute-start.11 = (bf16[80,128]{1,0:T(8,128)(2,1)S(1)}, bf16[80,128]{1,0:T(8,128)(2,1)S(1)}, u32[]{:S(2)}, u32[]{:S(2)}) collective-permute-start(bf16[80,128]{1,0:T(8,128)(2,1)S(1)} %get-tuple-element.81), channel_id=1, source_target_pairs={{0,6},{2,4},{4,2},{6,0},{8,14},{10,12},{12,10},{14,8},{16,22},{18,... | collective-permute-start | bytes 61448 | tf_op jit(solution)/shard_map/ppermute | solution.py:307
  25.3 1.4 %collective-permute-start.8 = (bf16[8,64,128]{2,1,0:T(8,128)(2,1)S(1)}, bf16[8,64,128]{2,1,0:T(8,128)(2,1)S(1)}, u32[]{:S(2)}, u32[]{:S(2)}) collective-permute-start(bf16[8,64,128]{2,1,0:T(8,128)(2,1)S(1)} %shard_map.119.g), channel_id=1, source_target_pairs={{0,28},{2,30},{4,0},{6,2},{8,4},{10,6},{12,8},{14,10},{16,12},{18,... | collective-permute-start | bytes 393224 | tf_op jit(solution)/shard_map/ppermute | solution.py:307
  26.9 1.2 %collective-permute-start.14 = (bf16[80,128]{1,0:T(8,128)(2,1)S(1)}, bf16[80,128]{1,0:T(8,128)(2,1)S(1)}, u32[]{:S(2)}, u32[]{:S(2)}) collective-permute-start(bf16[80,128]{1,0:T(8,128)(2,1)S(1)} %shard_map.122.refs_0_), channel_id=1, source_target_pairs={{0,24},{2,26},{4,28},{6,30},{8,16},{10,18},{12,20},{14,22},{16,8},... | collective-permute-start | bytes 61448 | tf_op jit(solution)/shard_map/ppermute | solution.py:307
  28.2 1.5 %collective-permute-start.13 = (bf16[80,128]{1,0:T(8,128)(2,1)S(1)}, bf16[80,128]{1,0:T(8,128)(2,1)S(1)}, u32[]{:S(2)}, u32[]{:S(2)}) collective-permute-start(bf16[80,128]{1,0:T(8,128)(2,1)S(1)} %shard_map.122.refs_0_), channel_id=1, source_target_pairs={{0,16},{2,18},{4,20},{6,22},{8,24},{10,26},{12,28},{14,30},{16,0},... | collective-permute-start | bytes 61448 | tf_op jit(solution)/shard_map/ppermute | solution.py:307
  29.7 1.7 %collective-permute-start.12 = (bf16[80,128]{1,0:T(8,128)(2,1)S(1)}, bf16[80,128]{1,0:T(8,128)(2,1)S(1)}, u32[]{:S(2)}, u32[]{:S(2)}) collective-permute-start(bf16[80,128]{1,0:T(8,128)(2,1)S(1)} %shard_map.122.refs_0_), channel_id=1, source_target_pairs={{0,8},{2,10},{4,12},{6,14},{8,0},{10,2},{12,4},{14,6},{16,24},{18,... | collective-permute-start | bytes 61448 | tf_op jit(solution)/shard_map/ppermute | solution.py:307
  31.4 1.5 %shard_map.120 = (f32[9,64,128]{2,1,0:T(8,128)S(1)}, bf16[1024,128]{1,0:T(8,128)(2,1)}) custom-call(s32[1]{0:T(128)S(6)} %copy.12.count, s32[96]{0:T(128)S(1)} %get-tuple-element.49.index, bf16[24,128,128]{2,1,0:T(8,128)(2,1)S(1)} %get-tuple-element.51.tiles, bf16[8,64,128]{2,1,0:T(8,128)(2,1)S(1)} %shard_map.119.g, ...), custom_call_target="tpu_custom_call" | custom-call | flops 50331648 | bytes 1048576 | tf_op jit(solution)/shard_map/pallas_call | solution.py:433
  33.0 0.8 %collective-permute-done.12.refs_1_ = bf16[80,128]{1,0:T(8,128)(2,1)S(1)} collective-permute-done((bf16[80,128]{1,0:T(8,128)(2,1)S(1)}, bf16[80,128]{1,0:T(8,128)(2,1)S(1)}, u32[]{:S(2)}, u32[]{:S(2)}) %collective-permute-start.12) | collective-permute-done | bytes 20512 | tf_op jit(solution)/shard_map/ppermute | solution.py:307
  33.9 0.9 %shard_map.124 = (f32[9,64,128]{2,1,0:T(8,128)S(1)}, f32[9,64,128]{2,1,0:T(8,128)S(1)}) custom-call(s32[1]{0:T(128)S(6)} %copy.12.count, s32[96]{0:T(128)S(1)} %get-tuple-element.49.index, bf16[24,128,128]{2,1,0:T(8,128)(2,1)S(1)} %get-tuple-element.56.tiles2, bf16[24,128,128]{2,1,0:T(8,128)(2,1)S(1)} %get-tuple-element.57.tiles3, ...), custom_call_target="tpu_custom_call" | custom-call | flops 100663296 | bytes 1048576 | tf_op jit(solution)/shard_map/pallas_call | solution.py:445
  34.8 0.4 %collective-permute-done.15.got = bf16[592,128]{1,0:T(8,128)(2,1)S(1)} collective-permute-done((bf16[592,128]{1,0:T(8,128)(2,1)S(1)}, bf16[592,128]{1,0:T(8,128)(2,1)S(1)}, u32[]{:S(2)}, u32[]{:S(2)}) %collective-permute-start.15) | collective-permute-done | bytes 151584 | tf_op jit(solution)/shard_map/ppermute | solution.py:307
  35.2 1.6 %shard_map.125 = (bf16[64,1024]{1,0:T(8,128)(2,1)}, f32[128,128]{1,0:T(8,128)}, f32[1,128]{1,0:T(1,128)}) custom-call(s32[1]{0:T(128)S(6)} %copy.12.count, s32[96]{0:T(128)S(1)} %get-tuple-element.49.index, bf16[24,128,128]{2,1,0:T(8,128)(2,1)S(1)} %get-tuple-element.74.tiles1, bf16[592,128]{1,0:T(8,128)(2,1)S(1)} %shard_map.123.sent, ...), custom_call_target="tpu_custom_call" | custom-call | flops 50331648 | bytes 1048576 | tf_op jit(solution)/shard_map/pallas_call | solution.py:448
  (27 shorter events, 1.2 us)
Async XLA Ops:
  0.6 10.7 %copy-start = (bf16[128,128]{1,0:T(8,128)(2,1)S(1)}, bf16[128,128]{1,0:T(8,128)(2,1)}, u32[]{:S(2)}) copy-start(bf16[128,128]{1,0:T(8,128)(2,1)} %w_ref.5) | copy-start | bytes 98308
  0.6 10.7 %copy-start.1 = (f32[128]{0:T(128)S(1)}, f32[128]{0:T(128)}, u32[]{:S(2)}) copy-start(f32[128]{0:T(128)} %param.10) | copy-start | bytes 1540
  3.7 1.9 %collective-permute-start.1 = (bf16[8,128,128]{2,1,0:T(8,128)(2,1)S(1)}, bf16[8,128,128]{2,1,0:T(8,128)(2,1)S(1)}, u32[]{:S(2)}, u32[]{:S(2)}) collective-permute-start(bf16[8,128,128]{2,1,0:T(8,128)(2,1)S(1)} %get-tuple-element.60), channel_id=1, source_target_pairs={{0,2},{2,0},{4,6},{6,4},{8,10},{10,8},{12,14},{14,12},{16,18},{18,... | collective-permute-start | bytes 786440 | tf_op jit(solution)/shard_map/ppermute | solution.py:307
  5.6 8.0 %collective-permute-start.4 = (bf16[4,128,128]{2,1,0:T(8,128)(2,1)S(1)}, bf16[4,128,128]{2,1,0:T(8,128)(2,1)S(1)}, u32[]{:S(2)}, u32[]{:S(2)}) collective-permute-start(bf16[4,128,128]{2,1,0:T(8,128)(2,1)S(1)} %get-tuple-element.67), channel_id=1, source_target_pairs={{0,2},{2,8},{4,6},{6,12},{8,10},{10,16},{12,14},{14,20},{16,18},{1... | collective-permute-start | bytes 393224 | tf_op jit(solution)/shard_map/ppermute | solution.py:307
  5.9 10.8 %collective-permute-start.5 = (bf16[4,128,128]{2,1,0:T(8,128)(2,1)S(1)}, bf16[4,128,128]{2,1,0:T(8,128)(2,1)S(1)}, u32[]{:S(2)}, u32[]{:S(2)}) collective-permute-start(bf16[4,128,128]{2,1,0:T(8,128)(2,1)S(1)} %get-tuple-element.68), channel_id=1, source_target_pairs={{0,4},{2,6},{4,8},{6,10},{8,12},{10,14},{12,16},{14,18},{16,20},{1... | collective-permute-start | bytes 393224 | tf_op jit(solution)/shard_map/ppermute | solution.py:307
  9.4 9.7 %collective-permute-start = (bf16[4,128,128]{2,1,0:T(8,128)(2,1)S(1)}, bf16[4,128,128]{2,1,0:T(8,128)(2,1)S(1)}, u32[]{:S(2)}, u32[]{:S(2)}) collective-permute-start(bf16[4,128,128]{2,1,0:T(8,128)(2,1)S(1)} %get-tuple-element.58), channel_id=1, source_target_pairs={{0,2},{2,8},{4,6},{6,12},{8,10},{10,16},{12,14},{14,20},{16,18},{1... | collective-permute-start | bytes 393224 | tf_op jit(solution)/shard_map/ppermute | solution.py:307
  9.8 9.7 %collective-permute-start.2 = (bf16[4,128,128]{2,1,0:T(8,128)(2,1)S(1)}, bf16[4,128,128]{2,1,0:T(8,128)(2,1)S(1)}, u32[]{:S(2)}, u32[]{:S(2)}) collective-permute-start(bf16[4,128,128]{2,1,0:T(8,128)(2,1)S(1)} %get-tuple-element.64), channel_id=1, source_target_pairs={{0,4},{2,6},{4,8},{6,10},{8,12},{10,14},{12,16},{14,18},{16,20},{1... | collective-permute-start | bytes 393224 | tf_op jit(solution)/shard_map/ppermute | solution.py:307
  17.6 7.7 %collective-permute-start.6 = (bf16[4,64,128]{2,1,0:T(8,128)(2,1)S(1)}, bf16[4,64,128]{2,1,0:T(8,128)(2,1)S(1)}, u32[]{:S(2)}, u32[]{:S(2)}) collective-permute-start(bf16[4,64,128]{2,1,0:T(8,128)(2,1)S(1)} %get-tuple-element.70), channel_id=1, source_target_pairs={{0,1},{1,0},{2,3},{3,2},{4,5},{5,4},{6,7},{7,6},{8,9},{9,8},{10,11... | collective-permute-start | bytes 196616 | tf_op jit(solution)/shard_map/ppermute | solution.py:307
  20.4 4.9 %collective-permute-start.3 = (bf16[4,64,128]{2,1,0:T(8,128)(2,1)S(1)}, bf16[4,64,128]{2,1,0:T(8,128)(2,1)S(1)}, u32[]{:S(2)}, u32[]{:S(2)}) collective-permute-start(bf16[4,64,128]{2,1,0:T(8,128)(2,1)S(1)} %get-tuple-element.66), channel_id=1, source_target_pairs={{0,1},{1,0},{2,3},{3,2},{4,5},{5,4},{6,7},{7,6},{8,9},{9,8},{10,11... | collective-permute-start | bytes 196616 | tf_op jit(solution)/shard_map/ppermute | solution.py:307
  22.1 4.6 %collective-permute-start.10 = (bf16[80,128]{1,0:T(8,128)(2,1)S(1)}, bf16[80,128]{1,0:T(8,128)(2,1)S(1)}, u32[]{:S(2)}, u32[]{:S(2)}) collective-permute-start(bf16[80,128]{1,0:T(8,128)(2,1)S(1)} %get-tuple-element.80.refs_0_), channel_id=1, source_target_pairs={{0,4},{2,6},{4,0},{6,2},{8,12},{10,14},{12,8},{14,10},{16,20},{18,... | collective-permute-start | bytes 61448 | tf_op jit(solution)/shard_map/ppermute | solution.py:307
  23.5 3.4 %collective-permute-start.11 = (bf16[80,128]{1,0:T(8,128)(2,1)S(1)}, bf16[80,128]{1,0:T(8,128)(2,1)S(1)}, u32[]{:S(2)}, u32[]{:S(2)}) collective-permute-start(bf16[80,128]{1,0:T(8,128)(2,1)S(1)} %get-tuple-element.81), channel_id=1, source_target_pairs={{0,6},{2,4},{4,2},{6,0},{8,14},{10,12},{12,10},{14,8},{16,22},{18,... | collective-permute-start | bytes 61448 | tf_op jit(solution)/shard_map/ppermute | solution.py:307
  25.2 1.7 %collective-permute-start.9 = (bf16[80,128]{1,0:T(8,128)(2,1)S(1)}, bf16[80,128]{1,0:T(8,128)(2,1)S(1)}, u32[]{:S(2)}, u32[]{:S(2)}) collective-permute-start(bf16[80,128]{1,0:T(8,128)(2,1)S(1)} %get-tuple-element.81), channel_id=1, source_target_pairs={{0,2},{2,0},{4,6},{6,4},{8,10},{10,8},{12,14},{14,12},{16,18},{18,... | collective-permute-start | bytes 61448 | tf_op jit(solution)/shard_map/ppermute | solution.py:307
  25.3 8.5 %collective-permute-start.8 = (bf16[8,64,128]{2,1,0:T(8,128)(2,1)S(1)}, bf16[8,64,128]{2,1,0:T(8,128)(2,1)S(1)}, u32[]{:S(2)}, u32[]{:S(2)}) collective-permute-start(bf16[8,64,128]{2,1,0:T(8,128)(2,1)S(1)} %shard_map.119.g), channel_id=1, source_target_pairs={{0,28},{2,30},{4,0},{6,2},{8,4},{10,6},{12,8},{14,10},{16,12},{18,... | collective-permute-start | bytes 393224 | tf_op jit(solution)/shard_map/ppermute | solution.py:307
  26.7 7.1 %collective-permute-start.7 = (bf16[8,64,128]{2,1,0:T(8,128)(2,1)S(1)}, bf16[8,64,128]{2,1,0:T(8,128)(2,1)S(1)}, u32[]{:S(2)}, u32[]{:S(2)}) collective-permute-start(bf16[8,64,128]{2,1,0:T(8,128)(2,1)S(1)} %shard_map.119.g), channel_id=1, source_target_pairs={{0,26},{2,0},{4,30},{6,4},{8,2},{10,8},{12,6},{14,12},{16,10},{18,... | collective-permute-start | bytes 393224 | tf_op jit(solution)/shard_map/ppermute | solution.py:307
  26.9 6.0 %collective-permute-start.14 = (bf16[80,128]{1,0:T(8,128)(2,1)S(1)}, bf16[80,128]{1,0:T(8,128)(2,1)S(1)}, u32[]{:S(2)}, u32[]{:S(2)}) collective-permute-start(bf16[80,128]{1,0:T(8,128)(2,1)S(1)} %shard_map.122.refs_0_), channel_id=1, source_target_pairs={{0,24},{2,26},{4,28},{6,30},{8,16},{10,18},{12,20},{14,22},{16,8},... | collective-permute-start | bytes 61448 | tf_op jit(solution)/shard_map/ppermute | solution.py:307
  28.2 4.8 %collective-permute-start.13 = (bf16[80,128]{1,0:T(8,128)(2,1)S(1)}, bf16[80,128]{1,0:T(8,128)(2,1)S(1)}, u32[]{:S(2)}, u32[]{:S(2)}) collective-permute-start(bf16[80,128]{1,0:T(8,128)(2,1)S(1)} %shard_map.122.refs_0_), channel_id=1, source_target_pairs={{0,16},{2,18},{4,20},{6,22},{8,24},{10,26},{12,28},{14,30},{16,0},... | collective-permute-start | bytes 61448 | tf_op jit(solution)/shard_map/ppermute | solution.py:307
  29.7 4.0 %collective-permute-start.12 = (bf16[80,128]{1,0:T(8,128)(2,1)S(1)}, bf16[80,128]{1,0:T(8,128)(2,1)S(1)}, u32[]{:S(2)}, u32[]{:S(2)}) collective-permute-start(bf16[80,128]{1,0:T(8,128)(2,1)S(1)} %shard_map.122.refs_0_), channel_id=1, source_target_pairs={{0,8},{2,10},{4,12},{6,14},{8,0},{10,2},{12,4},{14,6},{16,24},{18,... | collective-permute-start | bytes 61448 | tf_op jit(solution)/shard_map/ppermute | solution.py:307
  33.8 1.4 %collective-permute-start.15 = (bf16[592,128]{1,0:T(8,128)(2,1)S(1)}, bf16[592,128]{1,0:T(8,128)(2,1)S(1)}, u32[]{:S(2)}, u32[]{:S(2)}) collective-permute-start(bf16[592,128]{1,0:T(8,128)(2,1)S(1)} %shard_map.123.sent), channel_id=1, source_target_pairs={{0,2},{2,0},{4,6},{6,4},{8,10},{10,8},{12,14},{14,12},{16,18},{18,... | collective-permute-start | bytes 454664 | tf_op jit(solution)/shard_map/ppermute | solution.py:307

commit v7 on v6

--- a/solution.py
+++ b/solution.py
@@ -18,13 +18,14 @@
 HBM = pl.BlockSpec(memory_space=pltpu.HBM)
 
 
-def call(kernel, out_shape, in_specs, out_specs, scratch=(), flops=0):
+def call(kernel, out_shape, in_specs, out_specs, scratch=(), flops=0, aliases=None):
     return pl.pallas_call(
         kernel,
         out_shape=out_shape,
         in_specs=in_specs,
         out_specs=out_specs,
         scratch_shapes=list(scratch),
+        input_output_aliases=aliases or {},
         compiler_params=pltpu.CompilerParams(vmem_limit_bytes=24 * 1024 * 1024),
         cost_estimate=pl.CostEstimate(flops=flops, bytes_accessed=2**20, transcendentals=0),
     )
@@ -243,20 +244,23 @@
     out[blocks * width :, :hid] = total
 
 
-def backward_own_kernel(count, index, tiles, g, *refs):
-    acts, (acc, out, rows, sems) = refs[:-4], refs[-4:]
-    copies, first = [], 0
-    for i, act in enumerate(acts):
-        for col in range(0, act.shape[1], BLOCK):
-            rows[first + col : first + col + BLOCK, :] = turned(act[:, col : col + BLOCK])
-        part = pl.ds(first, act.shape[1])
-        copies.append(pltpu.make_async_copy(rows.at[part], out.at[part], sems.at[i]))
-        copies[-1].start()
-        first += act.shape[1]
+def turned_rows(act, rows, out, first, sem):
+    for col in range(0, act.shape[1], BLOCK):
+        rows[col : col + BLOCK, :] = turned(act[:, col : col + BLOCK])
+    copy = pltpu.make_async_copy(rows, out.at[pl.ds(first, act.shape[1])], sem)
+    copy.start()
+    return copy
+
+
+def activation_kernel(first, act, out, rows, sem):
+    turned_rows(act, rows, out, first, sem).wait()
+
+
+def backward_own_kernel(count, index, tiles, g, act, out_before, acc, out, rows, sem):
+    copy = turned_rows(act, rows, out, 0, sem)
     acc[...] = jnp.zeros_like(acc)
     pull_all(index, count[0], (lambda d: g[d], tiles, acc, 0))
-    for c in copies:
-        c.wait()
+    copy.wait()
 
 
 def backward_near_kernel(count, index, tiles2, tiles3, g2, g3, acc2, acc3):
@@ -360,22 +364,23 @@
     )(tile_counts, *(in_hbm(a) for a in (tile_src, tile_dst, node_features, tiles)))
     index = (tile_counts, index)
     swap = moved(swap, "dom", swapped)
-    cut = 2 if blocks % 2 == 0 else 1
-    starts = range(0, blocks, blocks // cut)
-    half = jax.ShapeDtypeStruct((blocks // cut, width, BLOCK), BF16)
-    half_x = jax.ShapeDtypeStruct((blocks // cut, f_in, BLOCK), BF16)
-    half_wide = jax.ShapeDtypeStruct(half.shape, F32)
-    half_rows = jax.ShapeDtypeStruct((hid, nodes // cut), BF16)
-    half_columns = jax.ShapeDtypeStruct((f_in + 32, nodes // cut), BF16)
+    cut = 2
+    sizes = (blocks * 3 // 8, blocks - blocks * 3 // 8)
+    starts = (0, sizes[0])
+    half = [jax.ShapeDtypeStruct((n, width, BLOCK), BF16) for n in sizes]
+    half_x = [jax.ShapeDtypeStruct((n, f_in, BLOCK), BF16) for n in sizes]
+    half_wide = [jax.ShapeDtypeStruct((n, width, BLOCK), F32) for n in sizes]
+    half_rows = [jax.ShapeDtypeStruct((hid, n * BLOCK), BF16) for n in sizes]
+    half_columns = [jax.ShapeDtypeStruct((f_in + 32, n * BLOCK), BF16) for n in sizes]
     acc2, *direct = call(
         forward_send_kernel,
-        [totals_x] + [half_x] * cut,
+        [totals_x] + half_x,
         [SMEM] * 2 + [VMEM] * 3,
         [VMEM] * (1 + cut),
         [acc_x],
         2 * flops,
     )(*index, xt, tiles2, tiles3)
-    chip = call(functools.partial(sum_kernel, 2, 0), [half_x] * cut, [VMEM] * 2, [VMEM] * cut)(acc2, swap)
+    chip = call(functools.partial(sum_kernel, 2, 0), half_x, [VMEM] * 2, [VMEM] * cut)(acc2, swap)
     chip = lax.optimization_barrier((*chip, *direct[1:]))
     direct, chip = [direct[0], *chip[cut:]], chip[:cut]
     chip = [moved(c, "dom", lambda i: i + 2) for c in chip]
@@ -394,23 +399,31 @@
         flops,
     )(*index, xt, bias.reshape(1, hid), weight, in_hbm(out_grad), in_hbm(tiles))
     direct = [moved(d, "dom", lambda i: i + 1 + 2 * (i % 2)) for d in direct]
-    h_list = []
-    for first, c, d in zip(starts, chip, direct):
-        (h,) = call(functools.partial(sum_kernel, 3, first), [half_x], [VMEM] * 3, [VMEM])(acc0, d, c)
-        h_list.append(h)
-    acts, hts, grads, g_list = [], [], [], []
-    for first, h in zip(starts, h_list):
-        act, ht, grad, g_own, *g_others = call(
-            functools.partial(middle_kernel, parts, first),
-            [half_rows, half_columns, half_rows, half_wide] + [half] * (parts - 1),
+    halves = [None, None]
+    for i in (1, 0):
+        (h,) = call(functools.partial(sum_kernel, 3, starts[i]), [half_x[i]], [VMEM] * 3, [VMEM])(
+            acc0, direct[i], chip[i]
+        )
+        halves[i] = call(
+            functools.partial(middle_kernel, parts, starts[i]),
+            [half_rows[i], half_columns[i], half_rows[i], half_wide[i]] + [half[i]] * (parts - 1),
             [VMEM] * 5,
             [VMEM] * (3 + parts),
             (),
-            4 * nodes * f_in * hid // cut,
+            4 * sizes[i] * BLOCK * f_in * hid,
         )(bias_t, weight, w_t, og_t, h)
-        acts.append(act)
-        hts.append(ht)
-        grads.append(grad)
+        if i == 1:
+            (output,) = call(
+                functools.partial(activation_kernel, starts[1] * BLOCK),
+                [rows],
+                [VMEM],
+                [HBM],
+                [pltpu.VMEM((sizes[1] * BLOCK, hid), BF16), pltpu.SemaphoreType.DMA],
+            )(halves[1][0])
+            acc0, output = lax.optimization_barrier((acc0, output))
+    acts, hts, grads, *_ = zip(*halves)
+    g_list = []
+    for _, _, _, g_own, *g_others in halves:
         g_list += [g_own] + [moved(g, "feat", lambda i, q=q + 1: i + q) for q, g in enumerate(g_others)]
     wg, wg_other = call(
         functools.partial(weight_grad_kernel, cut),
@@ -433,11 +446,12 @@
     back0, output = call(
         backward_own_kernel,
         [totals, rows],
-        [SMEM] * 2 + [VMEM] * (2 + cut),
+        [SMEM] * 2 + [VMEM] * 3 + [HBM],
         [VMEM, HBM],
-        [pltpu.VMEM(rows.shape, BF16), pltpu.SemaphoreType.DMA((cut,))],
+        [pltpu.VMEM((sizes[0] * BLOCK, hid), BF16), pltpu.SemaphoreType.DMA],
         flops,
-    )(*index, tiles0, g, *acts)
+        {5: 1},
+    )(*index, tiles0, g, acts[0], output)
     g_direct, g_chip, back0, *wgs = lax.optimization_barrier((g_direct, g_chip, back0, *wgs))
     payload = jax.ShapeDtypeStruct((blocks * width + gradient.shape[0], BLOCK), BF16)
     (sent,) = call(swap_payload_kernel, [payload], [VMEM] * (1 + len(wgs)), [VMEM])(g_chip, *wgs)

time: 37.1 us -> 37.8 us (1.019)
  Pallas kernels: 12.1 us -> 12.9 us
  starting transfers between devices: 18.3 us -> 17.8 us
  waiting for transfers between devices: 5.04 us -> 5.49 us
    pallas_call x7 -> x8, Pallas kernels: 4.63 us -> 5.45 us  [the longest x2 1.66 us: shards(): call(functools.partial(middle_kernel, parts, starts[i]), [half_rows[i], h...]
    ppermute x16, starting transfers between devices: 18.3 us -> 17.8 us  [moved(): return lax.ppermute(block, axis, [(i, target(i) % n) for i in range(n)])]
    ppermute x16, waiting for transfers between devices: 5.04 us -> 5.49 us  [moved(): return lax.ppermute(block, axis, [(i, target(i) % n) for i in range(n)])]
  transfers between devices with their start and end apart: 16 -> 16, of which waited for: 6 -> 5; matrix products, arithmetic and copies ran while one was open for 0% -> 0% of each run, Pallas kernels for 22% -> 24%
where the time goes in v7:
time: 37.8 us; the launch traced here: 37.7 us
  starting transfers between devices  17.8 us (47%)
  Pallas kernels  12.9 us (34%)
  waiting for transfers between devices  5.49 us (15%)
  between operations  1.46 us (4%)
    ppermute x16, starting transfers between devices, moved(): return lax.ppermute(block, axis, [(i, target(i) % n) for i in range(n)])  17.8 us
    ppermute x16, waiting for transfers between devices, moved(): return lax.ppermute(block, axis, [(i, target(i) % n) for i in range(n)])  5.49 us
    pallas_call x1, Pallas kernels, shards(): call(forward_swap_kernel, [plane, plane, plane, piece_x, piece_x, slots],...  2.35 us
    pallas_call x1, Pallas kernels, shards(): call(forward_own_kernel, [totals_x, plane, jax.ShapeDtypeStruct((hid, BLO...  2.26 us
    pallas_call x2, Pallas kernels, shards(): call(functools.partial(middle_kernel, parts, starts[i]), [half_rows[i], h...  1.66 us
    pallas_call x1, Pallas kernels, shards(): call(backward_last_kernel, [jax.ShapeDtypeStruct((width, nodes), BF16), j...  1.58 us
    pallas_call x1, Pallas kernels, shards(): call(backward_own_kernel, [totals, rows], [SMEM] * 2 + [VMEM] * 3 + [HBM]...  1.39 us
    pallas_call x1, Pallas kernels, shards(): call(forward_send_kernel, [totals_x] + half_x, [SMEM] * 2 + [VMEM] * 3, [...  1.33 us
  transfers between devices with their start and end apart: 16, of which 5 were waited for; matrix products, arithmetic and copies ran while one was open for 0% of the time, Pallas kernels for 24%

profile of v7, /device:TPU:0, one launch (start us, length us, event | category | flops | bytes accessed | tf_op | source)
XLA Modules:
  0.0 37.7 jit_solution(15555865639762827250)
XLA Ops:
  1.3 2.3 %shard_map.111 = (bf16[24,128,128]{2,1,0:T(8,128)(2,1)S(1)}, bf16[24,128,128]{2,1,0:T(8,128)(2,1)S(1)}, bf16[24,128,128]{2,1,0:T(8,128)(2,1)S(1)}, bf16[8,128,12...) custom-call(s32[1]{0:T(128)S(6)} %copy.14.count, s32[96]{0:T(128)} %src_hbm.1, s32[96]{0:T(128)} %dst_hbm.1, ...), custom_call_target="tpu_custom_call" | custom-call | flops 50331648 | bytes 1048576 | tf_op jit(solution)/shard_map/pallas_call | solution.py:351
  3.7 0.5 %collective-permute-start = (bf16[8,128,128]{2,1,0:T(8,128)(2,1)S(1)}, bf16[8,128,128]{2,1,0:T(8,128)(2,1)S(1)}, u32[]{:S(2)}, u32[]{:S(2)}) collective-permute-start(bf16[8,128,128]{2,1,0:T(8,128)(2,1)S(1)} %get-tuple-element.61), channel_id=1, source_target_pairs={{0,2},{2,0},{4,6},{6,4},{8,10},{10,8},{12,14},{14,12},{16,18},{18,... | collective-permute-start | bytes 786440 | tf_op jit(solution)/shard_map/ppermute | solution.py:311
  4.2 1.3 %shard_map.113 = (f32[9,128,128]{2,1,0:T(8,128)S(1)}, bf16[3,128,128]{2,1,0:T(8,128)(2,1)S(1)}, bf16[5,128,128]{2,1,0:T(8,128)(2,1)S(1)}) custom-call(s32[1]{0:T(128)S(6)} %copy.14.count, s32[96]{0:T(128)S(1)} %get-tuple-element.51.index, bf16[8,128,128]{2,1,0:T(8,128)(2,1)S(1)} %get-tuple-element.52.xt, bf16[24,128,128]{2,1,0:T(8,128)(2,1)S(1)} %get-tuple-element.58.tiles2, ...), custom_call_target="tpu_custom_call" | custom-call | flops 100663296 | bytes 1048576 | tf_op jit(solution)/shard_map/pallas_call | solution.py:375
  5.9 2.8 %collective-permute-start.2 = (bf16[5,128,128]{2,1,0:T(8,128)(2,1)S(1)}, bf16[5,128,128]{2,1,0:T(8,128)(2,1)S(1)}, u32[]{:S(2)}, u32[]{:S(2)}) collective-permute-start(bf16[5,128,128]{2,1,0:T(8,128)(2,1)S(1)} %get-tuple-element.66), channel_id=1, source_target_pairs={{0,4},{2,6},{4,8},{6,10},{8,12},{10,14},{12,16},{14,18},{16,20},{1... | collective-permute-start | bytes 491528 | tf_op jit(solution)/shard_map/ppermute | solution.py:311
  8.7 1.1 %collective-permute-start.3 = (bf16[3,128,128]{2,1,0:T(8,128)(2,1)S(1)}, bf16[3,128,128]{2,1,0:T(8,128)(2,1)S(1)}, u32[]{:S(2)}, u32[]{:S(2)}) collective-permute-start(bf16[3,128,128]{2,1,0:T(8,128)(2,1)S(1)} %get-tuple-element.69), channel_id=1, source_target_pairs={{0,2},{2,8},{4,6},{6,12},{8,10},{10,16},{12,14},{14,20},{16,18},{1... | collective-permute-start | bytes 294920 | tf_op jit(solution)/shard_map/ppermute | solution.py:311
  9.8 1.5 %collective-permute-start.4 = (bf16[3,128,128]{2,1,0:T(8,128)(2,1)S(1)}, bf16[3,128,128]{2,1,0:T(8,128)(2,1)S(1)}, u32[]{:S(2)}, u32[]{:S(2)}) collective-permute-start(bf16[3,128,128]{2,1,0:T(8,128)(2,1)S(1)} %get-tuple-element.70), channel_id=1, source_target_pairs={{0,4},{2,6},{4,8},{6,10},{8,12},{10,14},{12,16},{14,18},{16,20},{1... | collective-permute-start | bytes 294920 | tf_op jit(solution)/shard_map/ppermute | solution.py:311
  11.3 2.3 %shard_map.112 = (f32[9,128,128]{2,1,0:T(8,128)S(1)}, bf16[24,128,128]{2,1,0:T(8,128)(2,1)S(1)}, f32[128,128]{1,0:T(8,128)S(1)}, bf16[128,128]{1,0:T(8,128)(2,1)S(1)}, bf16[128,1024]{1,0:T(8,128)(2,1)S(1)}) custom-call(s32[1]{0:T(128)S(6)} %copy.14.count, s32[96]{0:T(128)S(1)} %get-tuple-element.51.index, bf16[8,128,128]{2,1,0:T(8,128)(2,1)S(1)} %get-tuple-element.52.xt, ...), custom_call_target="tpu_custom_call" | custom-call | flops 50331648 | bytes 1048576 | tf_op jit(solution)/shard_map/pallas_call | solution.py:387
  13.6 3.8 %collective-permute-done.2.refs_2_ = bf16[5,128,128]{2,1,0:T(8,128)(2,1)S(1)} collective-permute-done((bf16[5,128,128]{2,1,0:T(8,128)(2,1)S(1)}, bf16[5,128,128]{2,1,0:T(8,128)(2,1)S(1)}, u32[]{:S(2)}, u32[]{:S(2)}) %collective-permute-start.2) | collective-permute-done | bytes 163872 | tf_op jit(solution)/shard_map/ppermute | solution.py:311
  17.4 1.0 %shard_map.116 = (bf16[128,640]{1,0:T(8,128)(2,1)S(1)}, bf16[160,640]{1,0:T(8,128)(2,1)S(1)}, bf16[128,640]{1,0:T(8,128)(2,1)S(1)}, f32[5,64,128]{2,1,0:T(8,128)S(1)}, bf16[5,64,128]{2,1,0:T(8,128)(2,1)S(1)}) custom-call(f32[128,128]{1,0:T(8,128)S(1)} %get-tuple-element.54.bias_ref, bf16[128,128]{1,0:T(8,128)(2,1)S(1)} %copy-done, ...), custom_call_target="tpu_custom_call" | custom-call | flops 41943040 | bytes 1048576 | tf_op jit(solution)/shard_map/pallas_call | solution.py:407
  18.5 1.6 %collective-permute-start.6 = (bf16[5,64,128]{2,1,0:T(8,128)(2,1)S(1)}, bf16[5,64,128]{2,1,0:T(8,128)(2,1)S(1)}, u32[]{:S(2)}, u32[]{:S(2)}) collective-permute-start(bf16[5,64,128]{2,1,0:T(8,128)(2,1)S(1)} %get-tuple-element.74), channel_id=1, source_target_pairs={{0,1},{1,0},{2,3},{3,2},{4,5},{5,4},{6,7},{7,6},{8,9},{9,8},{10,11... | collective-permute-start | bytes 245768 | tf_op jit(solution)/shard_map/ppermute | solution.py:311
  20.1 0.9 %shard_map.117.out_before = bf16[1024,128]{1,0:T(8,128)(2,1)} custom-call(bf16[128,640]{1,0:T(8,128)(2,1)S(1)} %get-tuple-element.67.act), custom_call_target="tpu_custom_call" | custom-call | bytes 1048576 | tf_op jit(solution)/shard_map/pallas_call | solution.py:416
  21.0 0.6 %shard_map.119 = (bf16[128,384]{1,0:T(8,128)(2,1)S(1)}, bf16[160,384]{1,0:T(8,128)(2,1)S(1)}, bf16[128,384]{1,0:T(8,128)(2,1)S(1)}, f32[3,64,128]{2,1,0:T(8,128)S(1)}, bf16[3,64,128]{2,1,0:T(8,128)(2,1)S(1)}) custom-call(f32[128,128]{1,0:T(8,128)S(1)} %get-tuple-element.54.bias_ref, bf16[128,128]{1,0:T(8,128)(2,1)S(1)} %copy-done, ...), custom_call_target="tpu_custom_call" | custom-call | flops 25165824 | bytes 1048576 | tf_op jit(solution)/shard_map/pallas_call | solution.py:407
  21.7 0.6 %collective-permute-start.5 = (bf16[3,64,128]{2,1,0:T(8,128)(2,1)S(1)}, bf16[3,64,128]{2,1,0:T(8,128)(2,1)S(1)}, u32[]{:S(2)}, u32[]{:S(2)}) collective-permute-start(bf16[3,64,128]{2,1,0:T(8,128)(2,1)S(1)} %get-tuple-element.72), channel_id=1, source_target_pairs={{0,1},{1,0},{2,3},{3,2},{4,5},{5,4},{6,7},{7,6},{8,9},{9,8},{10,11... | collective-permute-start | bytes 147464 | tf_op jit(solution)/shard_map/ppermute | solution.py:311
  22.5 1.0 %collective-permute-start.10 = (bf16[80,128]{1,0:T(8,128)(2,1)S(1)}, bf16[80,128]{1,0:T(8,128)(2,1)S(1)}, u32[]{:S(2)}, u32[]{:S(2)}) collective-permute-start(bf16[80,128]{1,0:T(8,128)(2,1)S(1)} %get-tuple-element.84.refs_0_), channel_id=1, source_target_pairs={{0,4},{2,6},{4,0},{6,2},{8,12},{10,14},{12,8},{14,10},{16,20},{18,... | collective-permute-start | bytes 61448 | tf_op jit(solution)/shard_map/ppermute | solution.py:311
  23.5 1.7 %collective-permute-start.11 = (bf16[80,128]{1,0:T(8,128)(2,1)S(1)}, bf16[80,128]{1,0:T(8,128)(2,1)S(1)}, u32[]{:S(2)}, u32[]{:S(2)}) collective-permute-start(bf16[80,128]{1,0:T(8,128)(2,1)S(1)} %get-tuple-element.85), channel_id=1, source_target_pairs={{0,6},{2,4},{4,2},{6,0},{8,14},{10,12},{12,10},{14,8},{16,22},{18,... | collective-permute-start | bytes 61448 | tf_op jit(solution)/shard_map/ppermute | solution.py:311
  25.2 0.7 %collective-permute-done.5.refs_1_ = bf16[3,64,128]{2,1,0:T(8,128)(2,1)S(1)} collective-permute-done((bf16[3,64,128]{2,1,0:T(8,128)(2,1)S(1)}, bf16[3,64,128]{2,1,0:T(8,128)(2,1)S(1)}, u32[]{:S(2)}, u32[]{:S(2)}) %collective-permute-start.5) | collective-permute-done | bytes 49184 | tf_op jit(solution)/shard_map/ppermute | solution.py:311
  25.9 2.0 %collective-permute-start.8 = (bf16[8,64,128]{2,1,0:T(8,128)(2,1)S(1)}, bf16[8,64,128]{2,1,0:T(8,128)(2,1)S(1)}, u32[]{:S(2)}, u32[]{:S(2)}) collective-permute-start(bf16[8,64,128]{2,1,0:T(8,128)(2,1)S(1)} %shard_map.120.g), channel_id=1, source_target_pairs={{0,28},{2,30},{4,0},{6,2},{8,4},{10,6},{12,8},{14,10},{16,12},{18,... | collective-permute-start | bytes 393224 | tf_op jit(solution)/shard_map/ppermute | solution.py:311
  28.2 1.0 %collective-permute-start.14 = (bf16[80,128]{1,0:T(8,128)(2,1)S(1)}, bf16[80,128]{1,0:T(8,128)(2,1)S(1)}, u32[]{:S(2)}, u32[]{:S(2)}) collective-permute-start(bf16[80,128]{1,0:T(8,128)(2,1)S(1)} %shard_map.123.refs_0_), channel_id=1, source_target_pairs={{0,24},{2,26},{4,28},{6,30},{8,16},{10,18},{12,20},{14,22},{16,8},... | collective-permute-start | bytes 61448 | tf_op jit(solution)/shard_map/ppermute | solution.py:311
  29.1 1.5 %collective-permute-start.13 = (bf16[80,128]{1,0:T(8,128)(2,1)S(1)}, bf16[80,128]{1,0:T(8,128)(2,1)S(1)}, u32[]{:S(2)}, u32[]{:S(2)}) collective-permute-start(bf16[80,128]{1,0:T(8,128)(2,1)S(1)} %shard_map.123.refs_0_), channel_id=1, source_target_pairs={{0,16},{2,18},{4,20},{6,22},{8,24},{10,26},{12,28},{14,30},{16,0},... | collective-permute-start | bytes 61448 | tf_op jit(solution)/shard_map/ppermute | solution.py:311
  30.7 2.0 %collective-permute-start.12 = (bf16[80,128]{1,0:T(8,128)(2,1)S(1)}, bf16[80,128]{1,0:T(8,128)(2,1)S(1)}, u32[]{:S(2)}, u32[]{:S(2)}) collective-permute-start(bf16[80,128]{1,0:T(8,128)(2,1)S(1)} %shard_map.123.refs_0_), channel_id=1, source_target_pairs={{0,8},{2,10},{4,12},{6,14},{8,0},{10,2},{12,4},{14,6},{16,24},{18,... | collective-permute-start | bytes 61448 | tf_op jit(solution)/shard_map/ppermute | solution.py:311
  32.6 1.4 %shard_map.121 = (f32[9,64,128]{2,1,0:T(8,128)S(1)}, bf16[1024,128]{1,0:T(8,128)(2,1)}) custom-call(s32[1]{0:T(128)S(6)} %copy.14.count, s32[96]{0:T(128)S(1)} %get-tuple-element.51.index, bf16[24,128,128]{2,1,0:T(8,128)(2,1)S(1)} %get-tuple-element.53.tiles, bf16[8,64,128]{2,1,0:T(8,128)(2,1)S(1)} %shard_map.120.g, ...), custom_call_target="tpu_custom_call", output_to_operand_aliasing={{1}: (5, {})} | custom-call | flops 50331648 | bytes 1048576 | tf_op jit(solution)/shard_map/pallas_call | solution.py:446
  34.0 0.4 %collective-permute-done.14.refs_3_ = bf16[80,128]{1,0:T(8,128)(2,1)S(1)} collective-permute-done((bf16[80,128]{1,0:T(8,128)(2,1)S(1)}, bf16[80,128]{1,0:T(8,128)(2,1)S(1)}, u32[]{:S(2)}, u32[]{:S(2)}) %collective-permute-start.14) | collective-permute-done | bytes 20512 | tf_op jit(solution)/shard_map/ppermute | solution.py:311
  34.7 0.9 %shard_map.125 = (f32[9,64,128]{2,1,0:T(8,128)S(1)}, f32[9,64,128]{2,1,0:T(8,128)S(1)}) custom-call(s32[1]{0:T(128)S(6)} %copy.14.count, s32[96]{0:T(128)S(1)} %get-tuple-element.51.index, bf16[24,128,128]{2,1,0:T(8,128)(2,1)S(1)} %get-tuple-element.58.tiles2, bf16[24,128,128]{2,1,0:T(8,128)(2,1)S(1)} %get-tuple-element.59.tiles3, ...), custom_call_target="tpu_custom_call" | custom-call | flops 100663296 | bytes 1048576 | tf_op jit(solution)/shard_map/pallas_call | solution.py:459
  36.1 1.6 %shard_map.126 = (bf16[64,1024]{1,0:T(8,128)(2,1)}, f32[128,128]{1,0:T(8,128)}, f32[1,128]{1,0:T(1,128)}) custom-call(s32[1]{0:T(128)S(6)} %copy.14.count, s32[96]{0:T(128)S(1)} %get-tuple-element.51.index, bf16[24,128,128]{2,1,0:T(8,128)(2,1)S(1)} %get-tuple-element.78.tiles1, bf16[592,128]{1,0:T(8,128)(2,1)S(1)} %shard_map.124.sent, ...), custom_call_target="tpu_custom_call" | custom-call | flops 50331648 | bytes 1048576 | tf_op jit(solution)/shard_map/pallas_call | solution.py:462
  (28 shorter events, 1.7 us)
Async XLA Ops:
  0.6 10.7 %copy-start = (bf16[128,128]{1,0:T(8,128)(2,1)S(1)}, bf16[128,128]{1,0:T(8,128)(2,1)}, u32[]{:S(2)}) copy-start(bf16[128,128]{1,0:T(8,128)(2,1)} %w_ref.5) | copy-start | bytes 98308
  0.6 10.7 %copy-start.1 = (f32[128]{0:T(128)S(1)}, f32[128]{0:T(128)}, u32[]{:S(2)}) copy-start(f32[128]{0:T(128)} %param.10) | copy-start | bytes 1540
  3.7 1.9 %collective-permute-start = (bf16[8,128,128]{2,1,0:T(8,128)(2,1)S(1)}, bf16[8,128,128]{2,1,0:T(8,128)(2,1)S(1)}, u32[]{:S(2)}, u32[]{:S(2)}) collective-permute-start(bf16[8,128,128]{2,1,0:T(8,128)(2,1)S(1)} %get-tuple-element.61), channel_id=1, source_target_pairs={{0,2},{2,0},{4,6},{6,4},{8,10},{10,8},{12,14},{14,12},{16,18},{18,... | collective-permute-start | bytes 786440 | tf_op jit(solution)/shard_map/ppermute | solution.py:311
  5.6 8.0 %collective-permute-start.1 = (bf16[5,128,128]{2,1,0:T(8,128)(2,1)S(1)}, bf16[5,128,128]{2,1,0:T(8,128)(2,1)S(1)}, u32[]{:S(2)}, u32[]{:S(2)}) collective-permute-start(bf16[5,128,128]{2,1,0:T(8,128)(2,1)S(1)} %get-tuple-element.65), channel_id=1, source_target_pairs={{0,2},{2,8},{4,6},{6,12},{8,10},{10,16},{12,14},{14,20},{16,18},{1... | collective-permute-start | bytes 491528 | tf_op jit(solution)/shard_map/ppermute | solution.py:311
  5.9 11.5 %collective-permute-start.2 = (bf16[5,128,128]{2,1,0:T(8,128)(2,1)S(1)}, bf16[5,128,128]{2,1,0:T(8,128)(2,1)S(1)}, u32[]{:S(2)}, u32[]{:S(2)}) collective-permute-start(bf16[5,128,128]{2,1,0:T(8,128)(2,1)S(1)} %get-tuple-element.66), channel_id=1, source_target_pairs={{0,4},{2,6},{4,8},{6,10},{8,12},{10,14},{12,16},{14,18},{16,20},{1... | collective-permute-start | bytes 491528 | tf_op jit(solution)/shard_map/ppermute | solution.py:311
  8.7 12.3 %collective-permute-start.3 = (bf16[3,128,128]{2,1,0:T(8,128)(2,1)S(1)}, bf16[3,128,128]{2,1,0:T(8,128)(2,1)S(1)}, u32[]{:S(2)}, u32[]{:S(2)}) collective-permute-start(bf16[3,128,128]{2,1,0:T(8,128)(2,1)S(1)} %get-tuple-element.69), channel_id=1, source_target_pairs={{0,2},{2,8},{4,6},{6,12},{8,10},{10,16},{12,14},{14,20},{16,18},{1... | collective-permute-start | bytes 294920 | tf_op jit(solution)/shard_map/ppermute | solution.py:311
  9.8 11.2 %collective-permute-start.4 = (bf16[3,128,128]{2,1,0:T(8,128)(2,1)S(1)}, bf16[3,128,128]{2,1,0:T(8,128)(2,1)S(1)}, u32[]{:S(2)}, u32[]{:S(2)}) collective-permute-start(bf16[3,128,128]{2,1,0:T(8,128)(2,1)S(1)} %get-tuple-element.70), channel_id=1, source_target_pairs={{0,4},{2,6},{4,8},{6,10},{8,12},{10,14},{12,16},{14,18},{16,20},{1... | collective-permute-start | bytes 294920 | tf_op jit(solution)/shard_map/ppermute | solution.py:311
  18.5 7.4 %collective-permute-start.6 = (bf16[5,64,128]{2,1,0:T(8,128)(2,1)S(1)}, bf16[5,64,128]{2,1,0:T(8,128)(2,1)S(1)}, u32[]{:S(2)}, u32[]{:S(2)}) collective-permute-start(bf16[5,64,128]{2,1,0:T(8,128)(2,1)S(1)} %get-tuple-element.74), channel_id=1, source_target_pairs={{0,1},{1,0},{2,3},{3,2},{4,5},{5,4},{6,7},{7,6},{8,9},{9,8},{10,11... | collective-permute-start | bytes 245768 | tf_op jit(solution)/shard_map/ppermute | solution.py:311
  21.7 4.2 %collective-permute-start.5 = (bf16[3,64,128]{2,1,0:T(8,128)(2,1)S(1)}, bf16[3,64,128]{2,1,0:T(8,128)(2,1)S(1)}, u32[]{:S(2)}, u32[]{:S(2)}) collective-permute-start(bf16[3,64,128]{2,1,0:T(8,128)(2,1)S(1)} %get-tuple-element.72), channel_id=1, source_target_pairs={{0,1},{1,0},{2,3},{3,2},{4,5},{5,4},{6,7},{7,6},{8,9},{9,8},{10,11... | collective-permute-start | bytes 147464 | tf_op jit(solution)/shard_map/ppermute | solution.py:311
  22.5 5.6 %collective-permute-start.10 = (bf16[80,128]{1,0:T(8,128)(2,1)S(1)}, bf16[80,128]{1,0:T(8,128)(2,1)S(1)}, u32[]{:S(2)}, u32[]{:S(2)}) collective-permute-start(bf16[80,128]{1,0:T(8,128)(2,1)S(1)} %get-tuple-element.84.refs_0_), channel_id=1, source_target_pairs={{0,4},{2,6},{4,0},{6,2},{8,12},{10,14},{12,8},{14,10},{16,20},{18,... | collective-permute-start | bytes 61448 | tf_op jit(solution)/shard_map/ppermute | solution.py:311
  23.5 4.7 %collective-permute-start.11 = (bf16[80,128]{1,0:T(8,128)(2,1)S(1)}, bf16[80,128]{1,0:T(8,128)(2,1)S(1)}, u32[]{:S(2)}, u32[]{:S(2)}) collective-permute-start(bf16[80,128]{1,0:T(8,128)(2,1)S(1)} %get-tuple-element.85), channel_id=1, source_target_pairs={{0,6},{2,4},{4,2},{6,0},{8,14},{10,12},{12,10},{14,8},{16,22},{18,... | collective-permute-start | bytes 61448 | tf_op jit(solution)/shard_map/ppermute | solution.py:311
  25.2 3.0 %collective-permute-start.9 = (bf16[80,128]{1,0:T(8,128)(2,1)S(1)}, bf16[80,128]{1,0:T(8,128)(2,1)S(1)}, u32[]{:S(2)}, u32[]{:S(2)}) collective-permute-start(bf16[80,128]{1,0:T(8,128)(2,1)S(1)} %get-tuple-element.85), channel_id=1, source_target_pairs={{0,2},{2,0},{4,6},{6,4},{8,10},{10,8},{12,14},{14,12},{16,18},{18,... | collective-permute-start | bytes 61448 | tf_op jit(solution)/shard_map/ppermute | solution.py:311
  25.9 8.8 %collective-permute-start.8 = (bf16[8,64,128]{2,1,0:T(8,128)(2,1)S(1)}, bf16[8,64,128]{2,1,0:T(8,128)(2,1)S(1)}, u32[]{:S(2)}, u32[]{:S(2)}) collective-permute-start(bf16[8,64,128]{2,1,0:T(8,128)(2,1)S(1)} %shard_map.120.g), channel_id=1, source_target_pairs={{0,28},{2,30},{4,0},{6,2},{8,4},{10,6},{12,8},{14,10},{16,12},{18,... | collective-permute-start | bytes 393224 | tf_op jit(solution)/shard_map/ppermute | solution.py:311
  27.9 6.8 %collective-permute-start.7 = (bf16[8,64,128]{2,1,0:T(8,128)(2,1)S(1)}, bf16[8,64,128]{2,1,0:T(8,128)(2,1)S(1)}, u32[]{:S(2)}, u32[]{:S(2)}) collective-permute-start(bf16[8,64,128]{2,1,0:T(8,128)(2,1)S(1)} %shard_map.120.g), channel_id=1, source_target_pairs={{0,26},{2,0},{4,30},{6,4},{8,2},{10,8},{12,6},{14,12},{16,10},{18,... | collective-permute-start | bytes 393224 | tf_op jit(solution)/shard_map/ppermute | solution.py:311
  28.2 6.3 %collective-permute-start.14 = (bf16[80,128]{1,0:T(8,128)(2,1)S(1)}, bf16[80,128]{1,0:T(8,128)(2,1)S(1)}, u32[]{:S(2)}, u32[]{:S(2)}) collective-permute-start(bf16[80,128]{1,0:T(8,128)(2,1)S(1)} %shard_map.123.refs_0_), channel_id=1, source_target_pairs={{0,24},{2,26},{4,28},{6,30},{8,16},{10,18},{12,20},{14,22},{16,8},... | collective-permute-start | bytes 61448 | tf_op jit(solution)/shard_map/ppermute | solution.py:311
  29.1 5.3 %collective-permute-start.13 = (bf16[80,128]{1,0:T(8,128)(2,1)S(1)}, bf16[80,128]{1,0:T(8,128)(2,1)S(1)}, u32[]{:S(2)}, u32[]{:S(2)}) collective-permute-start(bf16[80,128]{1,0:T(8,128)(2,1)S(1)} %shard_map.123.refs_0_), channel_id=1, source_target_pairs={{0,16},{2,18},{4,20},{6,22},{8,24},{10,26},{12,28},{14,30},{16,0},... | collective-permute-start | bytes 61448 | tf_op jit(solution)/shard_map/ppermute | solution.py:311
  30.7 3.9 %collective-permute-start.12 = (bf16[80,128]{1,0:T(8,128)(2,1)S(1)}, bf16[80,128]{1,0:T(8,128)(2,1)S(1)}, u32[]{:S(2)}, u32[]{:S(2)}) collective-permute-start(bf16[80,128]{1,0:T(8,128)(2,1)S(1)} %shard_map.123.refs_0_), channel_id=1, source_target_pairs={{0,8},{2,10},{4,12},{6,14},{8,0},{10,2},{12,4},{14,6},{16,24},{18,... | collective-permute-start | bytes 61448 | tf_op jit(solution)/shard_map/ppermute | solution.py:311
  34.7 1.4 %collective-permute-start.15 = (bf16[592,128]{1,0:T(8,128)(2,1)S(1)}, bf16[592,128]{1,0:T(8,128)(2,1)S(1)}, u32[]{:S(2)}, u32[]{:S(2)}) collective-permute-start(bf16[592,128]{1,0:T(8,128)(2,1)S(1)} %shard_map.124.sent), channel_id=1, source_target_pairs={{0,2},{2,0},{4,6},{6,4},{8,10},{10,8},{12,14},{14,12},{16,18},{18,... | collective-permute-start | bytes 454664 | tf_op jit(solution)/shard_map/ppermute | solution.py:311

commit v8 on v6

--- a/solution.py
+++ b/solution.py
@@ -376,8 +376,8 @@
         2 * flops,
     )(*index, xt, tiles2, tiles3)
     chip = call(functools.partial(sum_kernel, 2, 0), [half_x] * cut, [VMEM] * 2, [VMEM] * cut)(acc2, swap)
-    chip = lax.optimization_barrier((*chip, *direct[1:]))
-    direct, chip = [direct[0], *chip[cut:]], chip[:cut]
+    chip = lax.optimization_barrier((*chip, *direct))
+    direct, chip = chip[cut:], chip[:cut]
     chip = [moved(c, "dom", lambda i: i + 2) for c in chip]
     acc0, tiles0, bias_t, w_t, og_t = call(
         forward_own_kernel,
@@ -396,7 +396,7 @@
     direct = [moved(d, "dom", lambda i: i + 1 + 2 * (i % 2)) for d in direct]
     h_list = []
     for first, c, d in zip(starts, chip, direct):
-        (h,) = call(functools.partial(sum_kernel, 3, first), [half_x], [VMEM] * 3, [VMEM])(acc0, d, c)
+        (h,) = call(functools.partial(sum_kernel, 3, first), [half_x], [VMEM] * 3, [VMEM])(acc0, c, d)
         h_list.append(h)
     acts, hts, grads, g_list = [], [], [], []
     for first, h in zip(starts, h_list):

time: 37.1 us -> 38.3 us (1.032)
  starting transfers between devices: 18.3 us -> 21.1 us
  waiting for transfers between devices: 5.04 us -> 3.15 us
    ppermute x16, starting transfers between devices: 18.3 us -> 21.1 us  [moved(): return lax.ppermute(block, axis, [(i, target(i) % n) for i in range(n)])]
    ppermute x16, waiting for transfers between devices: 5.04 us -> 3.15 us  [moved(): return lax.ppermute(block, axis, [(i, target(i) % n) for i in range(n)])]
  transfers between devices with their start and end apart: 16 -> 16, of which waited for: 6 -> 5; matrix products, arithmetic and copies ran while one was open for 0% -> 0% of each run, Pallas kernels for 22% -> 21%
where the time goes in v8:
time: 38.3 us; the launch traced here: 37.8 us
  starting transfers between devices  21.1 us (55%)
  Pallas kernels  12.1 us (32%)
  waiting for transfers between devices  3.15 us (8%)
  between operations  1.44 us (4%)
    ppermute x16, starting transfers between devices, moved(): return lax.ppermute(block, axis, [(i, target(i) % n) for i in range(n)])  21.1 us
    ppermute x16, waiting for transfers between devices, moved(): return lax.ppermute(block, axis, [(i, target(i) % n) for i in range(n)])  3.15 us
    pallas_call x1, Pallas kernels, shards(): call(forward_swap_kernel, [plane, plane, plane, piece_x, piece_x, slots],...  2.35 us
    pallas_call x1, Pallas kernels, shards(): call(forward_own_kernel, [totals_x, plane, jax.ShapeDtypeStruct((hid, BLO...  2.25 us
    pallas_call x2, Pallas kernels, shards(): call(functools.partial(middle_kernel, parts, first), [half_rows, half_col...  1.62 us
    pallas_call x1, Pallas kernels, shards(): call(backward_last_kernel, [jax.ShapeDtypeStruct((width, nodes), BF16), j...  1.58 us
    pallas_call x1, Pallas kernels, shards(): call(backward_own_kernel, [totals, rows], [SMEM] * 2 + [VMEM] * (2 + cut)...  1.5 us
    pallas_call x1, Pallas kernels, shards(): call(forward_send_kernel, [totals_x] + [half_x] * cut, [SMEM] * 2 + [VMEM...  1.33 us
  transfers between devices with their start and end apart: 16, of which 5 were waited for; matrix products, arithmetic and copies ran while one was open for 0% of the time, Pallas kernels for 21%

profile of v8, /device:TPU:0, one launch (start us, length us, event | category | flops | bytes accessed | tf_op | source)
XLA Modules:
  0.0 37.8 jit_solution(7064559437619785254)
XLA Ops:
  1.3 2.3 %shard_map.111 = (bf16[24,128,128]{2,1,0:T(8,128)(2,1)S(1)}, bf16[24,128,128]{2,1,0:T(8,128)(2,1)S(1)}, bf16[24,128,128]{2,1,0:T(8,128)(2,1)S(1)}, bf16[8,128,12...) custom-call(s32[1]{0:T(128)S(6)} %copy.12.count, s32[96]{0:T(128)} %src_hbm.1, s32[96]{0:T(128)} %dst_hbm.1, ...), custom_call_target="tpu_custom_call" | custom-call | flops 50331648 | bytes 1048576 | tf_op jit(solution)/shard_map/pallas_call | solution.py:347
  3.7 0.5 %collective-permute-start = (bf16[8,128,128]{2,1,0:T(8,128)(2,1)S(1)}, bf16[8,128,128]{2,1,0:T(8,128)(2,1)S(1)}, u32[]{:S(2)}, u32[]{:S(2)}) collective-permute-start(bf16[8,128,128]{2,1,0:T(8,128)(2,1)S(1)} %get-tuple-element.60), channel_id=1, source_target_pairs={{0,2},{2,0},{4,6},{6,4},{8,10},{10,8},{12,14},{14,12},{16,18},{18,... | collective-permute-start | bytes 786440 | tf_op jit(solution)/shard_map/ppermute | solution.py:307
  4.2 1.3 %shard_map.113 = (f32[9,128,128]{2,1,0:T(8,128)S(1)}, bf16[4,128,128]{2,1,0:T(8,128)(2,1)S(1)}, bf16[4,128,128]{2,1,0:T(8,128)(2,1)S(1)}) custom-call(s32[1]{0:T(128)S(6)} %copy.12.count, s32[96]{0:T(128)S(1)} %get-tuple-element.50.index, bf16[8,128,128]{2,1,0:T(8,128)(2,1)S(1)} %get-tuple-element.51.xt, bf16[24,128,128]{2,1,0:T(8,128)(2,1)S(1)} %get-tuple-element.57.tiles2, ...), custom_call_target="tpu_custom_call" | custom-call | flops 100663296 | bytes 1048576 | tf_op jit(solution)/shard_map/pallas_call | solution.py:370
  5.6 3.6 %collective-permute-start.4 = (bf16[4,128,128]{2,1,0:T(8,128)(2,1)S(1)}, bf16[4,128,128]{2,1,0:T(8,128)(2,1)S(1)}, u32[]{:S(2)}, u32[]{:S(2)}) collective-permute-start(bf16[4,128,128]{2,1,0:T(8,128)(2,1)S(1)} %get-tuple-element.69), channel_id=1, source_target_pairs={{0,4},{2,6},{4,8},{6,10},{8,12},{10,14},{12,16},{14,18},{16,20},{1... | collective-permute-start | bytes 393224 | tf_op jit(solution)/shard_map/ppermute | solution.py:307
  9.3 1.3 %collective-permute-start.1 = (bf16[4,128,128]{2,1,0:T(8,128)(2,1)S(1)}, bf16[4,128,128]{2,1,0:T(8,128)(2,1)S(1)}, u32[]{:S(2)}, u32[]{:S(2)}) collective-permute-start(bf16[4,128,128]{2,1,0:T(8,128)(2,1)S(1)} %get-tuple-element.65), channel_id=1, source_target_pairs={{0,4},{2,6},{4,8},{6,10},{8,12},{10,14},{12,16},{14,18},{16,20},{1... | collective-permute-start | bytes 393224 | tf_op jit(solution)/shard_map/ppermute | solution.py:307
  10.6 0.7 %collective-permute-start.2 = (bf16[4,128,128]{2,1,0:T(8,128)(2,1)S(1)}, bf16[4,128,128]{2,1,0:T(8,128)(2,1)S(1)}, u32[]{:S(2)}, u32[]{:S(2)}) collective-permute-start(bf16[4,128,128]{2,1,0:T(8,128)(2,1)S(1)} %get-tuple-element.66), channel_id=1, source_target_pairs={{0,2},{2,8},{4,6},{6,12},{8,10},{10,16},{12,14},{14,20},{16,18},{1... | collective-permute-start | bytes 393224 | tf_op jit(solution)/shard_map/ppermute | solution.py:307
  11.3 2.3 %shard_map.112 = (f32[9,128,128]{2,1,0:T(8,128)S(1)}, bf16[24,128,128]{2,1,0:T(8,128)(2,1)S(1)}, f32[128,128]{1,0:T(8,128)S(1)}, bf16[128,128]{1,0:T(8,128)(2,1)S(1)}, bf16[128,1024]{1,0:T(8,128)(2,1)S(1)}) custom-call(s32[1]{0:T(128)S(6)} %copy.12.count, s32[96]{0:T(128)S(1)} %get-tuple-element.50.index, bf16[8,128,128]{2,1,0:T(8,128)(2,1)S(1)} %get-tuple-element.51.xt, ...), custom_call_target="tpu_custom_call" | custom-call | flops 50331648 | bytes 1048576 | tf_op jit(solution)/shard_map/pallas_call | solution.py:382
  13.6 2.1 %collective-permute-done.4.refs_1_ = bf16[4,128,128]{2,1,0:T(8,128)(2,1)S(1)} collective-permute-done((bf16[4,128,128]{2,1,0:T(8,128)(2,1)S(1)}, bf16[4,128,128]{2,1,0:T(8,128)(2,1)S(1)}, u32[]{:S(2)}, u32[]{:S(2)}) %collective-permute-start.4) | collective-permute-done | bytes 131104 | tf_op jit(solution)/shard_map/ppermute | solution.py:307
  15.7 0.8 %shard_map.118 = (bf16[128,512]{1,0:T(8,128)(2,1)S(1)}, bf16[160,512]{1,0:T(8,128)(2,1)S(1)}, bf16[128,512]{1,0:T(8,128)(2,1)S(1)}, f32[4,64,128]{2,1,0:T(8,128)S(1)}, bf16[4,64,128]{2,1,0:T(8,128)(2,1)S(1)}) custom-call(f32[128,128]{1,0:T(8,128)S(1)} %get-tuple-element.53.bias_ref, bf16[128,128]{1,0:T(8,128)(2,1)S(1)} %copy-done, ...), custom_call_target="tpu_custom_call" | custom-call | flops 33554432 | bytes 1048576 | tf_op jit(solution)/shard_map/pallas_call | solution.py:403
  16.5 1.7 %collective-permute-start.6 = (bf16[4,64,128]{2,1,0:T(8,128)(2,1)S(1)}, bf16[4,64,128]{2,1,0:T(8,128)(2,1)S(1)}, u32[]{:S(2)}, u32[]{:S(2)}) collective-permute-start(bf16[4,64,128]{2,1,0:T(8,128)(2,1)S(1)} %get-tuple-element.72), channel_id=1, source_target_pairs={{0,1},{1,0},{2,3},{3,2},{4,5},{5,4},{6,7},{7,6},{8,9},{9,8},{10,11... | collective-permute-start | bytes 196616 | tf_op jit(solution)/shard_map/ppermute | solution.py:307
  18.2 0.2 collective-permute-done.1.refs_1_
  18.5 0.8 %shard_map.116 = (bf16[128,512]{1,0:T(8,128)(2,1)S(1)}, bf16[160,512]{1,0:T(8,128)(2,1)S(1)}, bf16[128,512]{1,0:T(8,128)(2,1)S(1)}, f32[4,64,128]{2,1,0:T(8,128)S(1)}, bf16[4,64,128]{2,1,0:T(8,128)(2,1)S(1)}) custom-call(f32[128,128]{1,0:T(8,128)S(1)} %get-tuple-element.53.bias_ref, bf16[128,128]{1,0:T(8,128)(2,1)S(1)} %copy-done, ...), custom_call_target="tpu_custom_call" | custom-call | flops 33554432 | bytes 1048576 | tf_op jit(solution)/shard_map/pallas_call | solution.py:403
  19.3 1.7 %collective-permute-start.3 = (bf16[4,64,128]{2,1,0:T(8,128)(2,1)S(1)}, bf16[4,64,128]{2,1,0:T(8,128)(2,1)S(1)}, u32[]{:S(2)}, u32[]{:S(2)}) collective-permute-start(bf16[4,64,128]{2,1,0:T(8,128)(2,1)S(1)} %get-tuple-element.68), channel_id=1, source_target_pairs={{0,1},{1,0},{2,3},{3,2},{4,5},{5,4},{6,7},{7,6},{8,9},{9,8},{10,11... | collective-permute-start | bytes 196616 | tf_op jit(solution)/shard_map/ppermute | solution.py:307
  21.0 0.2 shard_map.121
  21.3 3.0 %collective-permute-start.10 = (bf16[80,128]{1,0:T(8,128)(2,1)S(1)}, bf16[80,128]{1,0:T(8,128)(2,1)S(1)}, u32[]{:S(2)}, u32[]{:S(2)}) collective-permute-start(bf16[80,128]{1,0:T(8,128)(2,1)S(1)} %get-tuple-element.82.refs_0_), channel_id=1, source_target_pairs={{0,4},{2,6},{4,0},{6,2},{8,12},{10,14},{12,8},{14,10},{16,20},{18,... | collective-permute-start | bytes 61448 | tf_op jit(solution)/shard_map/ppermute | solution.py:307
  24.5 3.8 %collective-permute-start.8 = (bf16[8,64,128]{2,1,0:T(8,128)(2,1)S(1)}, bf16[8,64,128]{2,1,0:T(8,128)(2,1)S(1)}, u32[]{:S(2)}, u32[]{:S(2)}) collective-permute-start(bf16[8,64,128]{2,1,0:T(8,128)(2,1)S(1)} %shard_map.119.g), channel_id=1, source_target_pairs={{0,28},{2,30},{4,0},{6,2},{8,4},{10,6},{12,8},{14,10},{16,12},{18,... | collective-permute-start | bytes 393224 | tf_op jit(solution)/shard_map/ppermute | solution.py:307
  28.3 1.3 %collective-permute-start.14 = (bf16[80,128]{1,0:T(8,128)(2,1)S(1)}, bf16[80,128]{1,0:T(8,128)(2,1)S(1)}, u32[]{:S(2)}, u32[]{:S(2)}) collective-permute-start(bf16[80,128]{1,0:T(8,128)(2,1)S(1)} %shard_map.122.refs_0_), channel_id=1, source_target_pairs={{0,24},{2,26},{4,28},{6,30},{8,16},{10,18},{12,20},{14,22},{16,8},... | collective-permute-start | bytes 61448 | tf_op jit(solution)/shard_map/ppermute | solution.py:307
  29.6 1.3 %collective-permute-start.13 = (bf16[80,128]{1,0:T(8,128)(2,1)S(1)}, bf16[80,128]{1,0:T(8,128)(2,1)S(1)}, u32[]{:S(2)}, u32[]{:S(2)}) collective-permute-start(bf16[80,128]{1,0:T(8,128)(2,1)S(1)} %shard_map.122.refs_0_), channel_id=1, source_target_pairs={{0,16},{2,18},{4,20},{6,22},{8,24},{10,26},{12,28},{14,30},{16,0},... | collective-permute-start | bytes 61448 | tf_op jit(solution)/shard_map/ppermute | solution.py:307
  30.9 1.9 %collective-permute-start.12 = (bf16[80,128]{1,0:T(8,128)(2,1)S(1)}, bf16[80,128]{1,0:T(8,128)(2,1)S(1)}, u32[]{:S(2)}, u32[]{:S(2)}) collective-permute-start(bf16[80,128]{1,0:T(8,128)(2,1)S(1)} %shard_map.122.refs_0_), channel_id=1, source_target_pairs={{0,8},{2,10},{4,12},{6,14},{8,0},{10,2},{12,4},{14,6},{16,24},{18,... | collective-permute-start | bytes 61448 | tf_op jit(solution)/shard_map/ppermute | solution.py:307
  32.8 1.5 %shard_map.120 = (f32[9,64,128]{2,1,0:T(8,128)S(1)}, bf16[1024,128]{1,0:T(8,128)(2,1)}) custom-call(s32[1]{0:T(128)S(6)} %copy.12.count, s32[96]{0:T(128)S(1)} %get-tuple-element.50.index, bf16[24,128,128]{2,1,0:T(8,128)(2,1)S(1)} %get-tuple-element.52.tiles, bf16[8,64,128]{2,1,0:T(8,128)(2,1)S(1)} %shard_map.119.g, ...), custom_call_target="tpu_custom_call" | custom-call | flops 50331648 | bytes 1048576 | tf_op jit(solution)/shard_map/pallas_call | solution.py:433
  34.3 0.2 collective-permute-done.13.refs_2_
  34.9 0.9 %shard_map.124 = (f32[9,64,128]{2,1,0:T(8,128)S(1)}, f32[9,64,128]{2,1,0:T(8,128)S(1)}) custom-call(s32[1]{0:T(128)S(6)} %copy.12.count, s32[96]{0:T(128)S(1)} %get-tuple-element.50.index, bf16[24,128,128]{2,1,0:T(8,128)(2,1)S(1)} %get-tuple-element.57.tiles2, bf16[24,128,128]{2,1,0:T(8,128)(2,1)S(1)} %get-tuple-element.58.tiles3, ...), custom_call_target="tpu_custom_call" | custom-call | flops 100663296 | bytes 1048576 | tf_op jit(solution)/shard_map/pallas_call | solution.py:445
  35.8 0.4 %collective-permute-done.15.got = bf16[592,128]{1,0:T(8,128)(2,1)S(1)} collective-permute-done((bf16[592,128]{1,0:T(8,128)(2,1)S(1)}, bf16[592,128]{1,0:T(8,128)(2,1)S(1)}, u32[]{:S(2)}, u32[]{:S(2)}) %collective-permute-start.15) | collective-permute-done | bytes 151584 | tf_op jit(solution)/shard_map/ppermute | solution.py:307
  36.2 1.6 %shard_map.125 = (bf16[64,1024]{1,0:T(8,128)(2,1)}, f32[128,128]{1,0:T(8,128)}, f32[1,128]{1,0:T(1,128)}) custom-call(s32[1]{0:T(128)S(6)} %copy.12.count, s32[96]{0:T(128)S(1)} %get-tuple-element.50.index, bf16[24,128,128]{2,1,0:T(8,128)(2,1)S(1)} %get-tuple-element.76.tiles1, bf16[592,128]{1,0:T(8,128)(2,1)S(1)} %shard_map.123.sent, ...), custom_call_target="tpu_custom_call" | custom-call | flops 50331648 | bytes 1048576 | tf_op jit(solution)/shard_map/pallas_call | solution.py:448
  (27 shorter events, 0.7 us)
Async XLA Ops:
  0.6 10.7 %copy-start = (bf16[128,128]{1,0:T(8,128)(2,1)S(1)}, bf16[128,128]{1,0:T(8,128)(2,1)}, u32[]{:S(2)}) copy-start(bf16[128,128]{1,0:T(8,128)(2,1)} %w_ref.5) | copy-start | bytes 98308
  0.6 10.7 %copy-start.1 = (f32[128]{0:T(128)S(1)}, f32[128]{0:T(128)}, u32[]{:S(2)}) copy-start(f32[128]{0:T(128)} %param.10) | copy-start | bytes 1540
  3.7 1.9 %collective-permute-start = (bf16[8,128,128]{2,1,0:T(8,128)(2,1)S(1)}, bf16[8,128,128]{2,1,0:T(8,128)(2,1)S(1)}, u32[]{:S(2)}, u32[]{:S(2)}) collective-permute-start(bf16[8,128,128]{2,1,0:T(8,128)(2,1)S(1)} %get-tuple-element.60), channel_id=1, source_target_pairs={{0,2},{2,0},{4,6},{6,4},{8,10},{10,8},{12,14},{14,12},{16,18},{18,... | collective-permute-start | bytes 786440 | tf_op jit(solution)/shard_map/ppermute | solution.py:307
  5.6 10.0 %collective-permute-start.4 = (bf16[4,128,128]{2,1,0:T(8,128)(2,1)S(1)}, bf16[4,128,128]{2,1,0:T(8,128)(2,1)S(1)}, u32[]{:S(2)}, u32[]{:S(2)}) collective-permute-start(bf16[4,128,128]{2,1,0:T(8,128)(2,1)S(1)} %get-tuple-element.69), channel_id=1, source_target_pairs={{0,4},{2,6},{4,8},{6,10},{8,12},{10,14},{12,16},{14,18},{16,20},{1... | collective-permute-start | bytes 393224 | tf_op jit(solution)/shard_map/ppermute | solution.py:307
  9.3 6.4 %collective-permute-start.5 = (bf16[4,128,128]{2,1,0:T(8,128)(2,1)S(1)}, bf16[4,128,128]{2,1,0:T(8,128)(2,1)S(1)}, u32[]{:S(2)}, u32[]{:S(2)}) collective-permute-start(bf16[4,128,128]{2,1,0:T(8,128)(2,1)S(1)} %get-tuple-element.70), channel_id=1, source_target_pairs={{0,2},{2,8},{4,6},{6,12},{8,10},{10,16},{12,14},{14,20},{16,18},{1... | collective-permute-start | bytes 393224 | tf_op jit(solution)/shard_map/ppermute | solution.py:307
  9.3 9.2 %collective-permute-start.1 = (bf16[4,128,128]{2,1,0:T(8,128)(2,1)S(1)}, bf16[4,128,128]{2,1,0:T(8,128)(2,1)S(1)}, u32[]{:S(2)}, u32[]{:S(2)}) collective-permute-start(bf16[4,128,128]{2,1,0:T(8,128)(2,1)S(1)} %get-tuple-element.65), channel_id=1, source_target_pairs={{0,4},{2,6},{4,8},{6,10},{8,12},{10,14},{12,16},{14,18},{16,20},{1... | collective-permute-start | bytes 393224 | tf_op jit(solution)/shard_map/ppermute | solution.py:307
  10.6 7.9 %collective-permute-start.2 = (bf16[4,128,128]{2,1,0:T(8,128)(2,1)S(1)}, bf16[4,128,128]{2,1,0:T(8,128)(2,1)S(1)}, u32[]{:S(2)}, u32[]{:S(2)}) collective-permute-start(bf16[4,128,128]{2,1,0:T(8,128)(2,1)S(1)} %get-tuple-element.66), channel_id=1, source_target_pairs={{0,2},{2,8},{4,6},{6,12},{8,10},{10,16},{12,14},{14,20},{16,18},{1... | collective-permute-start | bytes 393224 | tf_op jit(solution)/shard_map/ppermute | solution.py:307
  16.5 7.9 %collective-permute-start.6 = (bf16[4,64,128]{2,1,0:T(8,128)(2,1)S(1)}, bf16[4,64,128]{2,1,0:T(8,128)(2,1)S(1)}, u32[]{:S(2)}, u32[]{:S(2)}) collective-permute-start(bf16[4,64,128]{2,1,0:T(8,128)(2,1)S(1)} %get-tuple-element.72), channel_id=1, source_target_pairs={{0,1},{1,0},{2,3},{3,2},{4,5},{5,4},{6,7},{7,6},{8,9},{9,8},{10,11... | collective-permute-start | bytes 196616 | tf_op jit(solution)/shard_map/ppermute | solution.py:307
  19.3 5.1 %collective-permute-start.3 = (bf16[4,64,128]{2,1,0:T(8,128)(2,1)S(1)}, bf16[4,64,128]{2,1,0:T(8,128)(2,1)S(1)}, u32[]{:S(2)}, u32[]{:S(2)}) collective-permute-start(bf16[4,64,128]{2,1,0:T(8,128)(2,1)S(1)} %get-tuple-element.68), channel_id=1, source_target_pairs={{0,1},{1,0},{2,3},{3,2},{4,5},{5,4},{6,7},{7,6},{8,9},{9,8},{10,11... | collective-permute-start | bytes 196616 | tf_op jit(solution)/shard_map/ppermute | solution.py:307
  21.3 7.0 %collective-permute-start.10 = (bf16[80,128]{1,0:T(8,128)(2,1)S(1)}, bf16[80,128]{1,0:T(8,128)(2,1)S(1)}, u32[]{:S(2)}, u32[]{:S(2)}) collective-permute-start(bf16[80,128]{1,0:T(8,128)(2,1)S(1)} %get-tuple-element.82.refs_0_), channel_id=1, source_target_pairs={{0,4},{2,6},{4,0},{6,2},{8,12},{10,14},{12,8},{14,10},{16,20},{18,... | collective-permute-start | bytes 61448 | tf_op jit(solution)/shard_map/ppermute | solution.py:307
  24.3 4.1 %collective-permute-start.11 = (bf16[80,128]{1,0:T(8,128)(2,1)S(1)}, bf16[80,128]{1,0:T(8,128)(2,1)S(1)}, u32[]{:S(2)}, u32[]{:S(2)}) collective-permute-start(bf16[80,128]{1,0:T(8,128)(2,1)S(1)} %get-tuple-element.83), channel_id=1, source_target_pairs={{0,6},{2,4},{4,2},{6,0},{8,14},{10,12},{12,10},{14,8},{16,22},{18,... | collective-permute-start | bytes 61448 | tf_op jit(solution)/shard_map/ppermute | solution.py:307
  24.3 4.1 %collective-permute-start.9 = (bf16[80,128]{1,0:T(8,128)(2,1)S(1)}, bf16[80,128]{1,0:T(8,128)(2,1)S(1)}, u32[]{:S(2)}, u32[]{:S(2)}) collective-permute-start(bf16[80,128]{1,0:T(8,128)(2,1)S(1)} %get-tuple-element.83), channel_id=1, source_target_pairs={{0,2},{2,0},{4,6},{6,4},{8,10},{10,8},{12,14},{14,12},{16,18},{18,... | collective-permute-start | bytes 61448 | tf_op jit(solution)/shard_map/ppermute | solution.py:307
  24.5 10.3 %collective-permute-start.8 = (bf16[8,64,128]{2,1,0:T(8,128)(2,1)S(1)}, bf16[8,64,128]{2,1,0:T(8,128)(2,1)S(1)}, u32[]{:S(2)}, u32[]{:S(2)}) collective-permute-start(bf16[8,64,128]{2,1,0:T(8,128)(2,1)S(1)} %shard_map.119.g), channel_id=1, source_target_pairs={{0,28},{2,30},{4,0},{6,2},{8,4},{10,6},{12,8},{14,10},{16,12},{18,... | collective-permute-start | bytes 393224 | tf_op jit(solution)/shard_map/ppermute | solution.py:307
  28.3 6.4 %collective-permute-start.7 = (bf16[8,64,128]{2,1,0:T(8,128)(2,1)S(1)}, bf16[8,64,128]{2,1,0:T(8,128)(2,1)S(1)}, u32[]{:S(2)}, u32[]{:S(2)}) collective-permute-start(bf16[8,64,128]{2,1,0:T(8,128)(2,1)S(1)} %shard_map.119.g), channel_id=1, source_target_pairs={{0,26},{2,0},{4,30},{6,4},{8,2},{10,8},{12,6},{14,12},{16,10},{18,... | collective-permute-start | bytes 393224 | tf_op jit(solution)/shard_map/ppermute | solution.py:307
  28.3 6.0 %collective-permute-start.14 = (bf16[80,128]{1,0:T(8,128)(2,1)S(1)}, bf16[80,128]{1,0:T(8,128)(2,1)S(1)}, u32[]{:S(2)}, u32[]{:S(2)}) collective-permute-start(bf16[80,128]{1,0:T(8,128)(2,1)S(1)} %shard_map.122.refs_0_), channel_id=1, source_target_pairs={{0,24},{2,26},{4,28},{6,30},{8,16},{10,18},{12,20},{14,22},{16,8},... | collective-permute-start | bytes 61448 | tf_op jit(solution)/shard_map/ppermute | solution.py:307
  29.6 4.9 %collective-permute-start.13 = (bf16[80,128]{1,0:T(8,128)(2,1)S(1)}, bf16[80,128]{1,0:T(8,128)(2,1)S(1)}, u32[]{:S(2)}, u32[]{:S(2)}) collective-permute-start(bf16[80,128]{1,0:T(8,128)(2,1)S(1)} %shard_map.122.refs_0_), channel_id=1, source_target_pairs={{0,16},{2,18},{4,20},{6,22},{8,24},{10,26},{12,28},{14,30},{16,0},... | collective-permute-start | bytes 61448 | tf_op jit(solution)/shard_map/ppermute | solution.py:307
  30.9 3.8 %collective-permute-start.12 = (bf16[80,128]{1,0:T(8,128)(2,1)S(1)}, bf16[80,128]{1,0:T(8,128)(2,1)S(1)}, u32[]{:S(2)}, u32[]{:S(2)}) collective-permute-start(bf16[80,128]{1,0:T(8,128)(2,1)S(1)} %shard_map.122.refs_0_), channel_id=1, source_target_pairs={{0,8},{2,10},{4,12},{6,14},{8,0},{10,2},{12,4},{14,6},{16,24},{18,... | collective-permute-start | bytes 61448 | tf_op jit(solution)/shard_map/ppermute | solution.py:307
  34.8 1.4 %collective-permute-start.15 = (bf16[592,128]{1,0:T(8,128)(2,1)S(1)}, bf16[592,128]{1,0:T(8,128)(2,1)S(1)}, u32[]{:S(2)}, u32[]{:S(2)}) collective-permute-start(bf16[592,128]{1,0:T(8,128)(2,1)S(1)} %shard_map.123.sent), channel_id=1, source_target_pairs={{0,2},{2,0},{4,6},{6,4},{8,10},{10,8},{12,14},{14,12},{16,18},{18,... | collective-permute-start | bytes 454664 | tf_op jit(solution)/shard_map/ppermute | solution.py:307

commit v9 on v6

--- a/solution.py
+++ b/solution.py
@@ -396,7 +396,7 @@
     direct = [moved(d, "dom", lambda i: i + 1 + 2 * (i % 2)) for d in direct]
     h_list = []
     for first, c, d in zip(starts, chip, direct):
-        (h,) = call(functools.partial(sum_kernel, 3, first), [half_x], [VMEM] * 3, [VMEM])(acc0, d, c)
+        (h,) = call(functools.partial(sum_kernel, 3, first), [half_x], [VMEM] * 3, [VMEM])(acc0, c, d)
         h_list.append(h)
     acts, hts, grads, g_list = [], [], [], []
     for first, h in zip(starts, h_list):

time: 37.1 us -> 36.9 us (level)
  waiting for transfers between devices: 5.04 us -> 4.43 us
  starting transfers between devices: 18.3 us -> 18.9 us
    ppermute x16, starting transfers between devices: 18.3 us -> 18.9 us  [moved(): return lax.ppermute(block, axis, [(i, target(i) % n) for i in range(n)])]
    ppermute x16, waiting for transfers between devices: 5.04 us -> 4.43 us  [moved(): return lax.ppermute(block, axis, [(i, target(i) % n) for i in range(n)])]
where the time goes in v9:
time: 36.9 us; the launch traced here: 36.8 us
  starting transfers between devices  18.9 us (51%)
  Pallas kernels  12.1 us (33%)
  waiting for transfers between devices  4.43 us (12%)
  between operations  1.43 us (4%)
    ppermute x16, starting transfers between devices, moved(): return lax.ppermute(block, axis, [(i, target(i) % n) for i in range(n)])  18.9 us
    ppermute x16, waiting for transfers between devices, moved(): return lax.ppermute(block, axis, [(i, target(i) % n) for i in range(n)])  4.43 us
    pallas_call x1, Pallas kernels, shards(): call(forward_swap_kernel, [plane, plane, plane, piece_x, piece_x, slots],...  2.35 us
    pallas_call x1, Pallas kernels, shards(): call(forward_own_kernel, [totals_x, plane, jax.ShapeDtypeStruct((hid, BLO...  2.25 us
    pallas_call x2, Pallas kernels, shards(): call(functools.partial(middle_kernel, parts, first), [half_rows, half_col...  1.62 us
    pallas_call x1, Pallas kernels, shards(): call(backward_last_kernel, [jax.ShapeDtypeStruct((width, nodes), BF16), j...  1.58 us
    pallas_call x1, Pallas kernels, shards(): call(backward_own_kernel, [totals, rows], [SMEM] * 2 + [VMEM] * (2 + cut)...  1.5 us
    pallas_call x1, Pallas kernels, shards(): call(forward_send_kernel, [totals_x] + [half_x] * cut, [SMEM] * 2 + [VMEM...  1.33 us
  transfers between devices with their start and end apart: 16, of which 6 were waited for; matrix products, arithmetic and copies ran while one was open for 0% of the time, Pallas kernels for 22%

profile of v9, /device:TPU:0, one launch (start us, length us, event | category | flops | bytes accessed | tf_op | source)
XLA Modules:
  0.0 36.8 jit_solution(364439919642244547)
XLA Ops:
  1.3 2.3 %shard_map.111 = (bf16[24,128,128]{2,1,0:T(8,128)(2,1)S(1)}, bf16[24,128,128]{2,1,0:T(8,128)(2,1)S(1)}, bf16[24,128,128]{2,1,0:T(8,128)(2,1)S(1)}, bf16[8,128,12...) custom-call(s32[1]{0:T(128)S(6)} %copy.12.count, s32[96]{0:T(128)} %src_hbm.1, s32[96]{0:T(128)} %dst_hbm.1, ...), custom_call_target="tpu_custom_call" | custom-call | flops 50331648 | bytes 1048576 | tf_op jit(solution)/shard_map/pallas_call | solution.py:347
  3.7 0.5 %collective-permute-start = (bf16[8,128,128]{2,1,0:T(8,128)(2,1)S(1)}, bf16[8,128,128]{2,1,0:T(8,128)(2,1)S(1)}, u32[]{:S(2)}, u32[]{:S(2)}) collective-permute-start(bf16[8,128,128]{2,1,0:T(8,128)(2,1)S(1)} %get-tuple-element.59), channel_id=1, source_target_pairs={{0,2},{2,0},{4,6},{6,4},{8,10},{10,8},{12,14},{14,12},{16,18},{18,... | collective-permute-start | bytes 786440 | tf_op jit(solution)/shard_map/ppermute | solution.py:307
  4.2 1.3 %shard_map.113 = (f32[9,128,128]{2,1,0:T(8,128)S(1)}, bf16[4,128,128]{2,1,0:T(8,128)(2,1)S(1)}, bf16[4,128,128]{2,1,0:T(8,128)(2,1)S(1)}) custom-call(s32[1]{0:T(128)S(6)} %copy.12.count, s32[96]{0:T(128)S(1)} %get-tuple-element.49.index, bf16[8,128,128]{2,1,0:T(8,128)(2,1)S(1)} %get-tuple-element.50.xt, bf16[24,128,128]{2,1,0:T(8,128)(2,1)S(1)} %get-tuple-element.56.tiles2, ...), custom_call_target="tpu_custom_call" | custom-call | flops 100663296 | bytes 1048576 | tf_op jit(solution)/shard_map/pallas_call | solution.py:370
  5.6 2.8 %collective-permute-start.4 = (bf16[4,128,128]{2,1,0:T(8,128)(2,1)S(1)}, bf16[4,128,128]{2,1,0:T(8,128)(2,1)S(1)}, u32[]{:S(2)}, u32[]{:S(2)}) collective-permute-start(bf16[4,128,128]{2,1,0:T(8,128)(2,1)S(1)} %get-tuple-element.67), channel_id=1, source_target_pairs={{0,4},{2,6},{4,8},{6,10},{8,12},{10,14},{12,16},{14,18},{16,20},{1... | collective-permute-start | bytes 393224 | tf_op jit(solution)/shard_map/ppermute | solution.py:307
  8.4 0.7 %collective-permute-start.5 = (bf16[4,128,128]{2,1,0:T(8,128)(2,1)S(1)}, bf16[4,128,128]{2,1,0:T(8,128)(2,1)S(1)}, u32[]{:S(2)}, u32[]{:S(2)}) collective-permute-start(bf16[4,128,128]{2,1,0:T(8,128)(2,1)S(1)} %get-tuple-element.68), channel_id=1, source_target_pairs={{0,2},{2,8},{4,6},{6,12},{8,10},{10,16},{12,14},{14,20},{16,18},{1... | collective-permute-start | bytes 393224 | tf_op jit(solution)/shard_map/ppermute | solution.py:307
  9.1 1.0 %collective-permute-start.2 = (bf16[4,128,128]{2,1,0:T(8,128)(2,1)S(1)}, bf16[4,128,128]{2,1,0:T(8,128)(2,1)S(1)}, u32[]{:S(2)}, u32[]{:S(2)}) collective-permute-start(bf16[4,128,128]{2,1,0:T(8,128)(2,1)S(1)} %get-tuple-element.64), channel_id=1, source_target_pairs={{0,2},{2,8},{4,6},{6,12},{8,10},{10,16},{12,14},{14,20},{16,18},{1... | collective-permute-start | bytes 393224 | tf_op jit(solution)/shard_map/ppermute | solution.py:307
  10.1 1.5 %collective-permute-start.1 = (bf16[4,128,128]{2,1,0:T(8,128)(2,1)S(1)}, bf16[4,128,128]{2,1,0:T(8,128)(2,1)S(1)}, u32[]{:S(2)}, u32[]{:S(2)}) collective-permute-start(bf16[4,128,128]{2,1,0:T(8,128)(2,1)S(1)} %get-tuple-element.63), channel_id=1, source_target_pairs={{0,4},{2,6},{4,8},{6,10},{8,12},{10,14},{12,16},{14,18},{16,20},{1... | collective-permute-start | bytes 393224 | tf_op jit(solution)/shard_map/ppermute | solution.py:307
  11.6 2.3 %shard_map.112 = (f32[9,128,128]{2,1,0:T(8,128)S(1)}, bf16[24,128,128]{2,1,0:T(8,128)(2,1)S(1)}, f32[128,128]{1,0:T(8,128)S(1)}, bf16[128,128]{1,0:T(8,128)(2,1)S(1)}, bf16[128,1024]{1,0:T(8,128)(2,1)S(1)}) custom-call(s32[1]{0:T(128)S(6)} %copy.12.count, s32[96]{0:T(128)S(1)} %get-tuple-element.49.index, bf16[8,128,128]{2,1,0:T(8,128)(2,1)S(1)} %get-tuple-element.50.xt, ...), custom_call_target="tpu_custom_call" | custom-call | flops 50331648 | bytes 1048576 | tf_op jit(solution)/shard_map/pallas_call | solution.py:382
  13.8 2.8 %collective-permute-done.4.refs_1_ = bf16[4,128,128]{2,1,0:T(8,128)(2,1)S(1)} collective-permute-done((bf16[4,128,128]{2,1,0:T(8,128)(2,1)S(1)}, bf16[4,128,128]{2,1,0:T(8,128)(2,1)S(1)}, u32[]{:S(2)}, u32[]{:S(2)}) %collective-permute-start.4) | collective-permute-done | bytes 131104 | tf_op jit(solution)/shard_map/ppermute | solution.py:307
  16.7 0.8 %shard_map.118 = (bf16[128,512]{1,0:T(8,128)(2,1)S(1)}, bf16[160,512]{1,0:T(8,128)(2,1)S(1)}, bf16[128,512]{1,0:T(8,128)(2,1)S(1)}, f32[4,64,128]{2,1,0:T(8,128)S(1)}, bf16[4,64,128]{2,1,0:T(8,128)(2,1)S(1)}) custom-call(f32[128,128]{1,0:T(8,128)S(1)} %get-tuple-element.52.bias_ref, bf16[128,128]{1,0:T(8,128)(2,1)S(1)} %copy-done, ...), custom_call_target="tpu_custom_call" | custom-call | flops 33554432 | bytes 1048576 | tf_op jit(solution)/shard_map/pallas_call | solution.py:403
  17.5 1.5 %collective-permute-start.6 = (bf16[4,64,128]{2,1,0:T(8,128)(2,1)S(1)}, bf16[4,64,128]{2,1,0:T(8,128)(2,1)S(1)}, u32[]{:S(2)}, u32[]{:S(2)}) collective-permute-start(bf16[4,64,128]{2,1,0:T(8,128)(2,1)S(1)} %get-tuple-element.70), channel_id=1, source_target_pairs={{0,1},{1,0},{2,3},{3,2},{4,5},{5,4},{6,7},{7,6},{8,9},{9,8},{10,11... | collective-permute-start | bytes 196616 | tf_op jit(solution)/shard_map/ppermute | solution.py:307
  19.5 0.8 %shard_map.116 = (bf16[128,512]{1,0:T(8,128)(2,1)S(1)}, bf16[160,512]{1,0:T(8,128)(2,1)S(1)}, bf16[128,512]{1,0:T(8,128)(2,1)S(1)}, f32[4,64,128]{2,1,0:T(8,128)S(1)}, bf16[4,64,128]{2,1,0:T(8,128)(2,1)S(1)}) custom-call(f32[128,128]{1,0:T(8,128)S(1)} %get-tuple-element.52.bias_ref, bf16[128,128]{1,0:T(8,128)(2,1)S(1)} %copy-done, ...), custom_call_target="tpu_custom_call" | custom-call | flops 33554432 | bytes 1048576 | tf_op jit(solution)/shard_map/pallas_call | solution.py:403
  20.3 1.5 %collective-permute-start.3 = (bf16[4,64,128]{2,1,0:T(8,128)(2,1)S(1)}, bf16[4,64,128]{2,1,0:T(8,128)(2,1)S(1)}, u32[]{:S(2)}, u32[]{:S(2)}) collective-permute-start(bf16[4,64,128]{2,1,0:T(8,128)(2,1)S(1)} %get-tuple-element.66), channel_id=1, source_target_pairs={{0,1},{1,0},{2,3},{3,2},{4,5},{5,4},{6,7},{7,6},{8,9},{9,8},{10,11... | collective-permute-start | bytes 196616 | tf_op jit(solution)/shard_map/ppermute | solution.py:307
  22.1 1.2 %collective-permute-start.10 = (bf16[80,128]{1,0:T(8,128)(2,1)S(1)}, bf16[80,128]{1,0:T(8,128)(2,1)S(1)}, u32[]{:S(2)}, u32[]{:S(2)}) collective-permute-start(bf16[80,128]{1,0:T(8,128)(2,1)S(1)} %get-tuple-element.80.refs_0_), channel_id=1, source_target_pairs={{0,4},{2,6},{4,0},{6,2},{8,12},{10,14},{12,8},{14,10},{16,20},{18,... | collective-permute-start | bytes 61448 | tf_op jit(solution)/shard_map/ppermute | solution.py:307
  23.3 1.7 %collective-permute-start.11 = (bf16[80,128]{1,0:T(8,128)(2,1)S(1)}, bf16[80,128]{1,0:T(8,128)(2,1)S(1)}, u32[]{:S(2)}, u32[]{:S(2)}) collective-permute-start(bf16[80,128]{1,0:T(8,128)(2,1)S(1)} %get-tuple-element.81), channel_id=1, source_target_pairs={{0,6},{2,4},{4,2},{6,0},{8,14},{10,12},{12,10},{14,8},{16,22},{18,... | collective-permute-start | bytes 61448 | tf_op jit(solution)/shard_map/ppermute | solution.py:307
  25.0 1.9 %collective-permute-start.8 = (bf16[8,64,128]{2,1,0:T(8,128)(2,1)S(1)}, bf16[8,64,128]{2,1,0:T(8,128)(2,1)S(1)}, u32[]{:S(2)}, u32[]{:S(2)}) collective-permute-start(bf16[8,64,128]{2,1,0:T(8,128)(2,1)S(1)} %shard_map.119.g), channel_id=1, source_target_pairs={{0,28},{2,30},{4,0},{6,2},{8,4},{10,6},{12,8},{14,10},{16,12},{18,... | collective-permute-start | bytes 393224 | tf_op jit(solution)/shard_map/ppermute | solution.py:307
  27.0 1.5 %collective-permute-start.14 = (bf16[80,128]{1,0:T(8,128)(2,1)S(1)}, bf16[80,128]{1,0:T(8,128)(2,1)S(1)}, u32[]{:S(2)}, u32[]{:S(2)}) collective-permute-start(bf16[80,128]{1,0:T(8,128)(2,1)S(1)} %shard_map.122.refs_0_), channel_id=1, source_target_pairs={{0,24},{2,26},{4,28},{6,30},{8,16},{10,18},{12,20},{14,22},{16,8},... | collective-permute-start | bytes 61448 | tf_op jit(solution)/shard_map/ppermute | solution.py:307
  28.4 1.5 %collective-permute-start.13 = (bf16[80,128]{1,0:T(8,128)(2,1)S(1)}, bf16[80,128]{1,0:T(8,128)(2,1)S(1)}, u32[]{:S(2)}, u32[]{:S(2)}) collective-permute-start(bf16[80,128]{1,0:T(8,128)(2,1)S(1)} %shard_map.122.refs_0_), channel_id=1, source_target_pairs={{0,16},{2,18},{4,20},{6,22},{8,24},{10,26},{12,28},{14,30},{16,0},... | collective-permute-start | bytes 61448 | tf_op jit(solution)/shard_map/ppermute | solution.py:307
  30.0 1.5 %collective-permute-start.12 = (bf16[80,128]{1,0:T(8,128)(2,1)S(1)}, bf16[80,128]{1,0:T(8,128)(2,1)S(1)}, u32[]{:S(2)}, u32[]{:S(2)}) collective-permute-start(bf16[80,128]{1,0:T(8,128)(2,1)S(1)} %shard_map.122.refs_0_), channel_id=1, source_target_pairs={{0,8},{2,10},{4,12},{6,14},{8,0},{10,2},{12,4},{14,6},{16,24},{18,... | collective-permute-start | bytes 61448 | tf_op jit(solution)/shard_map/ppermute | solution.py:307
  31.4 1.5 %shard_map.120 = (f32[9,64,128]{2,1,0:T(8,128)S(1)}, bf16[1024,128]{1,0:T(8,128)(2,1)}) custom-call(s32[1]{0:T(128)S(6)} %copy.12.count, s32[96]{0:T(128)S(1)} %get-tuple-element.49.index, bf16[24,128,128]{2,1,0:T(8,128)(2,1)S(1)} %get-tuple-element.51.tiles, bf16[8,64,128]{2,1,0:T(8,128)(2,1)S(1)} %shard_map.119.g, ...), custom_call_target="tpu_custom_call" | custom-call | flops 50331648 | bytes 1048576 | tf_op jit(solution)/shard_map/pallas_call | solution.py:433
  33.0 0.4 %collective-permute-done.13.refs_2_ = bf16[80,128]{1,0:T(8,128)(2,1)S(1)} collective-permute-done((bf16[80,128]{1,0:T(8,128)(2,1)S(1)}, bf16[80,128]{1,0:T(8,128)(2,1)S(1)}, u32[]{:S(2)}, u32[]{:S(2)}) %collective-permute-start.13) | collective-permute-done | bytes 20512 | tf_op jit(solution)/shard_map/ppermute | solution.py:307
  33.9 0.9 %shard_map.124 = (f32[9,64,128]{2,1,0:T(8,128)S(1)}, f32[9,64,128]{2,1,0:T(8,128)S(1)}) custom-call(s32[1]{0:T(128)S(6)} %copy.12.count, s32[96]{0:T(128)S(1)} %get-tuple-element.49.index, bf16[24,128,128]{2,1,0:T(8,128)(2,1)S(1)} %get-tuple-element.56.tiles2, bf16[24,128,128]{2,1,0:T(8,128)(2,1)S(1)} %get-tuple-element.57.tiles3, ...), custom_call_target="tpu_custom_call" | custom-call | flops 100663296 | bytes 1048576 | tf_op jit(solution)/shard_map/pallas_call | solution.py:445
  34.8 0.4 %collective-permute-done.15.got = bf16[592,128]{1,0:T(8,128)(2,1)S(1)} collective-permute-done((bf16[592,128]{1,0:T(8,128)(2,1)S(1)}, bf16[592,128]{1,0:T(8,128)(2,1)S(1)}, u32[]{:S(2)}, u32[]{:S(2)}) %collective-permute-start.15) | collective-permute-done | bytes 151584 | tf_op jit(solution)/shard_map/ppermute | solution.py:307
  35.2 1.6 %shard_map.125 = (bf16[64,1024]{1,0:T(8,128)(2,1)}, f32[128,128]{1,0:T(8,128)}, f32[1,128]{1,0:T(1,128)}) custom-call(s32[1]{0:T(128)S(6)} %copy.12.count, s32[96]{0:T(128)S(1)} %get-tuple-element.49.index, bf16[24,128,128]{2,1,0:T(8,128)(2,1)S(1)} %get-tuple-element.74.tiles1, bf16[592,128]{1,0:T(8,128)(2,1)S(1)} %shard_map.123.sent, ...), custom_call_target="tpu_custom_call" | custom-call | flops 50331648 | bytes 1048576 | tf_op jit(solution)/shard_map/pallas_call | solution.py:448
  (27 shorter events, 1.4 us)
Async XLA Ops:
  0.6 10.9 %copy-start = (bf16[128,128]{1,0:T(8,128)(2,1)S(1)}, bf16[128,128]{1,0:T(8,128)(2,1)}, u32[]{:S(2)}) copy-start(bf16[128,128]{1,0:T(8,128)(2,1)} %w_ref.5) | copy-start | bytes 98308
  0.6 10.9 %copy-start.1 = (f32[128]{0:T(128)S(1)}, f32[128]{0:T(128)}, u32[]{:S(2)}) copy-start(f32[128]{0:T(128)} %param.10) | copy-start | bytes 1540
  3.7 1.9 %collective-permute-start = (bf16[8,128,128]{2,1,0:T(8,128)(2,1)S(1)}, bf16[8,128,128]{2,1,0:T(8,128)(2,1)S(1)}, u32[]{:S(2)}, u32[]{:S(2)}) collective-permute-start(bf16[8,128,128]{2,1,0:T(8,128)(2,1)S(1)} %get-tuple-element.59), channel_id=1, source_target_pairs={{0,2},{2,0},{4,6},{6,4},{8,10},{10,8},{12,14},{14,12},{16,18},{18,... | collective-permute-start | bytes 786440 | tf_op jit(solution)/shard_map/ppermute | solution.py:307
  5.6 11.0 %collective-permute-start.4 = (bf16[4,128,128]{2,1,0:T(8,128)(2,1)S(1)}, bf16[4,128,128]{2,1,0:T(8,128)(2,1)S(1)}, u32[]{:S(2)}, u32[]{:S(2)}) collective-permute-start(bf16[4,128,128]{2,1,0:T(8,128)(2,1)S(1)} %get-tuple-element.67), channel_id=1, source_target_pairs={{0,4},{2,6},{4,8},{6,10},{8,12},{10,14},{12,16},{14,18},{16,20},{1... | collective-permute-start | bytes 393224 | tf_op jit(solution)/shard_map/ppermute | solution.py:307
  8.4 8.2 %collective-permute-start.5 = (bf16[4,128,128]{2,1,0:T(8,128)(2,1)S(1)}, bf16[4,128,128]{2,1,0:T(8,128)(2,1)S(1)}, u32[]{:S(2)}, u32[]{:S(2)}) collective-permute-start(bf16[4,128,128]{2,1,0:T(8,128)(2,1)S(1)} %get-tuple-element.68), channel_id=1, source_target_pairs={{0,2},{2,8},{4,6},{6,12},{8,10},{10,16},{12,14},{14,20},{16,18},{1... | collective-permute-start | bytes 393224 | tf_op jit(solution)/shard_map/ppermute | solution.py:307
  9.1 9.9 %collective-permute-start.2 = (bf16[4,128,128]{2,1,0:T(8,128)(2,1)S(1)}, bf16[4,128,128]{2,1,0:T(8,128)(2,1)S(1)}, u32[]{:S(2)}, u32[]{:S(2)}) collective-permute-start(bf16[4,128,128]{2,1,0:T(8,128)(2,1)S(1)} %get-tuple-element.64), channel_id=1, source_target_pairs={{0,2},{2,8},{4,6},{6,12},{8,10},{10,16},{12,14},{14,20},{16,18},{1... | collective-permute-start | bytes 393224 | tf_op jit(solution)/shard_map/ppermute | solution.py:307
  10.1 9.3 %collective-permute-start.1 = (bf16[4,128,128]{2,1,0:T(8,128)(2,1)S(1)}, bf16[4,128,128]{2,1,0:T(8,128)(2,1)S(1)}, u32[]{:S(2)}, u32[]{:S(2)}) collective-permute-start(bf16[4,128,128]{2,1,0:T(8,128)(2,1)S(1)} %get-tuple-element.63), channel_id=1, source_target_pairs={{0,4},{2,6},{4,8},{6,10},{8,12},{10,14},{12,16},{14,18},{16,20},{1... | collective-permute-start | bytes 393224 | tf_op jit(solution)/shard_map/ppermute | solution.py:307
  17.5 7.5 %collective-permute-start.6 = (bf16[4,64,128]{2,1,0:T(8,128)(2,1)S(1)}, bf16[4,64,128]{2,1,0:T(8,128)(2,1)S(1)}, u32[]{:S(2)}, u32[]{:S(2)}) collective-permute-start(bf16[4,64,128]{2,1,0:T(8,128)(2,1)S(1)} %get-tuple-element.70), channel_id=1, source_target_pairs={{0,1},{1,0},{2,3},{3,2},{4,5},{5,4},{6,7},{7,6},{8,9},{9,8},{10,11... | collective-permute-start | bytes 196616 | tf_op jit(solution)/shard_map/ppermute | solution.py:307
  20.3 4.7 %collective-permute-start.3 = (bf16[4,64,128]{2,1,0:T(8,128)(2,1)S(1)}, bf16[4,64,128]{2,1,0:T(8,128)(2,1)S(1)}, u32[]{:S(2)}, u32[]{:S(2)}) collective-permute-start(bf16[4,64,128]{2,1,0:T(8,128)(2,1)S(1)} %get-tuple-element.66), channel_id=1, source_target_pairs={{0,1},{1,0},{2,3},{3,2},{4,5},{5,4},{6,7},{7,6},{8,9},{9,8},{10,11... | collective-permute-start | bytes 196616 | tf_op jit(solution)/shard_map/ppermute | solution.py:307
  22.1 4.9 %collective-permute-start.10 = (bf16[80,128]{1,0:T(8,128)(2,1)S(1)}, bf16[80,128]{1,0:T(8,128)(2,1)S(1)}, u32[]{:S(2)}, u32[]{:S(2)}) collective-permute-start(bf16[80,128]{1,0:T(8,128)(2,1)S(1)} %get-tuple-element.80.refs_0_), channel_id=1, source_target_pairs={{0,4},{2,6},{4,0},{6,2},{8,12},{10,14},{12,8},{14,10},{16,20},{18,... | collective-permute-start | bytes 61448 | tf_op jit(solution)/shard_map/ppermute | solution.py:307
  23.3 3.7 %collective-permute-start.11 = (bf16[80,128]{1,0:T(8,128)(2,1)S(1)}, bf16[80,128]{1,0:T(8,128)(2,1)S(1)}, u32[]{:S(2)}, u32[]{:S(2)}) collective-permute-start(bf16[80,128]{1,0:T(8,128)(2,1)S(1)} %get-tuple-element.81), channel_id=1, source_target_pairs={{0,6},{2,4},{4,2},{6,0},{8,14},{10,12},{12,10},{14,8},{16,22},{18,... | collective-permute-start | bytes 61448 | tf_op jit(solution)/shard_map/ppermute | solution.py:307
  25.0 2.0 %collective-permute-start.9 = (bf16[80,128]{1,0:T(8,128)(2,1)S(1)}, bf16[80,128]{1,0:T(8,128)(2,1)S(1)}, u32[]{:S(2)}, u32[]{:S(2)}) collective-permute-start(bf16[80,128]{1,0:T(8,128)(2,1)S(1)} %get-tuple-element.81), channel_id=1, source_target_pairs={{0,2},{2,0},{4,6},{6,4},{8,10},{10,8},{12,14},{14,12},{16,18},{18,... | collective-permute-start | bytes 61448 | tf_op jit(solution)/shard_map/ppermute | solution.py:307
  25.0 8.7 %collective-permute-start.8 = (bf16[8,64,128]{2,1,0:T(8,128)(2,1)S(1)}, bf16[8,64,128]{2,1,0:T(8,128)(2,1)S(1)}, u32[]{:S(2)}, u32[]{:S(2)}) collective-permute-start(bf16[8,64,128]{2,1,0:T(8,128)(2,1)S(1)} %shard_map.119.g), channel_id=1, source_target_pairs={{0,28},{2,30},{4,0},{6,2},{8,4},{10,6},{12,8},{14,10},{16,12},{18,... | collective-permute-start | bytes 393224 | tf_op jit(solution)/shard_map/ppermute | solution.py:307
  26.9 6.9 %collective-permute-start.7 = (bf16[8,64,128]{2,1,0:T(8,128)(2,1)S(1)}, bf16[8,64,128]{2,1,0:T(8,128)(2,1)S(1)}, u32[]{:S(2)}, u32[]{:S(2)}) collective-permute-start(bf16[8,64,128]{2,1,0:T(8,128)(2,1)S(1)} %shard_map.119.g), channel_id=1, source_target_pairs={{0,26},{2,0},{4,30},{6,4},{8,2},{10,8},{12,6},{14,12},{16,10},{18,... | collective-permute-start | bytes 393224 | tf_op jit(solution)/shard_map/ppermute | solution.py:307
  27.0 6.0 %collective-permute-start.14 = (bf16[80,128]{1,0:T(8,128)(2,1)S(1)}, bf16[80,128]{1,0:T(8,128)(2,1)S(1)}, u32[]{:S(2)}, u32[]{:S(2)}) collective-permute-start(bf16[80,128]{1,0:T(8,128)(2,1)S(1)} %shard_map.122.refs_0_), channel_id=1, source_target_pairs={{0,24},{2,26},{4,28},{6,30},{8,16},{10,18},{12,20},{14,22},{16,8},... | collective-permute-start | bytes 61448 | tf_op jit(solution)/shard_map/ppermute | solution.py:307
  28.4 5.0 %collective-permute-start.13 = (bf16[80,128]{1,0:T(8,128)(2,1)S(1)}, bf16[80,128]{1,0:T(8,128)(2,1)S(1)}, u32[]{:S(2)}, u32[]{:S(2)}) collective-permute-start(bf16[80,128]{1,0:T(8,128)(2,1)S(1)} %shard_map.122.refs_0_), channel_id=1, source_target_pairs={{0,16},{2,18},{4,20},{6,22},{8,24},{10,26},{12,28},{14,30},{16,0},... | collective-permute-start | bytes 61448 | tf_op jit(solution)/shard_map/ppermute | solution.py:307
  30.0 3.8 %collective-permute-start.12 = (bf16[80,128]{1,0:T(8,128)(2,1)S(1)}, bf16[80,128]{1,0:T(8,128)(2,1)S(1)}, u32[]{:S(2)}, u32[]{:S(2)}) collective-permute-start(bf16[80,128]{1,0:T(8,128)(2,1)S(1)} %shard_map.122.refs_0_), channel_id=1, source_target_pairs={{0,8},{2,10},{4,12},{6,14},{8,0},{10,2},{12,4},{14,6},{16,24},{18,... | collective-permute-start | bytes 61448 | tf_op jit(solution)/shard_map/ppermute | solution.py:307
  33.8 1.4 %collective-permute-start.15 = (bf16[592,128]{1,0:T(8,128)(2,1)S(1)}, bf16[592,128]{1,0:T(8,128)(2,1)S(1)}, u32[]{:S(2)}, u32[]{:S(2)}) collective-permute-start(bf16[592,128]{1,0:T(8,128)(2,1)S(1)} %shard_map.123.sent), channel_id=1, source_target_pairs={{0,2},{2,0},{4,6},{6,4},{8,10},{10,8},{12,14},{14,12},{16,18},{18,... | collective-permute-start | bytes 454664 | tf_op jit(solution)/shard_map/ppermute | solution.py:307

commit v10 on v9

--- a/solution.py
+++ b/solution.py
@@ -438,6 +438,7 @@
         [pltpu.VMEM(rows.shape, BF16), pltpu.SemaphoreType.DMA((cut,))],
         flops,
     )(*index, tiles0, g, *acts)
+    wgs.reverse()
     g_direct, g_chip, back0, *wgs = lax.optimization_barrier((g_direct, g_chip, back0, *wgs))
     payload = jax.ShapeDtypeStruct((blocks * width + gradient.shape[0], BLOCK), BF16)
     (sent,) = call(swap_payload_kernel, [payload], [VMEM] * (1 + len(wgs)), [VMEM])(g_chip, *wgs)

time: 36.9 us -> 37.7 us (1.022)
  Pallas kernels: 12.1 us -> 14.1 us
  waiting for transfers between devices: 4.43 us -> 3.01 us
    ppermute x16, waiting for transfers between devices: 4.43 us -> 3.01 us  [moved(): return lax.ppermute(block, axis, [(i, target(i) % n) for i in range(n)])]
    pallas_call x1, Pallas kernels: 1.33 us -> 1.99 us  [shards(): call(forward_send_kernel, [totals_x] + [half_x] * cut, [SMEM] * 2 + [VMEM...]
    pallas_call x1, Pallas kernels: 2.25 us -> 2.66 us  [shards(): call(forward_own_kernel, [totals_x, plane, jax.ShapeDtypeStruct((hid, BLO...]
    pallas_call x1, Pallas kernels: 2.35 us -> 2.74 us  [shards(): call(forward_swap_kernel, [plane, plane, plane, piece_x, piece_x, slots],...]
  transfers between devices with their start and end apart: 16 -> 16, of which waited for: 6 -> 6; matrix products, arithmetic and copies ran while one was open for 0% -> 0% of each run, Pallas kernels for 22% -> 25%
where the time goes in v10:
time: 37.7 us; the launch traced here: 37.8 us
  starting transfers between devices  19.2 us (51%)
  Pallas kernels  14.1 us (37%)
  waiting for transfers between devices  3.01 us (8%)
  between operations  1.42 us (4%)
    ppermute x16, starting transfers between devices, moved(): return lax.ppermute(block, axis, [(i, target(i) % n) for i in range(n)])  19.2 us
    ppermute x16, waiting for transfers between devices, moved(): return lax.ppermute(block, axis, [(i, target(i) % n) for i in range(n)])  3.01 us
    pallas_call x1, Pallas kernels, shards(): call(forward_swap_kernel, [plane, plane, plane, piece_x, piece_x, slots],...  2.74 us
    pallas_call x1, Pallas kernels, shards(): call(forward_own_kernel, [totals_x, plane, jax.ShapeDtypeStruct((hid, BLO...  2.66 us
    pallas_call x1, Pallas kernels, shards(): call(forward_send_kernel, [totals_x] + [half_x] * cut, [SMEM] * 2 + [VMEM...  1.99 us
    pallas_call x1, Pallas kernels, shards(): call(backward_last_kernel, [jax.ShapeDtypeStruct((width, nodes), BF16), j...  1.82 us
    pallas_call x2, Pallas kernels, shards(): call(functools.partial(middle_kernel, parts, first), [half_rows, half_col...  1.62 us
    pallas_call x1, Pallas kernels, shards(): call(backward_own_kernel, [totals, rows], [SMEM] * 2 + [VMEM] * (2 + cut)...  1.5 us
  transfers between devices with their start and end apart: 16, of which 6 were waited for; matrix products, arithmetic and copies ran while one was open for 0% of the time, Pallas kernels for 25%

profile of v10, /device:TPU:0, one launch (start us, length us, event | category | flops | bytes accessed | tf_op | source)
XLA Modules:
  0.0 37.8 jit_solution(12136469037021714102)
XLA Ops:
  1.3 2.7 %shard_map.111 = (bf16[24,128,128]{2,1,0:T(8,128)(2,1)S(1)}, bf16[24,128,128]{2,1,0:T(8,128)(2,1)S(1)}, bf16[24,128,128]{2,1,0:T(8,128)(2,1)S(1)}, bf16[8,128,12...) custom-call(s32[1]{0:T(128)S(6)} %copy.12.count, s32[96]{0:T(128)} %src_hbm.1, s32[96]{0:T(128)} %dst_hbm.1, ...), custom_call_target="tpu_custom_call" | custom-call | flops 50331648 | bytes 1048576 | tf_op jit(solution)/shard_map/pallas_call | solution.py:347
  4.1 0.5 %collective-permute-start = (bf16[8,128,128]{2,1,0:T(8,128)(2,1)S(1)}, bf16[8,128,128]{2,1,0:T(8,128)(2,1)S(1)}, u32[]{:S(2)}, u32[]{:S(2)}) collective-permute-start(bf16[8,128,128]{2,1,0:T(8,128)(2,1)S(1)} %get-tuple-element.59), channel_id=1, source_target_pairs={{0,2},{2,0},{4,6},{6,4},{8,10},{10,8},{12,14},{14,12},{16,18},{18,... | collective-permute-start | bytes 786440 | tf_op jit(solution)/shard_map/ppermute | solution.py:307
  4.6 2.0 %shard_map.113 = (f32[9,128,128]{2,1,0:T(8,128)S(1)}, bf16[4,128,128]{2,1,0:T(8,128)(2,1)S(1)}, bf16[4,128,128]{2,1,0:T(8,128)(2,1)S(1)}) custom-call(s32[1]{0:T(128)S(6)} %copy.12.count, s32[96]{0:T(128)S(1)} %get-tuple-element.49.index, bf16[8,128,128]{2,1,0:T(8,128)(2,1)S(1)} %get-tuple-element.50.xt, bf16[24,128,128]{2,1,0:T(8,128)(2,1)S(1)} %get-tuple-element.56.tiles2, ...), custom_call_target="tpu_custom_call" | custom-call | flops 100663296 | bytes 1048576 | tf_op jit(solution)/shard_map/pallas_call | solution.py:370
  6.7 1.7 %collective-permute-start.4 = (bf16[4,128,128]{2,1,0:T(8,128)(2,1)S(1)}, bf16[4,128,128]{2,1,0:T(8,128)(2,1)S(1)}, u32[]{:S(2)}, u32[]{:S(2)}) collective-permute-start(bf16[4,128,128]{2,1,0:T(8,128)(2,1)S(1)} %get-tuple-element.67), channel_id=1, source_target_pairs={{0,4},{2,6},{4,8},{6,10},{8,12},{10,14},{12,16},{14,18},{16,20},{1... | collective-permute-start | bytes 393224 | tf_op jit(solution)/shard_map/ppermute | solution.py:307
  8.4 1.7 %collective-permute-start.2 = (bf16[4,128,128]{2,1,0:T(8,128)(2,1)S(1)}, bf16[4,128,128]{2,1,0:T(8,128)(2,1)S(1)}, u32[]{:S(2)}, u32[]{:S(2)}) collective-permute-start(bf16[4,128,128]{2,1,0:T(8,128)(2,1)S(1)} %get-tuple-element.64), channel_id=1, source_target_pairs={{0,2},{2,8},{4,6},{6,12},{8,10},{10,16},{12,14},{14,20},{16,18},{1... | collective-permute-start | bytes 393224 | tf_op jit(solution)/shard_map/ppermute | solution.py:307
  10.1 1.6 %collective-permute-start.1 = (bf16[4,128,128]{2,1,0:T(8,128)(2,1)S(1)}, bf16[4,128,128]{2,1,0:T(8,128)(2,1)S(1)}, u32[]{:S(2)}, u32[]{:S(2)}) collective-permute-start(bf16[4,128,128]{2,1,0:T(8,128)(2,1)S(1)} %get-tuple-element.63), channel_id=1, source_target_pairs={{0,4},{2,6},{4,8},{6,10},{8,12},{10,14},{12,16},{14,18},{16,20},{1... | collective-permute-start | bytes 393224 | tf_op jit(solution)/shard_map/ppermute | solution.py:307
  11.6 2.7 %shard_map.112 = (f32[9,128,128]{2,1,0:T(8,128)S(1)}, bf16[24,128,128]{2,1,0:T(8,128)(2,1)S(1)}, f32[128,128]{1,0:T(8,128)S(1)}, bf16[128,128]{1,0:T(8,128)(2,1)S(1)}, bf16[128,1024]{1,0:T(8,128)(2,1)S(1)}) custom-call(s32[1]{0:T(128)S(6)} %copy.12.count, s32[96]{0:T(128)S(1)} %get-tuple-element.49.index, bf16[8,128,128]{2,1,0:T(8,128)(2,1)S(1)} %get-tuple-element.50.xt, ...), custom_call_target="tpu_custom_call" | custom-call | flops 50331648 | bytes 1048576 | tf_op jit(solution)/shard_map/pallas_call | solution.py:382
  14.3 1.4 %collective-permute-done.4.refs_1_ = bf16[4,128,128]{2,1,0:T(8,128)(2,1)S(1)} collective-permute-done((bf16[4,128,128]{2,1,0:T(8,128)(2,1)S(1)}, bf16[4,128,128]{2,1,0:T(8,128)(2,1)S(1)}, u32[]{:S(2)}, u32[]{:S(2)}) %collective-permute-start.4) | collective-permute-done | bytes 131104 | tf_op jit(solution)/shard_map/ppermute | solution.py:307
  15.8 0.8 %shard_map.118 = (bf16[128,512]{1,0:T(8,128)(2,1)S(1)}, bf16[160,512]{1,0:T(8,128)(2,1)S(1)}, bf16[128,512]{1,0:T(8,128)(2,1)S(1)}, f32[4,64,128]{2,1,0:T(8,128)S(1)}, bf16[4,64,128]{2,1,0:T(8,128)(2,1)S(1)}) custom-call(f32[128,128]{1,0:T(8,128)S(1)} %get-tuple-element.52.bias_ref, bf16[128,128]{1,0:T(8,128)(2,1)S(1)} %copy-done, ...), custom_call_target="tpu_custom_call" | custom-call | flops 33554432 | bytes 1048576 | tf_op jit(solution)/shard_map/pallas_call | solution.py:403
  16.6 2.5 %collective-permute-start.6 = (bf16[4,64,128]{2,1,0:T(8,128)(2,1)S(1)}, bf16[4,64,128]{2,1,0:T(8,128)(2,1)S(1)}, u32[]{:S(2)}, u32[]{:S(2)}) collective-permute-start(bf16[4,64,128]{2,1,0:T(8,128)(2,1)S(1)} %get-tuple-element.70), channel_id=1, source_target_pairs={{0,1},{1,0},{2,3},{3,2},{4,5},{5,4},{6,7},{7,6},{8,9},{9,8},{10,11... | collective-permute-start | bytes 196616 | tf_op jit(solution)/shard_map/ppermute | solution.py:307
  19.2 0.8 %shard_map.116 = (bf16[128,512]{1,0:T(8,128)(2,1)S(1)}, bf16[160,512]{1,0:T(8,128)(2,1)S(1)}, bf16[128,512]{1,0:T(8,128)(2,1)S(1)}, f32[4,64,128]{2,1,0:T(8,128)S(1)}, bf16[4,64,128]{2,1,0:T(8,128)(2,1)S(1)}) custom-call(f32[128,128]{1,0:T(8,128)S(1)} %get-tuple-element.52.bias_ref, bf16[128,128]{1,0:T(8,128)(2,1)S(1)} %copy-done, ...), custom_call_target="tpu_custom_call" | custom-call | flops 33554432 | bytes 1048576 | tf_op jit(solution)/shard_map/pallas_call | solution.py:403
  20.1 1.9 %collective-permute-start.3 = (bf16[4,64,128]{2,1,0:T(8,128)(2,1)S(1)}, bf16[4,64,128]{2,1,0:T(8,128)(2,1)S(1)}, u32[]{:S(2)}, u32[]{:S(2)}) collective-permute-start(bf16[4,64,128]{2,1,0:T(8,128)(2,1)S(1)} %get-tuple-element.66), channel_id=1, source_target_pairs={{0,1},{1,0},{2,3},{3,2},{4,5},{5,4},{6,7},{7,6},{8,9},{9,8},{10,11... | collective-permute-start | bytes 196616 | tf_op jit(solution)/shard_map/ppermute | solution.py:307
  21.9 0.2 shard_map.121
  22.2 1.6 %collective-permute-start.10 = (bf16[80,128]{1,0:T(8,128)(2,1)S(1)}, bf16[80,128]{1,0:T(8,128)(2,1)S(1)}, u32[]{:S(2)}, u32[]{:S(2)}) collective-permute-start(bf16[80,128]{1,0:T(8,128)(2,1)S(1)} %get-tuple-element.80.refs_0_), channel_id=1, source_target_pairs={{0,4},{2,6},{4,0},{6,2},{8,12},{10,14},{12,8},{14,10},{16,20},{18,... | collective-permute-start | bytes 61448 | tf_op jit(solution)/shard_map/ppermute | solution.py:307
  23.8 1.7 %collective-permute-start.11 = (bf16[80,128]{1,0:T(8,128)(2,1)S(1)}, bf16[80,128]{1,0:T(8,128)(2,1)S(1)}, u32[]{:S(2)}, u32[]{:S(2)}) collective-permute-start(bf16[80,128]{1,0:T(8,128)(2,1)S(1)} %get-tuple-element.81), channel_id=1, source_target_pairs={{0,6},{2,4},{4,2},{6,0},{8,14},{10,12},{12,10},{14,8},{16,22},{18,... | collective-permute-start | bytes 61448 | tf_op jit(solution)/shard_map/ppermute | solution.py:307
  25.6 1.3 %collective-permute-start.8 = (bf16[8,64,128]{2,1,0:T(8,128)(2,1)S(1)}, bf16[8,64,128]{2,1,0:T(8,128)(2,1)S(1)}, u32[]{:S(2)}, u32[]{:S(2)}) collective-permute-start(bf16[8,64,128]{2,1,0:T(8,128)(2,1)S(1)} %shard_map.119.g), channel_id=1, source_target_pairs={{0,28},{2,30},{4,0},{6,2},{8,4},{10,6},{12,8},{14,10},{16,12},{18,... | collective-permute-start | bytes 393224 | tf_op jit(solution)/shard_map/ppermute | solution.py:307
  27.2 1.2 %collective-permute-start.14 = (bf16[80,128]{1,0:T(8,128)(2,1)S(1)}, bf16[80,128]{1,0:T(8,128)(2,1)S(1)}, u32[]{:S(2)}, u32[]{:S(2)}) collective-permute-start(bf16[80,128]{1,0:T(8,128)(2,1)S(1)} %shard_map.122.refs_3_), channel_id=1, source_target_pairs={{0,8},{2,10},{4,12},{6,14},{8,0},{10,2},{12,4},{14,6},{16,24},{18,... | collective-permute-start | bytes 61448 | tf_op jit(solution)/shard_map/ppermute | solution.py:307
  28.5 0.4 %collective-permute-start.13 = (bf16[80,128]{1,0:T(8,128)(2,1)S(1)}, bf16[80,128]{1,0:T(8,128)(2,1)S(1)}, u32[]{:S(2)}, u32[]{:S(2)}) collective-permute-start(bf16[80,128]{1,0:T(8,128)(2,1)S(1)} %shard_map.122.refs_3_), channel_id=1, source_target_pairs={{0,16},{2,18},{4,20},{6,22},{8,24},{10,26},{12,28},{14,30},{16,0},... | collective-permute-start | bytes 61448 | tf_op jit(solution)/shard_map/ppermute | solution.py:307
  28.9 2.8 %collective-permute-start.12 = (bf16[80,128]{1,0:T(8,128)(2,1)S(1)}, bf16[80,128]{1,0:T(8,128)(2,1)S(1)}, u32[]{:S(2)}, u32[]{:S(2)}) collective-permute-start(bf16[80,128]{1,0:T(8,128)(2,1)S(1)} %shard_map.122.refs_3_), channel_id=1, source_target_pairs={{0,24},{2,26},{4,28},{6,30},{8,16},{10,18},{12,20},{14,22},{16,8},... | collective-permute-start | bytes 61448 | tf_op jit(solution)/shard_map/ppermute | solution.py:307
  31.7 1.5 %shard_map.120 = (f32[9,64,128]{2,1,0:T(8,128)S(1)}, bf16[1024,128]{1,0:T(8,128)(2,1)}) custom-call(s32[1]{0:T(128)S(6)} %copy.12.count, s32[96]{0:T(128)S(1)} %get-tuple-element.49.index, bf16[24,128,128]{2,1,0:T(8,128)(2,1)S(1)} %get-tuple-element.51.tiles, bf16[8,64,128]{2,1,0:T(8,128)(2,1)S(1)} %shard_map.119.g, ...), custom_call_target="tpu_custom_call" | custom-call | flops 50331648 | bytes 1048576 | tf_op jit(solution)/shard_map/pallas_call | solution.py:433
  33.2 0.6 %collective-permute-done.14.refs_2_ = bf16[80,128]{1,0:T(8,128)(2,1)S(1)} collective-permute-done((bf16[80,128]{1,0:T(8,128)(2,1)S(1)}, bf16[80,128]{1,0:T(8,128)(2,1)S(1)}, u32[]{:S(2)}, u32[]{:S(2)}) %collective-permute-start.14) | collective-permute-done | bytes 20512 | tf_op jit(solution)/shard_map/ppermute | solution.py:307
  33.8 0.7 %collective-permute-done.12.refs_0_ = bf16[80,128]{1,0:T(8,128)(2,1)S(1)} collective-permute-done((bf16[80,128]{1,0:T(8,128)(2,1)S(1)}, bf16[80,128]{1,0:T(8,128)(2,1)S(1)}, u32[]{:S(2)}, u32[]{:S(2)}) %collective-permute-start.12) | collective-permute-done | bytes 20512 | tf_op jit(solution)/shard_map/ppermute | solution.py:307
  34.6 1.3 %shard_map.124 = (f32[9,64,128]{2,1,0:T(8,128)S(1)}, f32[9,64,128]{2,1,0:T(8,128)S(1)}) custom-call(s32[1]{0:T(128)S(6)} %copy.12.count, s32[96]{0:T(128)S(1)} %get-tuple-element.49.index, bf16[24,128,128]{2,1,0:T(8,128)(2,1)S(1)} %get-tuple-element.56.tiles2, bf16[24,128,128]{2,1,0:T(8,128)(2,1)S(1)} %get-tuple-element.57.tiles3, ...), custom_call_target="tpu_custom_call" | custom-call | flops 100663296 | bytes 1048576 | tf_op jit(solution)/shard_map/pallas_call | solution.py:446
  36.0 1.8 %shard_map.125 = (bf16[64,1024]{1,0:T(8,128)(2,1)}, f32[128,128]{1,0:T(8,128)}, f32[1,128]{1,0:T(1,128)}) custom-call(s32[1]{0:T(128)S(6)} %copy.12.count, s32[96]{0:T(128)S(1)} %get-tuple-element.49.index, bf16[24,128,128]{2,1,0:T(8,128)(2,1)S(1)} %get-tuple-element.74.tiles1, bf16[592,128]{1,0:T(8,128)(2,1)S(1)} %shard_map.123.sent, ...), custom_call_target="tpu_custom_call" | custom-call | flops 50331648 | bytes 1048576 | tf_op jit(solution)/shard_map/pallas_call | solution.py:449
  (27 shorter events, 0.9 us)
Async XLA Ops:
  0.6 11.0 %copy-start = (bf16[128,128]{1,0:T(8,128)(2,1)S(1)}, bf16[128,128]{1,0:T(8,128)(2,1)}, u32[]{:S(2)}) copy-start(bf16[128,128]{1,0:T(8,128)(2,1)} %w_ref.5) | copy-start | bytes 98308
  0.6 11.0 %copy-start.1 = (f32[128]{0:T(128)S(1)}, f32[128]{0:T(128)}, u32[]{:S(2)}) copy-start(f32[128]{0:T(128)} %param.10) | copy-start | bytes 1540
  4.1 2.5 %collective-permute-start = (bf16[8,128,128]{2,1,0:T(8,128)(2,1)S(1)}, bf16[8,128,128]{2,1,0:T(8,128)(2,1)S(1)}, u32[]{:S(2)}, u32[]{:S(2)}) collective-permute-start(bf16[8,128,128]{2,1,0:T(8,128)(2,1)S(1)} %get-tuple-element.59), channel_id=1, source_target_pairs={{0,2},{2,0},{4,6},{6,4},{8,10},{10,8},{12,14},{14,12},{16,18},{18,... | collective-permute-start | bytes 786440 | tf_op jit(solution)/shard_map/ppermute | solution.py:307
  6.7 9.0 %collective-permute-start.4 = (bf16[4,128,128]{2,1,0:T(8,128)(2,1)S(1)}, bf16[4,128,128]{2,1,0:T(8,128)(2,1)S(1)}, u32[]{:S(2)}, u32[]{:S(2)}) collective-permute-start(bf16[4,128,128]{2,1,0:T(8,128)(2,1)S(1)} %get-tuple-element.67), channel_id=1, source_target_pairs={{0,4},{2,6},{4,8},{6,10},{8,12},{10,14},{12,16},{14,18},{16,20},{1... | collective-permute-start | bytes 393224 | tf_op jit(solution)/shard_map/ppermute | solution.py:307
  8.4 7.3 %collective-permute-start.5 = (bf16[4,128,128]{2,1,0:T(8,128)(2,1)S(1)}, bf16[4,128,128]{2,1,0:T(8,128)(2,1)S(1)}, u32[]{:S(2)}, u32[]{:S(2)}) collective-permute-start(bf16[4,128,128]{2,1,0:T(8,128)(2,1)S(1)} %get-tuple-element.68), channel_id=1, source_target_pairs={{0,2},{2,8},{4,6},{6,12},{8,10},{10,16},{12,14},{14,20},{16,18},{1... | collective-permute-start | bytes 393224 | tf_op jit(solution)/shard_map/ppermute | solution.py:307
  8.4 10.7 %collective-permute-start.2 = (bf16[4,128,128]{2,1,0:T(8,128)(2,1)S(1)}, bf16[4,128,128]{2,1,0:T(8,128)(2,1)S(1)}, u32[]{:S(2)}, u32[]{:S(2)}) collective-permute-start(bf16[4,128,128]{2,1,0:T(8,128)(2,1)S(1)} %get-tuple-element.64), channel_id=1, source_target_pairs={{0,2},{2,8},{4,6},{6,12},{8,10},{10,16},{12,14},{14,20},{16,18},{1... | collective-permute-start | bytes 393224 | tf_op jit(solution)/shard_map/ppermute | solution.py:307
  10.1 9.1 %collective-permute-start.1 = (bf16[4,128,128]{2,1,0:T(8,128)(2,1)S(1)}, bf16[4,128,128]{2,1,0:T(8,128)(2,1)S(1)}, u32[]{:S(2)}, u32[]{:S(2)}) collective-permute-start(bf16[4,128,128]{2,1,0:T(8,128)(2,1)S(1)} %get-tuple-element.63), channel_id=1, source_target_pairs={{0,4},{2,6},{4,8},{6,10},{8,12},{10,14},{12,16},{14,18},{16,20},{1... | collective-permute-start | bytes 393224 | tf_op jit(solution)/shard_map/ppermute | solution.py:307
  16.6 8.9 %collective-permute-start.6 = (bf16[4,64,128]{2,1,0:T(8,128)(2,1)S(1)}, bf16[4,64,128]{2,1,0:T(8,128)(2,1)S(1)}, u32[]{:S(2)}, u32[]{:S(2)}) collective-permute-start(bf16[4,64,128]{2,1,0:T(8,128)(2,1)S(1)} %get-tuple-element.70), channel_id=1, source_target_pairs={{0,1},{1,0},{2,3},{3,2},{4,5},{5,4},{6,7},{7,6},{8,9},{9,8},{10,11... | collective-permute-start | bytes 196616 | tf_op jit(solution)/shard_map/ppermute | solution.py:307
  20.1 5.5 %collective-permute-start.3 = (bf16[4,64,128]{2,1,0:T(8,128)(2,1)S(1)}, bf16[4,64,128]{2,1,0:T(8,128)(2,1)S(1)}, u32[]{:S(2)}, u32[]{:S(2)}) collective-permute-start(bf16[4,64,128]{2,1,0:T(8,128)(2,1)S(1)} %get-tuple-element.66), channel_id=1, source_target_pairs={{0,1},{1,0},{2,3},{3,2},{4,5},{5,4},{6,7},{7,6},{8,9},{9,8},{10,11... | collective-permute-start | bytes 196616 | tf_op jit(solution)/shard_map/ppermute | solution.py:307
  22.2 4.9 %collective-permute-start.10 = (bf16[80,128]{1,0:T(8,128)(2,1)S(1)}, bf16[80,128]{1,0:T(8,128)(2,1)S(1)}, u32[]{:S(2)}, u32[]{:S(2)}) collective-permute-start(bf16[80,128]{1,0:T(8,128)(2,1)S(1)} %get-tuple-element.80.refs_0_), channel_id=1, source_target_pairs={{0,4},{2,6},{4,0},{6,2},{8,12},{10,14},{12,8},{14,10},{16,20},{18,... | collective-permute-start | bytes 61448 | tf_op jit(solution)/shard_map/ppermute | solution.py:307
  23.8 3.4 %collective-permute-start.11 = (bf16[80,128]{1,0:T(8,128)(2,1)S(1)}, bf16[80,128]{1,0:T(8,128)(2,1)S(1)}, u32[]{:S(2)}, u32[]{:S(2)}) collective-permute-start(bf16[80,128]{1,0:T(8,128)(2,1)S(1)} %get-tuple-element.81), channel_id=1, source_target_pairs={{0,6},{2,4},{4,2},{6,0},{8,14},{10,12},{12,10},{14,8},{16,22},{18,... | collective-permute-start | bytes 61448 | tf_op jit(solution)/shard_map/ppermute | solution.py:307
  25.5 1.7 %collective-permute-start.9 = (bf16[80,128]{1,0:T(8,128)(2,1)S(1)}, bf16[80,128]{1,0:T(8,128)(2,1)S(1)}, u32[]{:S(2)}, u32[]{:S(2)}) collective-permute-start(bf16[80,128]{1,0:T(8,128)(2,1)S(1)} %get-tuple-element.81), channel_id=1, source_target_pairs={{0,2},{2,0},{4,6},{6,4},{8,10},{10,8},{12,14},{14,12},{16,18},{18,... | collective-permute-start | bytes 61448 | tf_op jit(solution)/shard_map/ppermute | solution.py:307
  25.6 8.9 %collective-permute-start.8 = (bf16[8,64,128]{2,1,0:T(8,128)(2,1)S(1)}, bf16[8,64,128]{2,1,0:T(8,128)(2,1)S(1)}, u32[]{:S(2)}, u32[]{:S(2)}) collective-permute-start(bf16[8,64,128]{2,1,0:T(8,128)(2,1)S(1)} %shard_map.119.g), channel_id=1, source_target_pairs={{0,28},{2,30},{4,0},{6,2},{8,4},{10,6},{12,8},{14,10},{16,12},{18,... | collective-permute-start | bytes 393224 | tf_op jit(solution)/shard_map/ppermute | solution.py:307
  26.9 7.6 %collective-permute-start.7 = (bf16[8,64,128]{2,1,0:T(8,128)(2,1)S(1)}, bf16[8,64,128]{2,1,0:T(8,128)(2,1)S(1)}, u32[]{:S(2)}, u32[]{:S(2)}) collective-permute-start(bf16[8,64,128]{2,1,0:T(8,128)(2,1)S(1)} %shard_map.119.g), channel_id=1, source_target_pairs={{0,26},{2,0},{4,30},{6,4},{8,2},{10,8},{12,6},{14,12},{16,10},{18,... | collective-permute-start | bytes 393224 | tf_op jit(solution)/shard_map/ppermute | solution.py:307
  27.2 6.6 %collective-permute-start.14 = (bf16[80,128]{1,0:T(8,128)(2,1)S(1)}, bf16[80,128]{1,0:T(8,128)(2,1)S(1)}, u32[]{:S(2)}, u32[]{:S(2)}) collective-permute-start(bf16[80,128]{1,0:T(8,128)(2,1)S(1)} %shard_map.122.refs_3_), channel_id=1, source_target_pairs={{0,8},{2,10},{4,12},{6,14},{8,0},{10,2},{12,4},{14,6},{16,24},{18,... | collective-permute-start | bytes 61448 | tf_op jit(solution)/shard_map/ppermute | solution.py:307
  28.5 5.4 %collective-permute-start.13 = (bf16[80,128]{1,0:T(8,128)(2,1)S(1)}, bf16[80,128]{1,0:T(8,128)(2,1)S(1)}, u32[]{:S(2)}, u32[]{:S(2)}) collective-permute-start(bf16[80,128]{1,0:T(8,128)(2,1)S(1)} %shard_map.122.refs_3_), channel_id=1, source_target_pairs={{0,16},{2,18},{4,20},{6,22},{8,24},{10,26},{12,28},{14,30},{16,0},... | collective-permute-start | bytes 61448 | tf_op jit(solution)/shard_map/ppermute | solution.py:307
  28.9 5.6 %collective-permute-start.12 = (bf16[80,128]{1,0:T(8,128)(2,1)S(1)}, bf16[80,128]{1,0:T(8,128)(2,1)S(1)}, u32[]{:S(2)}, u32[]{:S(2)}) collective-permute-start(bf16[80,128]{1,0:T(8,128)(2,1)S(1)} %shard_map.122.refs_3_), channel_id=1, source_target_pairs={{0,24},{2,26},{4,28},{6,30},{8,16},{10,18},{12,20},{14,22},{16,8},... | collective-permute-start | bytes 61448 | tf_op jit(solution)/shard_map/ppermute | solution.py:307
  34.5 1.4 %collective-permute-start.15 = (bf16[592,128]{1,0:T(8,128)(2,1)S(1)}, bf16[592,128]{1,0:T(8,128)(2,1)S(1)}, u32[]{:S(2)}, u32[]{:S(2)}) collective-permute-start(bf16[592,128]{1,0:T(8,128)(2,1)S(1)} %shard_map.123.sent), channel_id=1, source_target_pairs={{0,2},{2,0},{4,6},{6,4},{8,10},{10,8},{12,14},{14,12},{16,18},{18,... | collective-permute-start | bytes 454664 | tf_op jit(solution)/shard_map/ppermute | solution.py:307

commit v11 on v8

--- a/solution.py
+++ b/solution.py
@@ -396,7 +396,9 @@
     direct = [moved(d, "dom", lambda i: i + 1 + 2 * (i % 2)) for d in direct]
     h_list = []
     for first, c, d in zip(starts, chip, direct):
-        (h,) = call(functools.partial(sum_kernel, 3, first), [half_x], [VMEM] * 3, [VMEM])(acc0, c, d)
+        (h,) = call(functools.partial(sum_kernel, 3, first), [half_x], [VMEM] * 3, [VMEM])(
+            acc0, *((c, d) if first == 0 else (d, c))
+        )
         h_list.append(h)
     acts, hts, grads, g_list = [], [], [], []
     for first, h in zip(starts, h_list):

time: 38.3 us -> 38.1 us (level)
  waiting for transfers between devices: 3.15 us -> 3.76 us
  starting transfers between devices: 21.1 us -> 20.5 us
    ppermute x16, waiting for transfers between devices: 3.15 us -> 3.76 us  [moved(): return lax.ppermute(block, axis, [(i, target(i) % n) for i in range(n)])]
    ppermute x16, starting transfers between devices: 21.1 us -> 20.5 us  [moved(): return lax.ppermute(block, axis, [(i, target(i) % n) for i in range(n)])]
  transfers between devices with their start and end apart: 16 -> 16, of which waited for: 5 -> 7; matrix products, arithmetic and copies ran while one was open for 0% -> 0% of each run, Pallas kernels for 21% -> 21%
where the time goes in v11:
time: 38.1 us; the launch traced here: 37.8 us
  starting transfers between devices  20.5 us (54%)
  Pallas kernels  12.1 us (32%)
  waiting for transfers between devices  3.76 us (10%)
  between operations  1.42 us (4%)
    ppermute x16, starting transfers between devices, moved(): return lax.ppermute(block, axis, [(i, target(i) % n) for i in range(n)])  20.5 us
    ppermute x16, waiting for transfers between devices, moved(): return lax.ppermute(block, axis, [(i, target(i) % n) for i in range(n)])  3.76 us
    pallas_call x1, Pallas kernels, shards(): call(forward_swap_kernel, [plane, plane, plane, piece_x, piece_x, slots],...  2.35 us
    pallas_call x1, Pallas kernels, shards(): call(forward_own_kernel, [totals_x, plane, jax.ShapeDtypeStruct((hid, BLO...  2.26 us
    pallas_call x2, Pallas kernels, shards(): call(functools.partial(middle_kernel, parts, first), [half_rows, half_col...  1.62 us
    pallas_call x1, Pallas kernels, shards(): call(backward_last_kernel, [jax.ShapeDtypeStruct((width, nodes), BF16), j...  1.58 us
    pallas_call x1, Pallas kernels, shards(): call(backward_own_kernel, [totals, rows], [SMEM] * 2 + [VMEM] * (2 + cut)...  1.51 us
    pallas_call x1, Pallas kernels, shards(): call(forward_send_kernel, [totals_x] + [half_x] * cut, [SMEM] * 2 + [VMEM...  1.33 us
  transfers between devices with their start and end apart: 16, of which 7 were waited for; matrix products, arithmetic and copies ran while one was open for 0% of the time, Pallas kernels for 21%

profile of v11, /device:TPU:0, one launch (start us, length us, event | category | flops | bytes accessed | tf_op | source)
XLA Modules:
  0.0 37.8 jit_solution(7535511318854720164)
XLA Ops:
  1.3 2.3 %shard_map.111 = (bf16[24,128,128]{2,1,0:T(8,128)(2,1)S(1)}, bf16[24,128,128]{2,1,0:T(8,128)(2,1)S(1)}, bf16[24,128,128]{2,1,0:T(8,128)(2,1)S(1)}, bf16[8,128,12...) custom-call(s32[1]{0:T(128)S(6)} %copy.12.count, s32[96]{0:T(128)} %src_hbm.1, s32[96]{0:T(128)} %dst_hbm.1, ...), custom_call_target="tpu_custom_call" | custom-call | flops 50331648 | bytes 1048576 | tf_op jit(solution)/shard_map/pallas_call | solution.py:347
  3.7 0.5 %collective-permute-start = (bf16[8,128,128]{2,1,0:T(8,128)(2,1)S(1)}, bf16[8,128,128]{2,1,0:T(8,128)(2,1)S(1)}, u32[]{:S(2)}, u32[]{:S(2)}) collective-permute-start(bf16[8,128,128]{2,1,0:T(8,128)(2,1)S(1)} %get-tuple-element.60), channel_id=1, source_target_pairs={{0,2},{2,0},{4,6},{6,4},{8,10},{10,8},{12,14},{14,12},{16,18},{18,... | collective-permute-start | bytes 786440 | tf_op jit(solution)/shard_map/ppermute | solution.py:307
  4.2 1.3 %shard_map.113 = (f32[9,128,128]{2,1,0:T(8,128)S(1)}, bf16[4,128,128]{2,1,0:T(8,128)(2,1)S(1)}, bf16[4,128,128]{2,1,0:T(8,128)(2,1)S(1)}) custom-call(s32[1]{0:T(128)S(6)} %copy.12.count, s32[96]{0:T(128)S(1)} %get-tuple-element.50.index, bf16[8,128,128]{2,1,0:T(8,128)(2,1)S(1)} %get-tuple-element.51.xt, bf16[24,128,128]{2,1,0:T(8,128)(2,1)S(1)} %get-tuple-element.57.tiles2, ...), custom_call_target="tpu_custom_call" | custom-call | flops 100663296 | bytes 1048576 | tf_op jit(solution)/shard_map/pallas_call | solution.py:370
  5.9 3.5 %collective-permute-start.5 = (bf16[4,128,128]{2,1,0:T(8,128)(2,1)S(1)}, bf16[4,128,128]{2,1,0:T(8,128)(2,1)S(1)}, u32[]{:S(2)}, u32[]{:S(2)}) collective-permute-start(bf16[4,128,128]{2,1,0:T(8,128)(2,1)S(1)} %get-tuple-element.70), channel_id=1, source_target_pairs={{0,4},{2,6},{4,8},{6,10},{8,12},{10,14},{12,16},{14,18},{16,20},{1... | collective-permute-start | bytes 393224 | tf_op jit(solution)/shard_map/ppermute | solution.py:307
  9.4 0.8 %collective-permute-start.1 = (bf16[4,128,128]{2,1,0:T(8,128)(2,1)S(1)}, bf16[4,128,128]{2,1,0:T(8,128)(2,1)S(1)}, u32[]{:S(2)}, u32[]{:S(2)}) collective-permute-start(bf16[4,128,128]{2,1,0:T(8,128)(2,1)S(1)} %get-tuple-element.65), channel_id=1, source_target_pairs={{0,4},{2,6},{4,8},{6,10},{8,12},{10,14},{12,16},{14,18},{16,20},{1... | collective-permute-start | bytes 393224 | tf_op jit(solution)/shard_map/ppermute | solution.py:307
  10.2 0.8 %collective-permute-start.2 = (bf16[4,128,128]{2,1,0:T(8,128)(2,1)S(1)}, bf16[4,128,128]{2,1,0:T(8,128)(2,1)S(1)}, u32[]{:S(2)}, u32[]{:S(2)}) collective-permute-start(bf16[4,128,128]{2,1,0:T(8,128)(2,1)S(1)} %get-tuple-element.66), channel_id=1, source_target_pairs={{0,2},{2,8},{4,6},{6,12},{8,10},{10,16},{12,14},{14,20},{16,18},{1... | collective-permute-start | bytes 393224 | tf_op jit(solution)/shard_map/ppermute | solution.py:307
  11.1 2.3 %shard_map.112 = (f32[9,128,128]{2,1,0:T(8,128)S(1)}, bf16[24,128,128]{2,1,0:T(8,128)(2,1)S(1)}, f32[128,128]{1,0:T(8,128)S(1)}, bf16[128,128]{1,0:T(8,128)(2,1)S(1)}, bf16[128,1024]{1,0:T(8,128)(2,1)S(1)}) custom-call(s32[1]{0:T(128)S(6)} %copy.12.count, s32[96]{0:T(128)S(1)} %get-tuple-element.50.index, bf16[8,128,128]{2,1,0:T(8,128)(2,1)S(1)} %get-tuple-element.51.xt, ...), custom_call_target="tpu_custom_call" | custom-call | flops 50331648 | bytes 1048576 | tf_op jit(solution)/shard_map/pallas_call | solution.py:382
  13.4 2.6 %collective-permute-done.5.refs_2_ = bf16[4,128,128]{2,1,0:T(8,128)(2,1)S(1)} collective-permute-done((bf16[4,128,128]{2,1,0:T(8,128)(2,1)S(1)}, bf16[4,128,128]{2,1,0:T(8,128)(2,1)S(1)}, u32[]{:S(2)}, u32[]{:S(2)}) %collective-permute-start.5) | collective-permute-done | bytes 131104 | tf_op jit(solution)/shard_map/ppermute | solution.py:307
  16.1 0.8 %shard_map.118 = (bf16[128,512]{1,0:T(8,128)(2,1)S(1)}, bf16[160,512]{1,0:T(8,128)(2,1)S(1)}, bf16[128,512]{1,0:T(8,128)(2,1)S(1)}, f32[4,64,128]{2,1,0:T(8,128)S(1)}, bf16[4,64,128]{2,1,0:T(8,128)(2,1)S(1)}) custom-call(f32[128,128]{1,0:T(8,128)S(1)} %get-tuple-element.53.bias_ref, bf16[128,128]{1,0:T(8,128)(2,1)S(1)} %copy-done, ...), custom_call_target="tpu_custom_call" | custom-call | flops 33554432 | bytes 1048576 | tf_op jit(solution)/shard_map/pallas_call | solution.py:405
  16.9 1.7 %collective-permute-start.6 = (bf16[4,64,128]{2,1,0:T(8,128)(2,1)S(1)}, bf16[4,64,128]{2,1,0:T(8,128)(2,1)S(1)}, u32[]{:S(2)}, u32[]{:S(2)}) collective-permute-start(bf16[4,64,128]{2,1,0:T(8,128)(2,1)S(1)} %get-tuple-element.72), channel_id=1, source_target_pairs={{0,1},{1,0},{2,3},{3,2},{4,5},{5,4},{6,7},{7,6},{8,9},{9,8},{10,11... | collective-permute-start | bytes 196616 | tf_op jit(solution)/shard_map/ppermute | solution.py:307
  18.6 0.2 collective-permute-done.1.refs_1_
  18.9 0.8 %shard_map.116 = (bf16[128,512]{1,0:T(8,128)(2,1)S(1)}, bf16[160,512]{1,0:T(8,128)(2,1)S(1)}, bf16[128,512]{1,0:T(8,128)(2,1)S(1)}, f32[4,64,128]{2,1,0:T(8,128)S(1)}, bf16[4,64,128]{2,1,0:T(8,128)(2,1)S(1)}) custom-call(f32[128,128]{1,0:T(8,128)S(1)} %get-tuple-element.53.bias_ref, bf16[128,128]{1,0:T(8,128)(2,1)S(1)} %copy-done, ...), custom_call_target="tpu_custom_call" | custom-call | flops 33554432 | bytes 1048576 | tf_op jit(solution)/shard_map/pallas_call | solution.py:405
  19.7 1.7 %collective-permute-start.3 = (bf16[4,64,128]{2,1,0:T(8,128)(2,1)S(1)}, bf16[4,64,128]{2,1,0:T(8,128)(2,1)S(1)}, u32[]{:S(2)}, u32[]{:S(2)}) collective-permute-start(bf16[4,64,128]{2,1,0:T(8,128)(2,1)S(1)} %get-tuple-element.68), channel_id=1, source_target_pairs={{0,1},{1,0},{2,3},{3,2},{4,5},{5,4},{6,7},{7,6},{8,9},{9,8},{10,11... | collective-permute-start | bytes 196616 | tf_op jit(solution)/shard_map/ppermute | solution.py:307
  21.4 0.2 shard_map.121
  21.6 2.7 %collective-permute-start.10 = (bf16[80,128]{1,0:T(8,128)(2,1)S(1)}, bf16[80,128]{1,0:T(8,128)(2,1)S(1)}, u32[]{:S(2)}, u32[]{:S(2)}) collective-permute-start(bf16[80,128]{1,0:T(8,128)(2,1)S(1)} %get-tuple-element.82.refs_0_), channel_id=1, source_target_pairs={{0,4},{2,6},{4,0},{6,2},{8,12},{10,14},{12,8},{14,10},{16,20},{18,... | collective-permute-start | bytes 61448 | tf_op jit(solution)/shard_map/ppermute | solution.py:307
  24.6 3.4 %collective-permute-start.8 = (bf16[8,64,128]{2,1,0:T(8,128)(2,1)S(1)}, bf16[8,64,128]{2,1,0:T(8,128)(2,1)S(1)}, u32[]{:S(2)}, u32[]{:S(2)}) collective-permute-start(bf16[8,64,128]{2,1,0:T(8,128)(2,1)S(1)} %shard_map.119.g), channel_id=1, source_target_pairs={{0,28},{2,30},{4,0},{6,2},{8,4},{10,6},{12,8},{14,10},{16,12},{18,... | collective-permute-start | bytes 393224 | tf_op jit(solution)/shard_map/ppermute | solution.py:307
  28.0 0.4 collective-permute-start.7
  28.4 1.1 %collective-permute-start.14 = (bf16[80,128]{1,0:T(8,128)(2,1)S(1)}, bf16[80,128]{1,0:T(8,128)(2,1)S(1)}, u32[]{:S(2)}, u32[]{:S(2)}) collective-permute-start(bf16[80,128]{1,0:T(8,128)(2,1)S(1)} %shard_map.122.refs_0_), channel_id=1, source_target_pairs={{0,24},{2,26},{4,28},{6,30},{8,16},{10,18},{12,20},{14,22},{16,8},... | collective-permute-start | bytes 61448 | tf_op jit(solution)/shard_map/ppermute | solution.py:307
  29.5 1.2 %collective-permute-start.13 = (bf16[80,128]{1,0:T(8,128)(2,1)S(1)}, bf16[80,128]{1,0:T(8,128)(2,1)S(1)}, u32[]{:S(2)}, u32[]{:S(2)}) collective-permute-start(bf16[80,128]{1,0:T(8,128)(2,1)S(1)} %shard_map.122.refs_0_), channel_id=1, source_target_pairs={{0,16},{2,18},{4,20},{6,22},{8,24},{10,26},{12,28},{14,30},{16,0},... | collective-permute-start | bytes 61448 | tf_op jit(solution)/shard_map/ppermute | solution.py:307
  30.7 2.2 %collective-permute-start.12 = (bf16[80,128]{1,0:T(8,128)(2,1)S(1)}, bf16[80,128]{1,0:T(8,128)(2,1)S(1)}, u32[]{:S(2)}, u32[]{:S(2)}) collective-permute-start(bf16[80,128]{1,0:T(8,128)(2,1)S(1)} %shard_map.122.refs_0_), channel_id=1, source_target_pairs={{0,8},{2,10},{4,12},{6,14},{8,0},{10,2},{12,4},{14,6},{16,24},{18,... | collective-permute-start | bytes 61448 | tf_op jit(solution)/shard_map/ppermute | solution.py:307
  32.9 1.5 %shard_map.120 = (f32[9,64,128]{2,1,0:T(8,128)S(1)}, bf16[1024,128]{1,0:T(8,128)(2,1)}) custom-call(s32[1]{0:T(128)S(6)} %copy.12.count, s32[96]{0:T(128)S(1)} %get-tuple-element.50.index, bf16[24,128,128]{2,1,0:T(8,128)(2,1)S(1)} %get-tuple-element.52.tiles, bf16[8,64,128]{2,1,0:T(8,128)(2,1)S(1)} %shard_map.119.g, ...), custom_call_target="tpu_custom_call" | custom-call | flops 50331648 | bytes 1048576 | tf_op jit(solution)/shard_map/pallas_call | solution.py:435
  34.9 0.9 %shard_map.124 = (f32[9,64,128]{2,1,0:T(8,128)S(1)}, f32[9,64,128]{2,1,0:T(8,128)S(1)}) custom-call(s32[1]{0:T(128)S(6)} %copy.12.count, s32[96]{0:T(128)S(1)} %get-tuple-element.50.index, bf16[24,128,128]{2,1,0:T(8,128)(2,1)S(1)} %get-tuple-element.57.tiles2, bf16[24,128,128]{2,1,0:T(8,128)(2,1)S(1)} %get-tuple-element.58.tiles3, ...), custom_call_target="tpu_custom_call" | custom-call | flops 100663296 | bytes 1048576 | tf_op jit(solution)/shard_map/pallas_call | solution.py:447
  35.8 0.4 %collective-permute-done.15.got = bf16[592,128]{1,0:T(8,128)(2,1)S(1)} collective-permute-done((bf16[592,128]{1,0:T(8,128)(2,1)S(1)}, bf16[592,128]{1,0:T(8,128)(2,1)S(1)}, u32[]{:S(2)}, u32[]{:S(2)}) %collective-permute-start.15) | collective-permute-done | bytes 151584 | tf_op jit(solution)/shard_map/ppermute | solution.py:307
  36.2 1.6 %shard_map.125 = (bf16[64,1024]{1,0:T(8,128)(2,1)}, f32[128,128]{1,0:T(8,128)}, f32[1,128]{1,0:T(1,128)}) custom-call(s32[1]{0:T(128)S(6)} %copy.12.count, s32[96]{0:T(128)S(1)} %get-tuple-element.50.index, bf16[24,128,128]{2,1,0:T(8,128)(2,1)S(1)} %get-tuple-element.76.tiles1, bf16[592,128]{1,0:T(8,128)(2,1)S(1)} %shard_map.123.sent, ...), custom_call_target="tpu_custom_call" | custom-call | flops 50331648 | bytes 1048576 | tf_op jit(solution)/shard_map/pallas_call | solution.py:450
  (27 shorter events, 1.3 us)
Async XLA Ops:
  0.6 10.4 %copy-start = (bf16[128,128]{1,0:T(8,128)(2,1)S(1)}, bf16[128,128]{1,0:T(8,128)(2,1)}, u32[]{:S(2)}) copy-start(bf16[128,128]{1,0:T(8,128)(2,1)} %w_ref.5) | copy-start | bytes 98308
  0.6 10.4 %copy-start.1 = (f32[128]{0:T(128)S(1)}, f32[128]{0:T(128)}, u32[]{:S(2)}) copy-start(f32[128]{0:T(128)} %param.10) | copy-start | bytes 1540
  3.7 1.9 %collective-permute-start = (bf16[8,128,128]{2,1,0:T(8,128)(2,1)S(1)}, bf16[8,128,128]{2,1,0:T(8,128)(2,1)S(1)}, u32[]{:S(2)}, u32[]{:S(2)}) collective-permute-start(bf16[8,128,128]{2,1,0:T(8,128)(2,1)S(1)} %get-tuple-element.60), channel_id=1, source_target_pairs={{0,2},{2,0},{4,6},{6,4},{8,10},{10,8},{12,14},{14,12},{16,18},{18,... | collective-permute-start | bytes 786440 | tf_op jit(solution)/shard_map/ppermute | solution.py:307
  5.6 7.8 %collective-permute-start.4 = (bf16[4,128,128]{2,1,0:T(8,128)(2,1)S(1)}, bf16[4,128,128]{2,1,0:T(8,128)(2,1)S(1)}, u32[]{:S(2)}, u32[]{:S(2)}) collective-permute-start(bf16[4,128,128]{2,1,0:T(8,128)(2,1)S(1)} %get-tuple-element.69), channel_id=1, source_target_pairs={{0,2},{2,8},{4,6},{6,12},{8,10},{10,16},{12,14},{14,20},{16,18},{1... | collective-permute-start | bytes 393224 | tf_op jit(solution)/shard_map/ppermute | solution.py:307
  5.9 10.2 %collective-permute-start.5 = (bf16[4,128,128]{2,1,0:T(8,128)(2,1)S(1)}, bf16[4,128,128]{2,1,0:T(8,128)(2,1)S(1)}, u32[]{:S(2)}, u32[]{:S(2)}) collective-permute-start(bf16[4,128,128]{2,1,0:T(8,128)(2,1)S(1)} %get-tuple-element.70), channel_id=1, source_target_pairs={{0,4},{2,6},{4,8},{6,10},{8,12},{10,14},{12,16},{14,18},{16,20},{1... | collective-permute-start | bytes 393224 | tf_op jit(solution)/shard_map/ppermute | solution.py:307
  9.4 9.5 %collective-permute-start.1 = (bf16[4,128,128]{2,1,0:T(8,128)(2,1)S(1)}, bf16[4,128,128]{2,1,0:T(8,128)(2,1)S(1)}, u32[]{:S(2)}, u32[]{:S(2)}) collective-permute-start(bf16[4,128,128]{2,1,0:T(8,128)(2,1)S(1)} %get-tuple-element.65), channel_id=1, source_target_pairs={{0,4},{2,6},{4,8},{6,10},{8,12},{10,14},{12,16},{14,18},{16,20},{1... | collective-permute-start | bytes 393224 | tf_op jit(solution)/shard_map/ppermute | solution.py:307
  10.2 8.6 %collective-permute-start.2 = (bf16[4,128,128]{2,1,0:T(8,128)(2,1)S(1)}, bf16[4,128,128]{2,1,0:T(8,128)(2,1)S(1)}, u32[]{:S(2)}, u32[]{:S(2)}) collective-permute-start(bf16[4,128,128]{2,1,0:T(8,128)(2,1)S(1)} %get-tuple-element.66), channel_id=1, source_target_pairs={{0,2},{2,8},{4,6},{6,12},{8,10},{10,16},{12,14},{14,20},{16,18},{1... | collective-permute-start | bytes 393224 | tf_op jit(solution)/shard_map/ppermute | solution.py:307
  16.9 7.6 %collective-permute-start.6 = (bf16[4,64,128]{2,1,0:T(8,128)(2,1)S(1)}, bf16[4,64,128]{2,1,0:T(8,128)(2,1)S(1)}, u32[]{:S(2)}, u32[]{:S(2)}) collective-permute-start(bf16[4,64,128]{2,1,0:T(8,128)(2,1)S(1)} %get-tuple-element.72), channel_id=1, source_target_pairs={{0,1},{1,0},{2,3},{3,2},{4,5},{5,4},{6,7},{7,6},{8,9},{9,8},{10,11... | collective-permute-start | bytes 196616 | tf_op jit(solution)/shard_map/ppermute | solution.py:307
  19.7 4.9 %collective-permute-start.3 = (bf16[4,64,128]{2,1,0:T(8,128)(2,1)S(1)}, bf16[4,64,128]{2,1,0:T(8,128)(2,1)S(1)}, u32[]{:S(2)}, u32[]{:S(2)}) collective-permute-start(bf16[4,64,128]{2,1,0:T(8,128)(2,1)S(1)} %get-tuple-element.68), channel_id=1, source_target_pairs={{0,1},{1,0},{2,3},{3,2},{4,5},{5,4},{6,7},{7,6},{8,9},{9,8},{10,11... | collective-permute-start | bytes 196616 | tf_op jit(solution)/shard_map/ppermute | solution.py:307
  21.6 6.8 %collective-permute-start.10 = (bf16[80,128]{1,0:T(8,128)(2,1)S(1)}, bf16[80,128]{1,0:T(8,128)(2,1)S(1)}, u32[]{:S(2)}, u32[]{:S(2)}) collective-permute-start(bf16[80,128]{1,0:T(8,128)(2,1)S(1)} %get-tuple-element.82.refs_0_), channel_id=1, source_target_pairs={{0,4},{2,6},{4,0},{6,2},{8,12},{10,14},{12,8},{14,10},{16,20},{18,... | collective-permute-start | bytes 61448 | tf_op jit(solution)/shard_map/ppermute | solution.py:307
  24.3 4.1 %collective-permute-start.11 = (bf16[80,128]{1,0:T(8,128)(2,1)S(1)}, bf16[80,128]{1,0:T(8,128)(2,1)S(1)}, u32[]{:S(2)}, u32[]{:S(2)}) collective-permute-start(bf16[80,128]{1,0:T(8,128)(2,1)S(1)} %get-tuple-element.83), channel_id=1, source_target_pairs={{0,6},{2,4},{4,2},{6,0},{8,14},{10,12},{12,10},{14,8},{16,22},{18,... | collective-permute-start | bytes 61448 | tf_op jit(solution)/shard_map/ppermute | solution.py:307
  24.3 4.1 %collective-permute-start.9 = (bf16[80,128]{1,0:T(8,128)(2,1)S(1)}, bf16[80,128]{1,0:T(8,128)(2,1)S(1)}, u32[]{:S(2)}, u32[]{:S(2)}) collective-permute-start(bf16[80,128]{1,0:T(8,128)(2,1)S(1)} %get-tuple-element.83), channel_id=1, source_target_pairs={{0,2},{2,0},{4,6},{6,4},{8,10},{10,8},{12,14},{14,12},{16,18},{18,... | collective-permute-start | bytes 61448 | tf_op jit(solution)/shard_map/ppermute | solution.py:307
  24.6 10.1 %collective-permute-start.8 = (bf16[8,64,128]{2,1,0:T(8,128)(2,1)S(1)}, bf16[8,64,128]{2,1,0:T(8,128)(2,1)S(1)}, u32[]{:S(2)}, u32[]{:S(2)}) collective-permute-start(bf16[8,64,128]{2,1,0:T(8,128)(2,1)S(1)} %shard_map.119.g), channel_id=1, source_target_pairs={{0,28},{2,30},{4,0},{6,2},{8,4},{10,6},{12,8},{14,10},{16,12},{18,... | collective-permute-start | bytes 393224 | tf_op jit(solution)/shard_map/ppermute | solution.py:307
  28.0 6.7 %collective-permute-start.7 = (bf16[8,64,128]{2,1,0:T(8,128)(2,1)S(1)}, bf16[8,64,128]{2,1,0:T(8,128)(2,1)S(1)}, u32[]{:S(2)}, u32[]{:S(2)}) collective-permute-start(bf16[8,64,128]{2,1,0:T(8,128)(2,1)S(1)} %shard_map.119.g), channel_id=1, source_target_pairs={{0,26},{2,0},{4,30},{6,4},{8,2},{10,8},{12,6},{14,12},{16,10},{18,... | collective-permute-start | bytes 393224 | tf_op jit(solution)/shard_map/ppermute | solution.py:307
  28.4 6.1 %collective-permute-start.14 = (bf16[80,128]{1,0:T(8,128)(2,1)S(1)}, bf16[80,128]{1,0:T(8,128)(2,1)S(1)}, u32[]{:S(2)}, u32[]{:S(2)}) collective-permute-start(bf16[80,128]{1,0:T(8,128)(2,1)S(1)} %shard_map.122.refs_0_), channel_id=1, source_target_pairs={{0,24},{2,26},{4,28},{6,30},{8,16},{10,18},{12,20},{14,22},{16,8},... | collective-permute-start | bytes 61448 | tf_op jit(solution)/shard_map/ppermute | solution.py:307
  29.5 5.1 %collective-permute-start.13 = (bf16[80,128]{1,0:T(8,128)(2,1)S(1)}, bf16[80,128]{1,0:T(8,128)(2,1)S(1)}, u32[]{:S(2)}, u32[]{:S(2)}) collective-permute-start(bf16[80,128]{1,0:T(8,128)(2,1)S(1)} %shard_map.122.refs_0_), channel_id=1, source_target_pairs={{0,16},{2,18},{4,20},{6,22},{8,24},{10,26},{12,28},{14,30},{16,0},... | collective-permute-start | bytes 61448 | tf_op jit(solution)/shard_map/ppermute | solution.py:307
  30.7 4.1 %collective-permute-start.12 = (bf16[80,128]{1,0:T(8,128)(2,1)S(1)}, bf16[80,128]{1,0:T(8,128)(2,1)S(1)}, u32[]{:S(2)}, u32[]{:S(2)}) collective-permute-start(bf16[80,128]{1,0:T(8,128)(2,1)S(1)} %shard_map.122.refs_0_), channel_id=1, source_target_pairs={{0,8},{2,10},{4,12},{6,14},{8,0},{10,2},{12,4},{14,6},{16,24},{18,... | collective-permute-start | bytes 61448 | tf_op jit(solution)/shard_map/ppermute | solution.py:307
  34.8 1.4 %collective-permute-start.15 = (bf16[592,128]{1,0:T(8,128)(2,1)S(1)}, bf16[592,128]{1,0:T(8,128)(2,1)S(1)}, u32[]{:S(2)}, u32[]{:S(2)}) collective-permute-start(bf16[592,128]{1,0:T(8,128)(2,1)S(1)} %shard_map.123.sent), channel_id=1, source_target_pairs={{0,2},{2,0},{4,6},{6,4},{8,10},{10,8},{12,14},{14,12},{16,18},{18,... | collective-permute-start | bytes 454664 | tf_op jit(solution)/shard_map/ppermute | solution.py:307

commit v12 on v6

--- a/solution.py
+++ b/solution.py
@@ -206,7 +206,7 @@
     for b in range(blocks):
         cols = slice(b * BLOCK, (b + 1) * BLOCK)
         pre = jnp.dot(w_t_ref[...], h_ref[b], preferred_element_type=F32) + bias_ref[...]
-        s = jax.nn.sigmoid(pre)
+        s = 0.5 * jnp.tanh(0.5 * pre) + 0.5
         act[:, cols] = (pre * s).astype(BF16)
         og = og_ref[:, (first + b) * BLOCK : (first + b + 1) * BLOCK].astype(F32)
         grad = (og * s * (1.0 + pre * (1.0 - s))).astype(BF16)

time: 37.1 us -> 37.5 us (1.011)
  starting transfers between devices: 18.3 us -> 18.8 us
    ppermute x16, starting transfers between devices: 18.3 us -> 18.8 us  [moved(): return lax.ppermute(block, axis, [(i, target(i) % n) for i in range(n)])]
where the time goes in v12:
time: 37.5 us; the launch traced here: 37.4 us
  starting transfers between devices  18.8 us (50%)
  Pallas kernels  12.1 us (32%)
  waiting for transfers between devices  5.07 us (14%)
  between operations  1.43 us (4%)
    ppermute x16, starting transfers between devices, moved(): return lax.ppermute(block, axis, [(i, target(i) % n) for i in range(n)])  18.8 us
    ppermute x16, waiting for transfers between devices, moved(): return lax.ppermute(block, axis, [(i, target(i) % n) for i in range(n)])  5.07 us
    pallas_call x1, Pallas kernels, shards(): call(forward_swap_kernel, [plane, plane, plane, piece_x, piece_x, slots],...  2.35 us
    pallas_call x1, Pallas kernels, shards(): call(forward_own_kernel, [totals_x, plane, jax.ShapeDtypeStruct((hid, BLO...  2.26 us
    pallas_call x2, Pallas kernels, shards(): call(functools.partial(middle_kernel, parts, first), [half_rows, half_col...  1.67 us
    pallas_call x1, Pallas kernels, shards(): call(backward_last_kernel, [jax.ShapeDtypeStruct((width, nodes), BF16), j...  1.58 us
    pallas_call x1, Pallas kernels, shards(): call(backward_own_kernel, [totals, rows], [SMEM] * 2 + [VMEM] * (2 + cut)...  1.5 us
    pallas_call x1, Pallas kernels, shards(): call(forward_send_kernel, [totals_x] + [half_x] * cut, [SMEM] * 2 + [VMEM...  1.33 us
  transfers between devices with their start and end apart: 16, of which 6 were waited for; matrix products, arithmetic and copies ran while one was open for 0% of the time, Pallas kernels for 22%

profile of v12, /device:TPU:0, one launch (start us, length us, event | category | flops | bytes accessed | tf_op | source)
XLA Modules:
  0.0 37.4 jit_solution(5788220447449933570)
XLA Ops:
  1.3 2.3 %shard_map.111 = (bf16[24,128,128]{2,1,0:T(8,128)(2,1)S(1)}, bf16[24,128,128]{2,1,0:T(8,128)(2,1)S(1)}, bf16[24,128,128]{2,1,0:T(8,128)(2,1)S(1)}, bf16[8,128,12...) custom-call(s32[1]{0:T(128)S(6)} %copy.12.count, s32[96]{0:T(128)} %src_hbm.1, s32[96]{0:T(128)} %dst_hbm.1, ...), custom_call_target="tpu_custom_call" | custom-call | flops 50331648 | bytes 1048576 | tf_op jit(solution)/shard_map/pallas_call | solution.py:347
  3.7 0.5 %collective-permute-start.1 = (bf16[8,128,128]{2,1,0:T(8,128)(2,1)S(1)}, bf16[8,128,128]{2,1,0:T(8,128)(2,1)S(1)}, u32[]{:S(2)}, u32[]{:S(2)}) collective-permute-start(bf16[8,128,128]{2,1,0:T(8,128)(2,1)S(1)} %get-tuple-element.60), channel_id=1, source_target_pairs={{0,2},{2,0},{4,6},{6,4},{8,10},{10,8},{12,14},{14,12},{16,18},{18,... | collective-permute-start | bytes 786440 | tf_op jit(solution)/shard_map/ppermute | solution.py:307
  4.2 1.3 %shard_map.113 = (f32[9,128,128]{2,1,0:T(8,128)S(1)}, bf16[4,128,128]{2,1,0:T(8,128)(2,1)S(1)}, bf16[4,128,128]{2,1,0:T(8,128)(2,1)S(1)}) custom-call(s32[1]{0:T(128)S(6)} %copy.12.count, s32[96]{0:T(128)S(1)} %get-tuple-element.49.index, bf16[8,128,128]{2,1,0:T(8,128)(2,1)S(1)} %get-tuple-element.50.xt, bf16[24,128,128]{2,1,0:T(8,128)(2,1)S(1)} %get-tuple-element.56.tiles2, ...), custom_call_target="tpu_custom_call" | custom-call | flops 100663296 | bytes 1048576 | tf_op jit(solution)/shard_map/pallas_call | solution.py:370
  5.9 3.5 %collective-permute-start.5 = (bf16[4,128,128]{2,1,0:T(8,128)(2,1)S(1)}, bf16[4,128,128]{2,1,0:T(8,128)(2,1)S(1)}, u32[]{:S(2)}, u32[]{:S(2)}) collective-permute-start(bf16[4,128,128]{2,1,0:T(8,128)(2,1)S(1)} %get-tuple-element.68), channel_id=1, source_target_pairs={{0,4},{2,6},{4,8},{6,10},{8,12},{10,14},{12,16},{14,18},{16,20},{1... | collective-permute-start | bytes 393224 | tf_op jit(solution)/shard_map/ppermute | solution.py:307
  9.3 1.4 %collective-permute-start = (bf16[4,128,128]{2,1,0:T(8,128)(2,1)S(1)}, bf16[4,128,128]{2,1,0:T(8,128)(2,1)S(1)}, u32[]{:S(2)}, u32[]{:S(2)}) collective-permute-start(bf16[4,128,128]{2,1,0:T(8,128)(2,1)S(1)} %get-tuple-element.58), channel_id=1, source_target_pairs={{0,2},{2,8},{4,6},{6,12},{8,10},{10,16},{12,14},{14,20},{16,18},{1... | collective-permute-start | bytes 393224 | tf_op jit(solution)/shard_map/ppermute | solution.py:307
  10.7 0.6 %collective-permute-start.2 = (bf16[4,128,128]{2,1,0:T(8,128)(2,1)S(1)}, bf16[4,128,128]{2,1,0:T(8,128)(2,1)S(1)}, u32[]{:S(2)}, u32[]{:S(2)}) collective-permute-start(bf16[4,128,128]{2,1,0:T(8,128)(2,1)S(1)} %get-tuple-element.64), channel_id=1, source_target_pairs={{0,4},{2,6},{4,8},{6,10},{8,12},{10,14},{12,16},{14,18},{16,20},{1... | collective-permute-start | bytes 393224 | tf_op jit(solution)/shard_map/ppermute | solution.py:307
  11.3 2.3 %shard_map.112 = (f32[9,128,128]{2,1,0:T(8,128)S(1)}, bf16[24,128,128]{2,1,0:T(8,128)(2,1)S(1)}, f32[128,128]{1,0:T(8,128)S(1)}, bf16[128,128]{1,0:T(8,128)(2,1)S(1)}, bf16[128,1024]{1,0:T(8,128)(2,1)S(1)}) custom-call(s32[1]{0:T(128)S(6)} %copy.12.count, s32[96]{0:T(128)S(1)} %get-tuple-element.49.index, bf16[8,128,128]{2,1,0:T(8,128)(2,1)S(1)} %get-tuple-element.50.xt, ...), custom_call_target="tpu_custom_call" | custom-call | flops 50331648 | bytes 1048576 | tf_op jit(solution)/shard_map/pallas_call | solution.py:382
  13.6 3.0 %collective-permute-done.5.refs_2_ = bf16[4,128,128]{2,1,0:T(8,128)(2,1)S(1)} collective-permute-done((bf16[4,128,128]{2,1,0:T(8,128)(2,1)S(1)}, bf16[4,128,128]{2,1,0:T(8,128)(2,1)S(1)}, u32[]{:S(2)}, u32[]{:S(2)}) %collective-permute-start.5) | collective-permute-done | bytes 131104 | tf_op jit(solution)/shard_map/ppermute | solution.py:307
  16.7 0.8 %shard_map.118 = (bf16[128,512]{1,0:T(8,128)(2,1)S(1)}, bf16[160,512]{1,0:T(8,128)(2,1)S(1)}, bf16[128,512]{1,0:T(8,128)(2,1)S(1)}, f32[4,64,128]{2,1,0:T(8,128)S(1)}, bf16[4,64,128]{2,1,0:T(8,128)(2,1)S(1)}) custom-call(f32[128,128]{1,0:T(8,128)S(1)} %get-tuple-element.52.bias_ref, bf16[128,128]{1,0:T(8,128)(2,1)S(1)} %copy-done, ...), custom_call_target="tpu_custom_call" | custom-call | flops 33554432 | bytes 1048576 | tf_op jit(solution)/shard_map/pallas_call | solution.py:403
  17.5 1.5 %collective-permute-start.6 = (bf16[4,64,128]{2,1,0:T(8,128)(2,1)S(1)}, bf16[4,64,128]{2,1,0:T(8,128)(2,1)S(1)}, u32[]{:S(2)}, u32[]{:S(2)}) collective-permute-start(bf16[4,64,128]{2,1,0:T(8,128)(2,1)S(1)} %get-tuple-element.70), channel_id=1, source_target_pairs={{0,1},{1,0},{2,3},{3,2},{4,5},{5,4},{6,7},{7,6},{8,9},{9,8},{10,11... | collective-permute-start | bytes 196616 | tf_op jit(solution)/shard_map/ppermute | solution.py:307
  19.0 0.8 %collective-permute-done.2.refs_2_ = bf16[4,128,128]{2,1,0:T(8,128)(2,1)S(1)} collective-permute-done((bf16[4,128,128]{2,1,0:T(8,128)(2,1)S(1)}, bf16[4,128,128]{2,1,0:T(8,128)(2,1)S(1)}, u32[]{:S(2)}, u32[]{:S(2)}) %collective-permute-start.2) | collective-permute-done | bytes 131104 | tf_op jit(solution)/shard_map/ppermute | solution.py:307
  19.9 0.8 %shard_map.116 = (bf16[128,512]{1,0:T(8,128)(2,1)S(1)}, bf16[160,512]{1,0:T(8,128)(2,1)S(1)}, bf16[128,512]{1,0:T(8,128)(2,1)S(1)}, f32[4,64,128]{2,1,0:T(8,128)S(1)}, bf16[4,64,128]{2,1,0:T(8,128)(2,1)S(1)}) custom-call(f32[128,128]{1,0:T(8,128)S(1)} %get-tuple-element.52.bias_ref, bf16[128,128]{1,0:T(8,128)(2,1)S(1)} %copy-done, ...), custom_call_target="tpu_custom_call" | custom-call | flops 33554432 | bytes 1048576 | tf_op jit(solution)/shard_map/pallas_call | solution.py:403
  20.7 1.5 %collective-permute-start.3 = (bf16[4,64,128]{2,1,0:T(8,128)(2,1)S(1)}, bf16[4,64,128]{2,1,0:T(8,128)(2,1)S(1)}, u32[]{:S(2)}, u32[]{:S(2)}) collective-permute-start(bf16[4,64,128]{2,1,0:T(8,128)(2,1)S(1)} %get-tuple-element.66), channel_id=1, source_target_pairs={{0,1},{1,0},{2,3},{3,2},{4,5},{5,4},{6,7},{7,6},{8,9},{9,8},{10,11... | collective-permute-start | bytes 196616 | tf_op jit(solution)/shard_map/ppermute | solution.py:307
  22.5 1.3 %collective-permute-start.10 = (bf16[80,128]{1,0:T(8,128)(2,1)S(1)}, bf16[80,128]{1,0:T(8,128)(2,1)S(1)}, u32[]{:S(2)}, u32[]{:S(2)}) collective-permute-start(bf16[80,128]{1,0:T(8,128)(2,1)S(1)} %get-tuple-element.80.refs_0_), channel_id=1, source_target_pairs={{0,4},{2,6},{4,0},{6,2},{8,12},{10,14},{12,8},{14,10},{16,20},{18,... | collective-permute-start | bytes 61448 | tf_op jit(solution)/shard_map/ppermute | solution.py:307
  23.8 1.7 %collective-permute-start.11 = (bf16[80,128]{1,0:T(8,128)(2,1)S(1)}, bf16[80,128]{1,0:T(8,128)(2,1)S(1)}, u32[]{:S(2)}, u32[]{:S(2)}) collective-permute-start(bf16[80,128]{1,0:T(8,128)(2,1)S(1)} %get-tuple-element.81), channel_id=1, source_target_pairs={{0,6},{2,4},{4,2},{6,0},{8,14},{10,12},{12,10},{14,8},{16,22},{18,... | collective-permute-start | bytes 61448 | tf_op jit(solution)/shard_map/ppermute | solution.py:307
  25.6 1.9 %collective-permute-start.8 = (bf16[8,64,128]{2,1,0:T(8,128)(2,1)S(1)}, bf16[8,64,128]{2,1,0:T(8,128)(2,1)S(1)}, u32[]{:S(2)}, u32[]{:S(2)}) collective-permute-start(bf16[8,64,128]{2,1,0:T(8,128)(2,1)S(1)} %shard_map.119.g), channel_id=1, source_target_pairs={{0,28},{2,30},{4,0},{6,2},{8,4},{10,6},{12,8},{14,10},{16,12},{18,... | collective-permute-start | bytes 393224 | tf_op jit(solution)/shard_map/ppermute | solution.py:307
  27.6 1.5 %collective-permute-start.14 = (bf16[80,128]{1,0:T(8,128)(2,1)S(1)}, bf16[80,128]{1,0:T(8,128)(2,1)S(1)}, u32[]{:S(2)}, u32[]{:S(2)}) collective-permute-start(bf16[80,128]{1,0:T(8,128)(2,1)S(1)} %shard_map.122.refs_0_), channel_id=1, source_target_pairs={{0,24},{2,26},{4,28},{6,30},{8,16},{10,18},{12,20},{14,22},{16,8},... | collective-permute-start | bytes 61448 | tf_op jit(solution)/shard_map/ppermute | solution.py:307
  29.0 1.5 %collective-permute-start.13 = (bf16[80,128]{1,0:T(8,128)(2,1)S(1)}, bf16[80,128]{1,0:T(8,128)(2,1)S(1)}, u32[]{:S(2)}, u32[]{:S(2)}) collective-permute-start(bf16[80,128]{1,0:T(8,128)(2,1)S(1)} %shard_map.122.refs_0_), channel_id=1, source_target_pairs={{0,16},{2,18},{4,20},{6,22},{8,24},{10,26},{12,28},{14,30},{16,0},... | collective-permute-start | bytes 61448 | tf_op jit(solution)/shard_map/ppermute | solution.py:307
  30.6 1.5 %collective-permute-start.12 = (bf16[80,128]{1,0:T(8,128)(2,1)S(1)}, bf16[80,128]{1,0:T(8,128)(2,1)S(1)}, u32[]{:S(2)}, u32[]{:S(2)}) collective-permute-start(bf16[80,128]{1,0:T(8,128)(2,1)S(1)} %shard_map.122.refs_0_), channel_id=1, source_target_pairs={{0,8},{2,10},{4,12},{6,14},{8,0},{10,2},{12,4},{14,6},{16,24},{18,... | collective-permute-start | bytes 61448 | tf_op jit(solution)/shard_map/ppermute | solution.py:307
  32.0 1.5 %shard_map.120 = (f32[9,64,128]{2,1,0:T(8,128)S(1)}, bf16[1024,128]{1,0:T(8,128)(2,1)}) custom-call(s32[1]{0:T(128)S(6)} %copy.12.count, s32[96]{0:T(128)S(1)} %get-tuple-element.49.index, bf16[24,128,128]{2,1,0:T(8,128)(2,1)S(1)} %get-tuple-element.51.tiles, bf16[8,64,128]{2,1,0:T(8,128)(2,1)S(1)} %shard_map.119.g, ...), custom_call_target="tpu_custom_call" | custom-call | flops 50331648 | bytes 1048576 | tf_op jit(solution)/shard_map/pallas_call | solution.py:433
  33.6 0.4 %collective-permute-done.13.refs_2_ = bf16[80,128]{1,0:T(8,128)(2,1)S(1)} collective-permute-done((bf16[80,128]{1,0:T(8,128)(2,1)S(1)}, bf16[80,128]{1,0:T(8,128)(2,1)S(1)}, u32[]{:S(2)}, u32[]{:S(2)}) %collective-permute-start.13) | collective-permute-done | bytes 20512 | tf_op jit(solution)/shard_map/ppermute | solution.py:307
  34.5 0.9 %shard_map.124 = (f32[9,64,128]{2,1,0:T(8,128)S(1)}, f32[9,64,128]{2,1,0:T(8,128)S(1)}) custom-call(s32[1]{0:T(128)S(6)} %copy.12.count, s32[96]{0:T(128)S(1)} %get-tuple-element.49.index, bf16[24,128,128]{2,1,0:T(8,128)(2,1)S(1)} %get-tuple-element.56.tiles2, bf16[24,128,128]{2,1,0:T(8,128)(2,1)S(1)} %get-tuple-element.57.tiles3, ...), custom_call_target="tpu_custom_call" | custom-call | flops 100663296 | bytes 1048576 | tf_op jit(solution)/shard_map/pallas_call | solution.py:445
  35.4 0.4 %collective-permute-done.15.got = bf16[592,128]{1,0:T(8,128)(2,1)S(1)} collective-permute-done((bf16[592,128]{1,0:T(8,128)(2,1)S(1)}, bf16[592,128]{1,0:T(8,128)(2,1)S(1)}, u32[]{:S(2)}, u32[]{:S(2)}) %collective-permute-start.15) | collective-permute-done | bytes 151584 | tf_op jit(solution)/shard_map/ppermute | solution.py:307
  35.8 1.6 %shard_map.125 = (bf16[64,1024]{1,0:T(8,128)(2,1)}, f32[128,128]{1,0:T(8,128)}, f32[1,128]{1,0:T(1,128)}) custom-call(s32[1]{0:T(128)S(6)} %copy.12.count, s32[96]{0:T(128)S(1)} %get-tuple-element.49.index, bf16[24,128,128]{2,1,0:T(8,128)(2,1)S(1)} %get-tuple-element.74.tiles1, bf16[592,128]{1,0:T(8,128)(2,1)S(1)} %shard_map.123.sent, ...), custom_call_target="tpu_custom_call" | custom-call | flops 50331648 | bytes 1048576 | tf_op jit(solution)/shard_map/pallas_call | solution.py:448
  (27 shorter events, 1.3 us)
Async XLA Ops:
  0.6 10.7 %copy-start = (bf16[128,128]{1,0:T(8,128)(2,1)S(1)}, bf16[128,128]{1,0:T(8,128)(2,1)}, u32[]{:S(2)}) copy-start(bf16[128,128]{1,0:T(8,128)(2,1)} %w_ref.5) | copy-start | bytes 98308
  0.6 10.7 %copy-start.1 = (f32[128]{0:T(128)S(1)}, f32[128]{0:T(128)}, u32[]{:S(2)}) copy-start(f32[128]{0:T(128)} %param.10) | copy-start | bytes 1540
  3.7 1.9 %collective-permute-start.1 = (bf16[8,128,128]{2,1,0:T(8,128)(2,1)S(1)}, bf16[8,128,128]{2,1,0:T(8,128)(2,1)S(1)}, u32[]{:S(2)}, u32[]{:S(2)}) collective-permute-start(bf16[8,128,128]{2,1,0:T(8,128)(2,1)S(1)} %get-tuple-element.60), channel_id=1, source_target_pairs={{0,2},{2,0},{4,6},{6,4},{8,10},{10,8},{12,14},{14,12},{16,18},{18,... | collective-permute-start | bytes 786440 | tf_op jit(solution)/shard_map/ppermute | solution.py:307
  5.6 8.0 %collective-permute-start.4 = (bf16[4,128,128]{2,1,0:T(8,128)(2,1)S(1)}, bf16[4,128,128]{2,1,0:T(8,128)(2,1)S(1)}, u32[]{:S(2)}, u32[]{:S(2)}) collective-permute-start(bf16[4,128,128]{2,1,0:T(8,128)(2,1)S(1)} %get-tuple-element.67), channel_id=1, source_target_pairs={{0,2},{2,8},{4,6},{6,12},{8,10},{10,16},{12,14},{14,20},{16,18},{1... | collective-permute-start | bytes 393224 | tf_op jit(solution)/shard_map/ppermute | solution.py:307
  5.9 10.8 %collective-permute-start.5 = (bf16[4,128,128]{2,1,0:T(8,128)(2,1)S(1)}, bf16[4,128,128]{2,1,0:T(8,128)(2,1)S(1)}, u32[]{:S(2)}, u32[]{:S(2)}) collective-permute-start(bf16[4,128,128]{2,1,0:T(8,128)(2,1)S(1)} %get-tuple-element.68), channel_id=1, source_target_pairs={{0,4},{2,6},{4,8},{6,10},{8,12},{10,14},{12,16},{14,18},{16,20},{1... | collective-permute-start | bytes 393224 | tf_op jit(solution)/shard_map/ppermute | solution.py:307
  9.3 9.7 %collective-permute-start = (bf16[4,128,128]{2,1,0:T(8,128)(2,1)S(1)}, bf16[4,128,128]{2,1,0:T(8,128)(2,1)S(1)}, u32[]{:S(2)}, u32[]{:S(2)}) collective-permute-start(bf16[4,128,128]{2,1,0:T(8,128)(2,1)S(1)} %get-tuple-element.58), channel_id=1, source_target_pairs={{0,2},{2,8},{4,6},{6,12},{8,10},{10,16},{12,14},{14,20},{16,18},{1... | collective-permute-start | bytes 393224 | tf_op jit(solution)/shard_map/ppermute | solution.py:307
  10.7 9.1 %collective-permute-start.2 = (bf16[4,128,128]{2,1,0:T(8,128)(2,1)S(1)}, bf16[4,128,128]{2,1,0:T(8,128)(2,1)S(1)}, u32[]{:S(2)}, u32[]{:S(2)}) collective-permute-start(bf16[4,128,128]{2,1,0:T(8,128)(2,1)S(1)} %get-tuple-element.64), channel_id=1, source_target_pairs={{0,4},{2,6},{4,8},{6,10},{8,12},{10,14},{12,16},{14,18},{16,20},{1... | collective-permute-start | bytes 393224 | tf_op jit(solution)/shard_map/ppermute | solution.py:307
  17.5 8.0 %collective-permute-start.6 = (bf16[4,64,128]{2,1,0:T(8,128)(2,1)S(1)}, bf16[4,64,128]{2,1,0:T(8,128)(2,1)S(1)}, u32[]{:S(2)}, u32[]{:S(2)}) collective-permute-start(bf16[4,64,128]{2,1,0:T(8,128)(2,1)S(1)} %get-tuple-element.70), channel_id=1, source_target_pairs={{0,1},{1,0},{2,3},{3,2},{4,5},{5,4},{6,7},{7,6},{8,9},{9,8},{10,11... | collective-permute-start | bytes 196616 | tf_op jit(solution)/shard_map/ppermute | solution.py:307
  20.7 4.8 %collective-permute-start.3 = (bf16[4,64,128]{2,1,0:T(8,128)(2,1)S(1)}, bf16[4,64,128]{2,1,0:T(8,128)(2,1)S(1)}, u32[]{:S(2)}, u32[]{:S(2)}) collective-permute-start(bf16[4,64,128]{2,1,0:T(8,128)(2,1)S(1)} %get-tuple-element.66), channel_id=1, source_target_pairs={{0,1},{1,0},{2,3},{3,2},{4,5},{5,4},{6,7},{7,6},{8,9},{9,8},{10,11... | collective-permute-start | bytes 196616 | tf_op jit(solution)/shard_map/ppermute | solution.py:307
  22.5 5.1 %collective-permute-start.10 = (bf16[80,128]{1,0:T(8,128)(2,1)S(1)}, bf16[80,128]{1,0:T(8,128)(2,1)S(1)}, u32[]{:S(2)}, u32[]{:S(2)}) collective-permute-start(bf16[80,128]{1,0:T(8,128)(2,1)S(1)} %get-tuple-element.80.refs_0_), channel_id=1, source_target_pairs={{0,4},{2,6},{4,0},{6,2},{8,12},{10,14},{12,8},{14,10},{16,20},{18,... | collective-permute-start | bytes 61448 | tf_op jit(solution)/shard_map/ppermute | solution.py:307
  23.8 3.7 %collective-permute-start.11 = (bf16[80,128]{1,0:T(8,128)(2,1)S(1)}, bf16[80,128]{1,0:T(8,128)(2,1)S(1)}, u32[]{:S(2)}, u32[]{:S(2)}) collective-permute-start(bf16[80,128]{1,0:T(8,128)(2,1)S(1)} %get-tuple-element.81), channel_id=1, source_target_pairs={{0,6},{2,4},{4,2},{6,0},{8,14},{10,12},{12,10},{14,8},{16,22},{18,... | collective-permute-start | bytes 61448 | tf_op jit(solution)/shard_map/ppermute | solution.py:307
  25.5 2.0 %collective-permute-start.9 = (bf16[80,128]{1,0:T(8,128)(2,1)S(1)}, bf16[80,128]{1,0:T(8,128)(2,1)S(1)}, u32[]{:S(2)}, u32[]{:S(2)}) collective-permute-start(bf16[80,128]{1,0:T(8,128)(2,1)S(1)} %get-tuple-element.81), channel_id=1, source_target_pairs={{0,2},{2,0},{4,6},{6,4},{8,10},{10,8},{12,14},{14,12},{16,18},{18,... | collective-permute-start | bytes 61448 | tf_op jit(solution)/shard_map/ppermute | solution.py:307
  25.6 8.8 %collective-permute-start.8 = (bf16[8,64,128]{2,1,0:T(8,128)(2,1)S(1)}, bf16[8,64,128]{2,1,0:T(8,128)(2,1)S(1)}, u32[]{:S(2)}, u32[]{:S(2)}) collective-permute-start(bf16[8,64,128]{2,1,0:T(8,128)(2,1)S(1)} %shard_map.119.g), channel_id=1, source_target_pairs={{0,28},{2,30},{4,0},{6,2},{8,4},{10,6},{12,8},{14,10},{16,12},{18,... | collective-permute-start | bytes 393224 | tf_op jit(solution)/shard_map/ppermute | solution.py:307
  27.5 6.8 %collective-permute-start.7 = (bf16[8,64,128]{2,1,0:T(8,128)(2,1)S(1)}, bf16[8,64,128]{2,1,0:T(8,128)(2,1)S(1)}, u32[]{:S(2)}, u32[]{:S(2)}) collective-permute-start(bf16[8,64,128]{2,1,0:T(8,128)(2,1)S(1)} %shard_map.119.g), channel_id=1, source_target_pairs={{0,26},{2,0},{4,30},{6,4},{8,2},{10,8},{12,6},{14,12},{16,10},{18,... | collective-permute-start | bytes 393224 | tf_op jit(solution)/shard_map/ppermute | solution.py:307
  27.6 6.0 %collective-permute-start.14 = (bf16[80,128]{1,0:T(8,128)(2,1)S(1)}, bf16[80,128]{1,0:T(8,128)(2,1)S(1)}, u32[]{:S(2)}, u32[]{:S(2)}) collective-permute-start(bf16[80,128]{1,0:T(8,128)(2,1)S(1)} %shard_map.122.refs_0_), channel_id=1, source_target_pairs={{0,24},{2,26},{4,28},{6,30},{8,16},{10,18},{12,20},{14,22},{16,8},... | collective-permute-start | bytes 61448 | tf_op jit(solution)/shard_map/ppermute | solution.py:307
  29.0 5.0 %collective-permute-start.13 = (bf16[80,128]{1,0:T(8,128)(2,1)S(1)}, bf16[80,128]{1,0:T(8,128)(2,1)S(1)}, u32[]{:S(2)}, u32[]{:S(2)}) collective-permute-start(bf16[80,128]{1,0:T(8,128)(2,1)S(1)} %shard_map.122.refs_0_), channel_id=1, source_target_pairs={{0,16},{2,18},{4,20},{6,22},{8,24},{10,26},{12,28},{14,30},{16,0},... | collective-permute-start | bytes 61448 | tf_op jit(solution)/shard_map/ppermute | solution.py:307
  30.6 3.8 %collective-permute-start.12 = (bf16[80,128]{1,0:T(8,128)(2,1)S(1)}, bf16[80,128]{1,0:T(8,128)(2,1)S(1)}, u32[]{:S(2)}, u32[]{:S(2)}) collective-permute-start(bf16[80,128]{1,0:T(8,128)(2,1)S(1)} %shard_map.122.refs_0_), channel_id=1, source_target_pairs={{0,8},{2,10},{4,12},{6,14},{8,0},{10,2},{12,4},{14,6},{16,24},{18,... | collective-permute-start | bytes 61448 | tf_op jit(solution)/shard_map/ppermute | solution.py:307
  34.4 1.4 %collective-permute-start.15 = (bf16[592,128]{1,0:T(8,128)(2,1)S(1)}, bf16[592,128]{1,0:T(8,128)(2,1)S(1)}, u32[]{:S(2)}, u32[]{:S(2)}) collective-permute-start(bf16[592,128]{1,0:T(8,128)(2,1)S(1)} %shard_map.123.sent), channel_id=1, source_target_pairs={{0,2},{2,0},{4,6},{6,4},{8,10},{10,8},{12,14},{14,12},{16,18},{18,... | collective-permute-start | bytes 454664 | tf_op jit(solution)/shard_map/ppermute | solution.py:307
